TPU v7x, 128 devices: a whole 4x4x4 slice. The times are simulated.
128 devices in a mesh: ctx: 32 (over y, z, core), zero: 4 (over x).
Axes of the slice: x: 4, y: 4, z: 4, core: 2. Of those that a mesh axis runs over, the one named last changes fastest.
Arguments:
- inputs: bfloat16 [4, 4096, 2048], P('zero', 'ctx'), may hold values from -6 to 6
- grad_out: bfloat16 [4, 4096, 1024], P('zero', 'ctx'), may hold values from -6 to 6
- saved: float32 [4, 32, 8, 128, 128], P('zero', 'ctx'), may hold values from -6 to 6
- w_qkv: bfloat16 [2048, 3072], P('zero'), may hold values from -0.125 to 0.125
Outputs:
- grad_x: bfloat16 [4, 4096, 2048], P('zero', 'ctx')
- grad_w: float32 [2048, 3072], P(('ctx', 'zero'))
All inputs are finite; a program needn't handle non-finite values.
Results may differ from a plain program's by a relative error of at most 0.012.
Values may be sent and summed in bfloat16 or wider, within the bound.
No kernel may reach another device: no remote copies, remote signals or barrier semaphores. Data moves between devices by JAX's collectives and lax.ppermute only.
A program may use at most 192 MiB of HBM per device.

v0:
```python
import jax
import jax.numpy as jnp
from jax import lax
from jax.sharding import PartitionSpec as P


def passed_along(block, axis, distance):
    devices = range(lax.axis_size(axis))
    route = [(i - distance, i) for i in devices if i - distance in devices]
    return lax.ppermute(block, axis, route)


def body(inputs, grad_out, saved, w_qkv):
    full_w = lax.all_gather(w_qkv, "zero", axis=0, tiled=True)
    rows = inputs[0]
    cot = grad_out[0]
    state = saved[0, 0]
    tokens = rows.shape[0]
    width = cot.shape[1]
    heads = state.shape[0]
    head_size = state.shape[1]
    length = tokens * lax.axis_size("ctx")
    alpha = 1.0 / head_size**0.5
    beta = 1.0 / (head_size * length) ** 0.5
    qkv = jnp.dot(rows, full_w, preferred_element_type=jnp.float32).astype(jnp.bfloat16)
    query = qkv[:, :width].reshape(tokens, heads, head_size)
    keyed = qkv[:, width : 2 * width].reshape(tokens, heads, head_size)
    valued = qkv[:, 2 * width :].reshape(tokens, heads, head_size)
    cotr = cot.reshape(tokens, heads, head_size)
    local_r = jnp.einsum("thi,thj->hij", query, cotr, preferred_element_type=jnp.float32)
    empty = jnp.zeros_like(local_r)

    def passing(step, received):
        return passed_along(local_r + received, "ctx", -1)

    later = lax.fori_loop(0, lax.axis_size("ctx") - 1, passing, empty)
    position = jnp.arange(tokens)
    mask = (position[:, None] >= position[None, :])[None]
    first = jnp.where(
        mask, jnp.einsum("thj,shj->hts", cotr, valued, preferred_element_type=jnp.float32), 0.0
    ).astype(jnp.bfloat16)
    second = jnp.where(
        mask, jnp.einsum("thi,shi->hts", query, keyed, preferred_element_type=jnp.float32), 0.0
    ).astype(jnp.bfloat16)
    highest = lax.Precision.HIGHEST
    grad_q = alpha * jnp.einsum(
        "thj,hij->thi", cotr.astype(jnp.float32), state, precision=highest
    ) + beta * jnp.einsum("hts,shi->thi", first, keyed, preferred_element_type=jnp.float32)
    grad_k = beta * (
        jnp.einsum("hts,thi->shi", first, query, preferred_element_type=jnp.float32)
        + jnp.einsum("shj,hij->shi", valued.astype(jnp.float32), later, precision=highest)
    )
    grad_v = beta * (
        jnp.einsum("hts,thj->shj", second, cotr, preferred_element_type=jnp.float32)
        + jnp.einsum("shi,hij->shj", keyed.astype(jnp.float32), later, precision=highest)
    )
    dqkv = jnp.concatenate(
        [
            grad_q.reshape(tokens, width),
            grad_k.reshape(tokens, width),
            grad_v.reshape(tokens, width),
        ],
        axis=1,
    ).astype(jnp.bfloat16)
    grad_x = lax.dot_general(
        dqkv, full_w, (((1,), (1,)), ((), ())), preferred_element_type=jnp.float32
    ).astype(jnp.bfloat16)
    scale = 1.0 / (length * lax.axis_size("zero")) ** 0.5
    owned = lax.psum_scatter(
        lax.dot_general(rows, dqkv, (((0,), (0,)), ((), ())), preferred_element_type=jnp.float32),
        ("ctx", "zero"),
        scatter_dimension=0,
        tiled=True,
    )
    return (grad_x[None], owned * scale)


def solution(mesh):
    in_specs = (
        P("zero", "ctx", None),
        P("zero", "ctx", None),
        P("zero", "ctx", None, None, None),
        P("zero", None),
    )
    out_specs = (P("zero", "ctx", None), P(("ctx", "zero"), None))
    return jax.shard_map(body, mesh=mesh, in_specs=in_specs, out_specs=out_specs, check_vma=False)
```

profile of v0, /device:TPU:1, one launch (start us, length us, event | category | flops | bytes accessed | tf_op | source)
XLA Modules:
  0.0 829.6 jit_solution(2090666328456369642)
XLA Ops:
  8.8 122.7 %all-gather.2.cloned.1.call-done = bf16[2048,3072]{1,0:T(8,128)(2,1)} async-done(((bf16[512,3072]{1,0:T(8,128)(2,1)}), bf16[2048,3072]{1,0:T(8,128)(2,1)}) %all-gather.2.cloned.1.call-update) | async-done | bytes 12582928 | tf_op jit(solution)/shard_map/all_gather | solution.py:14
  131.5 6.4 convolution_convert_fusion
  139.6 358.1 %while.10 = (s32[]{:T(128)}, f32[8,128,128]{2,1,0:T(8,128)S(1)}, f32[8,128,128]{2,1,0:T(8,128)S(1)}, s32[]{:T(128)}) while((s32[]{:T(128)}, f32[8,128,128]{2,1,0:T(8,128)S(1)}, f32[8,128,128]{2,1,0:T(8,128)S(1)}, s32[]{:T(128)}) %tuple.28), condition=%wide.region_1.0_spmd, body=%wide.region_0.0_spmd.sunk | while | flops 131074 | bytes 3670109 | solution.py:36
  139.7 2.6 collective-permute-start
  142.3 8.0 collective-permute-done
  150.4 1.9 collective-permute-start
  152.3 8.6 %collective-permute-done = f32[8,128,128]{2,1,0:T(8,128)S(1)} collective-permute-done((f32[8,128,128]{2,1,0:T(8,128)S(1)}, f32[8,128,128]{2,1,0:T(8,128)S(1)}, u32[]{:S(2)}, u32[]{:S(2)}) %collective-permute-start) | collective-permute-done | bytes 524320 | tf_op jit(solution)/shard_map/while/body/eval_jaxpr/ppermute | solution.py:10
  162.9 8.6 %collective-permute-done = f32[8,128,128]{2,1,0:T(8,128)S(1)} collective-permute-done((f32[8,128,128]{2,1,0:T(8,128)S(1)}, f32[8,128,128]{2,1,0:T(8,128)S(1)}, u32[]{:S(2)}, u32[]{:S(2)}) %collective-permute-start) | collective-permute-done | bytes 524320 | tf_op jit(solution)/shard_map/while/body/eval_jaxpr/ppermute | solution.py:10
  173.4 8.6 %collective-permute-done = f32[8,128,128]{2,1,0:T(8,128)S(1)} collective-permute-done((f32[8,128,128]{2,1,0:T(8,128)S(1)}, f32[8,128,128]{2,1,0:T(8,128)S(1)}, u32[]{:S(2)}, u32[]{:S(2)}) %collective-permute-start) | collective-permute-done | bytes 524320 | tf_op jit(solution)/shard_map/while/body/eval_jaxpr/ppermute | solution.py:10
  182.1 1.9 collective-permute-start
  184.0 8.6 %collective-permute-done = f32[8,128,128]{2,1,0:T(8,128)S(1)} collective-permute-done((f32[8,128,128]{2,1,0:T(8,128)S(1)}, f32[8,128,128]{2,1,0:T(8,128)S(1)}, u32[]{:S(2)}, u32[]{:S(2)}) %collective-permute-start) | collective-permute-done | bytes 524320 | tf_op jit(solution)/shard_map/while/body/eval_jaxpr/ppermute | solution.py:10
  194.6 8.6 %collective-permute-done = f32[8,128,128]{2,1,0:T(8,128)S(1)} collective-permute-done((f32[8,128,128]{2,1,0:T(8,128)S(1)}, f32[8,128,128]{2,1,0:T(8,128)S(1)}, u32[]{:S(2)}, u32[]{:S(2)}) %collective-permute-start) | collective-permute-done | bytes 524320 | tf_op jit(solution)/shard_map/while/body/eval_jaxpr/ppermute | solution.py:10
  205.1 8.6 %collective-permute-done = f32[8,128,128]{2,1,0:T(8,128)S(1)} collective-permute-done((f32[8,128,128]{2,1,0:T(8,128)S(1)}, f32[8,128,128]{2,1,0:T(8,128)S(1)}, u32[]{:S(2)}, u32[]{:S(2)}) %collective-permute-start) | collective-permute-done | bytes 524320 | tf_op jit(solution)/shard_map/while/body/eval_jaxpr/ppermute | solution.py:10
  213.7 1.9 collective-permute-start
  215.7 8.6 %collective-permute-done = f32[8,128,128]{2,1,0:T(8,128)S(1)} collective-permute-done((f32[8,128,128]{2,1,0:T(8,128)S(1)}, f32[8,128,128]{2,1,0:T(8,128)S(1)}, u32[]{:S(2)}, u32[]{:S(2)}) %collective-permute-start) | collective-permute-done | bytes 524320 | tf_op jit(solution)/shard_map/while/body/eval_jaxpr/ppermute | solution.py:10
  226.2 8.6 %collective-permute-done = f32[8,128,128]{2,1,0:T(8,128)S(1)} collective-permute-done((f32[8,128,128]{2,1,0:T(8,128)S(1)}, f32[8,128,128]{2,1,0:T(8,128)S(1)}, u32[]{:S(2)}, u32[]{:S(2)}) %collective-permute-start) | collective-permute-done | bytes 524320 | tf_op jit(solution)/shard_map/while/body/eval_jaxpr/ppermute | solution.py:10
  236.8 8.6 %collective-permute-done = f32[8,128,128]{2,1,0:T(8,128)S(1)} collective-permute-done((f32[8,128,128]{2,1,0:T(8,128)S(1)}, f32[8,128,128]{2,1,0:T(8,128)S(1)}, u32[]{:S(2)}, u32[]{:S(2)}) %collective-permute-start) | collective-permute-done | bytes 524320 | tf_op jit(solution)/shard_map/while/body/eval_jaxpr/ppermute | solution.py:10
  245.4 1.9 collective-permute-start
  247.4 8.6 %collective-permute-done = f32[8,128,128]{2,1,0:T(8,128)S(1)} collective-permute-done((f32[8,128,128]{2,1,0:T(8,128)S(1)}, f32[8,128,128]{2,1,0:T(8,128)S(1)}, u32[]{:S(2)}, u32[]{:S(2)}) %collective-permute-start) | collective-permute-done | bytes 524320 | tf_op jit(solution)/shard_map/while/body/eval_jaxpr/ppermute | solution.py:10
  257.9 8.6 %collective-permute-done = f32[8,128,128]{2,1,0:T(8,128)S(1)} collective-permute-done((f32[8,128,128]{2,1,0:T(8,128)S(1)}, f32[8,128,128]{2,1,0:T(8,128)S(1)}, u32[]{:S(2)}, u32[]{:S(2)}) %collective-permute-start) | collective-permute-done | bytes 524320 | tf_op jit(solution)/shard_map/while/body/eval_jaxpr/ppermute | solution.py:10
  268.5 8.6 %collective-permute-done = f32[8,128,128]{2,1,0:T(8,128)S(1)} collective-permute-done((f32[8,128,128]{2,1,0:T(8,128)S(1)}, f32[8,128,128]{2,1,0:T(8,128)S(1)}, u32[]{:S(2)}, u32[]{:S(2)}) %collective-permute-start) | collective-permute-done | bytes 524320 | tf_op jit(solution)/shard_map/while/body/eval_jaxpr/ppermute | solution.py:10
  277.1 1.9 collective-permute-start
  279.0 8.6 %collective-permute-done = f32[8,128,128]{2,1,0:T(8,128)S(1)} collective-permute-done((f32[8,128,128]{2,1,0:T(8,128)S(1)}, f32[8,128,128]{2,1,0:T(8,128)S(1)}, u32[]{:S(2)}, u32[]{:S(2)}) %collective-permute-start) | collective-permute-done | bytes 524320 | tf_op jit(solution)/shard_map/while/body/eval_jaxpr/ppermute | solution.py:10
  289.6 8.6 %collective-permute-done = f32[8,128,128]{2,1,0:T(8,128)S(1)} collective-permute-done((f32[8,128,128]{2,1,0:T(8,128)S(1)}, f32[8,128,128]{2,1,0:T(8,128)S(1)}, u32[]{:S(2)}, u32[]{:S(2)}) %collective-permute-start) | collective-permute-done | bytes 524320 | tf_op jit(solution)/shard_map/while/body/eval_jaxpr/ppermute | solution.py:10
  300.2 8.6 %collective-permute-done = f32[8,128,128]{2,1,0:T(8,128)S(1)} collective-permute-done((f32[8,128,128]{2,1,0:T(8,128)S(1)}, f32[8,128,128]{2,1,0:T(8,128)S(1)}, u32[]{:S(2)}, u32[]{:S(2)}) %collective-permute-start) | collective-permute-done | bytes 524320 | tf_op jit(solution)/shard_map/while/body/eval_jaxpr/ppermute | solution.py:10
  310.7 9.6 %collective-permute-done = f32[8,128,128]{2,1,0:T(8,128)S(1)} collective-permute-done((f32[8,128,128]{2,1,0:T(8,128)S(1)}, f32[8,128,128]{2,1,0:T(8,128)S(1)}, u32[]{:S(2)}, u32[]{:S(2)}) %collective-permute-start) | collective-permute-done | bytes 524320 | tf_op jit(solution)/shard_map/while/body/eval_jaxpr/ppermute | solution.py:10
  320.4 1.9 collective-permute-start
  322.3 10.7 %collective-permute-done = f32[8,128,128]{2,1,0:T(8,128)S(1)} collective-permute-done((f32[8,128,128]{2,1,0:T(8,128)S(1)}, f32[8,128,128]{2,1,0:T(8,128)S(1)}, u32[]{:S(2)}, u32[]{:S(2)}) %collective-permute-start) | collective-permute-done | bytes 524320 | tf_op jit(solution)/shard_map/while/body/eval_jaxpr/ppermute | solution.py:10
  333.1 1.9 collective-permute-start
  335.0 10.7 %collective-permute-done = f32[8,128,128]{2,1,0:T(8,128)S(1)} collective-permute-done((f32[8,128,128]{2,1,0:T(8,128)S(1)}, f32[8,128,128]{2,1,0:T(8,128)S(1)}, u32[]{:S(2)}, u32[]{:S(2)}) %collective-permute-start) | collective-permute-done | bytes 524320 | tf_op jit(solution)/shard_map/while/body/eval_jaxpr/ppermute | solution.py:10
  345.7 1.9 collective-permute-start
  347.7 10.7 %collective-permute-done = f32[8,128,128]{2,1,0:T(8,128)S(1)} collective-permute-done((f32[8,128,128]{2,1,0:T(8,128)S(1)}, f32[8,128,128]{2,1,0:T(8,128)S(1)}, u32[]{:S(2)}, u32[]{:S(2)}) %collective-permute-start) | collective-permute-done | bytes 524320 | tf_op jit(solution)/shard_map/while/body/eval_jaxpr/ppermute | solution.py:10
  360.3 10.7 %collective-permute-done = f32[8,128,128]{2,1,0:T(8,128)S(1)} collective-permute-done((f32[8,128,128]{2,1,0:T(8,128)S(1)}, f32[8,128,128]{2,1,0:T(8,128)S(1)}, u32[]{:S(2)}, u32[]{:S(2)}) %collective-permute-start) | collective-permute-done | bytes 524320 | tf_op jit(solution)/shard_map/while/body/eval_jaxpr/ppermute | solution.py:10
  373.0 10.7 %collective-permute-done = f32[8,128,128]{2,1,0:T(8,128)S(1)} collective-permute-done((f32[8,128,128]{2,1,0:T(8,128)S(1)}, f32[8,128,128]{2,1,0:T(8,128)S(1)}, u32[]{:S(2)}, u32[]{:S(2)}) %collective-permute-start) | collective-permute-done | bytes 524320 | tf_op jit(solution)/shard_map/while/body/eval_jaxpr/ppermute | solution.py:10
  385.7 10.7 %collective-permute-done = f32[8,128,128]{2,1,0:T(8,128)S(1)} collective-permute-done((f32[8,128,128]{2,1,0:T(8,128)S(1)}, f32[8,128,128]{2,1,0:T(8,128)S(1)}, u32[]{:S(2)}, u32[]{:S(2)}) %collective-permute-start) | collective-permute-done | bytes 524320 | tf_op jit(solution)/shard_map/while/body/eval_jaxpr/ppermute | solution.py:10
  398.3 10.7 %collective-permute-done = f32[8,128,128]{2,1,0:T(8,128)S(1)} collective-permute-done((f32[8,128,128]{2,1,0:T(8,128)S(1)}, f32[8,128,128]{2,1,0:T(8,128)S(1)}, u32[]{:S(2)}, u32[]{:S(2)}) %collective-permute-start) | collective-permute-done | bytes 524320 | tf_op jit(solution)/shard_map/while/body/eval_jaxpr/ppermute | solution.py:10
  411.0 10.7 %collective-permute-done = f32[8,128,128]{2,1,0:T(8,128)S(1)} collective-permute-done((f32[8,128,128]{2,1,0:T(8,128)S(1)}, f32[8,128,128]{2,1,0:T(8,128)S(1)}, u32[]{:S(2)}, u32[]{:S(2)}) %collective-permute-start) | collective-permute-done | bytes 524320 | tf_op jit(solution)/shard_map/while/body/eval_jaxpr/ppermute | solution.py:10
  423.7 10.7 %collective-permute-done = f32[8,128,128]{2,1,0:T(8,128)S(1)} collective-permute-done((f32[8,128,128]{2,1,0:T(8,128)S(1)}, f32[8,128,128]{2,1,0:T(8,128)S(1)}, u32[]{:S(2)}, u32[]{:S(2)}) %collective-permute-start) | collective-permute-done | bytes 524320 | tf_op jit(solution)/shard_map/while/body/eval_jaxpr/ppermute | solution.py:10
  436.3 10.7 %collective-permute-done = f32[8,128,128]{2,1,0:T(8,128)S(1)} collective-permute-done((f32[8,128,128]{2,1,0:T(8,128)S(1)}, f32[8,128,128]{2,1,0:T(8,128)S(1)}, u32[]{:S(2)}, u32[]{:S(2)}) %collective-permute-start) | collective-permute-done | bytes 524320 | tf_op jit(solution)/shard_map/while/body/eval_jaxpr/ppermute | solution.py:10
  449.0 10.7 %collective-permute-done = f32[8,128,128]{2,1,0:T(8,128)S(1)} collective-permute-done((f32[8,128,128]{2,1,0:T(8,128)S(1)}, f32[8,128,128]{2,1,0:T(8,128)S(1)}, u32[]{:S(2)}, u32[]{:S(2)}) %collective-permute-start) | collective-permute-done | bytes 524320 | tf_op jit(solution)/shard_map/while/body/eval_jaxpr/ppermute | solution.py:10
  461.7 10.7 %collective-permute-done = f32[8,128,128]{2,1,0:T(8,128)S(1)} collective-permute-done((f32[8,128,128]{2,1,0:T(8,128)S(1)}, f32[8,128,128]{2,1,0:T(8,128)S(1)}, u32[]{:S(2)}, u32[]{:S(2)}) %collective-permute-start) | collective-permute-done | bytes 524320 | tf_op jit(solution)/shard_map/while/body/eval_jaxpr/ppermute | solution.py:10
  474.4 10.7 %collective-permute-done = f32[8,128,128]{2,1,0:T(8,128)S(1)} collective-permute-done((f32[8,128,128]{2,1,0:T(8,128)S(1)}, f32[8,128,128]{2,1,0:T(8,128)S(1)}, u32[]{:S(2)}, u32[]{:S(2)}) %collective-permute-start) | collective-permute-done | bytes 524320 | tf_op jit(solution)/shard_map/while/body/eval_jaxpr/ppermute | solution.py:10
  487.0 10.7 %collective-permute-done = f32[8,128,128]{2,1,0:T(8,128)S(1)} collective-permute-done((f32[8,128,128]{2,1,0:T(8,128)S(1)}, f32[8,128,128]{2,1,0:T(8,128)S(1)}, u32[]{:S(2)}, u32[]{:S(2)}) %collective-permute-start) | collective-permute-done | bytes 524320 | tf_op jit(solution)/shard_map/while/body/eval_jaxpr/ppermute | solution.py:10
  501.1 11.6 %convolution_bitcast_fusion = f32[2048,3072]{0,1:T(8,128)} fusion(bf16[1,128,2048]{2,1,0:T(8,128)(2,1)S(1)} %copy-done, bf16[128,1024]{0,1:T(8,128)(2,1)S(1)} %bitcast.82, bf16[128,1024]{0,1:T(8,128)(2,1)S(1)} %bitcast.80, bf16[128,1024]{0,1:T(8,128)(2,1)S(1)} %bitcast.78), kind=kOutput, calls=%fused_computation | convolution fusion | flops 1612972032 | bytes 26476544 | tf_op jit(solution)/shard_map/dot_general | solution.py:70
  512.7 24.7 %copy.43 = f32[2048,3072]{1,0:T(8,128)} copy(f32[2048,3072]{0,1:T(8,128)} %convolution_bitcast_fusion) | data formatting | bytes 50331648
  537.4 9.7 %fusion = bf16[1,128,2048]{2,1,0:T(8,128)(2,1)} fusion(bf16[2048,3072]{1,0:T(8,128)(2,1)} %all-gather.2.cloned.1.call-done, bf16[128,1024]{0,1:T(8,128)(2,1)S(1)} %bitcast.83, bf16[128,1024]{0,1:T(8,128)(2,1)S(1)} %bitcast.81, bf16[128,1024]{0,1:T(8,128)(2,1)S(1)} %bitcast.79), kind=kOutput, calls=%fused_computation.3 | convolution fusion | flops 1613234176 | bytes 13893632 | tf_op jit(solution)/shard_map/dot_general | solution.py:65
  547.1 270.4 %reduce-scatter.4.cloned.1.call-done = f32[16,3072]{1,0:T(8,128)} async-done(((f32[2048,3072]{1,0:T(8,128)}), f32[16,3072]{1,0:T(8,128)}) %reduce-scatter.4.cloned.1.call-update) | async-done | bytes 196624
  820.2 2.5 copy.37
  (83 shorter events, 53.3 us)
Async XLA Ops:
  7.2 124.4 %copy-start = (bf16[1,128,2048]{2,1,0:T(8,128)(2,1)S(1)}, bf16[1,128,2048]{2,1,0:T(8,128)(2,1)}, u32[]{:S(2)}) copy-start(bf16[1,128,2048]{2,1,0:T(8,128)(2,1)} %param.6) | copy-start | bytes 1572868
  7.2 1.0 copy-start.5
  7.2 1.2 copy-start.4
  7.2 124.3 %all-gather.2.cloned.1.call-start = ((), (), s32[]{:S(2)}) async-start(), calls=%async_computation.1 | async-start | bytes 15728640 | tf_op jit(solution)/shard_map/all_gather | solution.py:14
  7.9 809.6 %reduce-scatter.4.cloned.1.call-start = ((), (), s32[]{:S(2)}) async-start(), calls=%async_computation.2 | async-start | bytes 25362432
  138.0 0.7 copy-start.3
  139.7 10.6 %collective-permute-start = (f32[8,128,128]{2,1,0:T(8,128)S(1)}, f32[8,128,128]{2,1,0:T(8,128)S(1)}, u32[]{:S(2)}, u32[]{:S(2)}) collective-permute-start(f32[8,128,128]{2,1,0:T(8,128)S(1)} %add.41), channel_id=1, source_target_pairs={{4,0},{8,4},{12,8},{16,12},{20,16},{24,20},{28,24},{32,28},{36,32}... | collective-permute-start | bytes 1572872 | tf_op jit(solution)/shard_map/while/body/eval_jaxpr/ppermute | solution.py:10
  150.4 10.5 %collective-permute-start = (f32[8,128,128]{2,1,0:T(8,128)S(1)}, f32[8,128,128]{2,1,0:T(8,128)S(1)}, u32[]{:S(2)}, u32[]{:S(2)}) collective-permute-start(f32[8,128,128]{2,1,0:T(8,128)S(1)} %add.41), channel_id=1, source_target_pairs={{4,0},{8,4},{12,8},{16,12},{20,16},{24,20},{28,24},{32,28},{36,32}... | collective-permute-start | bytes 1572872 | tf_op jit(solution)/shard_map/while/body/eval_jaxpr/ppermute | solution.py:10
  160.9 10.5 %collective-permute-start = (f32[8,128,128]{2,1,0:T(8,128)S(1)}, f32[8,128,128]{2,1,0:T(8,128)S(1)}, u32[]{:S(2)}, u32[]{:S(2)}) collective-permute-start(f32[8,128,128]{2,1,0:T(8,128)S(1)} %add.41), channel_id=1, source_target_pairs={{4,0},{8,4},{12,8},{16,12},{20,16},{24,20},{28,24},{32,28},{36,32}... | collective-permute-start | bytes 1572872 | tf_op jit(solution)/shard_map/while/body/eval_jaxpr/ppermute | solution.py:10
  171.5 10.5 %collective-permute-start = (f32[8,128,128]{2,1,0:T(8,128)S(1)}, f32[8,128,128]{2,1,0:T(8,128)S(1)}, u32[]{:S(2)}, u32[]{:S(2)}) collective-permute-start(f32[8,128,128]{2,1,0:T(8,128)S(1)} %add.41), channel_id=1, source_target_pairs={{4,0},{8,4},{12,8},{16,12},{20,16},{24,20},{28,24},{32,28},{36,32}... | collective-permute-start | bytes 1572872 | tf_op jit(solution)/shard_map/while/body/eval_jaxpr/ppermute | solution.py:10
  182.1 10.5 %collective-permute-start = (f32[8,128,128]{2,1,0:T(8,128)S(1)}, f32[8,128,128]{2,1,0:T(8,128)S(1)}, u32[]{:S(2)}, u32[]{:S(2)}) collective-permute-start(f32[8,128,128]{2,1,0:T(8,128)S(1)} %add.41), channel_id=1, source_target_pairs={{4,0},{8,4},{12,8},{16,12},{20,16},{24,20},{28,24},{32,28},{36,32}... | collective-permute-start | bytes 1572872 | tf_op jit(solution)/shard_map/while/body/eval_jaxpr/ppermute | solution.py:10
  192.6 10.5 %collective-permute-start = (f32[8,128,128]{2,1,0:T(8,128)S(1)}, f32[8,128,128]{2,1,0:T(8,128)S(1)}, u32[]{:S(2)}, u32[]{:S(2)}) collective-permute-start(f32[8,128,128]{2,1,0:T(8,128)S(1)} %add.41), channel_id=1, source_target_pairs={{4,0},{8,4},{12,8},{16,12},{20,16},{24,20},{28,24},{32,28},{36,32}... | collective-permute-start | bytes 1572872 | tf_op jit(solution)/shard_map/while/body/eval_jaxpr/ppermute | solution.py:10
  203.2 10.5 %collective-permute-start = (f32[8,128,128]{2,1,0:T(8,128)S(1)}, f32[8,128,128]{2,1,0:T(8,128)S(1)}, u32[]{:S(2)}, u32[]{:S(2)}) collective-permute-start(f32[8,128,128]{2,1,0:T(8,128)S(1)} %add.41), channel_id=1, source_target_pairs={{4,0},{8,4},{12,8},{16,12},{20,16},{24,20},{28,24},{32,28},{36,32}... | collective-permute-start | bytes 1572872 | tf_op jit(solution)/shard_map/while/body/eval_jaxpr/ppermute | solution.py:10
  213.7 10.5 %collective-permute-start = (f32[8,128,128]{2,1,0:T(8,128)S(1)}, f32[8,128,128]{2,1,0:T(8,128)S(1)}, u32[]{:S(2)}, u32[]{:S(2)}) collective-permute-start(f32[8,128,128]{2,1,0:T(8,128)S(1)} %add.41), channel_id=1, source_target_pairs={{4,0},{8,4},{12,8},{16,12},{20,16},{24,20},{28,24},{32,28},{36,32}... | collective-permute-start | bytes 1572872 | tf_op jit(solution)/shard_map/while/body/eval_jaxpr/ppermute | solution.py:10
  224.3 10.5 %collective-permute-start = (f32[8,128,128]{2,1,0:T(8,128)S(1)}, f32[8,128,128]{2,1,0:T(8,128)S(1)}, u32[]{:S(2)}, u32[]{:S(2)}) collective-permute-start(f32[8,128,128]{2,1,0:T(8,128)S(1)} %add.41), channel_id=1, source_target_pairs={{4,0},{8,4},{12,8},{16,12},{20,16},{24,20},{28,24},{32,28},{36,32}... | collective-permute-start | bytes 1572872 | tf_op jit(solution)/shard_map/while/body/eval_jaxpr/ppermute | solution.py:10
  234.9 10.5 %collective-permute-start = (f32[8,128,128]{2,1,0:T(8,128)S(1)}, f32[8,128,128]{2,1,0:T(8,128)S(1)}, u32[]{:S(2)}, u32[]{:S(2)}) collective-permute-start(f32[8,128,128]{2,1,0:T(8,128)S(1)} %add.41), channel_id=1, source_target_pairs={{4,0},{8,4},{12,8},{16,12},{20,16},{24,20},{28,24},{32,28},{36,32}... | collective-permute-start | bytes 1572872 | tf_op jit(solution)/shard_map/while/body/eval_jaxpr/ppermute | solution.py:10
  245.4 10.5 %collective-permute-start = (f32[8,128,128]{2,1,0:T(8,128)S(1)}, f32[8,128,128]{2,1,0:T(8,128)S(1)}, u32[]{:S(2)}, u32[]{:S(2)}) collective-permute-start(f32[8,128,128]{2,1,0:T(8,128)S(1)} %add.41), channel_id=1, source_target_pairs={{4,0},{8,4},{12,8},{16,12},{20,16},{24,20},{28,24},{32,28},{36,32}... | collective-permute-start | bytes 1572872 | tf_op jit(solution)/shard_map/while/body/eval_jaxpr/ppermute | solution.py:10
  256.0 10.5 %collective-permute-start = (f32[8,128,128]{2,1,0:T(8,128)S(1)}, f32[8,128,128]{2,1,0:T(8,128)S(1)}, u32[]{:S(2)}, u32[]{:S(2)}) collective-permute-start(f32[8,128,128]{2,1,0:T(8,128)S(1)} %add.41), channel_id=1, source_target_pairs={{4,0},{8,4},{12,8},{16,12},{20,16},{24,20},{28,24},{32,28},{36,32}... | collective-permute-start | bytes 1572872 | tf_op jit(solution)/shard_map/while/body/eval_jaxpr/ppermute | solution.py:10
  266.5 10.5 %collective-permute-start = (f32[8,128,128]{2,1,0:T(8,128)S(1)}, f32[8,128,128]{2,1,0:T(8,128)S(1)}, u32[]{:S(2)}, u32[]{:S(2)}) collective-permute-start(f32[8,128,128]{2,1,0:T(8,128)S(1)} %add.41), channel_id=1, source_target_pairs={{4,0},{8,4},{12,8},{16,12},{20,16},{24,20},{28,24},{32,28},{36,32}... | collective-permute-start | bytes 1572872 | tf_op jit(solution)/shard_map/while/body/eval_jaxpr/ppermute | solution.py:10
  277.1 10.5 %collective-permute-start = (f32[8,128,128]{2,1,0:T(8,128)S(1)}, f32[8,128,128]{2,1,0:T(8,128)S(1)}, u32[]{:S(2)}, u32[]{:S(2)}) collective-permute-start(f32[8,128,128]{2,1,0:T(8,128)S(1)} %add.41), channel_id=1, source_target_pairs={{4,0},{8,4},{12,8},{16,12},{20,16},{24,20},{28,24},{32,28},{36,32}... | collective-permute-start | bytes 1572872 | tf_op jit(solution)/shard_map/while/body/eval_jaxpr/ppermute | solution.py:10
  287.7 10.5 %collective-permute-start = (f32[8,128,128]{2,1,0:T(8,128)S(1)}, f32[8,128,128]{2,1,0:T(8,128)S(1)}, u32[]{:S(2)}, u32[]{:S(2)}) collective-permute-start(f32[8,128,128]{2,1,0:T(8,128)S(1)} %add.41), channel_id=1, source_target_pairs={{4,0},{8,4},{12,8},{16,12},{20,16},{24,20},{28,24},{32,28},{36,32}... | collective-permute-start | bytes 1572872 | tf_op jit(solution)/shard_map/while/body/eval_jaxpr/ppermute | solution.py:10
  298.2 10.5 %collective-permute-start = (f32[8,128,128]{2,1,0:T(8,128)S(1)}, f32[8,128,128]{2,1,0:T(8,128)S(1)}, u32[]{:S(2)}, u32[]{:S(2)}) collective-permute-start(f32[8,128,128]{2,1,0:T(8,128)S(1)} %add.41), channel_id=1, source_target_pairs={{4,0},{8,4},{12,8},{16,12},{20,16},{24,20},{28,24},{32,28},{36,32}... | collective-permute-start | bytes 1572872 | tf_op jit(solution)/shard_map/while/body/eval_jaxpr/ppermute | solution.py:10
  308.8 11.5 %collective-permute-start = (f32[8,128,128]{2,1,0:T(8,128)S(1)}, f32[8,128,128]{2,1,0:T(8,128)S(1)}, u32[]{:S(2)}, u32[]{:S(2)}) collective-permute-start(f32[8,128,128]{2,1,0:T(8,128)S(1)} %add.41), channel_id=1, source_target_pairs={{4,0},{8,4},{12,8},{16,12},{20,16},{24,20},{28,24},{32,28},{36,32}... | collective-permute-start | bytes 1572872 | tf_op jit(solution)/shard_map/while/body/eval_jaxpr/ppermute | solution.py:10
  320.4 12.6 %collective-permute-start = (f32[8,128,128]{2,1,0:T(8,128)S(1)}, f32[8,128,128]{2,1,0:T(8,128)S(1)}, u32[]{:S(2)}, u32[]{:S(2)}) collective-permute-start(f32[8,128,128]{2,1,0:T(8,128)S(1)} %add.41), channel_id=1, source_target_pairs={{4,0},{8,4},{12,8},{16,12},{20,16},{24,20},{28,24},{32,28},{36,32}... | collective-permute-start | bytes 1572872 | tf_op jit(solution)/shard_map/while/body/eval_jaxpr/ppermute | solution.py:10
  333.1 12.6 %collective-permute-start = (f32[8,128,128]{2,1,0:T(8,128)S(1)}, f32[8,128,128]{2,1,0:T(8,128)S(1)}, u32[]{:S(2)}, u32[]{:S(2)}) collective-permute-start(f32[8,128,128]{2,1,0:T(8,128)S(1)} %add.41), channel_id=1, source_target_pairs={{4,0},{8,4},{12,8},{16,12},{20,16},{24,20},{28,24},{32,28},{36,32}... | collective-permute-start | bytes 1572872 | tf_op jit(solution)/shard_map/while/body/eval_jaxpr/ppermute | solution.py:10
  345.7 12.6 %collective-permute-start = (f32[8,128,128]{2,1,0:T(8,128)S(1)}, f32[8,128,128]{2,1,0:T(8,128)S(1)}, u32[]{:S(2)}, u32[]{:S(2)}) collective-permute-start(f32[8,128,128]{2,1,0:T(8,128)S(1)} %add.41), channel_id=1, source_target_pairs={{4,0},{8,4},{12,8},{16,12},{20,16},{24,20},{28,24},{32,28},{36,32}... | collective-permute-start | bytes 1572872 | tf_op jit(solution)/shard_map/while/body/eval_jaxpr/ppermute | solution.py:10
  358.4 12.6 %collective-permute-start = (f32[8,128,128]{2,1,0:T(8,128)S(1)}, f32[8,128,128]{2,1,0:T(8,128)S(1)}, u32[]{:S(2)}, u32[]{:S(2)}) collective-permute-start(f32[8,128,128]{2,1,0:T(8,128)S(1)} %add.41), channel_id=1, source_target_pairs={{4,0},{8,4},{12,8},{16,12},{20,16},{24,20},{28,24},{32,28},{36,32}... | collective-permute-start | bytes 1572872 | tf_op jit(solution)/shard_map/while/body/eval_jaxpr/ppermute | solution.py:10
  371.1 12.6 %collective-permute-start = (f32[8,128,128]{2,1,0:T(8,128)S(1)}, f32[8,128,128]{2,1,0:T(8,128)S(1)}, u32[]{:S(2)}, u32[]{:S(2)}) collective-permute-start(f32[8,128,128]{2,1,0:T(8,128)S(1)} %add.41), channel_id=1, source_target_pairs={{4,0},{8,4},{12,8},{16,12},{20,16},{24,20},{28,24},{32,28},{36,32}... | collective-permute-start | bytes 1572872 | tf_op jit(solution)/shard_map/while/body/eval_jaxpr/ppermute | solution.py:10
  383.7 12.6 %collective-permute-start = (f32[8,128,128]{2,1,0:T(8,128)S(1)}, f32[8,128,128]{2,1,0:T(8,128)S(1)}, u32[]{:S(2)}, u32[]{:S(2)}) collective-permute-start(f32[8,128,128]{2,1,0:T(8,128)S(1)} %add.41), channel_id=1, source_target_pairs={{4,0},{8,4},{12,8},{16,12},{20,16},{24,20},{28,24},{32,28},{36,32}... | collective-permute-start | bytes 1572872 | tf_op jit(solution)/shard_map/while/body/eval_jaxpr/ppermute | solution.py:10
  396.4 12.6 %collective-permute-start = (f32[8,128,128]{2,1,0:T(8,128)S(1)}, f32[8,128,128]{2,1,0:T(8,128)S(1)}, u32[]{:S(2)}, u32[]{:S(2)}) collective-permute-start(f32[8,128,128]{2,1,0:T(8,128)S(1)} %add.41), channel_id=1, source_target_pairs={{4,0},{8,4},{12,8},{16,12},{20,16},{24,20},{28,24},{32,28},{36,32}... | collective-permute-start | bytes 1572872 | tf_op jit(solution)/shard_map/while/body/eval_jaxpr/ppermute | solution.py:10
  409.1 12.6 %collective-permute-start = (f32[8,128,128]{2,1,0:T(8,128)S(1)}, f32[8,128,128]{2,1,0:T(8,128)S(1)}, u32[]{:S(2)}, u32[]{:S(2)}) collective-permute-start(f32[8,128,128]{2,1,0:T(8,128)S(1)} %add.41), channel_id=1, source_target_pairs={{4,0},{8,4},{12,8},{16,12},{20,16},{24,20},{28,24},{32,28},{36,32}... | collective-permute-start | bytes 1572872 | tf_op jit(solution)/shard_map/while/body/eval_jaxpr/ppermute | solution.py:10
  421.7 12.6 %collective-permute-start = (f32[8,128,128]{2,1,0:T(8,128)S(1)}, f32[8,128,128]{2,1,0:T(8,128)S(1)}, u32[]{:S(2)}, u32[]{:S(2)}) collective-permute-start(f32[8,128,128]{2,1,0:T(8,128)S(1)} %add.41), channel_id=1, source_target_pairs={{4,0},{8,4},{12,8},{16,12},{20,16},{24,20},{28,24},{32,28},{36,32}... | collective-permute-start | bytes 1572872 | tf_op jit(solution)/shard_map/while/body/eval_jaxpr/ppermute | solution.py:10
  434.4 12.6 %collective-permute-start = (f32[8,128,128]{2,1,0:T(8,128)S(1)}, f32[8,128,128]{2,1,0:T(8,128)S(1)}, u32[]{:S(2)}, u32[]{:S(2)}) collective-permute-start(f32[8,128,128]{2,1,0:T(8,128)S(1)} %add.41), channel_id=1, source_target_pairs={{4,0},{8,4},{12,8},{16,12},{20,16},{24,20},{28,24},{32,28},{36,32}... | collective-permute-start | bytes 1572872 | tf_op jit(solution)/shard_map/while/body/eval_jaxpr/ppermute | solution.py:10
  447.1 12.6 %collective-permute-start = (f32[8,128,128]{2,1,0:T(8,128)S(1)}, f32[8,128,128]{2,1,0:T(8,128)S(1)}, u32[]{:S(2)}, u32[]{:S(2)}) collective-permute-start(f32[8,128,128]{2,1,0:T(8,128)S(1)} %add.41), channel_id=1, source_target_pairs={{4,0},{8,4},{12,8},{16,12},{20,16},{24,20},{28,24},{32,28},{36,32}... | collective-permute-start | bytes 1572872 | tf_op jit(solution)/shard_map/while/body/eval_jaxpr/ppermute | solution.py:10
  459.8 12.6 %collective-permute-start = (f32[8,128,128]{2,1,0:T(8,128)S(1)}, f32[8,128,128]{2,1,0:T(8,128)S(1)}, u32[]{:S(2)}, u32[]{:S(2)}) collective-permute-start(f32[8,128,128]{2,1,0:T(8,128)S(1)} %add.41), channel_id=1, source_target_pairs={{4,0},{8,4},{12,8},{16,12},{20,16},{24,20},{28,24},{32,28},{36,32}... | collective-permute-start | bytes 1572872 | tf_op jit(solution)/shard_map/while/body/eval_jaxpr/ppermute | solution.py:10
  472.4 12.6 %collective-permute-start = (f32[8,128,128]{2,1,0:T(8,128)S(1)}, f32[8,128,128]{2,1,0:T(8,128)S(1)}, u32[]{:S(2)}, u32[]{:S(2)}) collective-permute-start(f32[8,128,128]{2,1,0:T(8,128)S(1)} %add.41), channel_id=1, source_target_pairs={{4,0},{8,4},{12,8},{16,12},{20,16},{24,20},{28,24},{32,28},{36,32}... | collective-permute-start | bytes 1572872 | tf_op jit(solution)/shard_map/while/body/eval_jaxpr/ppermute | solution.py:10
  485.1 12.6 %collective-permute-start = (f32[8,128,128]{2,1,0:T(8,128)S(1)}, f32[8,128,128]{2,1,0:T(8,128)S(1)}, u32[]{:S(2)}, u32[]{:S(2)}) collective-permute-start(f32[8,128,128]{2,1,0:T(8,128)S(1)} %add.41), channel_id=1, source_target_pairs={{4,0},{8,4},{12,8},{16,12},{20,16},{24,20},{28,24},{32,28},{36,32}... | collective-permute-start | bytes 1572872 | tf_op jit(solution)/shard_map/while/body/eval_jaxpr/ppermute | solution.py:10
  497.7 2.3 copy-start.2
  818.9 3.8 copy-start.1
Sparse Core Ops, SparseCore 0:
  9.7 121.7 all-gather.1
  537.5 279.9 reduce-scatter.3
where the time goes:
time: 832 us; the launch traced here: 830 us
  waiting for transfers between devices  689 us (83%)
  starting transfers between devices  60.3 us (7%)
  matrix products  32.6 us (4%)
  local copies, waits for them, and re-layouts  29.5 us (4%)
  between operations  14.2 us (2%)
    ppermute x31, waiting for transfers between devices, passed_along(): return lax.ppermute(block, axis, route)  296 us
    unnamed x3, waiting for transfers between devices  271 us
    all_gather x1, waiting for transfers between devices, body(): full_w = lax.all_gather(w_qkv, 'zero', axis=0, tiled=True)  123 us
    ppermute x31, starting transfers between devices, passed_along(): return lax.ppermute(block, axis, route)  60.2 us
    unnamed x16, local copies, waits for them, and re-layouts  29.3 us
  transfers between devices with their start and end apart: 33, of which 33 were waited for; matrix products, arithmetic and copies ran while one was open for 1% of the time, Pallas kernels for 0%

commit v1 on v0

v1 whole, which is shorter than its diff:
```python
import jax
import jax.numpy as jnp
from jax import lax
from jax.experimental import pallas as pl
from jax.experimental.pallas import tpu as pltpu
from jax.sharding import PartitionSpec as P

NY, NZ, NC, NX = 4, 4, 2, 4
TOK, HD = 128, 128
BF, F32 = jnp.bfloat16, jnp.float32


def ctx_index(y, z, c):
    return (y * NZ + z) * NC + c


def ctx_hop(block, dy=0, dz=0, dc=0):
    route = [
        (ctx_index(y, z, c), ctx_index((y + dy) % NY, (z + dz) % NZ, (c + dc) % NC))
        for y in range(NY)
        for z in range(NZ)
        for c in range(NC)
    ]
    return lax.ppermute(block, "ctx", route)


def x_hop(block, dx):
    return lax.ppermute(block, "zero", [(i, (i + dx) % NX) for i in range(NX)])


def dot(a, b):
    return lax.dot_general(a, b, (((1,), (0,)), ((), ())), preferred_element_type=F32)


def dot_nt(a, b):
    return lax.dot_general(a, b, (((1,), (1,)), ((), ())), preferred_element_type=F32)


def dot_tn(a, b):
    return lax.dot_general(a, b, (((0,), (0,)), ((), ())), preferred_element_type=F32)


def call(kernel, outs, ins, scratch=(), flops=0, limit=24):
    moved = sum(a.size * a.dtype.itemsize for a in list(ins) + list(outs))
    vmem = pl.BlockSpec(memory_space=pltpu.VMEM)
    return pl.pallas_call(
        kernel,
        out_shape=list(outs),
        in_specs=[pl.BlockSpec(memory_space=pltpu.SMEM)] + [vmem] * (len(ins) - 1),
        out_specs=[vmem] * len(outs),
        scratch_shapes=list(scratch),
        compiler_params=pltpu.CompilerParams(vmem_limit_bytes=limit << 20),
        cost_estimate=pl.CostEstimate(flops=flops, bytes_accessed=moved, transcendentals=0),
    )(*ins)


def shape(dims, dtype):
    return jax.ShapeDtypeStruct(dims, dtype)


def column_block(place, step):
    return pl.ds(pl.multiple_of(lax.rem(place + NX - step, NX) * 512, 512), 512)


def project(idx, *refs):
    xs, own, other, gs = refs[0:4], refs[4:8], refs[8:12], refs[12:16]
    qkv, r, xcat = refs[16], refs[17], refs[18]
    xi, ci = idx[0], idx[3]
    for s in range(NZ):
        xcat[s * TOK : (s + 1) * TOK, :] = xs[s][...]
    for j, w in enumerate((own, other)):
        acc = dot(xcat[:, column_block(xi, 0)], w[0][...])
        for s in range(1, NX):
            acc += dot(xcat[:, column_block(xi, s)], w[s][...])
        head = lax.rem(ci + j, 2)
        rounded = acc.astype(BF)
        qkv[head] = rounded
        for s in range(NZ):
            r[head, s] = dot_tn(rounded[s * TOK : (s + 1) * TOK, :HD], gs[s][0, head])


def within(alpha, beta, idx, *refs):
    xs, gs, qkv = refs[0:4], refs[4:8], refs[8]
    dq, dk0, dv0, xt = refs[9:]
    rowi = lax.broadcasted_iota(jnp.int32, (TOK, TOK), 0)
    coli = lax.broadcasted_iota(jnp.int32, (TOK, TOK), 1)
    mask = rowi >= coli
    for head in range(2):
        for s in range(NZ):
            rows = slice(s * TOK, (s + 1) * TOK)
            q, k, v = (qkv[head, rows, i * HD : (i + 1) * HD] for i in range(3))
            g, state = gs[s][0, head], gs[s][1, head]
            p1 = jnp.where(mask, dot_nt(g, v), 0.0).astype(BF)
            p2 = jnp.where(mask, dot_nt(q, k), 0.0).astype(BF)
            dq[head, rows, :] = (alpha * dot_nt(g, state) + beta * dot(p1, k)).astype(BF)
            dk0[head, rows, :] = dot_tn(p1, q)
            dv0[head, rows, :] = dot_tn(p2, g)
    for s in range(NZ):
        xt[:, s * TOK : (s + 1) * TOK] = xs[s][...].T


def finish(beta, idx, *refs):
    qkv, dq, dk0, dv0, r_own, r_other, t1, t2, t3, xt = refs[:10]
    dqkv, p_own, p_other, later = refs[10:]
    yi, zi, ci = idx[1], idx[2], idx[3]
    first = jnp.where(ci == 0, 1.0, 0.0).astype(F32)
    for head in range(2):
        acc = jnp.zeros((HD, HD), F32)
        for step, total in enumerate((t1, t2, t3)):
            use = jnp.where(yi < step + 1, 1.0, 0.0).astype(F32)
            acc += use * total[head].astype(F32)
        for z in range(NZ - 1, -1, -1):
            slot = lax.rem(zi + NZ - z, NZ)
            mate = r_other[head, slot]
            later[head, slot] = (acc + first * mate).astype(BF)
            acc += mate + r_own[head, slot]
        for s in range(NZ):
            rows = slice(s * TOK, (s + 1) * TOK)
            k, v = qkv[head, rows, HD : 2 * HD], qkv[head, rows, 2 * HD :]
            lat = later[head, s]
            dqkv[head, rows, :HD] = dq[head, rows, :]
            dqkv[head, rows, HD : 2 * HD] = (beta * (dk0[head, rows, :] + dot_nt(v, lat))).astype(BF)
            dqkv[head, rows, 2 * HD :] = (beta * (dv0[head, rows, :] + dot(k, lat))).astype(BF)
    for j, part in ((1, p_other), (0, p_own)):
        grads = dqkv[lax.rem(ci + j, 2)]
        for m in range(4):
            rows = slice(m * 512, (m + 1) * 512)
            part[rows, :] = dot(xt[rows, :], grads).astype(BF)


def back(idx, *refs):
    dqkv, own, other = refs[0], refs[1:5], refs[5:9]
    gx = refs[9:13]
    xi, ci = idx[0], idx[3]
    mine, theirs = dqkv[ci], dqkv[1 - ci]
    for s in range(NX):
        part = dot_nt(mine, own[s][...]) + dot_nt(theirs, other[s][...])
        for t in range(NZ):
            gx[t][:, column_block(xi, s)] = part[t * TOK : (t + 1) * TOK].astype(gx[t].dtype)


def split(idx, own, other, *outs):
    a, b = outs[:4], outs[4:]
    xi, yi = idx[0], idx[1]
    for s in range(4):
        to_x, to_y = lax.rem(xi + s, NX), lax.rem(yi + s, NY)
        for y in range(NY):
            for g in range(4):
                a[s][y, g] = (own[y, g, to_x].astype(F32) + other[y, g, to_x].astype(F32)).astype(BF)
        for g in range(4):
            for x in range(NX):
                b[s][g, x] = (own[to_y, 4 + g, x].astype(F32) + other[to_y, 4 + g, x].astype(F32)).astype(BF)


def turn(idx, *refs):
    a, b = refs[0:4], refs[4:8]
    a2, b2 = refs[8:12], refs[12:16]
    xi, yi = idx[0], idx[1]
    for s in range(4):
        to_x, to_y = lax.rem(xi + s, NX), lax.rem(yi + s, NY)
        for g in range(4):
            a2[s][g] = sum(p[to_y, g].astype(F32) for p in a).astype(BF)
            b2[s][g] = sum(p[g, to_x].astype(F32) for p in b).astype(BF)


def body(inputs, grad_out, saved, w_qkv):
    x = inputs[0]
    heads, head_size = saved.shape[2], saved.shape[3]
    length = x.shape[0] * lax.axis_size("ctx")
    alpha = 1.0 / head_size**0.5
    beta = 1.0 / (head_size * length) ** 0.5
    scale = 1.0 / (length * lax.axis_size("zero")) ** 0.5
    ctx = lax.axis_index("ctx")
    xi, yi, zi, ci = lax.axis_index("zero"), ctx // 8, (ctx // 2) % 4, ctx % 2
    idx = jnp.stack([xi, yi, zi, ci]).astype(jnp.int32)

    by_head = w_qkv.reshape(512, 3, heads, HD)
    own_w = lax.dynamic_index_in_dim(by_head, 2 * zi + ci, 2, keepdims=False).reshape(512, 3 * HD)
    other_w = lax.dynamic_index_in_dim(by_head, 2 * zi + 1 - ci, 2, keepdims=False).reshape(512, 3 * HD)
    steps = (1, 3, 2)
    xs = {0: x} | {s: ctx_hop(x, dz=s) for s in steps}
    own = {0: own_w} | {s: x_hop(own_w, s) for s in steps}
    other = {0: other_w} | {s: ctx_hop(own[s], dc=1) for s in steps}
    cot = grad_out[0].reshape(TOK, NZ, 2, HD).transpose(1, 2, 0, 3)
    state = saved[0, 0].astype(BF).reshape(NZ, 2, HD, HD)
    bundle = jnp.stack([cot, state], axis=1)
    gs = {}
    for s in range(4):
        piece = lax.dynamic_index_in_dim(bundle, (zi + s) % NZ, 0, keepdims=False)
        gs[s] = ctx_hop(piece, dz=s) if s else piece
    xs, own, other, gs = ([d[s] for s in range(4)] for d in (xs, own, other, gs))

    qkv, r = call(
        project,
        [shape((2, 512, 384), BF), shape((2, NZ, HD, HD), F32)],
        [idx, *xs, *own, *other, *gs],
        [pltpu.VMEM((512, 2048), BF)],
        flops=2 * 512 * 2048 * 768,
    )
    r_other = ctx_hop(r, dc=1)
    total = jnp.sum(r + r_other, axis=1).astype(BF)
    t = [ctx_hop(total, dy=s) for s in (1, 2, 3)]
    dq, dk0, dv0, xt = call(
        lambda *refs: within(alpha, beta, *refs),
        [shape((2, 512, HD), BF), shape((2, 512, HD), F32), shape((2, 512, HD), F32), shape((2048, 512), BF)],
        [idx, *xs, *gs, qkv],
        flops=8 * 6 * 2 * 128**3 * 4,
    )
    dqkv, p_own, p_other = call(
        lambda *refs: finish(beta, *refs),
        [shape((2, 512, 384), BF), shape((2048, 384), BF), shape((2048, 384), BF)],
        [idx, qkv, dq, dk0, dv0, r, r_other, *t, xt],
        [pltpu.VMEM((2, NZ, HD, HD), BF)],
        flops=2 * 512 * 2048 * 768,
    )
    p_mate = ctx_hop(p_other, dc=1)
    gx = call(
        back,
        [shape((TOK, 2048), F32)] + [shape((TOK, 2048), BF)] * 3,
        [idx, dqkv, *own, *other],
        flops=2 * 512 * 2048 * 768,
    )
    five = (NY, 8, NX, 16, 384)
    parts = call(
        split,
        [shape((NY, 4, 16, 384), BF)] * 4 + [shape((4, NX, 16, 384), BF)] * 4,
        [idx, p_own.reshape(five), p_mate.reshape(five)],
    )
    a, b = parts[:4], parts[4:]
    a = [a[0]] + [x_hop(a[s], s) for s in (1, 2, 3)]
    b = [b[0]] + [ctx_hop(b[s], dy=s) for s in (1, 2, 3)]
    gx = [gx[0]] + [ctx_hop(gx[s], dz=-s) for s in (1, 2, 3)]
    parts = call(turn, [shape((4, 16, 384), BF)] * 8, [idx, *a, *b])
    a, b = parts[:4], parts[4:]
    a = [a[0]] + [ctx_hop(a[s], dy=s) for s in (1, 2, 3)]
    b = [b[0]] + [x_hop(b[s], s) for s in (1, 2, 3)]
    owned = jnp.concatenate([sum(p.astype(F32) for p in a), sum(p.astype(F32) for p in b)], axis=0)
    groups = [[y * 8 + i for i in range(8)] for y in range(NY)]
    owned = lax.all_to_all(owned, "ctx", 0, 0, axis_index_groups=groups)
    owned = owned.reshape(heads, 16, 3, HD).transpose(1, 2, 0, 3).reshape(16, 3 * heads * HD)
    grad_x = sum(p.astype(F32) for p in gx).astype(BF)
    return (grad_x[None], owned * scale)


def solution(mesh):
    in_specs = (
        P("zero", "ctx", None),
        P("zero", "ctx", None),
        P("zero", "ctx", None, None, None),
        P("zero", None),
    )
    out_specs = (P("zero", "ctx", None), P(("ctx", "zero"), None))
    return jax.shard_map(body, mesh=mesh, in_specs=in_specs, out_specs=out_specs, check_vma=False)
```

time: 832 us -> 136 us (0.16)
  waiting for transfers between devices: 689 us -> 47.8 us
  matrix products: 32.6 us -> 0 us
  local copies, waits for them, and re-layouts: 29.5 us -> 10.1 us
  Pallas kernels: 0 us -> 15.9 us
  between operations: 14.2 us -> 0.95 us
    unnamed x3 -> x0, waiting for transfers between devices: 271 us -> none
    ppermute x31 -> x32, waiting for transfers between devices: 296 us -> 47.8 us  [the longest x23 38.1 us: ctx_hop(): return lax.ppermute(block, 'ctx', route)]
    all_gather x1 -> x0, waiting for transfers between devices: 123 us -> none  [body(): full_w = lax.all_gather(w_qkv, 'zero', axis=0, tiled=True)]
    dot_general x11 -> x0, matrix products: 32.6 us -> none  [the longest x1 11.6 us: body(): lax.dot_general(rows, dqkv, (((0,), (0,)), ((), ())), preferred_element_t...]
    unnamed x16 -> x4, local copies, waits for them, and re-layouts: 29.3 us -> 5.39 us
    pallas_call x0 -> x6, Pallas kernels: none -> 15.9 us  [call(): pl.pallas_call(kernel, out_shape=list(outs), in_specs=[pl.BlockSpec(memor...]
    ppermute x31 -> x32, starting transfers between devices: 60.2 us -> 46.9 us  [the longest x23 37.7 us: ctx_hop(): return lax.ppermute(block, 'ctx', route)]
    all_to_all x0 -> x1, starting transfers between devices: none -> 9.53 us  [body(): owned = lax.all_to_all(owned, 'ctx', 0, 0, axis_index_groups=groups)]
  transfers between devices with their start and end apart: 33 -> 33, of which waited for: 33 -> 12; matrix products, arithmetic and copies ran while one was open for 1% -> 8% of each run, Pallas kernels for 0% -> 5%
where the time goes in v1:
time: 136 us
  starting transfers between devices  56.4 us (41%)
  waiting for transfers between devices  47.8 us (35%)
  Pallas kernels  15.9 us (12%)
  local copies, waits for them, and re-layouts  10.1 us (7%)
  other arithmetic  4.31 us (3%)
    ppermute x23, waiting for transfers between devices, ctx_hop(): return lax.ppermute(block, 'ctx', route)  38.1 us
    ppermute x23, starting transfers between devices, ctx_hop(): return lax.ppermute(block, 'ctx', route)  37.7 us
    pallas_call x6, Pallas kernels, call(): pl.pallas_call(kernel, out_shape=list(outs), in_specs=[pl.BlockSpec(memor...  15.9 us
    ppermute x9, waiting for transfers between devices, x_hop(): return lax.ppermute(block, 'zero', [(i, (i + dx) % NX) for i in range(NX)])  9.68 us
    all_to_all x1, starting transfers between devices, body(): owned = lax.all_to_all(owned, 'ctx', 0, 0, axis_index_groups=groups)  9.53 us
    ppermute x9, starting transfers between devices, x_hop(): return lax.ppermute(block, 'zero', [(i, (i + dx) % NX) for i in range(NX)])  9.16 us
    unnamed x4, local copies, waits for them, and re-layouts  5.39 us
  transfers between devices with their start and end apart: 33, of which 12 were waited for; matrix products, arithmetic and copies ran while one was open for 8% of the time, Pallas kernels for 5%

profile of v1, /device:TPU:1, one launch (start us, length us, event | category | flops | bytes accessed | tf_op | source)
XLA Modules:
  0.0 135.5 jit_solution(16286775218151097656)
XLA Ops:
  0.7 1.1 reshape_squeeze.3
  1.9 1.1 convert_element_type.52
  3.1 4.7 %collective-permute-start.11 = (bf16[2,2,128,128]{3,2,1,0:T(8,128)(2,1)S(1)}, bf16[2,2,128,128]{3,2,1,0:T(8,128)(2,1)S(1)}, u32[]{:S(2)}, u32[]{:S(2)}) collective-permute-start(bf16[2,2,128,128]{3,2,1,0:T(8,128)(2,1)S(1)} %get-tuple-element.62), channel_id=1, source_target_pairs={{0,24},{4,28},{8,0},{12,4},{16,8},{20,12},{24,16},{28,20},{32,56},... | collective-permute-start | bytes 393224 | tf_op jit(solution)/shard_map/ppermute | solution.py:24
  7.7 4.7 %copy.20 = bf16[512,3072]{0,1:T(8,128)(2,1)} copy(bf16[512,3072]{1,0:T(8,128)(2,1)} %param.7) | data formatting | bytes 6291456 | tf_op args[3]
  12.4 2.0 %constant_dynamic-slice_fusion = (bf16[512,3,1,128]{0,3,2,1:T(8,128)(2,1)}, bf16[512,3,1,128]{0,3,2,1:T(8,128)(2,1)S(1)}) fusion(bf16[512,3,8,128]{0,3,2,1:T(8,128)(2,1)} %bitcast.41, s32[]{:T(128)S(6)} %select_n.59, s32[]{:T(128)S(6)} %select_n.58), kind=kLoop, calls=%fused_computation.25 | loop fusion | bytes 1572872 | tf_op jit(solution)/shard_map/jit(dynamic_index_in_dim)/dynamic_slice | solution.py:179
  14.6 2.5 %collective-permute-start.5 = (bf16[512,384]{1,0:T(8,128)(2,1)S(1)}, bf16[512,384]{1,0:T(8,128)(2,1)}, u32[]{:S(2)}, u32[]{:S(2)}) collective-permute-start(bf16[512,384]{1,0:T(8,128)(2,1)S(1)} %copy.26.refs_4_.refs_1_), channel_id=1, source_target_pairs={{0,3},{1,0},{2,1},{3,2},{4,7},{5,4},{6,5},{7,6},{8,11},{9,8},{10,9... | collective-permute-start | bytes 1179656 | tf_op jit(solution)/shard_map/ppermute | solution.py:28
  17.3 1.3 collective-permute-start.9
  18.6 0.5 collective-permute-start.4
  19.1 0.6 collective-permute-start.3
  19.8 2.6 %collective-permute-done.9.refs_13_.refs_6_ = bf16[2,2,128,128]{3,2,1,0:T(8,128)(2,1)S(1)} collective-permute-done((bf16[2,2,128,128]{3,2,1,0:T(8,128)(2,1)S(1)}, bf16[2,2,128,128]{3,2,1,0:T(8,128)(2,1)S(1)}, u32[]{:S(2)}, u32[]{:S(2)}) %collective-permute-start.9) | collective-permute-done | bytes 131104 | tf_op jit(solution)/shard_map/ppermute | solution.py:24
  22.3 0.9 collective-permute-start.10
  23.2 4.9 %collective-permute-done.10.refs_14_.refs_7_ = bf16[2,2,128,128]{3,2,1,0:T(8,128)(2,1)S(1)} collective-permute-done((bf16[2,2,128,128]{3,2,1,0:T(8,128)(2,1)S(1)}, bf16[2,2,128,128]{3,2,1,0:T(8,128)(2,1)S(1)}, u32[]{:S(2)}, u32[]{:S(2)}) %collective-permute-start.10) | collective-permute-done | bytes 131104 | tf_op jit(solution)/shard_map/ppermute | solution.py:24
  28.0 0.9 collective-permute-start.1
  28.9 6.3 %collective-permute-start = (bf16[128,2048]{1,0:T(8,128)(2,1)S(1)}, bf16[128,2048]{1,0:T(8,128)(2,1)S(1)}, u32[]{:S(2)}, u32[]{:S(2)}) collective-permute-start(bf16[128,2048]{1,0:T(8,128)(2,1)S(1)} %bitcast.38), channel_id=1, source_target_pairs={{0,8},{4,12},{8,16},{12,20},{16,24},{20,28},{24,0},{28,4},{32,40},... | collective-permute-start | bytes 1572872 | tf_op jit(solution)/shard_map/ppermute | solution.py:24
  35.2 2.6 %collective-permute-start.8 = (bf16[512,384]{1,0:T(8,128)(2,1)}, bf16[512,384]{1,0:T(8,128)(2,1)}, u32[]{:S(2)}, u32[]{:S(2)}) collective-permute-start(bf16[512,384]{1,0:T(8,128)(2,1)} %collective-permute-done.5.refs_7_.refs_4_), channel_id=1, source_target_pairs={{0,4},{4,0},{8,12},{12,8},{16,20},{20,16},{24,28},{28,24},{32,36},... | collective-permute-start | bytes 1179656 | tf_op jit(solution)/shard_map/ppermute | solution.py:24
  37.8 1.9 %collective-permute-done.3.refs_5_.refs_2_ = bf16[512,384]{1,0:T(8,128)(2,1)} collective-permute-done((bf16[512,384]{1,0:T(8,128)(2,1)S(1)}, bf16[512,384]{1,0:T(8,128)(2,1)}, u32[]{:S(2)}, u32[]{:S(2)}) %collective-permute-start.3) | collective-permute-done | bytes 393248 | tf_op jit(solution)/shard_map/ppermute | solution.py:28
  40.2 1.2 copy.27.refs_8_.refs_5_
  41.5 13.1 %collective-permute-done.refs_1_.refs_2_ = bf16[128,2048]{1,0:T(8,128)(2,1)S(1)} collective-permute-done((bf16[128,2048]{1,0:T(8,128)(2,1)S(1)}, bf16[128,2048]{1,0:T(8,128)(2,1)S(1)}, u32[]{:S(2)}, u32[]{:S(2)}) %collective-permute-start) | collective-permute-done | bytes 524320 | tf_op jit(solution)/shard_map/ppermute | solution.py:24
  54.6 4.4 %shard_map.59 = (bf16[2,512,384]{2,1,0:T(8,128)(2,1)S(1)}, f32[2,4,128,128]{3,2,1,0:T(8,128)S(1)}) custom-call(s32[4]{0:T(128)S(1)} %pad_add_fusion.idx.refs_0_, bf16[128,2048]{1,0:T(8,128)(2,1)S(1)} %bitcast.39, bf16[128,2048]{1,0:T(8,128)(2,1)S(1)} %collective-permute-done.refs_1_.refs_2_, bf16[128,2048]{1,0:T(8,128)(2,1)S(1)} %collective-permute-done.1.refs_2_.refs_3_, ...), custom_call_target="tpu_custom_call" | custom-call | flops 1610612736 | bytes 7077904 | tf_op jit(solution)/shard_map/pallas_call | solution.py:46
  59.0 0.6 collective-permute-start.12
  59.6 1.5 %collective-permute-done.12.refs_6_ = f32[2,4,128,128]{3,2,1,0:T(8,128)S(1)} collective-permute-done((f32[2,4,128,128]{3,2,1,0:T(8,128)S(1)}, f32[2,4,128,128]{3,2,1,0:T(8,128)S(1)}, u32[]{:S(2)}, u32[]{:S(2)}) %collective-permute-start.12) | collective-permute-done | bytes 524320 | tf_op jit(solution)/shard_map/ppermute | solution.py:24
  61.2 3.0 %collective-permute-start.14 = (bf16[2,128,128]{2,1,0:T(8,128)(2,1)S(1)}, bf16[2,128,128]{2,1,0:T(8,128)(2,1)S(1)}, u32[]{:S(2)}, u32[]{:S(2)}) collective-permute-start(bf16[2,128,128]{2,1,0:T(8,128)(2,1)S(1)} %add_reduce_fusion), channel_id=1, source_target_pairs={{0,64},{4,68},{8,72},{12,76},{16,80},{20,84},{24,88},{28,92},{32,9... | collective-permute-start | bytes 196616 | tf_op jit(solution)/shard_map/ppermute | solution.py:24
  64.6 2.3 %collective-permute-start.15 = (bf16[2,128,128]{2,1,0:T(8,128)(2,1)S(1)}, bf16[2,128,128]{2,1,0:T(8,128)(2,1)S(1)}, u32[]{:S(2)}, u32[]{:S(2)}) collective-permute-start(bf16[2,128,128]{2,1,0:T(8,128)(2,1)S(1)} %add_reduce_fusion), channel_id=1, source_target_pairs={{0,96},{4,100},{8,104},{12,108},{16,112},{20,116},{24,120},{28,124... | collective-permute-start | bytes 196616 | tf_op jit(solution)/shard_map/ppermute | solution.py:24
  66.8 2.5 %shard_map.60 = (bf16[2,512,128]{2,1,0:T(8,128)(2,1)S(1)}, f32[2,512,128]{2,1,0:T(8,128)S(1)}, f32[2,512,128]{2,1,0:T(8,128)S(1)}, bf16[2048,512]{1,0:T(8,128)(2,1)S(1)}) custom-call(s32[4]{0:T(128)S(1)} %pad_add_fusion.idx.refs_0_, bf16[128,2048]{1,0:T(8,128)(2,1)S(1)} %bitcast.40, bf16[128,2048]{1,0:T(8,128)(2,1)S(1)} %collective-permute-done.refs_1_.refs_2_, ...), custom_call_target="tpu_custom_call" | custom-call | flops 805306368 | bytes 6815760 | tf_op jit(solution)/shard_map/pallas_call | solution.py:46
  69.4 3.4 %shard_map.61 = (bf16[2,512,384]{2,1,0:T(8,128)(2,1)S(1)}, bf16[2048,384]{1,0:T(8,128)(2,1)S(1)}, bf16[2048,384]{1,0:T(8,128)(2,1)S(1)}) custom-call(s32[4]{0:T(128)S(1)} %pad_add_fusion.idx.refs_0_, bf16[2,512,384]{2,1,0:T(8,128)(2,1)S(1)} %get-tuple-element.31.refs_9_.refs_1_, bf16[2,512,128]{2,1,0:T(8,128)(2,1)S(1)} %get-tuple-element.32.refs_2_, ...), custom_call_target="tpu_custom_call" | custom-call | flops 1610612736 | bytes 9371664 | tf_op jit(solution)/shard_map/pallas_call | solution.py:46
  72.8 1.3 collective-permute-start.19
  74.1 3.0 %collective-permute-done.19 = bf16[2048,384]{1,0:T(8,128)(2,1)S(1)} collective-permute-done((bf16[2048,384]{1,0:T(8,128)(2,1)S(1)}, bf16[2048,384]{1,0:T(8,128)(2,1)S(1)}, u32[]{:S(2)}, u32[]{:S(2)}) %collective-permute-start.19) | collective-permute-done | bytes 1572896 | tf_op jit(solution)/shard_map/ppermute | solution.py:24
  77.1 0.9 shard_map.63
  78.1 1.7 %collective-permute-start.21 = (bf16[4,4,16,384]{3,2,1,0:T(8,128)(2,1)S(1)}, bf16[4,4,16,384]{3,2,1,0:T(8,128)(2,1)S(1)}, u32[]{:S(2)}, u32[]{:S(2)}) collective-permute-start(bf16[4,4,16,384]{3,2,1,0:T(8,128)(2,1)S(1)} %get-tuple-element.46), channel_id=1, source_target_pairs={{0,2},{1,3},{2,0},{3,1},{4,6},{5,7},{6,4},{7,5},{8,10},{9,11},{10,... | collective-permute-start | bytes 589832 | tf_op jit(solution)/shard_map/ppermute | solution.py:28
  79.9 0.9 collective-permute-start.22
  80.8 3.8 %collective-permute-start.24 = (bf16[4,4,16,384]{3,2,1,0:T(8,128)(2,1)S(1)}, bf16[4,4,16,384]{3,2,1,0:T(8,128)(2,1)S(1)}, u32[]{:S(2)}, u32[]{:S(2)}) collective-permute-start(bf16[4,4,16,384]{3,2,1,0:T(8,128)(2,1)S(1)} %get-tuple-element.50), channel_id=1, source_target_pairs={{0,64},{4,68},{8,72},{12,76},{16,80},{20,84},{24,88},{28,92},{32,9... | collective-permute-start | bytes 589832 | tf_op jit(solution)/shard_map/ppermute | solution.py:24
  84.6 5.0 %collective-permute-done.20.refs_1_ = bf16[4,4,16,384]{3,2,1,0:T(8,128)(2,1)S(1)} collective-permute-done((bf16[4,4,16,384]{3,2,1,0:T(8,128)(2,1)S(1)}, bf16[4,4,16,384]{3,2,1,0:T(8,128)(2,1)S(1)}, u32[]{:S(2)}, u32[]{:S(2)}) %collective-permute-start.20) | collective-permute-done | bytes 196640 | tf_op jit(solution)/shard_map/ppermute | solution.py:28
  89.7 2.6 %collective-permute-start.25 = (bf16[4,4,16,384]{3,2,1,0:T(8,128)(2,1)S(1)}, bf16[4,4,16,384]{3,2,1,0:T(8,128)(2,1)S(1)}, u32[]{:S(2)}, u32[]{:S(2)}) collective-permute-start(bf16[4,4,16,384]{3,2,1,0:T(8,128)(2,1)S(1)} %get-tuple-element.51), channel_id=1, source_target_pairs={{0,96},{4,100},{8,104},{12,108},{16,112},{20,116},{24,120},{28,124... | collective-permute-start | bytes 589832 | tf_op jit(solution)/shard_map/ppermute | solution.py:24
  92.3 0.5 collective-permute-done.24.refs_6_
  92.8 2.5 %collective-permute-done.25.refs_7_ = bf16[4,4,16,384]{3,2,1,0:T(8,128)(2,1)S(1)} collective-permute-done((bf16[4,4,16,384]{3,2,1,0:T(8,128)(2,1)S(1)}, bf16[4,4,16,384]{3,2,1,0:T(8,128)(2,1)S(1)}, u32[]{:S(2)}, u32[]{:S(2)}) %collective-permute-start.25) | collective-permute-done | bytes 196640 | tf_op jit(solution)/shard_map/ppermute | solution.py:24
  95.3 0.7 shard_map.64
  96.1 4.6 %collective-permute-start.27 = (bf16[4,16,384]{2,1,0:T(8,128)(2,1)S(1)}, bf16[4,16,384]{2,1,0:T(8,128)(2,1)S(1)}, u32[]{:S(2)}, u32[]{:S(2)}) collective-permute-start(bf16[4,16,384]{2,1,0:T(8,128)(2,1)S(1)} %get-tuple-element.54), channel_id=1, source_target_pairs={{0,64},{4,68},{8,72},{12,76},{16,80},{20,84},{24,88},{28,92},{32,9... | collective-permute-start | bytes 147464 | tf_op jit(solution)/shard_map/ppermute | solution.py:24
  100.7 4.0 %shard_map.62 = (f32[128,2048]{1,0:T(8,128)S(1)}, bf16[128,2048]{1,0:T(8,128)(2,1)S(1)}, bf16[128,2048]{1,0:T(8,128)(2,1)S(1)}, bf16[128,2048]{1,0:T(8,128)(2,1)S(1)}) custom-call(s32[4]{0:T(128)S(1)} %pad_add_fusion.idx.refs_0_, bf16[2,512,384]{2,1,0:T(8,128)(2,1)S(1)} %get-tuple-element.37.refs_0_, bf16[512,384]{1,0:T(8,128)(2,1)S(1)} %copy.26.refs_4_.refs_1_, ...), custom_call_target="tpu_custom_call" | custom-call | flops 1610612736 | bytes 6553616 | tf_op jit(solution)/shard_map/pallas_call | solution.py:46
  105.1 0.8 collective-permute-start.17
  105.9 0.5 collective-permute-start.18
  106.5 2.7 %collective-permute-start.31 = (bf16[4,16,384]{2,1,0:T(8,128)(2,1)S(1)}, bf16[4,16,384]{2,1,0:T(8,128)(2,1)S(1)}, u32[]{:S(2)}, u32[]{:S(2)}) collective-permute-start(bf16[4,16,384]{2,1,0:T(8,128)(2,1)S(1)} %get-tuple-element.59), channel_id=1, source_target_pairs={{0,3},{1,0},{2,1},{3,2},{4,7},{5,4},{6,5},{7,6},{8,11},{9,8},{10,9... | collective-permute-start | bytes 147464 | tf_op jit(solution)/shard_map/ppermute | solution.py:28
  109.3 1.7 %collective-permute-done.30 = bf16[4,16,384]{2,1,0:T(8,128)(2,1)S(1)} collective-permute-done((bf16[4,16,384]{2,1,0:T(8,128)(2,1)S(1)}, bf16[4,16,384]{2,1,0:T(8,128)(2,1)S(1)}, u32[]{:S(2)}, u32[]{:S(2)}) %collective-permute-start.30) | collective-permute-done | bytes 49184 | tf_op jit(solution)/shard_map/ppermute | solution.py:28
  110.9 1.1 collective-permute-done.31
  112.0 0.7 pad_maximum_fusion
  112.7 9.5 %all-to-all-start = ((f32[8,16,384]{2,1,0:T(8,128)}), f32[8,16,384]{2,1,0:T(8,128)S(1)}, u32[]{:S(2)}, u32[]{:S(2)}) async-start(f32[8,16,384]{2,1,0:T(8,128)} %pad_maximum_fusion), calls=%async_computation | async-start | bytes 393216 | tf_op jit(solution)/shard_map/all_to_all | solution.py:239
  122.3 10.0 %collective-permute-done.18 = bf16[128,2048]{1,0:T(8,128)(2,1)} collective-permute-done((bf16[128,2048]{1,0:T(8,128)(2,1)S(1)}, bf16[128,2048]{1,0:T(8,128)(2,1)}, u32[]{:S(2)}, u32[]{:S(2)}) %collective-permute-start.18) | collective-permute-done | bytes 524320 | tf_op jit(solution)/shard_map/ppermute | solution.py:24
  132.3 2.3 %fusion = bf16[1,128,2048]{2,1,0:T(8,128)(2,1)} fusion(bf16[128,2048]{1,0:T(8,128)(2,1)} %collective-permute-done.18, bf16[128,2048]{1,0:T(8,128)(2,1)} %collective-permute-done.17, f32[128,2048]{1,0:T(8,128)S(1)} %get-tuple-element.38, bf16[128,2048]{1,0:T(8,128)(2,1)S(1)} %collective-permute-done.16), kind=kLoop, calls=%fused_computation.9 | loop fusion | flops 1835008 | bytes 3145728 | tf_op jit(solution)/shard_map/broadcast_in_dim | solution.py:242
  134.8 0.7 copy.35
  (44 shorter events, 2.4 us)
Async XLA Ops:
  3.1 16.1 %collective-permute-start.11 = (bf16[2,2,128,128]{3,2,1,0:T(8,128)(2,1)S(1)}, bf16[2,2,128,128]{3,2,1,0:T(8,128)(2,1)S(1)}, u32[]{:S(2)}, u32[]{:S(2)}) collective-permute-start(bf16[2,2,128,128]{3,2,1,0:T(8,128)(2,1)S(1)} %get-tuple-element.62), channel_id=1, source_target_pairs={{0,24},{4,28},{8,0},{12,4},{16,8},{20,12},{24,16},{28,20},{32,56},... | collective-permute-start | bytes 393224 | tf_op jit(solution)/shard_map/ppermute | solution.py:24
  12.4 4.8 %copy-start = (bf16[1,128,2048]{2,1,0:T(8,128)(2,1)S(1)}, bf16[1,128,2048]{2,1,0:T(8,128)(2,1)}, u32[]{:S(2)}) copy-start(bf16[1,128,2048]{2,1,0:T(8,128)(2,1)} %param.4) | copy-start | bytes 1572868
  14.6 14.3 %collective-permute-start.5 = (bf16[512,384]{1,0:T(8,128)(2,1)S(1)}, bf16[512,384]{1,0:T(8,128)(2,1)}, u32[]{:S(2)}, u32[]{:S(2)}) collective-permute-start(bf16[512,384]{1,0:T(8,128)(2,1)S(1)} %copy.26.refs_4_.refs_1_), channel_id=1, source_target_pairs={{0,3},{1,0},{2,1},{3,2},{4,7},{5,4},{6,5},{7,6},{8,11},{9,8},{10,9... | collective-permute-start | bytes 1179656 | tf_op jit(solution)/shard_map/ppermute | solution.py:28
  17.2 23.0 %collective-permute-start.2 = (bf16[128,2048]{1,0:T(8,128)(2,1)S(1)}, bf16[128,2048]{1,0:T(8,128)(2,1)S(1)}, u32[]{:S(2)}, u32[]{:S(2)}) collective-permute-start(bf16[128,2048]{1,0:T(8,128)(2,1)S(1)} %bitcast.36), channel_id=1, source_target_pairs={{0,24},{4,28},{8,0},{12,4},{16,8},{20,12},{24,16},{28,20},{32,56},... | collective-permute-start | bytes 1572872 | tf_op jit(solution)/shard_map/ppermute | solution.py:24
  17.3 5.0 %collective-permute-start.9 = (bf16[2,2,128,128]{3,2,1,0:T(8,128)(2,1)S(1)}, bf16[2,2,128,128]{3,2,1,0:T(8,128)(2,1)S(1)}, u32[]{:S(2)}, u32[]{:S(2)}) collective-permute-start(bf16[2,2,128,128]{3,2,1,0:T(8,128)(2,1)S(1)} %get-tuple-element.64), channel_id=1, source_target_pairs={{0,8},{4,12},{8,16},{12,20},{16,24},{20,28},{24,0},{28,4},{32,40},... | collective-permute-start | bytes 393224 | tf_op jit(solution)/shard_map/ppermute | solution.py:24
  18.6 16.6 %collective-permute-start.4 = (bf16[512,384]{1,0:T(8,128)(2,1)S(1)}, bf16[512,384]{1,0:T(8,128)(2,1)}, u32[]{:S(2)}, u32[]{:S(2)}) collective-permute-start(bf16[512,384]{1,0:T(8,128)(2,1)S(1)} %copy.26.refs_4_.refs_1_), channel_id=1, source_target_pairs={{0,2},{1,3},{2,0},{3,1},{4,6},{5,7},{6,4},{7,5},{8,10},{9,11},{10,... | collective-permute-start | bytes 1179656 | tf_op jit(solution)/shard_map/ppermute | solution.py:28
  19.1 20.5 %collective-permute-start.3 = (bf16[512,384]{1,0:T(8,128)(2,1)S(1)}, bf16[512,384]{1,0:T(8,128)(2,1)}, u32[]{:S(2)}, u32[]{:S(2)}) collective-permute-start(bf16[512,384]{1,0:T(8,128)(2,1)S(1)} %copy.26.refs_4_.refs_1_), channel_id=1, source_target_pairs={{0,1},{1,2},{2,3},{3,0},{4,5},{5,6},{6,7},{7,4},{8,9},{9,10},{10,1... | collective-permute-start | bytes 1179656 | tf_op jit(solution)/shard_map/ppermute | solution.py:28
  22.3 5.7 %collective-permute-start.10 = (bf16[2,2,128,128]{3,2,1,0:T(8,128)(2,1)S(1)}, bf16[2,2,128,128]{3,2,1,0:T(8,128)(2,1)S(1)}, u32[]{:S(2)}, u32[]{:S(2)}) collective-permute-start(bf16[2,2,128,128]{3,2,1,0:T(8,128)(2,1)S(1)} %get-tuple-element.65), channel_id=1, source_target_pairs={{0,16},{4,20},{8,24},{12,28},{16,0},{20,4},{24,8},{28,12},{32,48},... | collective-permute-start | bytes 393224 | tf_op jit(solution)/shard_map/ppermute | solution.py:24
  28.0 13.5 %collective-permute-start.1 = (bf16[128,2048]{1,0:T(8,128)(2,1)S(1)}, bf16[128,2048]{1,0:T(8,128)(2,1)S(1)}, u32[]{:S(2)}, u32[]{:S(2)}) collective-permute-start(bf16[128,2048]{1,0:T(8,128)(2,1)S(1)} %bitcast.37), channel_id=1, source_target_pairs={{0,16},{4,20},{8,24},{12,28},{16,0},{20,4},{24,8},{28,12},{32,48},... | collective-permute-start | bytes 1572872 | tf_op jit(solution)/shard_map/ppermute | solution.py:24
  28.9 25.7 %collective-permute-start = (bf16[128,2048]{1,0:T(8,128)(2,1)S(1)}, bf16[128,2048]{1,0:T(8,128)(2,1)S(1)}, u32[]{:S(2)}, u32[]{:S(2)}) collective-permute-start(bf16[128,2048]{1,0:T(8,128)(2,1)S(1)} %bitcast.38), channel_id=1, source_target_pairs={{0,8},{4,12},{8,16},{12,20},{16,24},{20,28},{24,0},{28,4},{32,40},... | collective-permute-start | bytes 1572872 | tf_op jit(solution)/shard_map/ppermute | solution.py:24
  35.2 19.4 %collective-permute-start.8 = (bf16[512,384]{1,0:T(8,128)(2,1)}, bf16[512,384]{1,0:T(8,128)(2,1)}, u32[]{:S(2)}, u32[]{:S(2)}) collective-permute-start(bf16[512,384]{1,0:T(8,128)(2,1)} %collective-permute-done.5.refs_7_.refs_4_), channel_id=1, source_target_pairs={{0,4},{4,0},{8,12},{12,8},{16,20},{20,16},{24,28},{28,24},{32,36},... | collective-permute-start | bytes 1179656 | tf_op jit(solution)/shard_map/ppermute | solution.py:24
  39.7 14.9 %collective-permute-start.7 = (bf16[512,384]{1,0:T(8,128)(2,1)}, bf16[512,384]{1,0:T(8,128)(2,1)}, u32[]{:S(2)}, u32[]{:S(2)}) collective-permute-start(bf16[512,384]{1,0:T(8,128)(2,1)} %collective-permute-done.4.refs_6_.refs_3_), channel_id=1, source_target_pairs={{0,4},{4,0},{8,12},{12,8},{16,20},{20,16},{24,28},{28,24},{32,36},... | collective-permute-start | bytes 1179656 | tf_op jit(solution)/shard_map/ppermute | solution.py:24
  40.2 14.4 %collective-permute-start.6 = (bf16[512,384]{1,0:T(8,128)(2,1)}, bf16[512,384]{1,0:T(8,128)(2,1)}, u32[]{:S(2)}, u32[]{:S(2)}) collective-permute-start(bf16[512,384]{1,0:T(8,128)(2,1)} %collective-permute-done.3.refs_5_.refs_2_), channel_id=1, source_target_pairs={{0,4},{4,0},{8,12},{12,8},{16,20},{20,16},{24,28},{28,24},{32,36},... | collective-permute-start | bytes 1179656 | tf_op jit(solution)/shard_map/ppermute | solution.py:24
  59.0 2.1 %collective-permute-start.12 = (f32[2,4,128,128]{3,2,1,0:T(8,128)S(1)}, f32[2,4,128,128]{3,2,1,0:T(8,128)S(1)}, u32[]{:S(2)}, u32[]{:S(2)}) collective-permute-start(f32[2,4,128,128]{3,2,1,0:T(8,128)S(1)} %get-tuple-element.35.refs_5_), channel_id=1, source_target_pairs={{0,4},{4,0},{8,12},{12,8},{16,20},{20,16},{24,28},{28,24},{32,36},... | collective-permute-start | bytes 1572872 | tf_op jit(solution)/shard_map/ppermute | solution.py:24
  61.2 8.2 %collective-permute-start.14 = (bf16[2,128,128]{2,1,0:T(8,128)(2,1)S(1)}, bf16[2,128,128]{2,1,0:T(8,128)(2,1)S(1)}, u32[]{:S(2)}, u32[]{:S(2)}) collective-permute-start(bf16[2,128,128]{2,1,0:T(8,128)(2,1)S(1)} %add_reduce_fusion), channel_id=1, source_target_pairs={{0,64},{4,68},{8,72},{12,76},{16,80},{20,84},{24,88},{28,92},{32,9... | collective-permute-start | bytes 196616 | tf_op jit(solution)/shard_map/ppermute | solution.py:24
  64.2 5.2 %collective-permute-start.13 = (bf16[2,128,128]{2,1,0:T(8,128)(2,1)S(1)}, bf16[2,128,128]{2,1,0:T(8,128)(2,1)S(1)}, u32[]{:S(2)}, u32[]{:S(2)}) collective-permute-start(bf16[2,128,128]{2,1,0:T(8,128)(2,1)S(1)} %add_reduce_fusion), channel_id=1, source_target_pairs={{0,32},{4,36},{8,40},{12,44},{16,48},{20,52},{24,56},{28,60},{32,6... | collective-permute-start | bytes 196616 | tf_op jit(solution)/shard_map/ppermute | solution.py:24
  64.6 4.8 %collective-permute-start.15 = (bf16[2,128,128]{2,1,0:T(8,128)(2,1)S(1)}, bf16[2,128,128]{2,1,0:T(8,128)(2,1)S(1)}, u32[]{:S(2)}, u32[]{:S(2)}) collective-permute-start(bf16[2,128,128]{2,1,0:T(8,128)(2,1)S(1)} %add_reduce_fusion), channel_id=1, source_target_pairs={{0,96},{4,100},{8,104},{12,108},{16,112},{20,116},{24,120},{28,124... | collective-permute-start | bytes 196616 | tf_op jit(solution)/shard_map/ppermute | solution.py:24
  72.8 4.3 %collective-permute-start.19 = (bf16[2048,384]{1,0:T(8,128)(2,1)S(1)}, bf16[2048,384]{1,0:T(8,128)(2,1)S(1)}, u32[]{:S(2)}, u32[]{:S(2)}) collective-permute-start(bf16[2048,384]{1,0:T(8,128)(2,1)S(1)} %get-tuple-element.43), channel_id=1, source_target_pairs={{0,4},{4,0},{8,12},{12,8},{16,20},{20,16},{24,28},{28,24},{32,36},... | collective-permute-start | bytes 4718600 | tf_op jit(solution)/shard_map/ppermute | solution.py:24
  78.0 11.6 %collective-permute-start.20 = (bf16[4,4,16,384]{3,2,1,0:T(8,128)(2,1)S(1)}, bf16[4,4,16,384]{3,2,1,0:T(8,128)(2,1)S(1)}, u32[]{:S(2)}, u32[]{:S(2)}) collective-permute-start(bf16[4,4,16,384]{3,2,1,0:T(8,128)(2,1)S(1)} %get-tuple-element.45), channel_id=1, source_target_pairs={{0,1},{1,2},{2,3},{3,0},{4,5},{5,6},{6,7},{7,4},{8,9},{9,10},{10,1... | collective-permute-start | bytes 589832 | tf_op jit(solution)/shard_map/ppermute | solution.py:28
  78.1 14.2 %collective-permute-start.21 = (bf16[4,4,16,384]{3,2,1,0:T(8,128)(2,1)S(1)}, bf16[4,4,16,384]{3,2,1,0:T(8,128)(2,1)S(1)}, u32[]{:S(2)}, u32[]{:S(2)}) collective-permute-start(bf16[4,4,16,384]{3,2,1,0:T(8,128)(2,1)S(1)} %get-tuple-element.46), channel_id=1, source_target_pairs={{0,2},{1,3},{2,0},{3,1},{4,6},{5,7},{6,4},{7,5},{8,10},{9,11},{10,... | collective-permute-start | bytes 589832 | tf_op jit(solution)/shard_map/ppermute | solution.py:28
  79.9 12.4 %collective-permute-start.22 = (bf16[4,4,16,384]{3,2,1,0:T(8,128)(2,1)S(1)}, bf16[4,4,16,384]{3,2,1,0:T(8,128)(2,1)S(1)}, u32[]{:S(2)}, u32[]{:S(2)}) collective-permute-start(bf16[4,4,16,384]{3,2,1,0:T(8,128)(2,1)S(1)} %get-tuple-element.47), channel_id=1, source_target_pairs={{0,3},{1,0},{2,1},{3,2},{4,7},{5,4},{6,5},{7,6},{8,11},{9,8},{10,9... | collective-permute-start | bytes 589832 | tf_op jit(solution)/shard_map/ppermute | solution.py:28
  80.8 11.5 %collective-permute-start.23 = (bf16[4,4,16,384]{3,2,1,0:T(8,128)(2,1)S(1)}, bf16[4,4,16,384]{3,2,1,0:T(8,128)(2,1)S(1)}, u32[]{:S(2)}, u32[]{:S(2)}) collective-permute-start(bf16[4,4,16,384]{3,2,1,0:T(8,128)(2,1)S(1)} %get-tuple-element.49), channel_id=1, source_target_pairs={{0,32},{4,36},{8,40},{12,44},{16,48},{20,52},{24,56},{28,60},{32,6... | collective-permute-start | bytes 589832 | tf_op jit(solution)/shard_map/ppermute | solution.py:24
  80.8 12.0 %collective-permute-start.24 = (bf16[4,4,16,384]{3,2,1,0:T(8,128)(2,1)S(1)}, bf16[4,4,16,384]{3,2,1,0:T(8,128)(2,1)S(1)}, u32[]{:S(2)}, u32[]{:S(2)}) collective-permute-start(bf16[4,4,16,384]{3,2,1,0:T(8,128)(2,1)S(1)} %get-tuple-element.50), channel_id=1, source_target_pairs={{0,64},{4,68},{8,72},{12,76},{16,80},{20,84},{24,88},{28,92},{32,9... | collective-permute-start | bytes 589832 | tf_op jit(solution)/shard_map/ppermute | solution.py:24
  89.7 5.6 %collective-permute-start.25 = (bf16[4,4,16,384]{3,2,1,0:T(8,128)(2,1)S(1)}, bf16[4,4,16,384]{3,2,1,0:T(8,128)(2,1)S(1)}, u32[]{:S(2)}, u32[]{:S(2)}) collective-permute-start(bf16[4,4,16,384]{3,2,1,0:T(8,128)(2,1)S(1)} %get-tuple-element.51), channel_id=1, source_target_pairs={{0,96},{4,100},{8,104},{12,108},{16,112},{20,116},{24,120},{28,124... | collective-permute-start | bytes 589832 | tf_op jit(solution)/shard_map/ppermute | solution.py:24
  96.0 9.1 %collective-permute-start.26 = (bf16[4,16,384]{2,1,0:T(8,128)(2,1)S(1)}, bf16[4,16,384]{2,1,0:T(8,128)(2,1)S(1)}, u32[]{:S(2)}, u32[]{:S(2)}) collective-permute-start(bf16[4,16,384]{2,1,0:T(8,128)(2,1)S(1)} %get-tuple-element.53), channel_id=1, source_target_pairs={{0,32},{4,36},{8,40},{12,44},{16,48},{20,52},{24,56},{28,60},{32,6... | collective-permute-start | bytes 147464 | tf_op jit(solution)/shard_map/ppermute | solution.py:24
  96.1 9.8 %collective-permute-start.27 = (bf16[4,16,384]{2,1,0:T(8,128)(2,1)S(1)}, bf16[4,16,384]{2,1,0:T(8,128)(2,1)S(1)}, u32[]{:S(2)}, u32[]{:S(2)}) collective-permute-start(bf16[4,16,384]{2,1,0:T(8,128)(2,1)S(1)} %get-tuple-element.54), channel_id=1, source_target_pairs={{0,64},{4,68},{8,72},{12,76},{16,80},{20,84},{24,88},{28,92},{32,9... | collective-permute-start | bytes 147464 | tf_op jit(solution)/shard_map/ppermute | solution.py:24
  100.7 5.8 %collective-permute-start.28 = (bf16[4,16,384]{2,1,0:T(8,128)(2,1)S(1)}, bf16[4,16,384]{2,1,0:T(8,128)(2,1)S(1)}, u32[]{:S(2)}, u32[]{:S(2)}) collective-permute-start(bf16[4,16,384]{2,1,0:T(8,128)(2,1)S(1)} %get-tuple-element.55), channel_id=1, source_target_pairs={{0,96},{4,100},{8,104},{12,108},{16,112},{20,116},{24,120},{28,124... | collective-permute-start | bytes 147464 | tf_op jit(solution)/shard_map/ppermute | solution.py:24
  100.7 5.8 %collective-permute-start.29 = (bf16[4,16,384]{2,1,0:T(8,128)(2,1)S(1)}, bf16[4,16,384]{2,1,0:T(8,128)(2,1)S(1)}, u32[]{:S(2)}, u32[]{:S(2)}) collective-permute-start(bf16[4,16,384]{2,1,0:T(8,128)(2,1)S(1)} %get-tuple-element.57), channel_id=1, source_target_pairs={{0,1},{1,2},{2,3},{3,0},{4,5},{5,6},{6,7},{7,4},{8,9},{9,10},{10,1... | collective-permute-start | bytes 147464 | tf_op jit(solution)/shard_map/ppermute | solution.py:28
  104.7 17.6 %collective-permute-start.16 = (bf16[128,2048]{1,0:T(8,128)(2,1)S(1)}, bf16[128,2048]{1,0:T(8,128)(2,1)S(1)}, u32[]{:S(2)}, u32[]{:S(2)}) collective-permute-start(bf16[128,2048]{1,0:T(8,128)(2,1)S(1)} %get-tuple-element.39), channel_id=1, source_target_pairs={{0,24},{4,28},{8,0},{12,4},{16,8},{20,12},{24,16},{28,20},{32,56},... | collective-permute-start | bytes 1572872 | tf_op jit(solution)/shard_map/ppermute | solution.py:24
  105.1 17.2 %collective-permute-start.17 = (bf16[128,2048]{1,0:T(8,128)(2,1)S(1)}, bf16[128,2048]{1,0:T(8,128)(2,1)}, u32[]{:S(2)}, u32[]{:S(2)}) collective-permute-start(bf16[128,2048]{1,0:T(8,128)(2,1)S(1)} %get-tuple-element.40), channel_id=1, source_target_pairs={{0,16},{4,20},{8,24},{12,28},{16,0},{20,4},{24,8},{28,12},{32,48},... | collective-permute-start | bytes 1572872 | tf_op jit(solution)/shard_map/ppermute | solution.py:24
  105.9 26.4 %collective-permute-start.18 = (bf16[128,2048]{1,0:T(8,128)(2,1)S(1)}, bf16[128,2048]{1,0:T(8,128)(2,1)}, u32[]{:S(2)}, u32[]{:S(2)}) collective-permute-start(bf16[128,2048]{1,0:T(8,128)(2,1)S(1)} %get-tuple-element.41), channel_id=1, source_target_pairs={{0,8},{4,12},{8,16},{12,20},{16,24},{20,28},{24,0},{28,4},{32,40},... | collective-permute-start | bytes 1572872 | tf_op jit(solution)/shard_map/ppermute | solution.py:24
  106.5 4.4 %collective-permute-start.30 = (bf16[4,16,384]{2,1,0:T(8,128)(2,1)S(1)}, bf16[4,16,384]{2,1,0:T(8,128)(2,1)S(1)}, u32[]{:S(2)}, u32[]{:S(2)}) collective-permute-start(bf16[4,16,384]{2,1,0:T(8,128)(2,1)S(1)} %get-tuple-element.58), channel_id=1, source_target_pairs={{0,2},{1,3},{2,0},{3,1},{4,6},{5,7},{6,4},{7,5},{8,10},{9,11},{10,... | collective-permute-start | bytes 147464 | tf_op jit(solution)/shard_map/ppermute | solution.py:28
  106.5 5.5 %collective-permute-start.31 = (bf16[4,16,384]{2,1,0:T(8,128)(2,1)S(1)}, bf16[4,16,384]{2,1,0:T(8,128)(2,1)S(1)}, u32[]{:S(2)}, u32[]{:S(2)}) collective-permute-start(bf16[4,16,384]{2,1,0:T(8,128)(2,1)S(1)} %get-tuple-element.59), channel_id=1, source_target_pairs={{0,3},{1,0},{2,1},{3,2},{4,7},{5,4},{6,5},{7,6},{8,11},{9,8},{10,9... | collective-permute-start | bytes 147464 | tf_op jit(solution)/shard_map/ppermute | solution.py:28
  112.7 21.8 %all-to-all-start = ((f32[8,16,384]{2,1,0:T(8,128)}), f32[8,16,384]{2,1,0:T(8,128)S(1)}, u32[]{:S(2)}, u32[]{:S(2)}) async-start(f32[8,16,384]{2,1,0:T(8,128)} %pad_maximum_fusion), calls=%async_computation | async-start | bytes 393216 | tf_op jit(solution)/shard_map/all_to_all | solution.py:239

commit v2 on v1

v2 whole, which is shorter than its diff:
```python
import jax
import jax.numpy as jnp
from jax import lax
from jax.experimental import pallas as pl
from jax.experimental.pallas import tpu as pltpu
from jax.sharding import PartitionSpec as P

NY, NZ, NC, NX = 4, 4, 2, 4
TOK, HD = 128, 128
BF, F32 = jnp.bfloat16, jnp.float32


def ctx_index(y, z, c):
    return (y * NZ + z) * NC + c


def ctx_hop(block, dy=0, dz=0, dc=0):
    route = [
        (ctx_index(y, z, c), ctx_index((y + dy) % NY, (z + dz) % NZ, (c + dc) % NC))
        for y in range(NY)
        for z in range(NZ)
        for c in range(NC)
    ]
    return lax.ppermute(block, "ctx", route)


def x_hop(block, dx):
    return lax.ppermute(block, "zero", [(i, (i + dx) % NX) for i in range(NX)])


def dot(a, b):
    return lax.dot_general(a, b, (((1,), (0,)), ((), ())), preferred_element_type=F32)


def dot_nt(a, b):
    return lax.dot_general(a, b, (((1,), (1,)), ((), ())), preferred_element_type=F32)


def dot_tn(a, b):
    return lax.dot_general(a, b, (((0,), (0,)), ((), ())), preferred_element_type=F32)


def call(kernel, outs, ins, scratch=(), flops=0, limit=16):
    moved = sum(a.size * a.dtype.itemsize for a in list(ins) + list(outs))
    vmem = pl.BlockSpec(memory_space=pltpu.VMEM)
    return pl.pallas_call(
        kernel,
        out_shape=list(outs),
        in_specs=[pl.BlockSpec(memory_space=pltpu.SMEM)] + [vmem] * (len(ins) - 1),
        out_specs=[vmem] * len(outs),
        scratch_shapes=list(scratch),
        compiler_params=pltpu.CompilerParams(vmem_limit_bytes=limit << 20),
        cost_estimate=pl.CostEstimate(flops=flops, bytes_accessed=moved, transcendentals=0),
    )(*ins)


def shape(dims, dtype):
    return jax.ShapeDtypeStruct(dims, dtype)


def after(value, deps):
    return lax.optimization_barrier((value, deps))[0]


def columns(place, step, start=0, size=512):
    block = lax.rem(place + NX - step, NX)
    return pl.ds(pl.multiple_of(block * 512 + start, 256), size)


PIECES = ((0, 0, 512), (1, 0, 512), (3, 0, 512), (2, 0, 256), (2, 256, 256))
TOKENS = ((0, 0, 128), (1, 0, 128), (3, 0, 128), (2, 0, 64), (2, 64, 64))


def take(idx, w, own, other, sem):
    head = 2 * idx[2] + idx[3]
    mate = 2 * idx[2] + 1 - idx[3]
    copies = []
    for i in range(3):
        for j, (h, out) in enumerate(((head, own), (mate, other))):
            at = pl.multiple_of(i * 1024 + h * HD, HD)
            copies.append(
                pltpu.make_async_copy(
                    w.at[:, pl.ds(at, HD)], out.at[:, i * HD : (i + 1) * HD], sem.at[2 * i + j]
                )
            )
    for copy in copies:
        copy.start()
    for copy in copies:
        copy.wait()


def project(idx, *refs):
    xs, mates, w, gs = refs[0:5], refs[5:10], refs[10:15], refs[15]
    xcat, qkv, r, total = refs[16:]
    xi, zi, ci = idx[0], idx[2], idx[3]
    for parity, parts in ((ci, xs), (1 - ci, mates)):
        for part, (s, start, size) in zip(parts, TOKENS, strict=True):
            block = lax.rem(zi + NZ - s, NZ) * 2 + parity
            xcat[pl.ds(pl.multiple_of(block * TOK + start, 64), size), :] = part[...]
    whole = jnp.zeros((HD, HD), F32)
    for m in range(4):
        rows = slice(m * 256, (m + 1) * 256)
        acc = jnp.zeros((256, 384), F32)
        for part, (s, start, size) in zip(w, PIECES, strict=True):
            acc += dot(xcat[rows, columns(xi, s, start, size)], part[...])
        rounded = acc.astype(BF)
        qkv[rows, :] = rounded
        for i in range(2):
            piece = dot_tn(rounded[i * TOK : (i + 1) * TOK, :HD], gs[2 * m + i, 0])
            r[2 * m + i] = piece
            whole += piece
    total[...] = whole.astype(BF)


def within(alpha, beta, idx, xcat, gs, qkv, dq, dk0, dv0, xt):
    rowi = lax.broadcasted_iota(jnp.int32, (TOK, TOK), 0)
    coli = lax.broadcasted_iota(jnp.int32, (TOK, TOK), 1)
    mask = rowi >= coli
    for b in range(8):
        rows = slice(b * TOK, (b + 1) * TOK)
        q, k, v = (qkv[rows, i * HD : (i + 1) * HD] for i in range(3))
        g, state = gs[b, 0], gs[b, 1]
        p1 = jnp.where(mask, dot_nt(g, v), 0.0).astype(BF)
        p2 = jnp.where(mask, dot_nt(q, k), 0.0).astype(BF)
        dq[rows, :] = (alpha * dot_nt(g, state) + beta * dot(p1, k)).astype(BF)
        dk0[rows, :] = dot_tn(p1, q)
        dv0[rows, :] = dot_tn(p2, g)
        xt[:, rows] = xcat[rows, :].T


def finish(beta, idx, qkv, dq, dk0, dv0, r, t1, t2, t3, dqkv, keep, send):
    yi, ci = idx[1], idx[3]
    acc = jnp.zeros((HD, HD), F32)
    for step, total in enumerate((t1, t2, t3)):
        use = jnp.where(yi < step + 1, 1.0, 0.0).astype(F32)
        acc += use * total[...].astype(F32)
    for b in range(7, -1, -1):
        rows = slice(b * TOK, (b + 1) * TOK)
        k, v = qkv[rows, HD : 2 * HD], qkv[rows, 2 * HD :]
        later = acc.astype(BF)
        dqkv[rows, :HD] = dq[rows, :]
        dqkv[rows, HD : 2 * HD] = (beta * (dk0[rows, :] + dot_nt(v, later))).astype(BF)
        dqkv[rows, 2 * HD :] = (beta * (dv0[rows, :] + dot(k, later))).astype(BF)
        acc += r[b]
    for z in range(NZ):
        keep[z] = dqkv[pl.ds(pl.multiple_of((2 * z + ci) * TOK, TOK), TOK), :]
        send[z] = dqkv[pl.ds(pl.multiple_of((2 * z + 1 - ci) * TOK, TOK), TOK), :]


def weights(idx, xt, dqkv, *refs):
    a, b, buf = refs[:4], refs[4:8], refs[8]
    xi, yi = idx[0], idx[1]
    for m in range(4):
        tile = dot(xt[m * 512 : (m + 1) * 512, :], dqkv[...])
        buf[m] = tile.reshape(8, NX, 16, 384)
    for s in range(4):
        to_x, to_y = lax.rem(xi + s, NX), lax.rem(yi + s, NY)
        for i in range(4):
            for g in range(4):
                a[s][i, g] = buf[i, g, to_x].astype(BF)
                b[s][g, i] = buf[to_y, 4 + g, i].astype(BF)


def back(idx, *refs):
    keep, got, own, other = refs[0], refs[1], refs[2:7], refs[7:12]
    mine_gx, up, down, far_up, far_down, gx = refs[12:]
    xi, zi = idx[0], idx[2]
    mine = keep[...].reshape(512, 384)
    theirs = got[...].reshape(512, 384)
    for p, q, (s, start, size) in zip(own, other, PIECES, strict=True):
        part = dot_nt(mine, p[...]) + dot_nt(theirs, q[...])
        gx[:, :, columns(xi, s, start, size)] = part.reshape(NZ, TOK, size)
    mine_gx[...] = gx[zi]
    up[...] = gx[lax.rem(zi + 1, NZ)].astype(BF)
    down[...] = gx[lax.rem(zi + 3, NZ)].astype(BF)
    far = lax.rem(zi + 2, NZ)
    far_up[...] = gx[far, :64, :].astype(BF)
    far_down[...] = gx[far, 64:, :].astype(BF)


def merge(idx, up, down, from_low, from_high, new_up, new_down):
    new_up[:64, :] = (up[:64, :].astype(F32) + from_low[...].astype(F32)).astype(BF)
    new_up[64:, :] = up[64:, :]
    new_down[:64, :] = down[:64, :]
    new_down[64:, :] = (down[64:, :].astype(F32) + from_high[...].astype(F32)).astype(BF)


def turn(idx, *refs):
    a, b = refs[0:4], refs[4:8]
    a2, b2 = refs[8:12], refs[12:16]
    xi, yi = idx[0], idx[1]
    for s in range(4):
        to_x, to_y = lax.rem(xi + s, NX), lax.rem(yi + s, NY)
        for g in range(4):
            a2[s][g] = sum(p[to_y, g].astype(F32) for p in a).astype(BF)
            b2[s][g] = sum(p[g, to_x].astype(F32) for p in b).astype(BF)


def body(inputs, grad_out, saved, w_qkv):
    x = inputs[0]
    heads, head_size = saved.shape[2], saved.shape[3]
    length = x.shape[0] * lax.axis_size("ctx")
    alpha = 1.0 / head_size**0.5
    beta = 1.0 / (head_size * length) ** 0.5
    scale = 1.0 / (length * lax.axis_size("zero")) ** 0.5
    ctx = lax.axis_index("ctx")
    xi, yi, zi, ci = lax.axis_index("zero"), ctx // 8, (ctx // 2) % 4, ctx % 2
    idx = jnp.stack([xi, yi, zi, ci]).astype(jnp.int32)
    rows_y = [[ctx_index(y, z, c) for z in range(NZ) for c in range(NC)] for y in range(NY)]

    x1, x3 = ctx_hop(x, dz=1), ctx_hop(x, dz=-1)
    own_w, other_w = pl.pallas_call(
        take,
        out_shape=[shape((512, 384), BF)] * 2,
        in_specs=[pl.BlockSpec(memory_space=pltpu.SMEM), pl.BlockSpec(memory_space=pltpu.HBM)],
        out_specs=[pl.BlockSpec(memory_space=pltpu.VMEM)] * 2,
        scratch_shapes=[pltpu.SemaphoreType.DMA((6,))],
        compiler_params=pltpu.CompilerParams(vmem_limit_bytes=4 << 20),
    )(idx, w_qkv)
    w1, w3 = x_hop(own_w, 1), x_hop(own_w, -1)
    x2a, x2b = ctx_hop(x1[:64], dz=1), ctx_hop(x3[64:], dz=-1)
    w2a, w2b = x_hop(w1[:256], 1), x_hop(w3[256:], -1)
    xs, own = [x, x1, x3, x2a, x2b], [own_w, w1, w3, w2a, w2b]
    mates = [ctx_hop(p, dc=1) for p in xs]
    other = [other_w] + [ctx_hop(p, dc=1) for p in own[1:]]
    cot = grad_out[0].reshape(TOK, heads, HD).transpose(1, 0, 2)
    bundle = jnp.stack([cot, saved[0, 0].astype(BF)], axis=1)
    gs = lax.all_to_all(bundle, "ctx", 0, 0, axis_index_groups=rows_y)

    big = 2 * 1024 * 2048 * 384
    xcat, qkv, r, total = call(
        project,
        [shape((1024, 2048), BF), shape((1024, 384), BF), shape((8, HD, HD), F32), shape((HD, HD), BF)],
        [idx, *xs, *mates, *own, gs],
        flops=big,
    )
    totals = [ctx_hop(total, dy=s) for s in (1, 2, 3)]
    dq, dk0, dv0, xt = call(
        lambda *refs: within(alpha, beta, *refs),
        [shape((1024, HD), BF), shape((1024, HD), F32), shape((1024, HD), F32), shape((2048, 1024), BF)],
        [idx, xcat, gs, qkv],
        flops=big // 4,
    )
    dqkv, keep, send = call(
        lambda *refs: finish(beta, *refs),
        [shape((1024, 384), BF), shape((NZ, TOK, 384), BF), shape((NZ, TOK, 384), BF)],
        [after(idx, other), qkv, dq, dk0, dv0, r, *totals],
        flops=big // 16,
    )
    got = ctx_hop(send, dc=1)
    parts = call(
        weights,
        [shape((NY, 4, 16, 384), BF)] * 4 + [shape((4, NX, 16, 384), BF)] * 4,
        [idx, xt, dqkv],
        [pltpu.VMEM((NY, 8, NX, 16, 384), F32)],
        flops=big,
    )
    a, b = parts[:4], parts[4:]
    a = [a[0]] + [x_hop(a[s], s) for s in (1, 2, 3)]
    b = [b[0]] + [ctx_hop(b[s], dy=s) for s in (1, 2, 3)]
    gx, up, down, far_up, far_down = call(
        back,
        [shape((TOK, 2048), F32)] + [shape((TOK, 2048), BF)] * 2 + [shape((64, 2048), BF)] * 2,
        [idx, keep, got, *own, *other],
        [pltpu.VMEM((NZ, TOK, 2048), F32)],
        flops=big,
    )
    far_up, far_down = ctx_hop(far_up, dz=1), ctx_hop(far_down, dz=-1)
    up, down = call(merge, [shape((TOK, 2048), BF)] * 2, [idx, up, down, far_up, far_down])
    parts = call(turn, [shape((4, 16, 384), BF)] * 8, [after(idx, up), *a, *b])
    up, down = ctx_hop(up, dz=1), ctx_hop(down, dz=-1)
    a, b = parts[:4], parts[4:]
    a = [a[0]] + [ctx_hop(a[s], dy=s) for s in (1, 2, 3)]
    b = [b[0]] + [x_hop(b[s], s) for s in (1, 2, 3)]
    owned = jnp.concatenate([sum(p.astype(F32) for p in a), sum(p.astype(F32) for p in b)], axis=0)
    owned = lax.all_to_all(owned, "ctx", 0, 0, axis_index_groups=rows_y)
    owned = owned.reshape(heads, 16, 3, HD).transpose(1, 2, 0, 3).reshape(16, 3 * heads * HD)
    grad_x = (gx + up.astype(F32) + down.astype(F32)).astype(BF)
    return (grad_x[None], owned * scale)


def solution(mesh):
    in_specs = (
        P("zero", "ctx", None),
        P("zero", "ctx", None),
        P("zero", "ctx", None, None, None),
        P("zero", None),
    )
    out_specs = (P("zero", "ctx", None), P(("ctx", "zero"), None))
    return jax.shard_map(body, mesh=mesh, in_specs=in_specs, out_specs=out_specs, check_vma=False)
```

time: 136 us -> 128 us (0.941)
  blocking collectives: 0 us -> 19 us
  waiting for transfers between devices: 47.8 us -> 29.9 us
  starting transfers between devices: 56.4 us -> 46.2 us
  Pallas kernels: 15.9 us -> 17.9 us
    ppermute x23 -> x27, waiting for transfers between devices: 38.1 us -> 15.1 us  [ctx_hop(): return lax.ppermute(block, 'ctx', route)]
    all_to_all x0 -> x1, blocking collectives: none -> 19 us  [body(): owned = lax.all_to_all(owned, 'ctx', 0, 0, axis_index_groups=rows_y)]
    all_to_all x1, waiting for transfers between devices: 0.01 us -> 8.96 us  [body(): gs = lax.all_to_all(bundle, 'ctx', 0, 0, axis_index_groups=rows_y)]
    ppermute x23 -> x27, starting transfers between devices: 37.7 us -> 32 us  [ctx_hop(): return lax.ppermute(block, 'ctx', route)]
    all_to_all x1, starting transfers between devices: 9.53 us -> 5.09 us  [body(): gs = lax.all_to_all(bundle, 'ctx', 0, 0, axis_index_groups=rows_y)]
    ppermute x9 -> x10, waiting for transfers between devices: 9.68 us -> 5.78 us  [x_hop(): return lax.ppermute(block, 'zero', [(i, (i + dx) % NX) for i in range(NX)])]
    unnamed x4 -> x30, local copies, waits for them, and re-layouts: 5.39 us -> 7.38 us
    dynamic_slice x1 -> x0, local copies, waits for them, and re-layouts: 1.99 us -> none  [body(): lax.dynamic_index_in_dim(by_head, 2 * zi + 1 - ci, 2, keepdims=False)]
  transfers between devices with their start and end apart: 33 -> 38, of which waited for: 12 -> 13; matrix products, arithmetic and copies ran while one was open for 8% -> 5% of each run, Pallas kernels for 5% -> 6%
where the time goes in v2:
time: 128 us
  starting transfers between devices  46.2 us (36%)
  waiting for transfers between devices  29.9 us (23%)
  blocking collectives  19 us (15%)
  Pallas kernels  17.9 us (14%)
  local copies, waits for them, and re-layouts  9.21 us (7%)
  other arithmetic  4.78 us (4%)
    ppermute x27, starting transfers between devices, ctx_hop(): return lax.ppermute(block, 'ctx', route)  32 us
    all_to_all x1, blocking collectives, body(): owned = lax.all_to_all(owned, 'ctx', 0, 0, axis_index_groups=rows_y)  19 us
    pallas_call x7, Pallas kernels, call(): pl.pallas_call(kernel, out_shape=list(outs), in_specs=[pl.BlockSpec(memor...  17.1 us
    ppermute x27, waiting for transfers between devices, ctx_hop(): return lax.ppermute(block, 'ctx', route)  15.1 us
    ppermute x10, starting transfers between devices, x_hop(): return lax.ppermute(block, 'zero', [(i, (i + dx) % NX) for i in range(NX)])  9.18 us
    all_to_all x1, waiting for transfers between devices, body(): gs = lax.all_to_all(bundle, 'ctx', 0, 0, axis_index_groups=rows_y)  8.96 us
    unnamed x30, local copies, waits for them, and re-layouts  7.38 us
    ppermute x10, waiting for transfers between devices, x_hop(): return lax.ppermute(block, 'zero', [(i, (i + dx) % NX) for i in range(NX)])  5.78 us
  transfers between devices with their start and end apart: 38, of which 13 were waited for; matrix products, arithmetic and copies ran while one was open for 5% of the time, Pallas kernels for 6%

profile of v2, /device:TPU:1, one launch (start us, length us, event | category | flops | bytes accessed | tf_op | source)
XLA Modules:
  0.0 128.0 jit_solution(6708548166218627448)
XLA Ops:
  0.6 2.5 %collective-permute-start.8 = (bf16[128,2048]{1,0:T(8,128)(2,1)}, bf16[128,2048]{1,0:T(8,128)(2,1)S(1)}, u32[]{:S(2)}, u32[]{:S(2)}) collective-permute-start(bf16[128,2048]{1,0:T(8,128)(2,1)} %bitcast.19), channel_id=1, source_target_pairs={{0,8},{4,12},{8,16},{12,20},{16,24},{20,28},{24,0},{28,4},{32,40},... | collective-permute-start | bytes 1572872 | tf_op jit(solution)/shard_map/ppermute | solution.py:24
  3.2 1.9 %copy-done = bf16[512,3072]{1,0:T(8,128)(2,1)S(1)} copy-done((bf16[512,3072]{1,0:T(8,128)(2,1)S(1)}, bf16[512,3072]{1,0:T(8,128)(2,1)}, u32[]{:S(2)}) %copy-start) | copy-done | bytes 3145752
  5.1 0.8 shard_map.59
  6.0 0.8 copy-done.11
  6.8 1.2 collective-permute-start
  8.0 1.5 %collective-permute-start.2 = (bf16[512,384]{1,0:T(8,128)(2,1)S(1)}, bf16[512,384]{1,0:T(8,128)(2,1)S(1)}, u32[]{:S(2)}, u32[]{:S(2)}) collective-permute-start(bf16[512,384]{1,0:T(8,128)(2,1)S(1)} %get-tuple-element.41.refs_10_.refs_2_), channel_id=1, source_target_pairs={{0,3},{1,0},{2,1},{3,2},{4,7},{5,4},{6,5},{7,6},{8,11},{9,8},{10,9... | collective-permute-start | bytes 1179656 | tf_op jit(solution)/shard_map/ppermute | solution.py:28
  9.4 2.2 %collective-permute-start.9 = (bf16[128,2048]{1,0:T(8,128)(2,1)}, bf16[128,2048]{1,0:T(8,128)(2,1)S(1)}, u32[]{:S(2)}, u32[]{:S(2)}) collective-permute-start(bf16[128,2048]{1,0:T(8,128)(2,1)} %bitcast.20), channel_id=1, source_target_pairs={{0,24},{4,28},{8,0},{12,4},{16,8},{20,12},{24,16},{28,20},{32,56},... | collective-permute-start | bytes 1572872 | tf_op jit(solution)/shard_map/ppermute | solution.py:24
  11.6 5.5 %collective-permute-done.8.refs_1_ = bf16[128,2048]{1,0:T(8,128)(2,1)S(1)} collective-permute-done((bf16[128,2048]{1,0:T(8,128)(2,1)}, bf16[128,2048]{1,0:T(8,128)(2,1)S(1)}, u32[]{:S(2)}, u32[]{:S(2)}) %collective-permute-start.8) | collective-permute-done | bytes 524320 | tf_op jit(solution)/shard_map/ppermute | solution.py:24
  17.7 0.9 collective-permute-start.4
  18.6 1.9 %collective-permute-start.6 = (bf16[256,384]{1,0:T(8,128)(2,1)S(1)}, bf16[256,384]{1,0:T(8,128)(2,1)S(1)}, u32[]{:S(2)}, u32[]{:S(2)}) collective-permute-start(bf16[256,384]{1,0:T(8,128)(2,1)S(1)} %slice.17), channel_id=1, source_target_pairs={{0,3},{1,0},{2,1},{3,2},{4,7},{5,4},{6,5},{7,6},{8,11},{9,8},{10,9... | collective-permute-start | bytes 589832 | tf_op jit(solution)/shard_map/ppermute | solution.py:28
  20.5 1.4 %collective-permute-done.9.refs_2_ = bf16[128,2048]{1,0:T(8,128)(2,1)S(1)} collective-permute-done((bf16[128,2048]{1,0:T(8,128)(2,1)}, bf16[128,2048]{1,0:T(8,128)(2,1)S(1)}, u32[]{:S(2)}, u32[]{:S(2)}) %collective-permute-start.9) | collective-permute-done | bytes 524320 | tf_op jit(solution)/shard_map/ppermute | solution.py:24
  22.6 3.3 %collective-permute-start.11 = (bf16[64,2048]{1,0:T(8,128)(2,1)}, bf16[64,2048]{1,0:T(8,128)(2,1)}, u32[]{:S(2)}, u32[]{:S(2)}) collective-permute-start(bf16[64,2048]{1,0:T(8,128)(2,1)} %slice.19), channel_id=1, source_target_pairs={{0,24},{4,28},{8,0},{12,4},{16,8},{20,12},{24,16},{28,20},{32,56},... | collective-permute-start | bytes 786440 | tf_op jit(solution)/shard_map/ppermute | solution.py:24
  25.9 2.4 %collective-permute-start.1 = (bf16[512,384]{1,0:T(8,128)(2,1)S(1)}, bf16[512,384]{1,0:T(8,128)(2,1)}, u32[]{:S(2)}, u32[]{:S(2)}) collective-permute-start(bf16[512,384]{1,0:T(8,128)(2,1)S(1)} %collective-permute-done.refs_11_.refs_3_), channel_id=1, source_target_pairs={{0,4},{4,0},{8,12},{12,8},{16,20},{20,16},{24,28},{28,24},{32,36},... | collective-permute-start | bytes 1179656 | tf_op jit(solution)/shard_map/ppermute | solution.py:24
  29.8 1.1 copy.9
  30.9 0.9 copy.10
  31.8 1.0 collective-permute-start.12
  33.3 1.9 %pad_maximum_fusion = bf16[8,2,128,128]{3,2,1,0:T(8,128)(2,1)} fusion(bf16[8,1,128,128]{3,2,1,0:T(8,128)(2,1)} %convert_bitcast_fusion, bf16[8,1,128,128]{3,2,1,0:T(8,128)(2,1)} %bitcast.25), kind=kLoop, calls=%fused_computation.2 | loop fusion | flops 262144 | bytes 1048576 | tf_op jit(solution)/shard_map/stack | solution.py:227
  35.2 5.1 %all-to-all-start = ((bf16[8,2,128,128]{3,2,1,0:T(8,128)(2,1)}), bf16[8,2,128,128]{3,2,1,0:T(8,128)(2,1)S(1)}, u32[]{:S(2)}, u32[]{:S(2)}) async-start(bf16[8,2,128,128]{3,2,1,0:T(8,128)(2,1)} %pad_maximum_fusion), calls=%async_computation | async-start | bytes 1048576 | tf_op jit(solution)/shard_map/all_to_all | solution.py:228
  40.8 9.0 %all-to-all-done.refs_15_.refs_2_ = bf16[8,2,128,128]{3,2,1,0:T(8,128)(2,1)S(1)} async-done(((bf16[8,2,128,128]{3,2,1,0:T(8,128)(2,1)}), bf16[8,2,128,128]{3,2,1,0:T(8,128)(2,1)S(1)}, u32[]{:S(2)}, u32[]{:S(2)}) %all-to-all-start) | async-done | bytes 524320 | tf_op jit(solution)/shard_map/all_to_all | solution.py:228
  49.8 1.0 copy-done.3
  50.8 0.9 copy-done.6
  51.7 0.9 copy-done.9
  52.6 4.8 %shard_map.60 = (bf16[1024,2048]{1,0:T(8,128)(2,1)S(1)}, bf16[1024,384]{1,0:T(8,128)(2,1)S(1)}, f32[8,128,128]{2,1,0:T(8,128)S(1)}, bf16[128,128]{1,0:T(8,128)(2,1)S(1)}) custom-call(s32[4]{0:T(128)S(1)} %pad_add_fusion.idx.refs_0_, bf16[128,2048]{1,0:T(8,128)(2,1)S(1)} %bitcast.22, bf16[128,2048]{1,0:T(8,128)(2,1)S(1)} %collective-permute-done.8.refs_1_, ...), custom_call_target="tpu_custom_call" | custom-call | flops 1610612736 | bytes 11829264 | tf_op jit(solution)/shard_map/pallas_call | solution.py:46
  57.5 1.4 %collective-permute-start.17 = (bf16[128,128]{1,0:T(8,128)(2,1)S(1)}, bf16[128,128]{1,0:T(8,128)(2,1)S(1)}, u32[]{:S(2)}, u32[]{:S(2)}) collective-permute-start(bf16[128,128]{1,0:T(8,128)(2,1)S(1)} %get-tuple-element.49), channel_id=1, source_target_pairs={{0,32},{4,36},{8,40},{12,44},{16,48},{20,52},{24,56},{28,60},{32,6... | collective-permute-start | bytes 98312 | tf_op jit(solution)/shard_map/ppermute | solution.py:24
  58.9 2.6 %collective-permute-start.18 = (bf16[128,128]{1,0:T(8,128)(2,1)S(1)}, bf16[128,128]{1,0:T(8,128)(2,1)S(1)}, u32[]{:S(2)}, u32[]{:S(2)}) collective-permute-start(bf16[128,128]{1,0:T(8,128)(2,1)S(1)} %get-tuple-element.49), channel_id=1, source_target_pairs={{0,64},{4,68},{8,72},{12,76},{16,80},{20,84},{24,88},{28,92},{32,9... | collective-permute-start | bytes 98312 | tf_op jit(solution)/shard_map/ppermute | solution.py:24
  61.5 1.1 collective-permute-start.19
  62.6 2.7 %shard_map.61 = (bf16[1024,128]{1,0:T(8,128)(2,1)S(1)}, f32[1024,128]{1,0:T(8,128)S(1)}, f32[1024,128]{1,0:T(8,128)S(1)}, bf16[2048,1024]{1,0:T(8,128)(2,1)S(1)}) custom-call(s32[4]{0:T(128)S(1)} %pad_add_fusion.idx.refs_0_, bf16[1024,2048]{1,0:T(8,128)(2,1)S(1)} %get-tuple-element.44.refs_1_, bf16[8,2,128,128]{3,2,1,0:T(8,128)(2,1)S(1)} %all-to-all-done.refs_15_.refs_2_, ...), custom_call_target="tpu_custom_call" | custom-call | flops 402653184 | bytes 11010064 | tf_op jit(solution)/shard_map/pallas_call | solution.py:46
  65.3 1.0 shard_map.62
  66.3 1.8 %collective-permute-start.20 = (bf16[4,128,384]{2,1,0:T(8,128)(2,1)S(1)}, bf16[4,128,384]{2,1,0:T(8,128)(2,1)S(1)}, u32[]{:S(2)}, u32[]{:S(2)}) collective-permute-start(bf16[4,128,384]{2,1,0:T(8,128)(2,1)S(1)} %get-tuple-element.51), channel_id=1, source_target_pairs={{0,4},{4,0},{8,12},{12,8},{16,20},{20,16},{24,28},{28,24},{32,36},... | collective-permute-start | bytes 1179656 | tf_op jit(solution)/shard_map/ppermute | solution.py:24
  68.1 1.3 %collective-permute-done.20.refs_1_ = bf16[4,128,384]{2,1,0:T(8,128)(2,1)S(1)} collective-permute-done((bf16[4,128,384]{2,1,0:T(8,128)(2,1)S(1)}, bf16[4,128,384]{2,1,0:T(8,128)(2,1)S(1)}, u32[]{:S(2)}, u32[]{:S(2)}) %collective-permute-start.20) | collective-permute-done | bytes 393248 | tf_op jit(solution)/shard_map/ppermute | solution.py:24
  69.5 3.9 %shard_map.63 = (f32[128,2048]{1,0:T(8,128)S(1)}, bf16[128,2048]{1,0:T(8,128)(2,1)S(1)}, bf16[128,2048]{1,0:T(8,128)(2,1)S(1)}, bf16[64,2048]{1,0:T(8,128)(2,1)S(1)}, bf16[64,2048]{1,0:T(8,128)(2,1)S(1)}) custom-call(s32[4]{0:T(128)S(1)} %pad_add_fusion.idx.refs_0_, bf16[4,128,384]{2,1,0:T(8,128)(2,1)S(1)} %get-tuple-element.50.refs_0_, ...), custom_call_target="tpu_custom_call" | custom-call | flops 1610612736 | bytes 6553616 | tf_op jit(solution)/shard_map/pallas_call | solution.py:46
  73.7 2.4 %collective-permute-start.22 = (bf16[64,2048]{1,0:T(8,128)(2,1)S(1)}, bf16[64,2048]{1,0:T(8,128)(2,1)S(1)}, u32[]{:S(2)}, u32[]{:S(2)}) collective-permute-start(bf16[64,2048]{1,0:T(8,128)(2,1)S(1)} %get-tuple-element.56), channel_id=1, source_target_pairs={{0,24},{4,28},{8,0},{12,4},{16,8},{20,12},{24,16},{28,20},{32,56},... | collective-permute-start | bytes 786440 | tf_op jit(solution)/shard_map/ppermute | solution.py:24
  76.1 3.3 %shard_map.65 = (bf16[4,4,16,384]{3,2,1,0:T(8,128)(2,1)S(1)}, bf16[4,4,16,384]{3,2,1,0:T(8,128)(2,1)S(1)}, bf16[4,4,16,384]{3,2,1,0:T(8,128)(2,1)S(1)}, bf16[4,4...) custom-call(s32[4]{0:T(128)S(1)} %pad_add_fusion.idx.refs_0_, ...), custom_call_target="tpu_custom_call" | custom-call | flops 1610612736 | bytes 6553616 | tf_op jit(solution)/shard_map/pallas_call | solution.py:46
  79.5 2.4 %collective-permute-start.26 = (bf16[4,4,16,384]{3,2,1,0:T(8,128)(2,1)S(1)}, bf16[4,4,16,384]{3,2,1,0:T(8,128)(2,1)S(1)}, u32[]{:S(2)}, u32[]{:S(2)}) collective-permute-start(bf16[4,4,16,384]{3,2,1,0:T(8,128)(2,1)S(1)} %get-tuple-element.64), channel_id=1, source_target_pairs={{0,2},{1,3},{2,0},{3,1},{4,6},{5,7},{6,4},{7,5},{8,10},{9,11},{10,... | collective-permute-start | bytes 589832 | tf_op jit(solution)/shard_map/ppermute | solution.py:28
  81.9 1.2 collective-permute-start.27
  83.1 3.3 %collective-permute-done.25.refs_1_ = bf16[4,4,16,384]{3,2,1,0:T(8,128)(2,1)S(1)} collective-permute-done((bf16[4,4,16,384]{3,2,1,0:T(8,128)(2,1)S(1)}, bf16[4,4,16,384]{3,2,1,0:T(8,128)(2,1)S(1)}, u32[]{:S(2)}, u32[]{:S(2)}) %collective-permute-start.25) | collective-permute-done | bytes 196640 | tf_op jit(solution)/shard_map/ppermute | solution.py:28
  86.7 2.9 %collective-permute-start.29 = (bf16[4,4,16,384]{3,2,1,0:T(8,128)(2,1)S(1)}, bf16[4,4,16,384]{3,2,1,0:T(8,128)(2,1)S(1)}, u32[]{:S(2)}, u32[]{:S(2)}) collective-permute-start(bf16[4,4,16,384]{3,2,1,0:T(8,128)(2,1)S(1)} %get-tuple-element.68), channel_id=1, source_target_pairs={{0,64},{4,68},{8,72},{12,76},{16,80},{20,84},{24,88},{28,92},{32,9... | collective-permute-start | bytes 589832 | tf_op jit(solution)/shard_map/ppermute | solution.py:24
  90.3 0.9 collective-permute-done.27.refs_3_
  91.2 0.8 collective-permute-done.28.refs_5_
  92.1 2.7 %collective-permute-done.29.refs_6_ = bf16[4,4,16,384]{3,2,1,0:T(8,128)(2,1)S(1)} collective-permute-done((bf16[4,4,16,384]{3,2,1,0:T(8,128)(2,1)S(1)}, bf16[4,4,16,384]{3,2,1,0:T(8,128)(2,1)S(1)}, u32[]{:S(2)}, u32[]{:S(2)}) %collective-permute-start.29) | collective-permute-done | bytes 196640 | tf_op jit(solution)/shard_map/ppermute | solution.py:24
  94.8 0.7 shard_map.66
  96.0 3.1 %collective-permute-start.32 = (bf16[4,16,384]{2,1,0:T(8,128)(2,1)S(1)}, bf16[4,16,384]{2,1,0:T(8,128)(2,1)S(1)}, u32[]{:S(2)}, u32[]{:S(2)}) collective-permute-start(bf16[4,16,384]{2,1,0:T(8,128)(2,1)S(1)} %get-tuple-element.72), channel_id=1, source_target_pairs={{0,64},{4,68},{8,72},{12,76},{16,80},{20,84},{24,88},{28,92},{32,9... | collective-permute-start | bytes 147464 | tf_op jit(solution)/shard_map/ppermute | solution.py:24
  99.2 2.3 %collective-permute-done.31 = bf16[4,16,384]{2,1,0:T(8,128)(2,1)S(1)} collective-permute-done((bf16[4,16,384]{2,1,0:T(8,128)(2,1)S(1)}, bf16[4,16,384]{2,1,0:T(8,128)(2,1)S(1)}, u32[]{:S(2)}, u32[]{:S(2)}) %collective-permute-start.31) | collective-permute-done | bytes 49184 | tf_op jit(solution)/shard_map/ppermute | solution.py:24
  101.5 0.8 collective-permute-done.32
  102.4 2.3 %collective-permute-start.24 = (bf16[128,2048]{1,0:T(8,128)(2,1)S(1)}, bf16[128,2048]{1,0:T(8,128)(2,1)}, u32[]{:S(2)}, u32[]{:S(2)}) collective-permute-start(bf16[128,2048]{1,0:T(8,128)(2,1)S(1)} %get-tuple-element.58), channel_id=1, source_target_pairs={{0,24},{4,28},{8,0},{12,4},{16,8},{20,12},{24,16},{28,20},{32,56},... | collective-permute-start | bytes 1572872 | tf_op jit(solution)/shard_map/ppermute | solution.py:24
  104.7 1.2 collective-permute-done.35
  106.0 19.0 %all_to_all.10 = f32[8,16,384]{2,1,0:T(8,128)S(1)} all-to-all(f32[8,16,384]{2,1,0:T(8,128)S(1)} %pad_maximum_fusion.1), channel_id=1, replica_groups={{0,4,8,12,16,20,24,28},{32,36,40,44,48,52,56,60},{64,68,72,76,80,84,88,..., dimensions={0} | all-to-all | bytes 393216 | tf_op jit(solution)/shard_map/all_to_all | solution.py:276
  125.9 2.0 %fusion = bf16[1,128,2048]{2,1,0:T(8,128)(2,1)} fusion(bf16[128,2048]{1,0:T(8,128)(2,1)} %collective-permute-done.24, f32[128,2048]{1,0:T(8,128)S(1)} %get-tuple-element.52, bf16[128,2048]{1,0:T(8,128)(2,1)S(1)} %collective-permute-done.23), kind=kLoop, calls=%fused_computation.1 | loop fusion | flops 1310720 | bytes 2621440 | tf_op jit(solution)/shard_map/broadcast_in_dim | solution.py:279
  (82 shorter events, 7.1 us)
Async XLA Ops:
  0.6 16.5 %collective-permute-start.8 = (bf16[128,2048]{1,0:T(8,128)(2,1)}, bf16[128,2048]{1,0:T(8,128)(2,1)S(1)}, u32[]{:S(2)}, u32[]{:S(2)}) collective-permute-start(bf16[128,2048]{1,0:T(8,128)(2,1)} %bitcast.19), channel_id=1, source_target_pairs={{0,8},{4,12},{8,16},{12,20},{16,24},{20,28},{24,0},{28,4},{32,40},... | collective-permute-start | bytes 1572872 | tf_op jit(solution)/shard_map/ppermute | solution.py:24
  3.2 1.9 %copy-start = (bf16[512,3072]{1,0:T(8,128)(2,1)S(1)}, bf16[512,3072]{1,0:T(8,128)(2,1)}, u32[]{:S(2)}) copy-start(bf16[512,3072]{1,0:T(8,128)(2,1)} %w.1) | copy-start | bytes 9437188
  5.1 24.0 %copy-start.13 = (f32[1,1,8,128,128]{4,3,2,1,0:T(8,128)S(1)}, f32[1,1,8,128,128]{4,3,2,1,0:T(8,128)}, u32[]{:S(2)}) copy-start(f32[1,1,8,128,128]{4,3,2,1,0:T(8,128)} %param.6) | copy-start | bytes 1572868
  5.1 26.7 %copy-start.1 = (bf16[1,128,2048]{2,1,0:T(8,128)(2,1)S(1)}, bf16[1,128,2048]{2,1,0:T(8,128)(2,1)}, u32[]{:S(2)}) copy-start(bf16[1,128,2048]{2,1,0:T(8,128)(2,1)} %param.4) | copy-start | bytes 1572868
  6.8 21.6 %copy-start.2 = (bf16[512,384]{1,0:T(8,128)(2,1)}, bf16[512,384]{1,0:T(8,128)(2,1)S(1)}, u32[]{:S(2)}) copy-start(bf16[512,384]{1,0:T(8,128)(2,1)S(1)} %get-tuple-element.41.refs_10_.refs_2_) | copy-start | bytes 1179652
  6.8 10.9 %collective-permute-start = (bf16[512,384]{1,0:T(8,128)(2,1)S(1)}, bf16[512,384]{1,0:T(8,128)(2,1)S(1)}, u32[]{:S(2)}, u32[]{:S(2)}) collective-permute-start(bf16[512,384]{1,0:T(8,128)(2,1)S(1)} %get-tuple-element.41.refs_10_.refs_2_), channel_id=1, source_target_pairs={{0,1},{1,2},{2,3},{3,0},{4,5},{5,6},{6,7},{7,4},{8,9},{9,10},{10,1... | collective-permute-start | bytes 1179656 | tf_op jit(solution)/shard_map/ppermute | solution.py:28
  8.0 10.6 %collective-permute-start.2 = (bf16[512,384]{1,0:T(8,128)(2,1)S(1)}, bf16[512,384]{1,0:T(8,128)(2,1)S(1)}, u32[]{:S(2)}, u32[]{:S(2)}) collective-permute-start(bf16[512,384]{1,0:T(8,128)(2,1)S(1)} %get-tuple-element.41.refs_10_.refs_2_), channel_id=1, source_target_pairs={{0,3},{1,0},{2,1},{3,2},{4,7},{5,4},{6,5},{7,6},{8,11},{9,8},{10,9... | collective-permute-start | bytes 1179656 | tf_op jit(solution)/shard_map/ppermute | solution.py:28
  9.4 12.5 %collective-permute-start.9 = (bf16[128,2048]{1,0:T(8,128)(2,1)}, bf16[128,2048]{1,0:T(8,128)(2,1)S(1)}, u32[]{:S(2)}, u32[]{:S(2)}) collective-permute-start(bf16[128,2048]{1,0:T(8,128)(2,1)} %bitcast.20), channel_id=1, source_target_pairs={{0,24},{4,28},{8,0},{12,4},{16,8},{20,12},{24,16},{28,20},{32,56},... | collective-permute-start | bytes 1572872 | tf_op jit(solution)/shard_map/ppermute | solution.py:24
  17.2 11.8 %collective-permute-start.10 = (bf16[64,2048]{1,0:T(8,128)(2,1)S(1)}, bf16[64,2048]{1,0:T(8,128)(2,1)}, u32[]{:S(2)}, u32[]{:S(2)}) collective-permute-start(bf16[64,2048]{1,0:T(8,128)(2,1)S(1)} %slice.18), channel_id=1, source_target_pairs={{0,8},{4,12},{8,16},{12,20},{16,24},{20,28},{24,0},{28,4},{32,40},... | collective-permute-start | bytes 786440 | tf_op jit(solution)/shard_map/ppermute | solution.py:24
  17.7 10.7 %collective-permute-start.4 = (bf16[256,384]{1,0:T(8,128)(2,1)S(1)}, bf16[256,384]{1,0:T(8,128)(2,1)S(1)}, u32[]{:S(2)}, u32[]{:S(2)}) collective-permute-start(bf16[256,384]{1,0:T(8,128)(2,1)S(1)} %slice.16), channel_id=1, source_target_pairs={{0,1},{1,2},{2,3},{3,0},{4,5},{5,6},{6,7},{7,4},{8,9},{9,10},{10,1... | collective-permute-start | bytes 589832 | tf_op jit(solution)/shard_map/ppermute | solution.py:28
  18.6 9.9 %collective-permute-start.6 = (bf16[256,384]{1,0:T(8,128)(2,1)S(1)}, bf16[256,384]{1,0:T(8,128)(2,1)S(1)}, u32[]{:S(2)}, u32[]{:S(2)}) collective-permute-start(bf16[256,384]{1,0:T(8,128)(2,1)S(1)} %slice.17), channel_id=1, source_target_pairs={{0,3},{1,0},{2,1},{3,2},{4,7},{5,4},{6,5},{7,6},{8,11},{9,8},{10,9... | collective-permute-start | bytes 589832 | tf_op jit(solution)/shard_map/ppermute | solution.py:28
  22.6 9.2 %collective-permute-start.11 = (bf16[64,2048]{1,0:T(8,128)(2,1)}, bf16[64,2048]{1,0:T(8,128)(2,1)}, u32[]{:S(2)}, u32[]{:S(2)}) collective-permute-start(bf16[64,2048]{1,0:T(8,128)(2,1)} %slice.19), channel_id=1, source_target_pairs={{0,24},{4,28},{8,0},{12,4},{16,8},{20,12},{24,16},{28,20},{32,56},... | collective-permute-start | bytes 786440 | tf_op jit(solution)/shard_map/ppermute | solution.py:24
  25.9 14.3 %collective-permute-start.1 = (bf16[512,384]{1,0:T(8,128)(2,1)S(1)}, bf16[512,384]{1,0:T(8,128)(2,1)}, u32[]{:S(2)}, u32[]{:S(2)}) collective-permute-start(bf16[512,384]{1,0:T(8,128)(2,1)S(1)} %collective-permute-done.refs_11_.refs_3_), channel_id=1, source_target_pairs={{0,4},{4,0},{8,12},{12,8},{16,20},{20,16},{24,28},{28,24},{32,36},... | collective-permute-start | bytes 1179656 | tf_op jit(solution)/shard_map/ppermute | solution.py:24
  28.4 6.8 %copy-start.5 = (bf16[256,384]{1,0:T(8,128)(2,1)}, bf16[256,384]{1,0:T(8,128)(2,1)S(1)}, u32[]{:S(2)}) copy-start(bf16[256,384]{1,0:T(8,128)(2,1)S(1)} %collective-permute-done.4.refs_13_.refs_5_) | copy-start | bytes 589828
  28.4 12.0 %collective-permute-start.3 = (bf16[512,384]{1,0:T(8,128)(2,1)S(1)}, bf16[512,384]{1,0:T(8,128)(2,1)}, u32[]{:S(2)}, u32[]{:S(2)}) collective-permute-start(bf16[512,384]{1,0:T(8,128)(2,1)S(1)} %collective-permute-done.2.refs_12_.refs_4_), channel_id=1, source_target_pairs={{0,4},{4,0},{8,12},{12,8},{16,20},{20,16},{24,28},{28,24},{32,36},... | collective-permute-start | bytes 1179656 | tf_op jit(solution)/shard_map/ppermute | solution.py:24
  28.5 6.7 %copy-start.8 = (bf16[256,384]{1,0:T(8,128)(2,1)}, bf16[256,384]{1,0:T(8,128)(2,1)S(1)}, u32[]{:S(2)}) copy-start(bf16[256,384]{1,0:T(8,128)(2,1)S(1)} %collective-permute-done.6.refs_14_.refs_6_) | copy-start | bytes 589828
  28.5 4.3 %collective-permute-start.5 = (bf16[256,384]{1,0:T(8,128)(2,1)S(1)}, bf16[256,384]{1,0:T(8,128)(2,1)}, u32[]{:S(2)}, u32[]{:S(2)}) collective-permute-start(bf16[256,384]{1,0:T(8,128)(2,1)S(1)} %collective-permute-done.4.refs_13_.refs_5_), channel_id=1, source_target_pairs={{0,4},{4,0},{8,12},{12,8},{16,20},{20,16},{24,28},{28,24},{32,36},... | collective-permute-start | bytes 589832 | tf_op jit(solution)/shard_map/ppermute | solution.py:24
  29.0 3.9 %collective-permute-start.7 = (bf16[256,384]{1,0:T(8,128)(2,1)S(1)}, bf16[256,384]{1,0:T(8,128)(2,1)}, u32[]{:S(2)}, u32[]{:S(2)}) collective-permute-start(bf16[256,384]{1,0:T(8,128)(2,1)S(1)} %collective-permute-done.6.refs_14_.refs_6_), channel_id=1, source_target_pairs={{0,4},{4,0},{8,12},{12,8},{16,20},{20,16},{24,28},{28,24},{32,36},... | collective-permute-start | bytes 589832 | tf_op jit(solution)/shard_map/ppermute | solution.py:24
  31.8 17.9 %collective-permute-start.12 = (bf16[128,2048]{1,0:T(8,128)(2,1)S(1)}, bf16[128,2048]{1,0:T(8,128)(2,1)S(1)}, u32[]{:S(2)}, u32[]{:S(2)}) collective-permute-start(bf16[128,2048]{1,0:T(8,128)(2,1)S(1)} %bitcast.21), channel_id=1, source_target_pairs={{0,4},{4,0},{8,12},{12,8},{16,20},{20,16},{24,28},{28,24},{32,36},... | collective-permute-start | bytes 1572872 | tf_op jit(solution)/shard_map/ppermute | solution.py:24
  32.8 17.0 %collective-permute-start.13 = (bf16[128,2048]{1,0:T(8,128)(2,1)S(1)}, bf16[128,2048]{1,0:T(8,128)(2,1)}, u32[]{:S(2)}, u32[]{:S(2)}) collective-permute-start(bf16[128,2048]{1,0:T(8,128)(2,1)S(1)} %collective-permute-done.8.refs_1_), channel_id=1, source_target_pairs={{0,4},{4,0},{8,12},{12,8},{16,20},{20,16},{24,28},{28,24},{32,36},... | collective-permute-start | bytes 1572872 | tf_op jit(solution)/shard_map/ppermute | solution.py:24
  32.9 16.9 %collective-permute-start.14 = (bf16[128,2048]{1,0:T(8,128)(2,1)S(1)}, bf16[128,2048]{1,0:T(8,128)(2,1)}, u32[]{:S(2)}, u32[]{:S(2)}) collective-permute-start(bf16[128,2048]{1,0:T(8,128)(2,1)S(1)} %collective-permute-done.9.refs_2_), channel_id=1, source_target_pairs={{0,4},{4,0},{8,12},{12,8},{16,20},{20,16},{24,28},{28,24},{32,36},... | collective-permute-start | bytes 1572872 | tf_op jit(solution)/shard_map/ppermute | solution.py:24
  35.2 14.6 %all-to-all-start = ((bf16[8,2,128,128]{3,2,1,0:T(8,128)(2,1)}), bf16[8,2,128,128]{3,2,1,0:T(8,128)(2,1)S(1)}, u32[]{:S(2)}, u32[]{:S(2)}) async-start(bf16[8,2,128,128]{3,2,1,0:T(8,128)(2,1)} %pad_maximum_fusion), calls=%async_computation | async-start | bytes 1048576 | tf_op jit(solution)/shard_map/all_to_all | solution.py:228
  40.3 9.5 %collective-permute-start.15 = (bf16[64,2048]{1,0:T(8,128)(2,1)}, bf16[64,2048]{1,0:T(8,128)(2,1)}, u32[]{:S(2)}, u32[]{:S(2)}) collective-permute-start(bf16[64,2048]{1,0:T(8,128)(2,1)} %collective-permute-done.10.refs_3_), channel_id=1, source_target_pairs={{0,4},{4,0},{8,12},{12,8},{16,20},{20,16},{24,28},{28,24},{32,36},... | collective-permute-start | bytes 786440 | tf_op jit(solution)/shard_map/ppermute | solution.py:24
  40.4 9.4 %collective-permute-start.16 = (bf16[64,2048]{1,0:T(8,128)(2,1)}, bf16[64,2048]{1,0:T(8,128)(2,1)}, u32[]{:S(2)}, u32[]{:S(2)}) collective-permute-start(bf16[64,2048]{1,0:T(8,128)(2,1)} %collective-permute-done.11.refs_4_), channel_id=1, source_target_pairs={{0,4},{4,0},{8,12},{12,8},{16,20},{20,16},{24,28},{28,24},{32,36},... | collective-permute-start | bytes 786440 | tf_op jit(solution)/shard_map/ppermute | solution.py:24
  57.5 12.0 %copy-start.4 = (bf16[512,384]{1,0:T(8,128)(2,1)S(1)}, bf16[512,384]{1,0:T(8,128)(2,1)}, u32[]{:S(2)}) copy-start(bf16[512,384]{1,0:T(8,128)(2,1)} %copy-done.2) | copy-start | bytes 1179652
  57.5 12.0 %copy-start.7 = (bf16[256,384]{1,0:T(8,128)(2,1)S(1)}, bf16[256,384]{1,0:T(8,128)(2,1)}, u32[]{:S(2)}) copy-start(bf16[256,384]{1,0:T(8,128)(2,1)} %copy-done.5) | copy-start | bytes 589828
  57.5 12.0 %copy-start.10 = (bf16[256,384]{1,0:T(8,128)(2,1)S(1)}, bf16[256,384]{1,0:T(8,128)(2,1)}, u32[]{:S(2)}) copy-start(bf16[256,384]{1,0:T(8,128)(2,1)} %copy-done.8) | copy-start | bytes 589828
  57.5 12.0 %copy-start.12 = (bf16[512,384]{1,0:T(8,128)(2,1)S(1)}, bf16[512,384]{1,0:T(8,128)(2,1)}, u32[]{:S(2)}) copy-start(bf16[512,384]{1,0:T(8,128)(2,1)} %copy-done.11) | copy-start | bytes 1179652
  57.5 7.8 %collective-permute-start.17 = (bf16[128,128]{1,0:T(8,128)(2,1)S(1)}, bf16[128,128]{1,0:T(8,128)(2,1)S(1)}, u32[]{:S(2)}, u32[]{:S(2)}) collective-permute-start(bf16[128,128]{1,0:T(8,128)(2,1)S(1)} %get-tuple-element.49), channel_id=1, source_target_pairs={{0,32},{4,36},{8,40},{12,44},{16,48},{20,52},{24,56},{28,60},{32,6... | collective-permute-start | bytes 98312 | tf_op jit(solution)/shard_map/ppermute | solution.py:24
  58.9 6.4 %collective-permute-start.18 = (bf16[128,128]{1,0:T(8,128)(2,1)S(1)}, bf16[128,128]{1,0:T(8,128)(2,1)S(1)}, u32[]{:S(2)}, u32[]{:S(2)}) collective-permute-start(bf16[128,128]{1,0:T(8,128)(2,1)S(1)} %get-tuple-element.49), channel_id=1, source_target_pairs={{0,64},{4,68},{8,72},{12,76},{16,80},{20,84},{24,88},{28,92},{32,9... | collective-permute-start | bytes 98312 | tf_op jit(solution)/shard_map/ppermute | solution.py:24
  61.5 3.8 %collective-permute-start.19 = (bf16[128,128]{1,0:T(8,128)(2,1)S(1)}, bf16[128,128]{1,0:T(8,128)(2,1)S(1)}, u32[]{:S(2)}, u32[]{:S(2)}) collective-permute-start(bf16[128,128]{1,0:T(8,128)(2,1)S(1)} %get-tuple-element.49), channel_id=1, source_target_pairs={{0,96},{4,100},{8,104},{12,108},{16,112},{20,116},{24,120},{28,124... | collective-permute-start | bytes 98312 | tf_op jit(solution)/shard_map/ppermute | solution.py:24
  66.3 3.1 %collective-permute-start.20 = (bf16[4,128,384]{2,1,0:T(8,128)(2,1)S(1)}, bf16[4,128,384]{2,1,0:T(8,128)(2,1)S(1)}, u32[]{:S(2)}, u32[]{:S(2)}) collective-permute-start(bf16[4,128,384]{2,1,0:T(8,128)(2,1)S(1)} %get-tuple-element.51), channel_id=1, source_target_pairs={{0,4},{4,0},{8,12},{12,8},{16,20},{20,16},{24,28},{28,24},{32,36},... | collective-permute-start | bytes 1179656 | tf_op jit(solution)/shard_map/ppermute | solution.py:24
  73.3 13.4 %collective-permute-start.21 = (bf16[64,2048]{1,0:T(8,128)(2,1)S(1)}, bf16[64,2048]{1,0:T(8,128)(2,1)S(1)}, u32[]{:S(2)}, u32[]{:S(2)}) collective-permute-start(bf16[64,2048]{1,0:T(8,128)(2,1)S(1)} %get-tuple-element.55), channel_id=1, source_target_pairs={{0,8},{4,12},{8,16},{12,20},{16,24},{20,28},{24,0},{28,4},{32,40},... | collective-permute-start | bytes 786440 | tf_op jit(solution)/shard_map/ppermute | solution.py:24
  73.7 15.9 %collective-permute-start.22 = (bf16[64,2048]{1,0:T(8,128)(2,1)S(1)}, bf16[64,2048]{1,0:T(8,128)(2,1)S(1)}, u32[]{:S(2)}, u32[]{:S(2)}) collective-permute-start(bf16[64,2048]{1,0:T(8,128)(2,1)S(1)} %get-tuple-element.56), channel_id=1, source_target_pairs={{0,24},{4,28},{8,0},{12,4},{16,8},{20,12},{24,16},{28,20},{32,56},... | collective-permute-start | bytes 786440 | tf_op jit(solution)/shard_map/ppermute | solution.py:24
  79.4 7.0 %collective-permute-start.25 = (bf16[4,4,16,384]{3,2,1,0:T(8,128)(2,1)S(1)}, bf16[4,4,16,384]{3,2,1,0:T(8,128)(2,1)S(1)}, u32[]{:S(2)}, u32[]{:S(2)}) collective-permute-start(bf16[4,4,16,384]{3,2,1,0:T(8,128)(2,1)S(1)} %get-tuple-element.63), channel_id=1, source_target_pairs={{0,1},{1,2},{2,3},{3,0},{4,5},{5,6},{6,7},{7,4},{8,9},{9,10},{10,1... | collective-permute-start | bytes 589832 | tf_op jit(solution)/shard_map/ppermute | solution.py:28
  79.5 10.9 %collective-permute-start.26 = (bf16[4,4,16,384]{3,2,1,0:T(8,128)(2,1)S(1)}, bf16[4,4,16,384]{3,2,1,0:T(8,128)(2,1)S(1)}, u32[]{:S(2)}, u32[]{:S(2)}) collective-permute-start(bf16[4,4,16,384]{3,2,1,0:T(8,128)(2,1)S(1)} %get-tuple-element.64), channel_id=1, source_target_pairs={{0,2},{1,3},{2,0},{3,1},{4,6},{5,7},{6,4},{7,5},{8,10},{9,11},{10,... | collective-permute-start | bytes 589832 | tf_op jit(solution)/shard_map/ppermute | solution.py:28
  81.9 9.3 %collective-permute-start.27 = (bf16[4,4,16,384]{3,2,1,0:T(8,128)(2,1)S(1)}, bf16[4,4,16,384]{3,2,1,0:T(8,128)(2,1)S(1)}, u32[]{:S(2)}, u32[]{:S(2)}) collective-permute-start(bf16[4,4,16,384]{3,2,1,0:T(8,128)(2,1)S(1)} %get-tuple-element.65), channel_id=1, source_target_pairs={{0,3},{1,0},{2,1},{3,2},{4,7},{5,4},{6,5},{7,6},{8,11},{9,8},{10,9... | collective-permute-start | bytes 589832 | tf_op jit(solution)/shard_map/ppermute | solution.py:28
  86.3 5.7 %collective-permute-start.28 = (bf16[4,4,16,384]{3,2,1,0:T(8,128)(2,1)S(1)}, bf16[4,4,16,384]{3,2,1,0:T(8,128)(2,1)S(1)}, u32[]{:S(2)}, u32[]{:S(2)}) collective-permute-start(bf16[4,4,16,384]{3,2,1,0:T(8,128)(2,1)S(1)} %get-tuple-element.67), channel_id=1, source_target_pairs={{0,32},{4,36},{8,40},{12,44},{16,48},{20,52},{24,56},{28,60},{32,6... | collective-permute-start | bytes 589832 | tf_op jit(solution)/shard_map/ppermute | solution.py:24
  86.7 8.0 %collective-permute-start.29 = (bf16[4,4,16,384]{3,2,1,0:T(8,128)(2,1)S(1)}, bf16[4,4,16,384]{3,2,1,0:T(8,128)(2,1)S(1)}, u32[]{:S(2)}, u32[]{:S(2)}) collective-permute-start(bf16[4,4,16,384]{3,2,1,0:T(8,128)(2,1)S(1)} %get-tuple-element.68), channel_id=1, source_target_pairs={{0,64},{4,68},{8,72},{12,76},{16,80},{20,84},{24,88},{28,92},{32,9... | collective-permute-start | bytes 589832 | tf_op jit(solution)/shard_map/ppermute | solution.py:24
  89.6 5.2 %collective-permute-start.30 = (bf16[4,4,16,384]{3,2,1,0:T(8,128)(2,1)S(1)}, bf16[4,4,16,384]{3,2,1,0:T(8,128)(2,1)S(1)}, u32[]{:S(2)}, u32[]{:S(2)}) collective-permute-start(bf16[4,4,16,384]{3,2,1,0:T(8,128)(2,1)S(1)} %get-tuple-element.69), channel_id=1, source_target_pairs={{0,96},{4,100},{8,104},{12,108},{16,112},{20,116},{24,120},{28,124... | collective-permute-start | bytes 589832 | tf_op jit(solution)/shard_map/ppermute | solution.py:24
  95.5 6.0 %collective-permute-start.31 = (bf16[4,16,384]{2,1,0:T(8,128)(2,1)S(1)}, bf16[4,16,384]{2,1,0:T(8,128)(2,1)S(1)}, u32[]{:S(2)}, u32[]{:S(2)}) collective-permute-start(bf16[4,16,384]{2,1,0:T(8,128)(2,1)S(1)} %get-tuple-element.71), channel_id=1, source_target_pairs={{0,32},{4,36},{8,40},{12,44},{16,48},{20,52},{24,56},{28,60},{32,6... | collective-permute-start | bytes 147464 | tf_op jit(solution)/shard_map/ppermute | solution.py:24
  96.0 6.3 %collective-permute-start.32 = (bf16[4,16,384]{2,1,0:T(8,128)(2,1)S(1)}, bf16[4,16,384]{2,1,0:T(8,128)(2,1)S(1)}, u32[]{:S(2)}, u32[]{:S(2)}) collective-permute-start(bf16[4,16,384]{2,1,0:T(8,128)(2,1)S(1)} %get-tuple-element.72), channel_id=1, source_target_pairs={{0,64},{4,68},{8,72},{12,76},{16,80},{20,84},{24,88},{28,92},{32,9... | collective-permute-start | bytes 147464 | tf_op jit(solution)/shard_map/ppermute | solution.py:24
  99.1 3.3 %collective-permute-start.33 = (bf16[4,16,384]{2,1,0:T(8,128)(2,1)S(1)}, bf16[4,16,384]{2,1,0:T(8,128)(2,1)S(1)}, u32[]{:S(2)}, u32[]{:S(2)}) collective-permute-start(bf16[4,16,384]{2,1,0:T(8,128)(2,1)S(1)} %get-tuple-element.73), channel_id=1, source_target_pairs={{0,96},{4,100},{8,104},{12,108},{16,112},{20,116},{24,120},{28,124... | collective-permute-start | bytes 147464 | tf_op jit(solution)/shard_map/ppermute | solution.py:24
  99.1 26.8 %collective-permute-start.23 = (bf16[128,2048]{1,0:T(8,128)(2,1)S(1)}, bf16[128,2048]{1,0:T(8,128)(2,1)S(1)}, u32[]{:S(2)}, u32[]{:S(2)}) collective-permute-start(bf16[128,2048]{1,0:T(8,128)(2,1)S(1)} %get-tuple-element.57), channel_id=1, source_target_pairs={{0,8},{4,12},{8,16},{12,20},{16,24},{20,28},{24,0},{28,4},{32,40},... | collective-permute-start | bytes 1572872 | tf_op jit(solution)/shard_map/ppermute | solution.py:24
  99.1 5.6 %collective-permute-start.34 = (bf16[4,16,384]{2,1,0:T(8,128)(2,1)S(1)}, bf16[4,16,384]{2,1,0:T(8,128)(2,1)S(1)}, u32[]{:S(2)}, u32[]{:S(2)}) collective-permute-start(bf16[4,16,384]{2,1,0:T(8,128)(2,1)S(1)} %get-tuple-element.75), channel_id=1, source_target_pairs={{0,1},{1,2},{2,3},{3,0},{4,5},{5,6},{6,7},{7,4},{8,9},{9,10},{10,1... | collective-permute-start | bytes 147464 | tf_op jit(solution)/shard_map/ppermute | solution.py:28
  101.5 4.4 %collective-permute-start.35 = (bf16[4,16,384]{2,1,0:T(8,128)(2,1)S(1)}, bf16[4,16,384]{2,1,0:T(8,128)(2,1)S(1)}, u32[]{:S(2)}, u32[]{:S(2)}) collective-permute-start(bf16[4,16,384]{2,1,0:T(8,128)(2,1)S(1)} %get-tuple-element.76), channel_id=1, source_target_pairs={{0,2},{1,3},{2,0},{3,1},{4,6},{5,7},{6,4},{7,5},{8,10},{9,11},{10,... | collective-permute-start | bytes 147464 | tf_op jit(solution)/shard_map/ppermute | solution.py:28
  102.3 3.7 %collective-permute-start.36 = (bf16[4,16,384]{2,1,0:T(8,128)(2,1)S(1)}, bf16[4,16,384]{2,1,0:T(8,128)(2,1)S(1)}, u32[]{:S(2)}, u32[]{:S(2)}) collective-permute-start(bf16[4,16,384]{2,1,0:T(8,128)(2,1)S(1)} %get-tuple-element.77), channel_id=1, source_target_pairs={{0,3},{1,0},{2,1},{3,2},{4,7},{5,4},{6,5},{7,6},{8,11},{9,8},{10,9... | collective-permute-start | bytes 147464 | tf_op jit(solution)/shard_map/ppermute | solution.py:28
  102.4 23.5 %collective-permute-start.24 = (bf16[128,2048]{1,0:T(8,128)(2,1)S(1)}, bf16[128,2048]{1,0:T(8,128)(2,1)}, u32[]{:S(2)}, u32[]{:S(2)}) collective-permute-start(bf16[128,2048]{1,0:T(8,128)(2,1)S(1)} %get-tuple-element.58), channel_id=1, source_target_pairs={{0,24},{4,28},{8,0},{12,4},{16,8},{20,12},{24,16},{28,20},{32,56},... | collective-permute-start | bytes 1572872 | tf_op jit(solution)/shard_map/ppermute | solution.py:24
  (4 other events, 3.6 us)

commit v3 on v2

--- a/solution.py
+++ b/solution.py
@@ -71,18 +71,14 @@
 TOKENS = ((0, 0, 128), (1, 0, 128), (3, 0, 128), (2, 0, 64), (2, 64, 64))
 
 
-def take(idx, w, own, other, sem):
+def take(idx, w, own, sem):
     head = 2 * idx[2] + idx[3]
-    mate = 2 * idx[2] + 1 - idx[3]
     copies = []
     for i in range(3):
-        for j, (h, out) in enumerate(((head, own), (mate, other))):
-            at = pl.multiple_of(i * 1024 + h * HD, HD)
-            copies.append(
-                pltpu.make_async_copy(
-                    w.at[:, pl.ds(at, HD)], out.at[:, i * HD : (i + 1) * HD], sem.at[2 * i + j]
-                )
-            )
+        at = pl.multiple_of(i * 1024 + head * HD, HD)
+        copies.append(
+            pltpu.make_async_copy(w.at[:, pl.ds(at, HD)], own.at[:, i * HD : (i + 1) * HD], sem.at[i])
+        )
     for copy in copies:
         copy.start()
     for copy in copies:
@@ -91,19 +87,18 @@
 
 def project(idx, *refs):
     xs, mates, w, gs = refs[0:5], refs[5:10], refs[10:15], refs[15]
-    xcat, qkv, r, total = refs[16:]
+    xcat, qkv, r, total, wkeep = refs[16:]
     xi, zi, ci = idx[0], idx[2], idx[3]
     for parity, parts in ((ci, xs), (1 - ci, mates)):
         for part, (s, start, size) in zip(parts, TOKENS, strict=True):
             block = lax.rem(zi + NZ - s, NZ) * 2 + parity
             xcat[pl.ds(pl.multiple_of(block * TOK + start, 64), size), :] = part[...]
+    for part, (s, start, size) in zip(w, PIECES, strict=True):
+        wkeep[columns(xi, s, start, size), :] = part[...]
     whole = jnp.zeros((HD, HD), F32)
     for m in range(4):
         rows = slice(m * 256, (m + 1) * 256)
-        acc = jnp.zeros((256, 384), F32)
-        for part, (s, start, size) in zip(w, PIECES, strict=True):
-            acc += dot(xcat[rows, columns(xi, s, start, size)], part[...])
-        rounded = acc.astype(BF)
+        rounded = dot(xcat[rows, :], wkeep[...]).astype(BF)
         qkv[rows, :] = rounded
         for i in range(2):
             piece = dot_tn(rounded[i * TOK : (i + 1) * TOK, :HD], gs[2 * m + i, 0])
@@ -147,29 +142,20 @@
         send[z] = dqkv[pl.ds(pl.multiple_of((2 * z + 1 - ci) * TOK, TOK), TOK), :]
 
 
-def weights(idx, xt, dqkv, *refs):
-    a, b, buf = refs[:4], refs[4:8], refs[8]
-    xi, yi = idx[0], idx[1]
+def weights(idx, xt, dqkv, part):
     for m in range(4):
-        tile = dot(xt[m * 512 : (m + 1) * 512, :], dqkv[...])
-        buf[m] = tile.reshape(8, NX, 16, 384)
-    for s in range(4):
-        to_x, to_y = lax.rem(xi + s, NX), lax.rem(yi + s, NY)
-        for i in range(4):
-            for g in range(4):
-                a[s][i, g] = buf[i, g, to_x].astype(BF)
-                b[s][g, i] = buf[to_y, 4 + g, i].astype(BF)
-
-
-def back(idx, *refs):
-    keep, got, own, other = refs[0], refs[1], refs[2:7], refs[7:12]
-    mine_gx, up, down, far_up, far_down, gx = refs[12:]
-    xi, zi = idx[0], idx[2]
+        rows = slice(m * 512, (m + 1) * 512)
+        part[rows, :] = dot(xt[rows, :], dqkv[...]).astype(BF)
+
+
+def back(idx, keep, got, own, other, mine_gx, up, down, far_up, far_down, gx):
+    zi = idx[2]
     mine = keep[...].reshape(512, 384)
     theirs = got[...].reshape(512, 384)
-    for p, q, (s, start, size) in zip(own, other, PIECES, strict=True):
-        part = dot_nt(mine, p[...]) + dot_nt(theirs, q[...])
-        gx[:, :, columns(xi, s, start, size)] = part.reshape(NZ, TOK, size)
+    for n in range(4):
+        cols = slice(n * 512, (n + 1) * 512)
+        part = dot_nt(mine, own[cols, :]) + dot_nt(theirs, other[cols, :])
+        gx[:, :, cols] = part.reshape(NZ, TOK, 512)
     mine_gx[...] = gx[zi]
     up[...] = gx[lax.rem(zi + 1, NZ)].astype(BF)
     down[...] = gx[lax.rem(zi + 3, NZ)].astype(BF)
@@ -185,15 +171,15 @@
     new_down[64:, :] = (down[64:, :].astype(F32) + from_high[...].astype(F32)).astype(BF)
 
 
-def turn(idx, *refs):
-    a, b = refs[0:4], refs[4:8]
-    a2, b2 = refs[8:12], refs[12:16]
-    xi, yi = idx[0], idx[1]
-    for s in range(4):
-        to_x, to_y = lax.rem(xi + s, NX), lax.rem(yi + s, NY)
-        for g in range(4):
-            a2[s][g] = sum(p[to_y, g].astype(F32) for p in a).astype(BF)
-            b2[s][g] = sum(p[g, to_x].astype(F32) for p in b).astype(BF)
+def collect(scale, idx, parts, out):
+    for head in range(8):
+        acc = jnp.zeros((16, 384), F32)
+        for y in range(NY):
+            for x in range(NX):
+                acc += parts[(y * 8 + head) * NX + x].astype(F32)
+        for i in range(3):
+            at = i * 1024 + head * HD
+            out[:, at : at + HD] = acc[:, i * HD : (i + 1) * HD] * scale
 
 
 def body(inputs, grad_out, saved, w_qkv):
@@ -209,32 +195,39 @@
     rows_y = [[ctx_index(y, z, c) for z in range(NZ) for c in range(NC)] for y in range(NY)]
 
     x1, x3 = ctx_hop(x, dz=1), ctx_hop(x, dz=-1)
-    own_w, other_w = pl.pallas_call(
+    (own_w,) = pl.pallas_call(
         take,
-        out_shape=[shape((512, 384), BF)] * 2,
+        out_shape=[shape((512, 384), BF)],
         in_specs=[pl.BlockSpec(memory_space=pltpu.SMEM), pl.BlockSpec(memory_space=pltpu.HBM)],
-        out_specs=[pl.BlockSpec(memory_space=pltpu.VMEM)] * 2,
-        scratch_shapes=[pltpu.SemaphoreType.DMA((6,))],
+        out_specs=[pl.BlockSpec(memory_space=pltpu.VMEM)],
+        scratch_shapes=[pltpu.SemaphoreType.DMA((3,))],
         compiler_params=pltpu.CompilerParams(vmem_limit_bytes=4 << 20),
+        cost_estimate=pl.CostEstimate(flops=0, bytes_accessed=2 * 512 * 384 * 2, transcendentals=0),
     )(idx, w_qkv)
+    cot = grad_out[0].reshape(TOK, heads, HD).transpose(1, 0, 2)
+    bundle = jnp.stack([cot, saved[0, 0].astype(BF)], axis=1)
+    gs = lax.all_to_all(bundle, "ctx", 0, 0, axis_index_groups=rows_y)
     w1, w3 = x_hop(own_w, 1), x_hop(own_w, -1)
     x2a, x2b = ctx_hop(x1[:64], dz=1), ctx_hop(x3[64:], dz=-1)
     w2a, w2b = x_hop(w1[:256], 1), x_hop(w3[256:], -1)
     xs, own = [x, x1, x3, x2a, x2b], [own_w, w1, w3, w2a, w2b]
-    mates = [ctx_hop(p, dc=1) for p in xs]
-    other = [other_w] + [ctx_hop(p, dc=1) for p in own[1:]]
-    cot = grad_out[0].reshape(TOK, heads, HD).transpose(1, 0, 2)
-    bundle = jnp.stack([cot, saved[0, 0].astype(BF)], axis=1)
-    gs = lax.all_to_all(bundle, "ctx", 0, 0, axis_index_groups=rows_y)
+    mates = [ctx_hop(after(p, gs) if i else p, dc=1) for i, p in enumerate(xs)]
 
     big = 2 * 1024 * 2048 * 384
-    xcat, qkv, r, total = call(
+    xcat, qkv, r, total, own_w = call(
         project,
-        [shape((1024, 2048), BF), shape((1024, 384), BF), shape((8, HD, HD), F32), shape((HD, HD), BF)],
+        [
+            shape((1024, 2048), BF),
+            shape((1024, 384), BF),
+            shape((8, HD, HD), F32),
+            shape((HD, HD), BF),
+            shape((2048, 384), BF),
+        ],
         [idx, *xs, *mates, *own, gs],
         flops=big,
     )
     totals = [ctx_hop(total, dy=s) for s in (1, 2, 3)]
+    other_w = ctx_hop(own_w, dc=1)
     dq, dk0, dv0, xt = call(
         lambda *refs: within(alpha, beta, *refs),
         [shape((1024, HD), BF), shape((1024, HD), F32), shape((1024, HD), F32), shape((2048, 1024), BF)],
@@ -244,39 +237,27 @@
     dqkv, keep, send = call(
         lambda *refs: finish(beta, *refs),
         [shape((1024, 384), BF), shape((NZ, TOK, 384), BF), shape((NZ, TOK, 384), BF)],
-        [after(idx, other), qkv, dq, dk0, dv0, r, *totals],
+        [idx, qkv, dq, dk0, dv0, r, *totals],
         flops=big // 16,
     )
     got = ctx_hop(send, dc=1)
-    parts = call(
-        weights,
-        [shape((NY, 4, 16, 384), BF)] * 4 + [shape((4, NX, 16, 384), BF)] * 4,
-        [idx, xt, dqkv],
-        [pltpu.VMEM((NY, 8, NX, 16, 384), F32)],
-        flops=big,
-    )
-    a, b = parts[:4], parts[4:]
-    a = [a[0]] + [x_hop(a[s], s) for s in (1, 2, 3)]
-    b = [b[0]] + [ctx_hop(b[s], dy=s) for s in (1, 2, 3)]
+    (part,) = call(weights, [shape((2048, 384), BF)], [idx, xt, dqkv], flops=big)
+    parts = lax.all_to_all(part.reshape(128, 16, 384), ("ctx", "zero"), 0, 0)
     gx, up, down, far_up, far_down = call(
         back,
         [shape((TOK, 2048), F32)] + [shape((TOK, 2048), BF)] * 2 + [shape((64, 2048), BF)] * 2,
-        [idx, keep, got, *own, *other],
+        [after(idx, part), keep, got, own_w, other_w],
         [pltpu.VMEM((NZ, TOK, 2048), F32)],
         flops=big,
     )
     far_up, far_down = ctx_hop(far_up, dz=1), ctx_hop(far_down, dz=-1)
     up, down = call(merge, [shape((TOK, 2048), BF)] * 2, [idx, up, down, far_up, far_down])
-    parts = call(turn, [shape((4, 16, 384), BF)] * 8, [after(idx, up), *a, *b])
     up, down = ctx_hop(up, dz=1), ctx_hop(down, dz=-1)
-    a, b = parts[:4], parts[4:]
-    a = [a[0]] + [ctx_hop(a[s], dy=s) for s in (1, 2, 3)]
-    b = [b[0]] + [x_hop(b[s], s) for s in (1, 2, 3)]
-    owned = jnp.concatenate([sum(p.astype(F32) for p in a), sum(p.astype(F32) for p in b)], axis=0)
-    owned = lax.all_to_all(owned, "ctx", 0, 0, axis_index_groups=rows_y)
-    owned = owned.reshape(heads, 16, 3, HD).transpose(1, 2, 0, 3).reshape(16, 3 * heads * HD)
+    (grad_w,) = call(
+        lambda *refs: collect(scale, *refs), [shape((16, 3 * heads * HD), F32)], [idx, parts]
+    )
     grad_x = (gx + up.astype(F32) + down.astype(F32)).astype(BF)
-    return (grad_x[None], owned * scale)
+    return (grad_x[None], grad_w)
 
 
 def solution(mesh):

time: 128 us -> 117 us (0.914)
  blocking collectives: 19 us -> 0 us
  waiting for transfers between devices: 29.9 us -> 40.6 us
  Pallas kernels: 17.9 us -> 21.1 us
  starting transfers between devices: 46.2 us -> 43.1 us
  local copies, waits for them, and re-layouts: 9.21 us -> 7.22 us
    all_to_all x1 -> x0, blocking collectives: 19 us -> none  [body(): owned = lax.all_to_all(owned, 'ctx', 0, 0, axis_index_groups=rows_y)]
    ppermute x27 -> x18, waiting for transfers between devices: 15.1 us -> 28.6 us  [ctx_hop(): return lax.ppermute(block, 'ctx', route)]
    all_to_all x1, waiting for transfers between devices: 8.96 us -> 0.49 us  [body(): gs = lax.all_to_all(bundle, 'ctx', 0, 0, axis_index_groups=rows_y)]
    all_to_all x0 -> x1, starting transfers between devices: none -> 7.23 us  [body(): parts = lax.all_to_all(part.reshape(128, 16, 384), ('ctx', 'zero'), 0, 0)]
    ppermute x27 -> x18, starting transfers between devices: 32 us -> 25.4 us  [ctx_hop(): return lax.ppermute(block, 'ctx', route)]
    ppermute x10 -> x4, waiting for transfers between devices: 5.78 us -> 11.5 us  [x_hop(): return lax.ppermute(block, 'zero', [(i, (i + dx) % NX) for i in range(NX)])]
    pallas_call x7, Pallas kernels: 17.1 us -> 20.4 us  [call(): pl.pallas_call(kernel, out_shape=list(outs), in_specs=[pl.BlockSpec(memor...]
    ppermute x10 -> x4, starting transfers between devices: 9.18 us -> 6.16 us  [x_hop(): return lax.ppermute(block, 'zero', [(i, (i + dx) % NX) for i in range(NX)])]
  transfers between devices with their start and end apart: 38 -> 24, of which waited for: 13 -> 8; matrix products, arithmetic and copies ran while one was open for 5% -> 4% of each run, Pallas kernels for 6% -> 13%
where the time goes in v3:
time: 117 us
  starting transfers between devices  43.1 us (37%)
  waiting for transfers between devices  40.6 us (35%)
  Pallas kernels  21.1 us (18%)
  local copies, waits for them, and re-layouts  7.22 us (6%)
  other arithmetic  4.18 us (4%)
    ppermute x18, waiting for transfers between devices, ctx_hop(): return lax.ppermute(block, 'ctx', route)  28.6 us
    ppermute x18, starting transfers between devices, ctx_hop(): return lax.ppermute(block, 'ctx', route)  25.4 us
    pallas_call x7, Pallas kernels, call(): pl.pallas_call(kernel, out_shape=list(outs), in_specs=[pl.BlockSpec(memor...  20.4 us
    ppermute x4, waiting for transfers between devices, x_hop(): return lax.ppermute(block, 'zero', [(i, (i + dx) % NX) for i in range(NX)])  11.5 us
    all_to_all x1, starting transfers between devices, body(): parts = lax.all_to_all(part.reshape(128, 16, 384), ('ctx', 'zero'), 0, 0)  7.23 us
    ppermute x4, starting transfers between devices, x_hop(): return lax.ppermute(block, 'zero', [(i, (i + dx) % NX) for i in range(NX)])  6.16 us
    unnamed x11, local copies, waits for them, and re-layouts  5.58 us
    all_to_all x1, starting transfers between devices, body(): gs = lax.all_to_all(bundle, 'ctx', 0, 0, axis_index_groups=rows_y)  4.35 us
  transfers between devices with their start and end apart: 24, of which 8 were waited for; matrix products, arithmetic and copies ran while one was open for 4% of the time, Pallas kernels for 13%

profile of v3, /device:TPU:1, one launch (start us, length us, event | category | flops | bytes accessed | tf_op | source)
XLA Modules:
  0.0 116.9 jit_solution(14569072949159410341)
XLA Ops:
  0.6 2.5 %collective-permute-start = (bf16[128,2048]{1,0:T(8,128)(2,1)}, bf16[128,2048]{1,0:T(8,128)(2,1)S(1)}, u32[]{:S(2)}, u32[]{:S(2)}) collective-permute-start(bf16[128,2048]{1,0:T(8,128)(2,1)} %bitcast.14), channel_id=1, source_target_pairs={{0,8},{4,12},{8,16},{12,20},{16,24},{20,28},{24,0},{28,4},{32,40},... | collective-permute-start | bytes 1572872 | tf_op jit(solution)/shard_map/ppermute | solution.py:24
  3.2 2.2 %collective-permute-start.1 = (bf16[128,2048]{1,0:T(8,128)(2,1)}, bf16[128,2048]{1,0:T(8,128)(2,1)S(1)}, u32[]{:S(2)}, u32[]{:S(2)}) collective-permute-start(bf16[128,2048]{1,0:T(8,128)(2,1)} %bitcast.15), channel_id=1, source_target_pairs={{0,24},{4,28},{8,0},{12,4},{16,8},{20,12},{24,16},{28,20},{32,56},... | collective-permute-start | bytes 1572872 | tf_op jit(solution)/shard_map/ppermute | solution.py:24
  5.4 1.1 convert_bitcast_fusion
  6.5 1.1 copy.6
  7.8 0.8 pad_maximum_fusion
  8.6 4.4 %all-to-all-start = ((bf16[8,2,128,128]{3,2,1,0:T(8,128)(2,1)}), bf16[8,2,128,128]{3,2,1,0:T(8,128)(2,1)S(1)}, u32[]{:S(2)}, u32[]{:S(2)}) async-start(bf16[8,2,128,128]{3,2,1,0:T(8,128)(2,1)} %pad_maximum_fusion), calls=%async_computation | async-start | bytes 1048576 | tf_op jit(solution)/shard_map/all_to_all | solution.py:209
  13.0 1.9 %copy-done = bf16[512,3072]{1,0:T(8,128)(2,1)S(1)} copy-done((bf16[512,3072]{1,0:T(8,128)(2,1)S(1)}, bf16[512,3072]{1,0:T(8,128)(2,1)}, u32[]{:S(2)}) %copy-start) | copy-done | bytes 3145752
  14.9 0.7 shard_map.59.refs_10_
  15.6 1.3 %collective-permute-start.9 = (bf16[512,384]{1,0:T(8,128)(2,1)S(1)}, bf16[512,384]{1,0:T(8,128)(2,1)S(1)}, u32[]{:S(2)}, u32[]{:S(2)}) collective-permute-start(bf16[512,384]{1,0:T(8,128)(2,1)S(1)} %shard_map.59.refs_10_), channel_id=1, source_target_pairs={{0,1},{1,2},{2,3},{3,0},{4,5},{5,6},{6,7},{7,4},{8,9},{9,10},{10,1... | collective-permute-start | bytes 1179656 | tf_op jit(solution)/shard_map/ppermute | solution.py:28
  16.9 0.4 collective-permute-start.4
  17.4 0.7 slice.16
  18.1 1.6 %collective-permute-start.2 = (bf16[64,2048]{1,0:T(8,128)(2,1)}, bf16[64,2048]{1,0:T(8,128)(2,1)S(1)}, u32[]{:S(2)}, u32[]{:S(2)}) collective-permute-start(bf16[64,2048]{1,0:T(8,128)(2,1)} %slice.16), channel_id=1, source_target_pairs={{0,8},{4,12},{8,16},{12,20},{16,24},{20,28},{24,0},{28,4},{32,40},... | collective-permute-start | bytes 786440 | tf_op jit(solution)/shard_map/ppermute | solution.py:24
  19.7 1.5 %collective-permute-start.10 = (bf16[512,384]{1,0:T(8,128)(2,1)S(1)}, bf16[512,384]{1,0:T(8,128)(2,1)S(1)}, u32[]{:S(2)}, u32[]{:S(2)}) collective-permute-start(bf16[512,384]{1,0:T(8,128)(2,1)S(1)} %shard_map.59.refs_10_), channel_id=1, source_target_pairs={{0,3},{1,0},{2,1},{3,2},{4,7},{5,4},{6,5},{7,6},{8,11},{9,8},{10,9... | collective-permute-start | bytes 1179656 | tf_op jit(solution)/shard_map/ppermute | solution.py:28
  21.1 0.7 slice.17
  21.8 1.9 %collective-permute-start.3 = (bf16[64,2048]{1,0:T(8,128)(2,1)}, bf16[64,2048]{1,0:T(8,128)(2,1)}, u32[]{:S(2)}, u32[]{:S(2)}) collective-permute-start(bf16[64,2048]{1,0:T(8,128)(2,1)} %slice.17), channel_id=1, source_target_pairs={{0,24},{4,28},{8,0},{12,4},{16,8},{20,12},{24,16},{28,20},{32,56},... | collective-permute-start | bytes 786440 | tf_op jit(solution)/shard_map/ppermute | solution.py:24
  23.7 0.5 all-to-all-done.refs_15_.refs_2_
  24.2 3.2 %collective-permute-done.9.refs_11_ = bf16[512,384]{1,0:T(8,128)(2,1)S(1)} collective-permute-done((bf16[512,384]{1,0:T(8,128)(2,1)S(1)}, bf16[512,384]{1,0:T(8,128)(2,1)S(1)}, u32[]{:S(2)}, u32[]{:S(2)}) %collective-permute-start.9) | collective-permute-done | bytes 393248 | tf_op jit(solution)/shard_map/ppermute | solution.py:28
  27.5 1.0 collective-permute-start.5
  28.4 0.3 collective-permute-done.2.refs_3_
  28.8 1.6 %collective-permute-start.6 = (bf16[128,2048]{1,0:T(8,128)(2,1)S(1)}, bf16[128,2048]{1,0:T(8,128)(2,1)S(1)}, u32[]{:S(2)}, u32[]{:S(2)}) collective-permute-start(bf16[128,2048]{1,0:T(8,128)(2,1)S(1)} %collective-permute-done.1.refs_2_), channel_id=1, source_target_pairs={{0,4},{4,0},{8,12},{12,8},{16,20},{20,16},{24,28},{28,24},{32,36},... | collective-permute-start | bytes 1572872 | tf_op jit(solution)/shard_map/ppermute | solution.py:24
  30.4 1.3 %collective-permute-start.11 = (bf16[256,384]{1,0:T(8,128)(2,1)S(1)}, bf16[256,384]{1,0:T(8,128)(2,1)S(1)}, u32[]{:S(2)}, u32[]{:S(2)}) collective-permute-start(bf16[256,384]{1,0:T(8,128)(2,1)S(1)} %slice.18), channel_id=1, source_target_pairs={{0,1},{1,2},{2,3},{3,0},{4,5},{5,6},{6,7},{7,4},{8,9},{9,10},{10,1... | collective-permute-start | bytes 589832 | tf_op jit(solution)/shard_map/ppermute | solution.py:28
  31.7 0.3 collective-permute-start.7
  32.0 0.2 collective-permute-start.8
  32.3 4.8 %collective-permute-done.11.refs_13_ = bf16[256,384]{1,0:T(8,128)(2,1)S(1)} collective-permute-done((bf16[256,384]{1,0:T(8,128)(2,1)S(1)}, bf16[256,384]{1,0:T(8,128)(2,1)S(1)}, u32[]{:S(2)}, u32[]{:S(2)}) %collective-permute-start.11) | collective-permute-done | bytes 196640 | tf_op jit(solution)/shard_map/ppermute | solution.py:28
  37.1 2.1 %collective-permute-start.12 = (bf16[256,384]{1,0:T(8,128)(2,1)S(1)}, bf16[256,384]{1,0:T(8,128)(2,1)S(1)}, u32[]{:S(2)}, u32[]{:S(2)}) collective-permute-start(bf16[256,384]{1,0:T(8,128)(2,1)S(1)} %slice.19), channel_id=1, source_target_pairs={{0,3},{1,0},{2,1},{3,2},{4,7},{5,4},{6,5},{7,6},{8,11},{9,8},{10,9... | collective-permute-start | bytes 589832 | tf_op jit(solution)/shard_map/ppermute | solution.py:28
  39.2 3.4 %collective-permute-done.12.refs_14_ = bf16[256,384]{1,0:T(8,128)(2,1)S(1)} collective-permute-done((bf16[256,384]{1,0:T(8,128)(2,1)S(1)}, bf16[256,384]{1,0:T(8,128)(2,1)S(1)}, u32[]{:S(2)}, u32[]{:S(2)}) %collective-permute-start.12) | collective-permute-done | bytes 196640 | tf_op jit(solution)/shard_map/ppermute | solution.py:28
  42.7 5.7 %shard_map.60 = (bf16[1024,2048]{1,0:T(8,128)(2,1)S(1)}, bf16[1024,384]{1,0:T(8,128)(2,1)S(1)}, f32[8,128,128]{2,1,0:T(8,128)S(1)}, bf16[128,128]{1,0:T(8,128)(2,1)S(1)}, bf16[2048,384]{1,0:T(8,128)(2,1)}) custom-call(s32[4]{0:T(128)S(1)} %pad_add_fusion.idx.refs_0_, bf16[128,2048]{1,0:T(8,128)(2,1)S(1)} %bitcast.17, ...), custom_call_target="tpu_custom_call" | custom-call | flops 1610612736 | bytes 13402128 | tf_op jit(solution)/shard_map/pallas_call | solution.py:46
  48.4 2.0 %collective-permute-start.17 = (bf16[2048,384]{1,0:T(8,128)(2,1)}, bf16[2048,384]{1,0:T(8,128)(2,1)S(1)}, u32[]{:S(2)}, u32[]{:S(2)}) collective-permute-start(bf16[2048,384]{1,0:T(8,128)(2,1)} %get-tuple-element.42.own), channel_id=1, source_target_pairs={{0,4},{4,0},{8,12},{12,8},{16,20},{20,16},{24,28},{28,24},{32,36},... | collective-permute-start | bytes 4718600 | tf_op jit(solution)/shard_map/ppermute | solution.py:24
  50.4 1.3 %collective-permute-start.13 = (bf16[128,128]{1,0:T(8,128)(2,1)S(1)}, bf16[128,128]{1,0:T(8,128)(2,1)S(1)}, u32[]{:S(2)}, u32[]{:S(2)}) collective-permute-start(bf16[128,128]{1,0:T(8,128)(2,1)S(1)} %get-tuple-element.37), channel_id=1, source_target_pairs={{0,32},{4,36},{8,40},{12,44},{16,48},{20,52},{24,56},{28,60},{32,6... | collective-permute-start | bytes 98312 | tf_op jit(solution)/shard_map/ppermute | solution.py:24
  51.7 2.6 %collective-permute-start.14 = (bf16[128,128]{1,0:T(8,128)(2,1)S(1)}, bf16[128,128]{1,0:T(8,128)(2,1)S(1)}, u32[]{:S(2)}, u32[]{:S(2)}) collective-permute-start(bf16[128,128]{1,0:T(8,128)(2,1)S(1)} %get-tuple-element.37), channel_id=1, source_target_pairs={{0,64},{4,68},{8,72},{12,76},{16,80},{20,84},{24,88},{28,92},{32,9... | collective-permute-start | bytes 98312 | tf_op jit(solution)/shard_map/ppermute | solution.py:24
  54.3 1.1 collective-permute-start.15
  55.4 2.7 %shard_map.61 = (bf16[1024,128]{1,0:T(8,128)(2,1)S(1)}, f32[1024,128]{1,0:T(8,128)S(1)}, f32[1024,128]{1,0:T(8,128)S(1)}, bf16[2048,1024]{1,0:T(8,128)(2,1)S(1)}) custom-call(s32[4]{0:T(128)S(1)} %pad_add_fusion.idx.refs_0_, bf16[1024,2048]{1,0:T(8,128)(2,1)S(1)} %get-tuple-element.30.refs_1_, bf16[8,2,128,128]{3,2,1,0:T(8,128)(2,1)S(1)} %all-to-all-done.refs_15_.refs_2_, ...), custom_call_target="tpu_custom_call" | custom-call | flops 402653184 | bytes 11010064 | tf_op jit(solution)/shard_map/pallas_call | solution.py:46
  58.2 1.0 shard_map.62
  59.2 4.0 %shard_map.63 = bf16[2048,384]{1,0:T(8,128)(2,1)} custom-call(s32[4]{0:T(128)S(1)} %pad_add_fusion.idx.refs_0_, bf16[2048,1024]{1,0:T(8,128)(2,1)S(1)} %get-tuple-element.32.xt, bf16[1024,384]{1,0:T(8,128)(2,1)S(1)} %get-tuple-element.38.dqkv), custom_call_target="tpu_custom_call" | custom-call | flops 1610612736 | bytes 6553616 | tf_op jit(solution)/shard_map/pallas_call | solution.py:46
  63.2 7.2 %all-to-all-start.1 = ((bf16[128,16,384]{2,1,0:T(8,128)(2,1)}), bf16[128,16,384]{2,1,0:T(8,128)(2,1)S(1)}, u32[]{:S(2)}, u32[]{:S(2)}) async-start(bf16[128,16,384]{2,1,0:T(8,128)(2,1)} %bitcast.10), calls=%async_computation.1 | async-start | bytes 3145728 | tf_op jit(solution)/shard_map/all_to_all | solution.py:245
  70.4 1.1 collective-permute-start.16
  71.6 1.6 %collective-permute-done.16.got = bf16[4,128,384]{2,1,0:T(8,128)(2,1)S(1)} collective-permute-done((bf16[4,128,384]{2,1,0:T(8,128)(2,1)}, bf16[4,128,384]{2,1,0:T(8,128)(2,1)S(1)}, u32[]{:S(2)}, u32[]{:S(2)}) %collective-permute-start.16) | collective-permute-done | bytes 393248 | tf_op jit(solution)/shard_map/ppermute | solution.py:24
  73.1 1.2 copy-done.2
  74.3 1.4 %copy-done.3 = bf16[2048,384]{1,0:T(8,128)(2,1)S(1)} copy-done((bf16[2048,384]{1,0:T(8,128)(2,1)S(1)}, bf16[2048,384]{1,0:T(8,128)(2,1)}, u32[]{:S(2)}) %copy-start.3) | copy-done | bytes 1572888
  75.7 4.1 %shard_map.64 = (f32[128,2048]{1,0:T(8,128)S(1)}, bf16[128,2048]{1,0:T(8,128)(2,1)S(1)}, bf16[128,2048]{1,0:T(8,128)(2,1)S(1)}, bf16[64,2048]{1,0:T(8,128)(2,1)S(1)}, bf16[64,2048]{1,0:T(8,128)(2,1)S(1)}) custom-call(s32[4]{0:T(128)S(1)} %pad_add_fusion.idx.refs_0_, bf16[4,128,384]{2,1,0:T(8,128)(2,1)S(1)} %get-tuple-element.40.keep, ...), custom_call_target="tpu_custom_call" | custom-call | flops 1610612736 | bytes 6553616 | tf_op jit(solution)/shard_map/pallas_call | solution.py:46
  79.8 0.9 collective-permute-start.18
  80.7 1.9 %collective-permute-start.19 = (bf16[64,2048]{1,0:T(8,128)(2,1)S(1)}, bf16[64,2048]{1,0:T(8,128)(2,1)S(1)}, u32[]{:S(2)}, u32[]{:S(2)}) collective-permute-start(bf16[64,2048]{1,0:T(8,128)(2,1)S(1)} %get-tuple-element.47), channel_id=1, source_target_pairs={{0,24},{4,28},{8,0},{12,4},{16,8},{20,12},{24,16},{28,20},{32,56},... | collective-permute-start | bytes 786440 | tf_op jit(solution)/shard_map/ppermute | solution.py:24
  82.6 16.1 %collective-permute-done.18.from_low = bf16[64,2048]{1,0:T(8,128)(2,1)S(1)} collective-permute-done((bf16[64,2048]{1,0:T(8,128)(2,1)S(1)}, bf16[64,2048]{1,0:T(8,128)(2,1)S(1)}, u32[]{:S(2)}, u32[]{:S(2)}) %collective-permute-start.18) | collective-permute-done | bytes 262176 | tf_op jit(solution)/shard_map/ppermute | solution.py:24
  98.7 1.4 %shard_map.65 = (bf16[128,2048]{1,0:T(8,128)(2,1)}, bf16[128,2048]{1,0:T(8,128)(2,1)S(1)}) custom-call(s32[4]{0:T(128)S(1)} %pad_add_fusion.idx.refs_0_, bf16[128,2048]{1,0:T(8,128)(2,1)S(1)} %get-tuple-element.44.up, bf16[128,2048]{1,0:T(8,128)(2,1)S(1)} %get-tuple-element.45.down, bf16[64,2048]{1,0:T(8,128)(2,1)S(1)} %collective-permute-done.18.from_low, ...), custom_call_target="tpu_custom_call" | custom-call | bytes 2621456 | tf_op jit(solution)/shard_map/pallas_call | solution.py:46
  100.1 2.7 %collective-permute-start.21 = (bf16[128,2048]{1,0:T(8,128)(2,1)S(1)}, bf16[128,2048]{1,0:T(8,128)(2,1)}, u32[]{:S(2)}, u32[]{:S(2)}) collective-permute-start(bf16[128,2048]{1,0:T(8,128)(2,1)S(1)} %get-tuple-element.49), channel_id=1, source_target_pairs={{0,24},{4,28},{8,0},{12,4},{16,8},{20,12},{24,16},{28,20},{32,56},... | collective-permute-start | bytes 1572872 | tf_op jit(solution)/shard_map/ppermute | solution.py:24
  102.8 1.4 %shard_map.66 = f32[16,3072]{1,0:T(8,128)} custom-call(s32[4]{0:T(128)S(1)} %pad_add_fusion.idx.refs_0_, bf16[128,16,384]{2,1,0:T(8,128)(2,1)S(1)} %all-to-all-done.1.refs_1_), custom_call_target="tpu_custom_call" | custom-call | bytes 1769488 | tf_op jit(solution)/shard_map/pallas_call | solution.py:46
  104.2 10.5 %collective-permute-done.20 = bf16[128,2048]{1,0:T(8,128)(2,1)} collective-permute-done((bf16[128,2048]{1,0:T(8,128)(2,1)}, bf16[128,2048]{1,0:T(8,128)(2,1)}, u32[]{:S(2)}, u32[]{:S(2)}) %collective-permute-start.20) | collective-permute-done | bytes 524320 | tf_op jit(solution)/shard_map/ppermute | solution.py:24
  114.7 2.2 %fusion = bf16[1,128,2048]{2,1,0:T(8,128)(2,1)} fusion(bf16[128,2048]{1,0:T(8,128)(2,1)} %collective-permute-done.21, f32[128,2048]{1,0:T(8,128)S(1)} %get-tuple-element.43, bf16[128,2048]{1,0:T(8,128)(2,1)} %collective-permute-done.20), kind=kLoop, calls=%fused_computation.1 | loop fusion | flops 1310720 | bytes 2621440 | tf_op jit(solution)/shard_map/broadcast_in_dim | solution.py:260
  (28 shorter events, 0.4 us)
Async XLA Ops:
  0.6 16.7 %collective-permute-start = (bf16[128,2048]{1,0:T(8,128)(2,1)}, bf16[128,2048]{1,0:T(8,128)(2,1)S(1)}, u32[]{:S(2)}, u32[]{:S(2)}) collective-permute-start(bf16[128,2048]{1,0:T(8,128)(2,1)} %bitcast.14), channel_id=1, source_target_pairs={{0,8},{4,12},{8,16},{12,20},{16,24},{20,28},{24,0},{28,4},{32,40},... | collective-permute-start | bytes 1572872 | tf_op jit(solution)/shard_map/ppermute | solution.py:24
  3.2 18.0 %collective-permute-start.1 = (bf16[128,2048]{1,0:T(8,128)(2,1)}, bf16[128,2048]{1,0:T(8,128)(2,1)S(1)}, u32[]{:S(2)}, u32[]{:S(2)}) collective-permute-start(bf16[128,2048]{1,0:T(8,128)(2,1)} %bitcast.15), channel_id=1, source_target_pairs={{0,24},{4,28},{8,0},{12,4},{16,8},{20,12},{24,16},{28,20},{32,56},... | collective-permute-start | bytes 1572872 | tf_op jit(solution)/shard_map/ppermute | solution.py:24
  8.6 15.6 %all-to-all-start = ((bf16[8,2,128,128]{3,2,1,0:T(8,128)(2,1)}), bf16[8,2,128,128]{3,2,1,0:T(8,128)(2,1)S(1)}, u32[]{:S(2)}, u32[]{:S(2)}) async-start(bf16[8,2,128,128]{3,2,1,0:T(8,128)(2,1)} %pad_maximum_fusion), calls=%async_computation | async-start | bytes 1048576 | tf_op jit(solution)/shard_map/all_to_all | solution.py:209
  13.0 1.9 %copy-start = (bf16[512,3072]{1,0:T(8,128)(2,1)S(1)}, bf16[512,3072]{1,0:T(8,128)(2,1)}, u32[]{:S(2)}) copy-start(bf16[512,3072]{1,0:T(8,128)(2,1)} %w.1) | copy-start | bytes 9437188
  14.9 2.0 %copy-start.1 = (bf16[1,128,2048]{2,1,0:T(8,128)(2,1)S(1)}, bf16[1,128,2048]{2,1,0:T(8,128)(2,1)}, u32[]{:S(2)}) copy-start(bf16[1,128,2048]{2,1,0:T(8,128)(2,1)} %param.4) | copy-start | bytes 1572868
  15.6 11.8 %collective-permute-start.9 = (bf16[512,384]{1,0:T(8,128)(2,1)S(1)}, bf16[512,384]{1,0:T(8,128)(2,1)S(1)}, u32[]{:S(2)}, u32[]{:S(2)}) collective-permute-start(bf16[512,384]{1,0:T(8,128)(2,1)S(1)} %shard_map.59.refs_10_), channel_id=1, source_target_pairs={{0,1},{1,2},{2,3},{3,0},{4,5},{5,6},{6,7},{7,4},{8,9},{9,10},{10,1... | collective-permute-start | bytes 1179656 | tf_op jit(solution)/shard_map/ppermute | solution.py:28
  16.9 15.1 %collective-permute-start.4 = (bf16[128,2048]{1,0:T(8,128)(2,1)S(1)}, bf16[128,2048]{1,0:T(8,128)(2,1)}, u32[]{:S(2)}, u32[]{:S(2)}) collective-permute-start(bf16[128,2048]{1,0:T(8,128)(2,1)S(1)} %bitcast.16), channel_id=1, source_target_pairs={{0,4},{4,0},{8,12},{12,8},{16,20},{20,16},{24,28},{28,24},{32,36},... | collective-permute-start | bytes 1572872 | tf_op jit(solution)/shard_map/ppermute | solution.py:24
  18.1 10.7 %collective-permute-start.2 = (bf16[64,2048]{1,0:T(8,128)(2,1)}, bf16[64,2048]{1,0:T(8,128)(2,1)S(1)}, u32[]{:S(2)}, u32[]{:S(2)}) collective-permute-start(bf16[64,2048]{1,0:T(8,128)(2,1)} %slice.16), channel_id=1, source_target_pairs={{0,8},{4,12},{8,16},{12,20},{16,24},{20,28},{24,0},{28,4},{32,40},... | collective-permute-start | bytes 786440 | tf_op jit(solution)/shard_map/ppermute | solution.py:24
  19.7 12.1 %collective-permute-start.10 = (bf16[512,384]{1,0:T(8,128)(2,1)S(1)}, bf16[512,384]{1,0:T(8,128)(2,1)S(1)}, u32[]{:S(2)}, u32[]{:S(2)}) collective-permute-start(bf16[512,384]{1,0:T(8,128)(2,1)S(1)} %shard_map.59.refs_10_), channel_id=1, source_target_pairs={{0,3},{1,0},{2,1},{3,2},{4,7},{5,4},{6,5},{7,6},{8,11},{9,8},{10,9... | collective-permute-start | bytes 1179656 | tf_op jit(solution)/shard_map/ppermute | solution.py:28
  21.8 8.6 %collective-permute-start.3 = (bf16[64,2048]{1,0:T(8,128)(2,1)}, bf16[64,2048]{1,0:T(8,128)(2,1)}, u32[]{:S(2)}, u32[]{:S(2)}) collective-permute-start(bf16[64,2048]{1,0:T(8,128)(2,1)} %slice.17), channel_id=1, source_target_pairs={{0,24},{4,28},{8,0},{12,4},{16,8},{20,12},{24,16},{28,20},{32,56},... | collective-permute-start | bytes 786440 | tf_op jit(solution)/shard_map/ppermute | solution.py:24
  27.5 15.2 %collective-permute-start.5 = (bf16[128,2048]{1,0:T(8,128)(2,1)S(1)}, bf16[128,2048]{1,0:T(8,128)(2,1)S(1)}, u32[]{:S(2)}, u32[]{:S(2)}) collective-permute-start(bf16[128,2048]{1,0:T(8,128)(2,1)S(1)} %collective-permute-done.refs_1_), channel_id=1, source_target_pairs={{0,4},{4,0},{8,12},{12,8},{16,20},{20,16},{24,28},{28,24},{32,36},... | collective-permute-start | bytes 1572872 | tf_op jit(solution)/shard_map/ppermute | solution.py:24
  28.8 13.9 %collective-permute-start.6 = (bf16[128,2048]{1,0:T(8,128)(2,1)S(1)}, bf16[128,2048]{1,0:T(8,128)(2,1)S(1)}, u32[]{:S(2)}, u32[]{:S(2)}) collective-permute-start(bf16[128,2048]{1,0:T(8,128)(2,1)S(1)} %collective-permute-done.1.refs_2_), channel_id=1, source_target_pairs={{0,4},{4,0},{8,12},{12,8},{16,20},{20,16},{24,28},{28,24},{32,36},... | collective-permute-start | bytes 1572872 | tf_op jit(solution)/shard_map/ppermute | solution.py:24
  30.4 6.6 %collective-permute-start.11 = (bf16[256,384]{1,0:T(8,128)(2,1)S(1)}, bf16[256,384]{1,0:T(8,128)(2,1)S(1)}, u32[]{:S(2)}, u32[]{:S(2)}) collective-permute-start(bf16[256,384]{1,0:T(8,128)(2,1)S(1)} %slice.18), channel_id=1, source_target_pairs={{0,1},{1,2},{2,3},{3,0},{4,5},{5,6},{6,7},{7,4},{8,9},{9,10},{10,1... | collective-permute-start | bytes 589832 | tf_op jit(solution)/shard_map/ppermute | solution.py:28
  31.7 10.9 %collective-permute-start.7 = (bf16[64,2048]{1,0:T(8,128)(2,1)S(1)}, bf16[64,2048]{1,0:T(8,128)(2,1)S(1)}, u32[]{:S(2)}, u32[]{:S(2)}) collective-permute-start(bf16[64,2048]{1,0:T(8,128)(2,1)S(1)} %collective-permute-done.2.refs_3_), channel_id=1, source_target_pairs={{0,4},{4,0},{8,12},{12,8},{16,20},{20,16},{24,28},{28,24},{32,36},... | collective-permute-start | bytes 786440 | tf_op jit(solution)/shard_map/ppermute | solution.py:24
  32.0 10.7 %collective-permute-start.8 = (bf16[64,2048]{1,0:T(8,128)(2,1)}, bf16[64,2048]{1,0:T(8,128)(2,1)S(1)}, u32[]{:S(2)}, u32[]{:S(2)}) collective-permute-start(bf16[64,2048]{1,0:T(8,128)(2,1)} %collective-permute-done.3.refs_4_), channel_id=1, source_target_pairs={{0,4},{4,0},{8,12},{12,8},{16,20},{20,16},{24,28},{28,24},{32,36},... | collective-permute-start | bytes 786440 | tf_op jit(solution)/shard_map/ppermute | solution.py:24
  37.1 5.6 %collective-permute-start.12 = (bf16[256,384]{1,0:T(8,128)(2,1)S(1)}, bf16[256,384]{1,0:T(8,128)(2,1)S(1)}, u32[]{:S(2)}, u32[]{:S(2)}) collective-permute-start(bf16[256,384]{1,0:T(8,128)(2,1)S(1)} %slice.19), channel_id=1, source_target_pairs={{0,3},{1,0},{2,1},{3,2},{4,7},{5,4},{6,5},{7,6},{8,11},{9,8},{10,9... | collective-permute-start | bytes 589832 | tf_op jit(solution)/shard_map/ppermute | solution.py:28
  48.4 24.8 %collective-permute-start.17 = (bf16[2048,384]{1,0:T(8,128)(2,1)}, bf16[2048,384]{1,0:T(8,128)(2,1)S(1)}, u32[]{:S(2)}, u32[]{:S(2)}) collective-permute-start(bf16[2048,384]{1,0:T(8,128)(2,1)} %get-tuple-element.42.own), channel_id=1, source_target_pairs={{0,4},{4,0},{8,12},{12,8},{16,20},{20,16},{24,28},{28,24},{32,36},... | collective-permute-start | bytes 4718600 | tf_op jit(solution)/shard_map/ppermute | solution.py:24
  50.4 7.7 %collective-permute-start.13 = (bf16[128,128]{1,0:T(8,128)(2,1)S(1)}, bf16[128,128]{1,0:T(8,128)(2,1)S(1)}, u32[]{:S(2)}, u32[]{:S(2)}) collective-permute-start(bf16[128,128]{1,0:T(8,128)(2,1)S(1)} %get-tuple-element.37), channel_id=1, source_target_pairs={{0,32},{4,36},{8,40},{12,44},{16,48},{20,52},{24,56},{28,60},{32,6... | collective-permute-start | bytes 98312 | tf_op jit(solution)/shard_map/ppermute | solution.py:24
  51.7 6.4 %collective-permute-start.14 = (bf16[128,128]{1,0:T(8,128)(2,1)S(1)}, bf16[128,128]{1,0:T(8,128)(2,1)S(1)}, u32[]{:S(2)}, u32[]{:S(2)}) collective-permute-start(bf16[128,128]{1,0:T(8,128)(2,1)S(1)} %get-tuple-element.37), channel_id=1, source_target_pairs={{0,64},{4,68},{8,72},{12,76},{16,80},{20,84},{24,88},{28,92},{32,9... | collective-permute-start | bytes 98312 | tf_op jit(solution)/shard_map/ppermute | solution.py:24
  54.3 3.8 %collective-permute-start.15 = (bf16[128,128]{1,0:T(8,128)(2,1)S(1)}, bf16[128,128]{1,0:T(8,128)(2,1)S(1)}, u32[]{:S(2)}, u32[]{:S(2)}) collective-permute-start(bf16[128,128]{1,0:T(8,128)(2,1)S(1)} %get-tuple-element.37), channel_id=1, source_target_pairs={{0,96},{4,100},{8,104},{12,108},{16,112},{20,116},{24,120},{28,124... | collective-permute-start | bytes 98312 | tf_op jit(solution)/shard_map/ppermute | solution.py:24
  59.2 4.0 %copy-start.4 = (bf16[4,128,384]{2,1,0:T(8,128)(2,1)}, bf16[4,128,384]{2,1,0:T(8,128)(2,1)S(1)}, u32[]{:S(2)}) copy-start(bf16[4,128,384]{2,1,0:T(8,128)(2,1)S(1)} %get-tuple-element.41) | copy-start | bytes 1179652
  63.2 39.6 %all-to-all-start.1 = ((bf16[128,16,384]{2,1,0:T(8,128)(2,1)}), bf16[128,16,384]{2,1,0:T(8,128)(2,1)S(1)}, u32[]{:S(2)}, u32[]{:S(2)}) async-start(bf16[128,16,384]{2,1,0:T(8,128)(2,1)} %bitcast.10), calls=%async_computation.1 | async-start | bytes 3145728 | tf_op jit(solution)/shard_map/all_to_all | solution.py:245
  70.4 2.7 %collective-permute-start.16 = (bf16[4,128,384]{2,1,0:T(8,128)(2,1)}, bf16[4,128,384]{2,1,0:T(8,128)(2,1)S(1)}, u32[]{:S(2)}, u32[]{:S(2)}) collective-permute-start(bf16[4,128,384]{2,1,0:T(8,128)(2,1)} %copy-done.4), channel_id=1, source_target_pairs={{0,4},{4,0},{8,12},{12,8},{16,20},{20,16},{24,28},{28,24},{32,36},... | collective-permute-start | bytes 1179656 | tf_op jit(solution)/shard_map/ppermute | solution.py:24
  73.1 1.2 copy-start.2
  74.3 1.4 %copy-start.3 = (bf16[2048,384]{1,0:T(8,128)(2,1)S(1)}, bf16[2048,384]{1,0:T(8,128)(2,1)}, u32[]{:S(2)}) copy-start(bf16[2048,384]{1,0:T(8,128)(2,1)} %copy-done.2) | copy-start | bytes 4718596
  79.8 18.8 %collective-permute-start.18 = (bf16[64,2048]{1,0:T(8,128)(2,1)S(1)}, bf16[64,2048]{1,0:T(8,128)(2,1)S(1)}, u32[]{:S(2)}, u32[]{:S(2)}) collective-permute-start(bf16[64,2048]{1,0:T(8,128)(2,1)S(1)} %get-tuple-element.46), channel_id=1, source_target_pairs={{0,8},{4,12},{8,16},{12,20},{16,24},{20,28},{24,0},{28,4},{32,40},... | collective-permute-start | bytes 786440 | tf_op jit(solution)/shard_map/ppermute | solution.py:24
  80.7 18.0 %collective-permute-start.19 = (bf16[64,2048]{1,0:T(8,128)(2,1)S(1)}, bf16[64,2048]{1,0:T(8,128)(2,1)S(1)}, u32[]{:S(2)}, u32[]{:S(2)}) collective-permute-start(bf16[64,2048]{1,0:T(8,128)(2,1)S(1)} %get-tuple-element.47), channel_id=1, source_target_pairs={{0,24},{4,28},{8,0},{12,4},{16,8},{20,12},{24,16},{28,20},{32,56},... | collective-permute-start | bytes 786440 | tf_op jit(solution)/shard_map/ppermute | solution.py:24
  100.1 14.6 %collective-permute-start.20 = (bf16[128,2048]{1,0:T(8,128)(2,1)}, bf16[128,2048]{1,0:T(8,128)(2,1)}, u32[]{:S(2)}, u32[]{:S(2)}) collective-permute-start(bf16[128,2048]{1,0:T(8,128)(2,1)} %get-tuple-element.48), channel_id=1, source_target_pairs={{0,8},{4,12},{8,16},{12,20},{16,24},{20,28},{24,0},{28,4},{32,40},... | collective-permute-start | bytes 1572872 | tf_op jit(solution)/shard_map/ppermute | solution.py:24
  100.1 14.6 %collective-permute-start.21 = (bf16[128,2048]{1,0:T(8,128)(2,1)S(1)}, bf16[128,2048]{1,0:T(8,128)(2,1)}, u32[]{:S(2)}, u32[]{:S(2)}) collective-permute-start(bf16[128,2048]{1,0:T(8,128)(2,1)S(1)} %get-tuple-element.49), channel_id=1, source_target_pairs={{0,24},{4,28},{8,0},{12,4},{16,8},{20,12},{24,16},{28,20},{32,56},... | collective-permute-start | bytes 1572872 | tf_op jit(solution)/shard_map/ppermute | solution.py:24

commit v4 on v3

--- a/solution.py
+++ b/solution.py
@@ -26,6 +26,18 @@
 
 def x_hop(block, dx):
     return lax.ppermute(block, "zero", [(i, (i + dx) % NX) for i in range(NX)])
+
+
+def plane_hop(block, step, stage):
+    route = []
+    for y in range(NY):
+        for z in range(NZ):
+            for c in range(NC):
+                for x in range(NX):
+                    dx, dy = (step, 0) if c == stage else (0, step)
+                    to = ctx_index((y + dy) % NY, z, c) * NX + (x + dx) % NX
+                    route.append((ctx_index(y, z, c) * NX + x, to))
+    return lax.ppermute(block, ("ctx", "zero"), route)
 
 
 def dot(a, b):
@@ -71,18 +83,10 @@
 TOKENS = ((0, 0, 128), (1, 0, 128), (3, 0, 128), (2, 0, 64), (2, 64, 64))
 
 
-def take(idx, w, own, sem):
-    head = 2 * idx[2] + idx[3]
-    copies = []
-    for i in range(3):
-        at = pl.multiple_of(i * 1024 + head * HD, HD)
-        copies.append(
-            pltpu.make_async_copy(w.at[:, pl.ds(at, HD)], own.at[:, i * HD : (i + 1) * HD], sem.at[i])
-        )
-    for copy in copies:
-        copy.start()
-    for copy in copies:
-        copy.wait()
+def pack(idx, cot, state, out):
+    for h in range(8):
+        out[h, 0] = cot[:, h * HD : (h + 1) * HD]
+        out[h, 1] = state[h].astype(BF)
 
 
 def project(idx, *refs):
@@ -142,10 +146,27 @@
         send[z] = dqkv[pl.ds(pl.multiple_of((2 * z + 1 - ci) * TOK, TOK), TOK), :]
 
 
-def weights(idx, xt, dqkv, part):
+def weights(idx, xt, dqkv, *refs):
+    outs, buf = refs[:4], refs[4]
+    xi, yi, ci = idx[0], idx[1], idx[3]
     for m in range(4):
-        rows = slice(m * 512, (m + 1) * 512)
-        part[rows, :] = dot(xt[rows, :], dqkv[...]).astype(BF)
+        tile = dot(xt[m * 512 : (m + 1) * 512, :], dqkv[...]).astype(BF)
+        buf[m] = tile.reshape(8, NX, 16, 384)
+    for s in range(4):
+        for j in range(4):
+            y = jnp.where(ci == 0, j, lax.rem(yi + s, NY))
+            x = jnp.where(ci == 0, lax.rem(xi + s, NX), j)
+            for g in range(8):
+                outs[s][j, g] = buf[y, g, x]
+
+
+def turn(idx, *refs):
+    parts, outs = refs[:4], refs[4:]
+    place = jnp.where(idx[3] == 0, idx[1], idx[0])
+    for s in range(4):
+        j = lax.rem(place + s, 4)
+        for g in range(8):
+            outs[s][g] = sum(p[j, g].astype(F32) for p in parts).astype(BF)
 
 
 def back(idx, keep, got, own, other, mine_gx, up, down, far_up, far_down, gx):
@@ -173,13 +194,9 @@
 
 def collect(scale, idx, parts, out):
     for head in range(8):
-        acc = jnp.zeros((16, 384), F32)
-        for y in range(NY):
-            for x in range(NX):
-                acc += parts[(y * 8 + head) * NX + x].astype(F32)
         for i in range(3):
             at = i * 1024 + head * HD
-            out[:, at : at + HD] = acc[:, i * HD : (i + 1) * HD] * scale
+            out[:, at : at + HD] = parts[head, :, i * HD : (i + 1) * HD] * scale
 
 
 def body(inputs, grad_out, saved, w_qkv):
@@ -195,23 +212,19 @@
     rows_y = [[ctx_index(y, z, c) for z in range(NZ) for c in range(NC)] for y in range(NY)]
 
     x1, x3 = ctx_hop(x, dz=1), ctx_hop(x, dz=-1)
-    (own_w,) = pl.pallas_call(
-        take,
-        out_shape=[shape((512, 384), BF)],
-        in_specs=[pl.BlockSpec(memory_space=pltpu.SMEM), pl.BlockSpec(memory_space=pltpu.HBM)],
-        out_specs=[pl.BlockSpec(memory_space=pltpu.VMEM)],
-        scratch_shapes=[pltpu.SemaphoreType.DMA((3,))],
-        compiler_params=pltpu.CompilerParams(vmem_limit_bytes=4 << 20),
-        cost_estimate=pl.CostEstimate(flops=0, bytes_accessed=2 * 512 * 384 * 2, transcendentals=0),
-    )(idx, w_qkv)
-    cot = grad_out[0].reshape(TOK, heads, HD).transpose(1, 0, 2)
-    bundle = jnp.stack([cot, saved[0, 0].astype(BF)], axis=1)
+    at = (2 * zi + ci) * HD
+    own_w = jnp.concatenate(
+        [lax.dynamic_slice(w_qkv, (0, i * heads * HD + at), (512, HD)) for i in range(3)], axis=1
+    )
+    (bundle,) = call(
+        pack, [shape((8, 2, HD, HD), BF)], [after(idx, own_w), grad_out[0], saved[0, 0]]
+    )
     gs = lax.all_to_all(bundle, "ctx", 0, 0, axis_index_groups=rows_y)
     w1, w3 = x_hop(own_w, 1), x_hop(own_w, -1)
     x2a, x2b = ctx_hop(x1[:64], dz=1), ctx_hop(x3[64:], dz=-1)
     w2a, w2b = x_hop(w1[:256], 1), x_hop(w3[256:], -1)
     xs, own = [x, x1, x3, x2a, x2b], [own_w, w1, w3, w2a, w2b]
-    mates = [ctx_hop(after(p, gs) if i else p, dc=1) for i, p in enumerate(xs)]
+    mates = [ctx_hop(after(p, gs) if i in (0, 3, 4) else p, dc=1) for i, p in enumerate(xs)]
 
     big = 2 * 1024 * 2048 * 384
     xcat, qkv, r, total, own_w = call(
@@ -227,7 +240,6 @@
         flops=big,
     )
     totals = [ctx_hop(total, dy=s) for s in (1, 2, 3)]
-    other_w = ctx_hop(own_w, dc=1)
     dq, dk0, dv0, xt = call(
         lambda *refs: within(alpha, beta, *refs),
         [shape((1024, HD), BF), shape((1024, HD), F32), shape((1024, HD), F32), shape((2048, 1024), BF)],
@@ -241,20 +253,32 @@
         flops=big // 16,
     )
     got = ctx_hop(send, dc=1)
-    (part,) = call(weights, [shape((2048, 384), BF)], [idx, xt, dqkv], flops=big)
-    parts = lax.all_to_all(part.reshape(128, 16, 384), ("ctx", "zero"), 0, 0)
+    other_w = ctx_hop(after(own_w, send), dc=1)
+    parts = call(
+        weights,
+        [shape((4, 8, 16, 384), BF)] * 4,
+        [idx, xt, dqkv],
+        [pltpu.VMEM((NY, 8, NX, 16, 384), BF)],
+        flops=big,
+    )
+    late = after(idx, parts[0])
+    parts = [parts[0]] + [plane_hop(parts[s], s, 0) for s in (1, 2, 3)]
     gx, up, down, far_up, far_down = call(
         back,
         [shape((TOK, 2048), F32)] + [shape((TOK, 2048), BF)] * 2 + [shape((64, 2048), BF)] * 2,
-        [after(idx, part), keep, got, own_w, other_w],
+        [late, keep, got, own_w, other_w],
         [pltpu.VMEM((NZ, TOK, 2048), F32)],
         flops=big,
     )
+    parts = call(turn, [shape((8, 16, 384), BF)] * 4, [after(idx, far_up), *parts])
+    parts = [parts[0]] + [plane_hop(parts[s], s, 1) for s in (1, 2, 3)]
+    owned = sum(p.astype(F32) for p in parts)
+    owned = lax.all_to_all(owned, "ctx", 0, 0, axis_index_groups=rows_y)
     far_up, far_down = ctx_hop(far_up, dz=1), ctx_hop(far_down, dz=-1)
     up, down = call(merge, [shape((TOK, 2048), BF)] * 2, [idx, up, down, far_up, far_down])
     up, down = ctx_hop(up, dz=1), ctx_hop(down, dz=-1)
     (grad_w,) = call(
-        lambda *refs: collect(scale, *refs), [shape((16, 3 * heads * HD), F32)], [idx, parts]
+        lambda *refs: collect(scale, *refs), [shape((16, 3 * heads * HD), F32)], [idx, owned]
     )
     grad_x = (gx + up.astype(F32) + down.astype(F32)).astype(BF)
     return (grad_x[None], grad_w)

time: 117 us -> 98.2 us (0.84)
  waiting for transfers between devices: 40.6 us -> 18.9 us
  blocking collectives: 0 us -> 10.8 us
  other arithmetic: 4.18 us -> 1.16 us
  Pallas kernels: 21.1 us -> 18.4 us
  local copies, waits for them, and re-layouts: 7.22 us -> 4.54 us
    ppermute x18, waiting for transfers between devices: 28.6 us -> 7.88 us  [ctx_hop(): return lax.ppermute(block, 'ctx', route)]
    all_to_all x0 -> x1, blocking collectives: none -> 10.8 us  [body(): owned = lax.all_to_all(owned, 'ctx', 0, 0, axis_index_groups=rows_y)]
    ppermute x0 -> x6, starting transfers between devices: none -> 9.54 us  [plane_hop(): return lax.ppermute(block, ('ctx', 'zero'), route)]
    ppermute x4, waiting for transfers between devices: 11.5 us -> 4.06 us  [x_hop(): return lax.ppermute(block, 'zero', [(i, (i + dx) % NX) for i in range(NX)])]
    all_to_all x1 -> x0, starting transfers between devices: 7.23 us -> none  [body(): parts = lax.all_to_all(part.reshape(128, 16, 384), ('ctx', 'zero'), 0, 0)]
    ppermute x0 -> x6, waiting for transfers between devices: none -> 3.77 us  [plane_hop(): return lax.ppermute(block, ('ctx', 'zero'), route)]
    unnamed x11 -> x6, local copies, waits for them, and re-layouts: 5.58 us -> 1.99 us
    all_to_all x1, waiting for transfers between devices: 0.49 us -> 3.14 us  [body(): gs = lax.all_to_all(bundle, 'ctx', 0, 0, axis_index_groups=rows_y)]
  transfers between devices with their start and end apart: 24 -> 29, of which waited for: 8 -> 11; matrix products, arithmetic and copies ran while one was open for 4% -> 3% of each run, Pallas kernels for 13% -> 13%
where the time goes in v4:
time: 98.2 us; the launch traced here: 97.8 us
  starting transfers between devices  43.3 us (44%)
  waiting for transfers between devices  18.9 us (19%)
  Pallas kernels  18.4 us (19%)
  blocking collectives  10.8 us (11%)
  local copies, waits for them, and re-layouts  4.54 us (5%)
  other arithmetic  1.16 us (1%)
    ppermute x18, starting transfers between devices, ctx_hop(): return lax.ppermute(block, 'ctx', route)  24 us
    pallas_call x9, Pallas kernels, call(): pl.pallas_call(kernel, out_shape=list(outs), in_specs=[pl.BlockSpec(memor...  18.4 us
    all_to_all x1, blocking collectives, body(): owned = lax.all_to_all(owned, 'ctx', 0, 0, axis_index_groups=rows_y)  10.8 us
    ppermute x6, starting transfers between devices, plane_hop(): return lax.ppermute(block, ('ctx', 'zero'), route)  9.54 us
    ppermute x18, waiting for transfers between devices, ctx_hop(): return lax.ppermute(block, 'ctx', route)  7.88 us
    ppermute x4, starting transfers between devices, x_hop(): return lax.ppermute(block, 'zero', [(i, (i + dx) % NX) for i in range(NX)])  5.42 us
    all_to_all x1, starting transfers between devices, body(): gs = lax.all_to_all(bundle, 'ctx', 0, 0, axis_index_groups=rows_y)  4.35 us
    ppermute x4, waiting for transfers between devices, x_hop(): return lax.ppermute(block, 'zero', [(i, (i + dx) % NX) for i in range(NX)])  4.06 us
  transfers between devices with their start and end apart: 29, of which 11 were waited for; matrix products, arithmetic and copies ran while one was open for 3% of the time, Pallas kernels for 13%

profile of v4, /device:TPU:1, one launch (start us, length us, event | category | flops | bytes accessed | tf_op | source)
XLA Modules:
  0.0 97.8 jit_solution(5406037949282027625)
XLA Ops:
  0.6 2.5 %collective-permute-start = (bf16[128,2048]{1,0:T(8,128)(2,1)}, bf16[128,2048]{1,0:T(8,128)(2,1)S(1)}, u32[]{:S(2)}, u32[]{:S(2)}) collective-permute-start(bf16[128,2048]{1,0:T(8,128)(2,1)} %bitcast.10), channel_id=1, source_target_pairs={{0,8},{4,12},{8,16},{12,20},{16,24},{20,28},{24,0},{28,4},{32,40},... | collective-permute-start | bytes 1572872 | tf_op jit(solution)/shard_map/ppermute | solution.py:24
  3.2 2.2 %collective-permute-start.1 = (bf16[128,2048]{1,0:T(8,128)(2,1)}, bf16[128,2048]{1,0:T(8,128)(2,1)S(1)}, u32[]{:S(2)}, u32[]{:S(2)}) collective-permute-start(bf16[128,2048]{1,0:T(8,128)(2,1)} %bitcast.11), channel_id=1, source_target_pairs={{0,24},{4,28},{8,0},{12,4},{16,8},{20,12},{24,16},{28,20},{32,56},... | collective-permute-start | bytes 1572872 | tf_op jit(solution)/shard_map/ppermute | solution.py:24
  5.5 1.1 %constant_dynamic-slice_fusion.2 = (bf16[512,128]{1,0:T(8,128)(2,1)S(1)}, bf16[512,128]{1,0:T(8,128)(2,1)S(1)}, bf16[512,128]{1,0:T(8,128)(2,1)S(1)}) fusion(bf16[512,3072]{1,0:T(8,128)(2,1)} %param.7, s32[]{:T(128)S(6)} %select_n.31, s32[]{:T(128)S(6)} %select_n.33, s32[]{:T(128)S(6)} %select_n.32), kind=kLoop, calls=%fused_computation.6 | loop fusion | bytes 786444 | tf_op jit(solution)/shard_map/dynamic_slice | solution.py:217
  6.6 1.0 %copy-done = f32[1,1,8,128,128]{4,3,2,1,0:T(8,128)S(1)} copy-done((f32[1,1,8,128,128]{4,3,2,1,0:T(8,128)S(1)}, f32[1,1,8,128,128]{4,3,2,1,0:T(8,128)}, u32[]{:S(2)}) %copy-start) | copy-done | bytes 524312
  7.6 0.9 copy-done.2
  8.6 1.4 %shard_map.59 = bf16[8,2,128,128]{3,2,1,0:T(8,128)(2,1)} custom-call(s32[4]{0:T(128)S(1)} %pad_add_fusion.idx.refs_0_, bf16[128,1024]{1,0:T(8,128)(2,1)S(1)} %bitcast.14, f32[8,128,128]{2,1,0:T(8,128)S(1)} %bitcast.9), custom_call_target="tpu_custom_call" | custom-call | bytes 1310736 | tf_op jit(solution)/shard_map/pallas_call | solution.py:58
  10.0 4.4 %all-to-all-start = ((bf16[8,2,128,128]{3,2,1,0:T(8,128)(2,1)}), bf16[8,2,128,128]{3,2,1,0:T(8,128)(2,1)S(1)}, u32[]{:S(2)}, u32[]{:S(2)}) async-start(bf16[8,2,128,128]{3,2,1,0:T(8,128)(2,1)} %shard_map.59), calls=%async_computation | async-start | bytes 1048576 | tf_op jit(solution)/shard_map/all_to_all | solution.py:222
  14.3 1.2 %collective-permute-start.9 = (bf16[512,384]{1,0:T(8,128)(2,1)S(1)}, bf16[512,384]{1,0:T(8,128)(2,1)S(1)}, u32[]{:S(2)}, u32[]{:S(2)}) collective-permute-start(bf16[512,384]{1,0:T(8,128)(2,1)S(1)} %pad_maximum_fusion.refs_10_), channel_id=1, source_target_pairs={{0,1},{1,2},{2,3},{3,0},{4,5},{5,6},{6,7},{7,4},{8,9},{9,10},{10,1... | collective-permute-start | bytes 1179656 | tf_op jit(solution)/shard_map/ppermute | solution.py:28
  15.5 1.5 %collective-permute-start.10 = (bf16[512,384]{1,0:T(8,128)(2,1)S(1)}, bf16[512,384]{1,0:T(8,128)(2,1)S(1)}, u32[]{:S(2)}, u32[]{:S(2)}) collective-permute-start(bf16[512,384]{1,0:T(8,128)(2,1)S(1)} %pad_maximum_fusion.refs_10_), channel_id=1, source_target_pairs={{0,3},{1,0},{2,1},{3,2},{4,7},{5,4},{6,5},{7,6},{8,11},{9,8},{10,9... | collective-permute-start | bytes 1179656 | tf_op jit(solution)/shard_map/ppermute | solution.py:28
  17.2 0.7 slice.16
  17.9 1.3 %collective-permute-start.2 = (bf16[64,2048]{1,0:T(8,128)(2,1)}, bf16[64,2048]{1,0:T(8,128)(2,1)S(1)}, u32[]{:S(2)}, u32[]{:S(2)}) collective-permute-start(bf16[64,2048]{1,0:T(8,128)(2,1)} %slice.16), channel_id=1, source_target_pairs={{0,8},{4,12},{8,16},{12,20},{16,24},{20,28},{24,0},{28,4},{32,40},... | collective-permute-start | bytes 786440 | tf_op jit(solution)/shard_map/ppermute | solution.py:24
  19.1 0.7 slice.17
  19.9 1.4 %collective-permute-start.3 = (bf16[64,2048]{1,0:T(8,128)(2,1)}, bf16[64,2048]{1,0:T(8,128)(2,1)}, u32[]{:S(2)}, u32[]{:S(2)}) collective-permute-start(bf16[64,2048]{1,0:T(8,128)(2,1)} %slice.17), channel_id=1, source_target_pairs={{0,24},{4,28},{8,0},{12,4},{16,8},{20,12},{24,16},{28,20},{32,56},... | collective-permute-start | bytes 786440 | tf_op jit(solution)/shard_map/ppermute | solution.py:24
  21.3 3.1 %all-to-all-done.refs_15_.refs_2_ = bf16[8,2,128,128]{3,2,1,0:T(8,128)(2,1)S(1)} async-done(((bf16[8,2,128,128]{3,2,1,0:T(8,128)(2,1)}), bf16[8,2,128,128]{3,2,1,0:T(8,128)(2,1)S(1)}, u32[]{:S(2)}, u32[]{:S(2)}) %all-to-all-start) | async-done | bytes 524320 | tf_op jit(solution)/shard_map/all_to_all | solution.py:222
  24.4 1.2 %collective-permute-start.4 = (bf16[128,2048]{1,0:T(8,128)(2,1)S(1)}, bf16[128,2048]{1,0:T(8,128)(2,1)S(1)}, u32[]{:S(2)}, u32[]{:S(2)}) collective-permute-start(bf16[128,2048]{1,0:T(8,128)(2,1)S(1)} %bitcast.12), channel_id=1, source_target_pairs={{0,4},{4,0},{8,12},{12,8},{16,20},{20,16},{24,28},{28,24},{32,36},... | collective-permute-start | bytes 1572872 | tf_op jit(solution)/shard_map/ppermute | solution.py:24
  25.6 0.5 collective-permute-done.9.refs_11_
  26.1 1.0 collective-permute-start.5
  27.1 1.8 %collective-permute-done.2.refs_3_ = bf16[64,2048]{1,0:T(8,128)(2,1)S(1)} collective-permute-done((bf16[64,2048]{1,0:T(8,128)(2,1)}, bf16[64,2048]{1,0:T(8,128)(2,1)S(1)}, u32[]{:S(2)}, u32[]{:S(2)}) %collective-permute-start.2) | collective-permute-done | bytes 262176 | tf_op jit(solution)/shard_map/ppermute | solution.py:24
  28.9 1.2 %collective-permute-start.11 = (bf16[256,384]{1,0:T(8,128)(2,1)S(1)}, bf16[256,384]{1,0:T(8,128)(2,1)S(1)}, u32[]{:S(2)}, u32[]{:S(2)}) collective-permute-start(bf16[256,384]{1,0:T(8,128)(2,1)S(1)} %slice.18), channel_id=1, source_target_pairs={{0,1},{1,2},{2,3},{3,0},{4,5},{5,6},{6,7},{7,4},{8,9},{9,10},{10,1... | collective-permute-start | bytes 589832 | tf_op jit(solution)/shard_map/ppermute | solution.py:28
  30.1 1.5 %collective-permute-start.12 = (bf16[256,384]{1,0:T(8,128)(2,1)S(1)}, bf16[256,384]{1,0:T(8,128)(2,1)S(1)}, u32[]{:S(2)}, u32[]{:S(2)}) collective-permute-start(bf16[256,384]{1,0:T(8,128)(2,1)S(1)} %slice.19), channel_id=1, source_target_pairs={{0,3},{1,0},{2,1},{3,2},{4,7},{5,4},{6,5},{7,6},{8,11},{9,8},{10,9... | collective-permute-start | bytes 589832 | tf_op jit(solution)/shard_map/ppermute | solution.py:28
  31.7 3.6 %collective-permute-done.11.refs_13_ = bf16[256,384]{1,0:T(8,128)(2,1)S(1)} collective-permute-done((bf16[256,384]{1,0:T(8,128)(2,1)S(1)}, bf16[256,384]{1,0:T(8,128)(2,1)S(1)}, u32[]{:S(2)}, u32[]{:S(2)}) %collective-permute-start.11) | collective-permute-done | bytes 196640 | tf_op jit(solution)/shard_map/ppermute | solution.py:28
  35.3 2.2 %collective-permute-start.7 = (bf16[64,2048]{1,0:T(8,128)(2,1)S(1)}, bf16[64,2048]{1,0:T(8,128)(2,1)S(1)}, u32[]{:S(2)}, u32[]{:S(2)}) collective-permute-start(bf16[64,2048]{1,0:T(8,128)(2,1)S(1)} %collective-permute-done.2.refs_3_), channel_id=1, source_target_pairs={{0,4},{4,0},{8,12},{12,8},{16,20},{20,16},{24,28},{28,24},{32,36},... | collective-permute-start | bytes 786440 | tf_op jit(solution)/shard_map/ppermute | solution.py:24
  37.5 1.1 %collective-permute-done.7.refs_8_ = bf16[64,2048]{1,0:T(8,128)(2,1)S(1)} collective-permute-done((bf16[64,2048]{1,0:T(8,128)(2,1)S(1)}, bf16[64,2048]{1,0:T(8,128)(2,1)S(1)}, u32[]{:S(2)}, u32[]{:S(2)}) %collective-permute-start.7) | collective-permute-done | bytes 262176 | tf_op jit(solution)/shard_map/ppermute | solution.py:24
  38.6 0.6 collective-permute-done.8.refs_9_
  39.2 4.4 %shard_map.60 = (bf16[1024,2048]{1,0:T(8,128)(2,1)S(1)}, bf16[1024,384]{1,0:T(8,128)(2,1)S(1)}, f32[8,128,128]{2,1,0:T(8,128)S(1)}, bf16[128,128]{1,0:T(8,128)(2,1)S(1)}, bf16[2048,384]{1,0:T(8,128)(2,1)S(1)}) custom-call(s32[4]{0:T(128)S(1)} %pad_add_fusion.idx.refs_0_, bf16[128,2048]{1,0:T(8,128)(2,1)S(1)} %bitcast.13, ...), custom_call_target="tpu_custom_call" | custom-call | flops 1610612736 | bytes 13402128 | tf_op jit(solution)/shard_map/pallas_call | solution.py:58
  43.6 1.4 %collective-permute-start.13 = (bf16[128,128]{1,0:T(8,128)(2,1)S(1)}, bf16[128,128]{1,0:T(8,128)(2,1)S(1)}, u32[]{:S(2)}, u32[]{:S(2)}) collective-permute-start(bf16[128,128]{1,0:T(8,128)(2,1)S(1)} %get-tuple-element.47), channel_id=1, source_target_pairs={{0,32},{4,36},{8,40},{12,44},{16,48},{20,52},{24,56},{28,60},{32,6... | collective-permute-start | bytes 98312 | tf_op jit(solution)/shard_map/ppermute | solution.py:24
  45.0 2.6 %collective-permute-start.14 = (bf16[128,128]{1,0:T(8,128)(2,1)S(1)}, bf16[128,128]{1,0:T(8,128)(2,1)S(1)}, u32[]{:S(2)}, u32[]{:S(2)}) collective-permute-start(bf16[128,128]{1,0:T(8,128)(2,1)S(1)} %get-tuple-element.47), channel_id=1, source_target_pairs={{0,64},{4,68},{8,72},{12,76},{16,80},{20,84},{24,88},{28,92},{32,9... | collective-permute-start | bytes 98312 | tf_op jit(solution)/shard_map/ppermute | solution.py:24
  47.6 1.1 %collective-permute-start.15 = (bf16[128,128]{1,0:T(8,128)(2,1)S(1)}, bf16[128,128]{1,0:T(8,128)(2,1)S(1)}, u32[]{:S(2)}, u32[]{:S(2)}) collective-permute-start(bf16[128,128]{1,0:T(8,128)(2,1)S(1)} %get-tuple-element.47), channel_id=1, source_target_pairs={{0,96},{4,100},{8,104},{12,108},{16,112},{20,116},{24,120},{28,124... | collective-permute-start | bytes 98312 | tf_op jit(solution)/shard_map/ppermute | solution.py:24
  48.7 2.7 %shard_map.61 = (bf16[1024,128]{1,0:T(8,128)(2,1)S(1)}, f32[1024,128]{1,0:T(8,128)S(1)}, f32[1024,128]{1,0:T(8,128)S(1)}, bf16[2048,1024]{1,0:T(8,128)(2,1)S(1)}) custom-call(s32[4]{0:T(128)S(1)} %pad_add_fusion.idx.refs_0_, bf16[1024,2048]{1,0:T(8,128)(2,1)S(1)} %get-tuple-element.40.refs_1_, bf16[8,2,128,128]{3,2,1,0:T(8,128)(2,1)S(1)} %all-to-all-done.refs_15_.refs_2_, ...), custom_call_target="tpu_custom_call" | custom-call | flops 402653184 | bytes 11010064 | tf_op jit(solution)/shard_map/pallas_call | solution.py:58
  51.4 1.0 shard_map.62
  52.4 1.3 %collective-permute-start.17 = (bf16[2048,384]{1,0:T(8,128)(2,1)S(1)}, bf16[2048,384]{1,0:T(8,128)(2,1)S(1)}, u32[]{:S(2)}, u32[]{:S(2)}) collective-permute-start(bf16[2048,384]{1,0:T(8,128)(2,1)S(1)} %get-tuple-element.54.own), channel_id=1, source_target_pairs={{0,4},{4,0},{8,12},{12,8},{16,20},{20,16},{24,28},{28,24},{32,36},... | collective-permute-start | bytes 4718600 | tf_op jit(solution)/shard_map/ppermute | solution.py:24
  54.0 3.0 %shard_map.63 = (bf16[4,8,16,384]{3,2,1,0:T(8,128)(2,1)S(1)}, bf16[4,8,16,384]{3,2,1,0:T(8,128)(2,1)S(1)}, bf16[4,8,16,384]{3,2,1,0:T(8,128)(2,1)S(1)}, bf16[4,8,16,384]{3,2,1,0:T(8,128)(2,1)S(1)}) custom-call(s32[4]{0:T(128)S(1)} %pad_add_fusion.idx.refs_0_, bf16[2048,1024]{1,0:T(8,128)(2,1)S(1)} %get-tuple-element.42.xt, ...), custom_call_target="tpu_custom_call" | custom-call | flops 1610612736 | bytes 6553616 | tf_op jit(solution)/shard_map/pallas_call | solution.py:58
  57.0 0.5 collective-permute-start.22
  57.5 2.9 %collective-permute-start.23 = (bf16[4,8,16,384]{3,2,1,0:T(8,128)(2,1)S(1)}, bf16[4,8,16,384]{3,2,1,0:T(8,128)(2,1)S(1)}, u32[]{:S(2)}, u32[]{:S(2)}) collective-permute-start(bf16[4,8,16,384]{3,2,1,0:T(8,128)(2,1)S(1)} %get-tuple-element.64), channel_id=1, source_target_pairs={{0,2},{1,3},{2,0},{3,1},{4,68},{5,69},{6,70},{7,71},{8,10},{9,11},... | collective-permute-start | bytes 1179656 | tf_op jit(solution)/shard_map/ppermute | solution.py:40
  60.4 3.2 %shard_map.64 = (f32[128,2048]{1,0:T(8,128)S(1)}, bf16[128,2048]{1,0:T(8,128)(2,1)S(1)}, bf16[128,2048]{1,0:T(8,128)(2,1)S(1)}, bf16[64,2048]{1,0:T(8,128)(2,1)S(1)}, bf16[64,2048]{1,0:T(8,128)(2,1)S(1)}) custom-call(s32[4]{0:T(128)S(1)} %pad_add_fusion.idx.refs_0_, bf16[4,128,384]{2,1,0:T(8,128)(2,1)S(1)} %get-tuple-element.51.keep, ...), custom_call_target="tpu_custom_call" | custom-call | flops 1610612736 | bytes 6553616 | tf_op jit(solution)/shard_map/pallas_call | solution.py:58
  64.0 2.3 %collective-permute-start.19 = (bf16[64,2048]{1,0:T(8,128)(2,1)S(1)}, bf16[64,2048]{1,0:T(8,128)(2,1)S(1)}, u32[]{:S(2)}, u32[]{:S(2)}) collective-permute-start(bf16[64,2048]{1,0:T(8,128)(2,1)S(1)} %get-tuple-element.59), channel_id=1, source_target_pairs={{0,24},{4,28},{8,0},{12,4},{16,8},{20,12},{24,16},{28,20},{32,56},... | collective-permute-start | bytes 786440 | tf_op jit(solution)/shard_map/ppermute | solution.py:24
  66.4 4.3 %collective-permute-done.18.from_low = bf16[64,2048]{1,0:T(8,128)(2,1)S(1)} collective-permute-done((bf16[64,2048]{1,0:T(8,128)(2,1)S(1)}, bf16[64,2048]{1,0:T(8,128)(2,1)S(1)}, u32[]{:S(2)}, u32[]{:S(2)}) %collective-permute-start.18) | collective-permute-done | bytes 262176 | tf_op jit(solution)/shard_map/ppermute | solution.py:24
  70.6 0.7 shard_map.65
  71.4 2.7 %collective-permute-start.21 = (bf16[128,2048]{1,0:T(8,128)(2,1)S(1)}, bf16[128,2048]{1,0:T(8,128)(2,1)S(1)}, u32[]{:S(2)}, u32[]{:S(2)}) collective-permute-start(bf16[128,2048]{1,0:T(8,128)(2,1)S(1)} %get-tuple-element.61), channel_id=1, source_target_pairs={{0,24},{4,28},{8,0},{12,4},{16,8},{20,12},{24,16},{28,20},{32,56},... | collective-permute-start | bytes 1572872 | tf_op jit(solution)/shard_map/ppermute | solution.py:24
  74.1 0.8 shard_map.66
  74.8 1.2 %collective-permute-start.25 = (bf16[8,16,384]{2,1,0:T(8,128)(2,1)S(1)}, bf16[8,16,384]{2,1,0:T(8,128)(2,1)S(1)}, u32[]{:S(2)}, u32[]{:S(2)}) collective-permute-start(bf16[8,16,384]{2,1,0:T(8,128)(2,1)S(1)} %get-tuple-element.67), channel_id=1, source_target_pairs={{0,32},{1,33},{2,34},{3,35},{4,5},{5,6},{6,7},{7,4},{8,40},{9,41},... | collective-permute-start | bytes 294920 | tf_op jit(solution)/shard_map/ppermute | solution.py:40
  76.0 5.0 %collective-permute-start.26 = (bf16[8,16,384]{2,1,0:T(8,128)(2,1)S(1)}, bf16[8,16,384]{2,1,0:T(8,128)(2,1)S(1)}, u32[]{:S(2)}, u32[]{:S(2)}) collective-permute-start(bf16[8,16,384]{2,1,0:T(8,128)(2,1)S(1)} %get-tuple-element.68), channel_id=1, source_target_pairs={{0,64},{1,65},{2,66},{3,67},{4,6},{5,7},{6,4},{7,5},{8,72},{9,73},... | collective-permute-start | bytes 294920 | tf_op jit(solution)/shard_map/ppermute | solution.py:40
  81.0 1.1 %collective-permute-done.25 = bf16[8,16,384]{2,1,0:T(8,128)(2,1)S(1)} collective-permute-done((bf16[8,16,384]{2,1,0:T(8,128)(2,1)S(1)}, bf16[8,16,384]{2,1,0:T(8,128)(2,1)S(1)}, u32[]{:S(2)}, u32[]{:S(2)}) %collective-permute-start.25) | collective-permute-done | bytes 98336 | tf_op jit(solution)/shard_map/ppermute | solution.py:40
  82.1 1.9 %collective-permute-done.26 = bf16[8,16,384]{2,1,0:T(8,128)(2,1)S(1)} collective-permute-done((bf16[8,16,384]{2,1,0:T(8,128)(2,1)S(1)}, bf16[8,16,384]{2,1,0:T(8,128)(2,1)S(1)}, u32[]{:S(2)}, u32[]{:S(2)}) %collective-permute-start.26) | collective-permute-done | bytes 98336 | tf_op jit(solution)/shard_map/ppermute | solution.py:40
  84.1 0.7 collective-permute-done.27
  84.8 10.8 %all_to_all.10.refs_1_ = f32[8,16,384]{2,1,0:T(8,128)S(1)} all-to-all(f32[8,16,384]{2,1,0:T(8,128)S(1)} %convert_add_fusion), channel_id=1, replica_groups={{0,4,8,12,16,20,24,28},{32,36,40,44,48,52,56,60},{64,68,72,76,80,84,88,..., dimensions={0} | all-to-all | bytes 393216 | tf_op jit(solution)/shard_map/all_to_all | solution.py:276
  95.6 1.2 %shard_map.67 = f32[16,3072]{1,0:T(8,128)} custom-call(s32[4]{0:T(128)S(1)} %pad_add_fusion.idx.refs_0_, f32[8,16,384]{2,1,0:T(8,128)S(1)} %all_to_all.10.refs_1_), custom_call_target="tpu_custom_call" | custom-call | bytes 393232 | tf_op jit(solution)/shard_map/pallas_call | solution.py:58
  96.9 1.0 %fusion = bf16[1,128,2048]{2,1,0:T(8,128)(2,1)} fusion(bf16[128,2048]{1,0:T(8,128)(2,1)S(1)} %collective-permute-done.21, f32[128,2048]{1,0:T(8,128)S(1)} %get-tuple-element.55, bf16[128,2048]{1,0:T(8,128)(2,1)S(1)} %collective-permute-done.20), kind=kLoop, calls=%fused_computation.1 | loop fusion | flops 1310720 | bytes 2621440 | tf_op jit(solution)/shard_map/broadcast_in_dim | solution.py:284
  (35 shorter events, 1.3 us)
Async XLA Ops:
  0.6 23.8 %copy-start.1 = (bf16[1,128,2048]{2,1,0:T(8,128)(2,1)S(1)}, bf16[1,128,2048]{2,1,0:T(8,128)(2,1)}, u32[]{:S(2)}) copy-start(bf16[1,128,2048]{2,1,0:T(8,128)(2,1)} %param.4) | copy-start | bytes 1572868
  0.6 16.5 %collective-permute-start = (bf16[128,2048]{1,0:T(8,128)(2,1)}, bf16[128,2048]{1,0:T(8,128)(2,1)S(1)}, u32[]{:S(2)}, u32[]{:S(2)}) collective-permute-start(bf16[128,2048]{1,0:T(8,128)(2,1)} %bitcast.10), channel_id=1, source_target_pairs={{0,8},{4,12},{8,16},{12,20},{16,24},{20,28},{24,0},{28,4},{32,40},... | collective-permute-start | bytes 1572872 | tf_op jit(solution)/shard_map/ppermute | solution.py:24
  3.2 16.0 %collective-permute-start.1 = (bf16[128,2048]{1,0:T(8,128)(2,1)}, bf16[128,2048]{1,0:T(8,128)(2,1)S(1)}, u32[]{:S(2)}, u32[]{:S(2)}) collective-permute-start(bf16[128,2048]{1,0:T(8,128)(2,1)} %bitcast.11), channel_id=1, source_target_pairs={{0,24},{4,28},{8,0},{12,4},{16,8},{20,12},{24,16},{28,20},{32,56},... | collective-permute-start | bytes 1572872 | tf_op jit(solution)/shard_map/ppermute | solution.py:24
  6.6 1.0 %copy-start = (f32[1,1,8,128,128]{4,3,2,1,0:T(8,128)S(1)}, f32[1,1,8,128,128]{4,3,2,1,0:T(8,128)}, u32[]{:S(2)}) copy-start(f32[1,1,8,128,128]{4,3,2,1,0:T(8,128)} %param.6) | copy-start | bytes 1572868
  7.6 0.9 copy-start.2
  10.0 14.4 %all-to-all-start = ((bf16[8,2,128,128]{3,2,1,0:T(8,128)(2,1)}), bf16[8,2,128,128]{3,2,1,0:T(8,128)(2,1)S(1)}, u32[]{:S(2)}, u32[]{:S(2)}) async-start(bf16[8,2,128,128]{3,2,1,0:T(8,128)(2,1)} %shard_map.59), calls=%async_computation | async-start | bytes 1048576 | tf_op jit(solution)/shard_map/all_to_all | solution.py:222
  14.3 11.8 %collective-permute-start.9 = (bf16[512,384]{1,0:T(8,128)(2,1)S(1)}, bf16[512,384]{1,0:T(8,128)(2,1)S(1)}, u32[]{:S(2)}, u32[]{:S(2)}) collective-permute-start(bf16[512,384]{1,0:T(8,128)(2,1)S(1)} %pad_maximum_fusion.refs_10_), channel_id=1, source_target_pairs={{0,1},{1,2},{2,3},{3,0},{4,5},{5,6},{6,7},{7,4},{8,9},{9,10},{10,1... | collective-permute-start | bytes 1179656 | tf_op jit(solution)/shard_map/ppermute | solution.py:28
  15.5 11.5 %collective-permute-start.10 = (bf16[512,384]{1,0:T(8,128)(2,1)S(1)}, bf16[512,384]{1,0:T(8,128)(2,1)S(1)}, u32[]{:S(2)}, u32[]{:S(2)}) collective-permute-start(bf16[512,384]{1,0:T(8,128)(2,1)S(1)} %pad_maximum_fusion.refs_10_), channel_id=1, source_target_pairs={{0,3},{1,0},{2,1},{3,2},{4,7},{5,4},{6,5},{7,6},{8,11},{9,8},{10,9... | collective-permute-start | bytes 1179656 | tf_op jit(solution)/shard_map/ppermute | solution.py:28
  17.9 11.0 %collective-permute-start.2 = (bf16[64,2048]{1,0:T(8,128)(2,1)}, bf16[64,2048]{1,0:T(8,128)(2,1)S(1)}, u32[]{:S(2)}, u32[]{:S(2)}) collective-permute-start(bf16[64,2048]{1,0:T(8,128)(2,1)} %slice.16), channel_id=1, source_target_pairs={{0,8},{4,12},{8,16},{12,20},{16,24},{20,28},{24,0},{28,4},{32,40},... | collective-permute-start | bytes 786440 | tf_op jit(solution)/shard_map/ppermute | solution.py:24
  19.9 10.3 %collective-permute-start.3 = (bf16[64,2048]{1,0:T(8,128)(2,1)}, bf16[64,2048]{1,0:T(8,128)(2,1)}, u32[]{:S(2)}, u32[]{:S(2)}) collective-permute-start(bf16[64,2048]{1,0:T(8,128)(2,1)} %slice.17), channel_id=1, source_target_pairs={{0,24},{4,28},{8,0},{12,4},{16,8},{20,12},{24,16},{28,20},{32,56},... | collective-permute-start | bytes 786440 | tf_op jit(solution)/shard_map/ppermute | solution.py:24
  24.4 13.1 %collective-permute-start.4 = (bf16[128,2048]{1,0:T(8,128)(2,1)S(1)}, bf16[128,2048]{1,0:T(8,128)(2,1)S(1)}, u32[]{:S(2)}, u32[]{:S(2)}) collective-permute-start(bf16[128,2048]{1,0:T(8,128)(2,1)S(1)} %bitcast.12), channel_id=1, source_target_pairs={{0,4},{4,0},{8,12},{12,8},{16,20},{20,16},{24,28},{28,24},{32,36},... | collective-permute-start | bytes 1572872 | tf_op jit(solution)/shard_map/ppermute | solution.py:24
  26.1 13.1 %collective-permute-start.5 = (bf16[128,2048]{1,0:T(8,128)(2,1)S(1)}, bf16[128,2048]{1,0:T(8,128)(2,1)S(1)}, u32[]{:S(2)}, u32[]{:S(2)}) collective-permute-start(bf16[128,2048]{1,0:T(8,128)(2,1)S(1)} %collective-permute-done.refs_1_), channel_id=1, source_target_pairs={{0,4},{4,0},{8,12},{12,8},{16,20},{20,16},{24,28},{28,24},{32,36},... | collective-permute-start | bytes 1572872 | tf_op jit(solution)/shard_map/ppermute | solution.py:24
  27.1 12.1 %collective-permute-start.6 = (bf16[128,2048]{1,0:T(8,128)(2,1)S(1)}, bf16[128,2048]{1,0:T(8,128)(2,1)S(1)}, u32[]{:S(2)}, u32[]{:S(2)}) collective-permute-start(bf16[128,2048]{1,0:T(8,128)(2,1)S(1)} %collective-permute-done.1.refs_2_), channel_id=1, source_target_pairs={{0,4},{4,0},{8,12},{12,8},{16,20},{20,16},{24,28},{28,24},{32,36},... | collective-permute-start | bytes 1572872 | tf_op jit(solution)/shard_map/ppermute | solution.py:24
  28.9 6.4 %collective-permute-start.11 = (bf16[256,384]{1,0:T(8,128)(2,1)S(1)}, bf16[256,384]{1,0:T(8,128)(2,1)S(1)}, u32[]{:S(2)}, u32[]{:S(2)}) collective-permute-start(bf16[256,384]{1,0:T(8,128)(2,1)S(1)} %slice.18), channel_id=1, source_target_pairs={{0,1},{1,2},{2,3},{3,0},{4,5},{5,6},{6,7},{7,4},{8,9},{9,10},{10,1... | collective-permute-start | bytes 589832 | tf_op jit(solution)/shard_map/ppermute | solution.py:28
  30.1 7.3 %collective-permute-start.12 = (bf16[256,384]{1,0:T(8,128)(2,1)S(1)}, bf16[256,384]{1,0:T(8,128)(2,1)S(1)}, u32[]{:S(2)}, u32[]{:S(2)}) collective-permute-start(bf16[256,384]{1,0:T(8,128)(2,1)S(1)} %slice.19), channel_id=1, source_target_pairs={{0,3},{1,0},{2,1},{3,2},{4,7},{5,4},{6,5},{7,6},{8,11},{9,8},{10,9... | collective-permute-start | bytes 589832 | tf_op jit(solution)/shard_map/ppermute | solution.py:28
  35.3 3.3 %collective-permute-start.7 = (bf16[64,2048]{1,0:T(8,128)(2,1)S(1)}, bf16[64,2048]{1,0:T(8,128)(2,1)S(1)}, u32[]{:S(2)}, u32[]{:S(2)}) collective-permute-start(bf16[64,2048]{1,0:T(8,128)(2,1)S(1)} %collective-permute-done.2.refs_3_), channel_id=1, source_target_pairs={{0,4},{4,0},{8,12},{12,8},{16,20},{20,16},{24,28},{28,24},{32,36},... | collective-permute-start | bytes 786440 | tf_op jit(solution)/shard_map/ppermute | solution.py:24
  37.4 1.7 %collective-permute-start.8 = (bf16[64,2048]{1,0:T(8,128)(2,1)}, bf16[64,2048]{1,0:T(8,128)(2,1)S(1)}, u32[]{:S(2)}, u32[]{:S(2)}) collective-permute-start(bf16[64,2048]{1,0:T(8,128)(2,1)} %collective-permute-done.3.refs_4_), channel_id=1, source_target_pairs={{0,4},{4,0},{8,12},{12,8},{16,20},{20,16},{24,28},{28,24},{32,36},... | collective-permute-start | bytes 786440 | tf_op jit(solution)/shard_map/ppermute | solution.py:24
  43.6 7.8 %collective-permute-start.13 = (bf16[128,128]{1,0:T(8,128)(2,1)S(1)}, bf16[128,128]{1,0:T(8,128)(2,1)S(1)}, u32[]{:S(2)}, u32[]{:S(2)}) collective-permute-start(bf16[128,128]{1,0:T(8,128)(2,1)S(1)} %get-tuple-element.47), channel_id=1, source_target_pairs={{0,32},{4,36},{8,40},{12,44},{16,48},{20,52},{24,56},{28,60},{32,6... | collective-permute-start | bytes 98312 | tf_op jit(solution)/shard_map/ppermute | solution.py:24
  45.0 6.4 %collective-permute-start.14 = (bf16[128,128]{1,0:T(8,128)(2,1)S(1)}, bf16[128,128]{1,0:T(8,128)(2,1)S(1)}, u32[]{:S(2)}, u32[]{:S(2)}) collective-permute-start(bf16[128,128]{1,0:T(8,128)(2,1)S(1)} %get-tuple-element.47), channel_id=1, source_target_pairs={{0,64},{4,68},{8,72},{12,76},{16,80},{20,84},{24,88},{28,92},{32,9... | collective-permute-start | bytes 98312 | tf_op jit(solution)/shard_map/ppermute | solution.py:24
  47.6 3.8 %collective-permute-start.15 = (bf16[128,128]{1,0:T(8,128)(2,1)S(1)}, bf16[128,128]{1,0:T(8,128)(2,1)S(1)}, u32[]{:S(2)}, u32[]{:S(2)}) collective-permute-start(bf16[128,128]{1,0:T(8,128)(2,1)S(1)} %get-tuple-element.47), channel_id=1, source_target_pairs={{0,96},{4,100},{8,104},{12,108},{16,112},{20,116},{24,120},{28,124... | collective-permute-start | bytes 98312 | tf_op jit(solution)/shard_map/ppermute | solution.py:24
  52.4 7.9 %collective-permute-start.17 = (bf16[2048,384]{1,0:T(8,128)(2,1)S(1)}, bf16[2048,384]{1,0:T(8,128)(2,1)S(1)}, u32[]{:S(2)}, u32[]{:S(2)}) collective-permute-start(bf16[2048,384]{1,0:T(8,128)(2,1)S(1)} %get-tuple-element.54.own), channel_id=1, source_target_pairs={{0,4},{4,0},{8,12},{12,8},{16,20},{20,16},{24,28},{28,24},{32,36},... | collective-permute-start | bytes 4718600 | tf_op jit(solution)/shard_map/ppermute | solution.py:24
  53.7 6.6 %collective-permute-start.16 = (bf16[4,128,384]{2,1,0:T(8,128)(2,1)S(1)}, bf16[4,128,384]{2,1,0:T(8,128)(2,1)S(1)}, u32[]{:S(2)}, u32[]{:S(2)}) collective-permute-start(bf16[4,128,384]{2,1,0:T(8,128)(2,1)S(1)} %get-tuple-element.52), channel_id=1, source_target_pairs={{0,4},{4,0},{8,12},{12,8},{16,20},{20,16},{24,28},{28,24},{32,36},... | collective-permute-start | bytes 1179656 | tf_op jit(solution)/shard_map/ppermute | solution.py:24
  57.0 17.0 %collective-permute-start.22 = (bf16[4,8,16,384]{3,2,1,0:T(8,128)(2,1)S(1)}, bf16[4,8,16,384]{3,2,1,0:T(8,128)(2,1)S(1)}, u32[]{:S(2)}, u32[]{:S(2)}) collective-permute-start(bf16[4,8,16,384]{3,2,1,0:T(8,128)(2,1)S(1)} %get-tuple-element.63), channel_id=1, source_target_pairs={{0,1},{1,2},{2,3},{3,0},{4,36},{5,37},{6,38},{7,39},{8,9},{9,10},{... | collective-permute-start | bytes 1179656 | tf_op jit(solution)/shard_map/ppermute | solution.py:40
  57.5 16.6 %collective-permute-start.23 = (bf16[4,8,16,384]{3,2,1,0:T(8,128)(2,1)S(1)}, bf16[4,8,16,384]{3,2,1,0:T(8,128)(2,1)S(1)}, u32[]{:S(2)}, u32[]{:S(2)}) collective-permute-start(bf16[4,8,16,384]{3,2,1,0:T(8,128)(2,1)S(1)} %get-tuple-element.64), channel_id=1, source_target_pairs={{0,2},{1,3},{2,0},{3,1},{4,68},{5,69},{6,70},{7,71},{8,10},{9,11},... | collective-permute-start | bytes 1179656 | tf_op jit(solution)/shard_map/ppermute | solution.py:40
  60.4 13.7 %collective-permute-start.24 = (bf16[4,8,16,384]{3,2,1,0:T(8,128)(2,1)S(1)}, bf16[4,8,16,384]{3,2,1,0:T(8,128)(2,1)S(1)}, u32[]{:S(2)}, u32[]{:S(2)}) collective-permute-start(bf16[4,8,16,384]{3,2,1,0:T(8,128)(2,1)S(1)} %get-tuple-element.65), channel_id=1, source_target_pairs={{0,3},{1,0},{2,1},{3,2},{4,100},{5,101},{6,102},{7,103},{8,11},{9,... | collective-permute-start | bytes 1179656 | tf_op jit(solution)/shard_map/ppermute | solution.py:40
  63.6 7.0 %collective-permute-start.18 = (bf16[64,2048]{1,0:T(8,128)(2,1)S(1)}, bf16[64,2048]{1,0:T(8,128)(2,1)S(1)}, u32[]{:S(2)}, u32[]{:S(2)}) collective-permute-start(bf16[64,2048]{1,0:T(8,128)(2,1)S(1)} %get-tuple-element.58), channel_id=1, source_target_pairs={{0,8},{4,12},{8,16},{12,20},{16,24},{20,28},{24,0},{28,4},{32,40},... | collective-permute-start | bytes 786440 | tf_op jit(solution)/shard_map/ppermute | solution.py:24
  64.0 6.6 %collective-permute-start.19 = (bf16[64,2048]{1,0:T(8,128)(2,1)S(1)}, bf16[64,2048]{1,0:T(8,128)(2,1)S(1)}, u32[]{:S(2)}, u32[]{:S(2)}) collective-permute-start(bf16[64,2048]{1,0:T(8,128)(2,1)S(1)} %get-tuple-element.59), channel_id=1, source_target_pairs={{0,24},{4,28},{8,0},{12,4},{16,8},{20,12},{24,16},{28,20},{32,56},... | collective-permute-start | bytes 786440 | tf_op jit(solution)/shard_map/ppermute | solution.py:24
  71.3 25.5 %collective-permute-start.20 = (bf16[128,2048]{1,0:T(8,128)(2,1)S(1)}, bf16[128,2048]{1,0:T(8,128)(2,1)S(1)}, u32[]{:S(2)}, u32[]{:S(2)}) collective-permute-start(bf16[128,2048]{1,0:T(8,128)(2,1)S(1)} %get-tuple-element.60), channel_id=1, source_target_pairs={{0,8},{4,12},{8,16},{12,20},{16,24},{20,28},{24,0},{28,4},{32,40},... | collective-permute-start | bytes 1572872 | tf_op jit(solution)/shard_map/ppermute | solution.py:24
  71.4 25.5 %collective-permute-start.21 = (bf16[128,2048]{1,0:T(8,128)(2,1)S(1)}, bf16[128,2048]{1,0:T(8,128)(2,1)S(1)}, u32[]{:S(2)}, u32[]{:S(2)}) collective-permute-start(bf16[128,2048]{1,0:T(8,128)(2,1)S(1)} %get-tuple-element.61), channel_id=1, source_target_pairs={{0,24},{4,28},{8,0},{12,4},{16,8},{20,12},{24,16},{28,20},{32,56},... | collective-permute-start | bytes 1572872 | tf_op jit(solution)/shard_map/ppermute | solution.py:24
  74.8 7.3 %collective-permute-start.25 = (bf16[8,16,384]{2,1,0:T(8,128)(2,1)S(1)}, bf16[8,16,384]{2,1,0:T(8,128)(2,1)S(1)}, u32[]{:S(2)}, u32[]{:S(2)}) collective-permute-start(bf16[8,16,384]{2,1,0:T(8,128)(2,1)S(1)} %get-tuple-element.67), channel_id=1, source_target_pairs={{0,32},{1,33},{2,34},{3,35},{4,5},{5,6},{6,7},{7,4},{8,40},{9,41},... | collective-permute-start | bytes 294920 | tf_op jit(solution)/shard_map/ppermute | solution.py:40
  76.0 8.1 %collective-permute-start.26 = (bf16[8,16,384]{2,1,0:T(8,128)(2,1)S(1)}, bf16[8,16,384]{2,1,0:T(8,128)(2,1)S(1)}, u32[]{:S(2)}, u32[]{:S(2)}) collective-permute-start(bf16[8,16,384]{2,1,0:T(8,128)(2,1)S(1)} %get-tuple-element.68), channel_id=1, source_target_pairs={{0,64},{1,65},{2,66},{3,67},{4,6},{5,7},{6,4},{7,5},{8,72},{9,73},... | collective-permute-start | bytes 294920 | tf_op jit(solution)/shard_map/ppermute | solution.py:40
  81.0 3.8 %collective-permute-start.27 = (bf16[8,16,384]{2,1,0:T(8,128)(2,1)S(1)}, bf16[8,16,384]{2,1,0:T(8,128)(2,1)S(1)}, u32[]{:S(2)}, u32[]{:S(2)}) collective-permute-start(bf16[8,16,384]{2,1,0:T(8,128)(2,1)S(1)} %get-tuple-element.69), channel_id=1, source_target_pairs={{0,96},{1,97},{2,98},{3,99},{4,7},{5,4},{6,5},{7,6},{8,104},{9,105... | collective-permute-start | bytes 294920 | tf_op jit(solution)/shard_map/ppermute | solution.py:40

commit v5 on v4

--- a/solution.py
+++ b/solution.py
@@ -52,18 +52,25 @@
     return lax.dot_general(a, b, (((0,), (0,)), ((), ())), preferred_element_type=F32)
 
 
-def call(kernel, outs, ins, scratch=(), flops=0, limit=16):
+def call(kernel, outs, ins, scratch=(), flops=0, limit=16, deps=(), free=()):
+    count = len(ins)
+
+    def run(*refs):
+        kernel(*refs[:count], *refs[count + len(deps) :])
+
     moved = sum(a.size * a.dtype.itemsize for a in list(ins) + list(outs))
     vmem = pl.BlockSpec(memory_space=pltpu.VMEM)
     return pl.pallas_call(
-        kernel,
+        run,
         out_shape=list(outs),
-        in_specs=[pl.BlockSpec(memory_space=pltpu.SMEM)] + [vmem] * (len(ins) - 1),
+        in_specs=[pl.BlockSpec(memory_space=pltpu.SMEM)]
+        + [pl.BlockSpec(memory_space=pl.ANY) if i in free else vmem for i in range(1, count)]
+        + [pl.BlockSpec(memory_space=pl.ANY)] * len(deps),
         out_specs=[vmem] * len(outs),
         scratch_shapes=list(scratch),
         compiler_params=pltpu.CompilerParams(vmem_limit_bytes=limit << 20),
         cost_estimate=pl.CostEstimate(flops=flops, bytes_accessed=moved, transcendentals=0),
-    )(*ins)
+    )(*ins, *deps)
 
 
 def shape(dims, dtype):
@@ -261,24 +268,29 @@
         [pltpu.VMEM((NY, 8, NX, 16, 384), BF)],
         flops=big,
     )
-    late = after(idx, parts[0])
-    parts = [parts[0]] + [plane_hop(parts[s], s, 0) for s in (1, 2, 3)]
     gx, up, down, far_up, far_down = call(
         back,
         [shape((TOK, 2048), F32)] + [shape((TOK, 2048), BF)] * 2 + [shape((64, 2048), BF)] * 2,
-        [late, keep, got, own_w, other_w],
+        [idx, keep, got, own_w, other_w],
         [pltpu.VMEM((NZ, TOK, 2048), F32)],
         flops=big,
-    )
-    parts = call(turn, [shape((8, 16, 384), BF)] * 4, [after(idx, far_up), *parts])
+        deps=(parts[0],),
+    )
+    parts = [parts[0]] + [plane_hop(parts[s], s, 0) for s in (1, 2, 3)]
+    far_up, far_down = ctx_hop(far_up, dz=1), ctx_hop(far_down, dz=-1)
+    parts = call(turn, [shape((8, 16, 384), BF)] * 4, [idx, *parts], deps=(gx,), limit=4)
+    up, down = call(
+        merge, [shape((TOK, 2048), BF)] * 2, [idx, up, down, far_up, far_down], deps=(parts[0],), limit=6
+    )
     parts = [parts[0]] + [plane_hop(parts[s], s, 1) for s in (1, 2, 3)]
+    up, down = ctx_hop(up, dz=1), ctx_hop(down, dz=-1)
     owned = sum(p.astype(F32) for p in parts)
     owned = lax.all_to_all(owned, "ctx", 0, 0, axis_index_groups=rows_y)
-    far_up, far_down = ctx_hop(far_up, dz=1), ctx_hop(far_down, dz=-1)
-    up, down = call(merge, [shape((TOK, 2048), BF)] * 2, [idx, up, down, far_up, far_down])
-    up, down = ctx_hop(up, dz=1), ctx_hop(down, dz=-1)
     (grad_w,) = call(
-        lambda *refs: collect(scale, *refs), [shape((16, 3 * heads * HD), F32)], [idx, owned]
+        lambda *refs: collect(scale, *refs),
+        [shape((16, 3 * heads * HD), F32)],
+        [idx, owned],
+        limit=4,
     )
     grad_x = (gx + up.astype(F32) + down.astype(F32)).astype(BF)
     return (grad_x[None], grad_w)

time: 98.2 us -> 97.4 us (level)
    ppermute x18, waiting for transfers between devices: 7.88 us -> 3.62 us  [ctx_hop(): return lax.ppermute(block, 'ctx', route)]
    ppermute x6, waiting for transfers between devices: 3.77 us -> 7.46 us  [plane_hop(): return lax.ppermute(block, ('ctx', 'zero'), route)]
where the time goes in v5:
time: 97.4 us; the launch traced here: 97 us
  starting transfers between devices  43 us (44%)
  Pallas kernels  18.4 us (19%)
  waiting for transfers between devices  18.3 us (19%)
  blocking collectives  10.8 us (11%)
  local copies, waits for them, and re-layouts  4.54 us (5%)
  other arithmetic  1.16 us (1%)
    ppermute x18, starting transfers between devices, ctx_hop(): return lax.ppermute(block, 'ctx', route)  24 us
    pallas_call x9, Pallas kernels, call(): pl.pallas_call(run, out_shape=list(outs), in_specs=[pl.BlockSpec(memory_s...  18.4 us
    all_to_all x1, blocking collectives, body(): owned = lax.all_to_all(owned, 'ctx', 0, 0, axis_index_groups=rows_y)  10.8 us
    ppermute x6, starting transfers between devices, plane_hop(): return lax.ppermute(block, ('ctx', 'zero'), route)  9.26 us
    ppermute x6, waiting for transfers between devices, plane_hop(): return lax.ppermute(block, ('ctx', 'zero'), route)  7.46 us
    ppermute x4, starting transfers between devices, x_hop(): return lax.ppermute(block, 'zero', [(i, (i + dx) % NX) for i in range(NX)])  5.42 us
    all_to_all x1, starting transfers between devices, body(): gs = lax.all_to_all(bundle, 'ctx', 0, 0, axis_index_groups=rows_y)  4.35 us
    ppermute x4, waiting for transfers between devices, x_hop(): return lax.ppermute(block, 'zero', [(i, (i + dx) % NX) for i in range(NX)])  4.06 us
  transfers between devices with their start and end apart: 29, of which 11 were waited for; matrix products, arithmetic and copies ran while one was open for 3% of the time, Pallas kernels for 13%

profile of v5, /device:TPU:1, one launch (start us, length us, event | category | flops | bytes accessed | tf_op | source)
XLA Modules:
  0.0 97.0 jit_solution(4125813942446435700)
XLA Ops:
  0.6 2.5 %collective-permute-start = (bf16[128,2048]{1,0:T(8,128)(2,1)}, bf16[128,2048]{1,0:T(8,128)(2,1)S(1)}, u32[]{:S(2)}, u32[]{:S(2)}) collective-permute-start(bf16[128,2048]{1,0:T(8,128)(2,1)} %bitcast.10), channel_id=1, source_target_pairs={{0,8},{4,12},{8,16},{12,20},{16,24},{20,28},{24,0},{28,4},{32,40},... | collective-permute-start | bytes 1572872 | tf_op jit(solution)/shard_map/ppermute | solution.py:24
  3.2 2.2 %collective-permute-start.1 = (bf16[128,2048]{1,0:T(8,128)(2,1)}, bf16[128,2048]{1,0:T(8,128)(2,1)S(1)}, u32[]{:S(2)}, u32[]{:S(2)}) collective-permute-start(bf16[128,2048]{1,0:T(8,128)(2,1)} %bitcast.11), channel_id=1, source_target_pairs={{0,24},{4,28},{8,0},{12,4},{16,8},{20,12},{24,16},{28,20},{32,56},... | collective-permute-start | bytes 1572872 | tf_op jit(solution)/shard_map/ppermute | solution.py:24
  5.5 1.1 %constant_dynamic-slice_fusion.2 = (bf16[512,128]{1,0:T(8,128)(2,1)S(1)}, bf16[512,128]{1,0:T(8,128)(2,1)S(1)}, bf16[512,128]{1,0:T(8,128)(2,1)S(1)}) fusion(bf16[512,3072]{1,0:T(8,128)(2,1)} %param.7, s32[]{:T(128)S(6)} %select_n.31, s32[]{:T(128)S(6)} %select_n.33, s32[]{:T(128)S(6)} %select_n.32), kind=kLoop, calls=%fused_computation.6 | loop fusion | bytes 786444 | tf_op jit(solution)/shard_map/dynamic_slice | solution.py:224
  6.6 1.0 %copy-done = f32[1,1,8,128,128]{4,3,2,1,0:T(8,128)S(1)} copy-done((f32[1,1,8,128,128]{4,3,2,1,0:T(8,128)S(1)}, f32[1,1,8,128,128]{4,3,2,1,0:T(8,128)}, u32[]{:S(2)}) %copy-start) | copy-done | bytes 524312
  7.6 0.9 copy-done.2
  8.6 1.4 %shard_map.59 = bf16[8,2,128,128]{3,2,1,0:T(8,128)(2,1)} custom-call(s32[4]{0:T(128)S(1)} %pad_add_fusion.refs_0_, bf16[128,1024]{1,0:T(8,128)(2,1)S(1)} %bitcast.14, f32[8,128,128]{2,1,0:T(8,128)S(1)} %bitcast.9), custom_call_target="tpu_custom_call" | custom-call | bytes 1310736 | tf_op jit(solution)/shard_map/pallas_call | solution.py:63
  10.0 4.4 %all-to-all-start = ((bf16[8,2,128,128]{3,2,1,0:T(8,128)(2,1)}), bf16[8,2,128,128]{3,2,1,0:T(8,128)(2,1)S(1)}, u32[]{:S(2)}, u32[]{:S(2)}) async-start(bf16[8,2,128,128]{3,2,1,0:T(8,128)(2,1)} %shard_map.59), calls=%async_computation | async-start | bytes 1048576 | tf_op jit(solution)/shard_map/all_to_all | solution.py:229
  14.3 1.2 %collective-permute-start.9 = (bf16[512,384]{1,0:T(8,128)(2,1)S(1)}, bf16[512,384]{1,0:T(8,128)(2,1)S(1)}, u32[]{:S(2)}, u32[]{:S(2)}) collective-permute-start(bf16[512,384]{1,0:T(8,128)(2,1)S(1)} %pad_maximum_fusion.refs_11_), channel_id=1, source_target_pairs={{0,1},{1,2},{2,3},{3,0},{4,5},{5,6},{6,7},{7,4},{8,9},{9,10},{10,1... | collective-permute-start | bytes 1179656 | tf_op jit(solution)/shard_map/ppermute | solution.py:28
  15.5 1.5 %collective-permute-start.10 = (bf16[512,384]{1,0:T(8,128)(2,1)S(1)}, bf16[512,384]{1,0:T(8,128)(2,1)S(1)}, u32[]{:S(2)}, u32[]{:S(2)}) collective-permute-start(bf16[512,384]{1,0:T(8,128)(2,1)S(1)} %pad_maximum_fusion.refs_11_), channel_id=1, source_target_pairs={{0,3},{1,0},{2,1},{3,2},{4,7},{5,4},{6,5},{7,6},{8,11},{9,8},{10,9... | collective-permute-start | bytes 1179656 | tf_op jit(solution)/shard_map/ppermute | solution.py:28
  17.2 0.7 slice.16
  17.9 1.3 %collective-permute-start.2 = (bf16[64,2048]{1,0:T(8,128)(2,1)}, bf16[64,2048]{1,0:T(8,128)(2,1)S(1)}, u32[]{:S(2)}, u32[]{:S(2)}) collective-permute-start(bf16[64,2048]{1,0:T(8,128)(2,1)} %slice.16), channel_id=1, source_target_pairs={{0,8},{4,12},{8,16},{12,20},{16,24},{20,28},{24,0},{28,4},{32,40},... | collective-permute-start | bytes 786440 | tf_op jit(solution)/shard_map/ppermute | solution.py:24
  19.1 0.7 slice.17
  19.9 1.4 %collective-permute-start.3 = (bf16[64,2048]{1,0:T(8,128)(2,1)}, bf16[64,2048]{1,0:T(8,128)(2,1)}, u32[]{:S(2)}, u32[]{:S(2)}) collective-permute-start(bf16[64,2048]{1,0:T(8,128)(2,1)} %slice.17), channel_id=1, source_target_pairs={{0,24},{4,28},{8,0},{12,4},{16,8},{20,12},{24,16},{28,20},{32,56},... | collective-permute-start | bytes 786440 | tf_op jit(solution)/shard_map/ppermute | solution.py:24
  21.3 3.1 %all-to-all-done.refs_16_.refs_2_ = bf16[8,2,128,128]{3,2,1,0:T(8,128)(2,1)S(1)} async-done(((bf16[8,2,128,128]{3,2,1,0:T(8,128)(2,1)}), bf16[8,2,128,128]{3,2,1,0:T(8,128)(2,1)S(1)}, u32[]{:S(2)}, u32[]{:S(2)}) %all-to-all-start) | async-done | bytes 524320 | tf_op jit(solution)/shard_map/all_to_all | solution.py:229
  24.4 1.2 %collective-permute-start.4 = (bf16[128,2048]{1,0:T(8,128)(2,1)S(1)}, bf16[128,2048]{1,0:T(8,128)(2,1)S(1)}, u32[]{:S(2)}, u32[]{:S(2)}) collective-permute-start(bf16[128,2048]{1,0:T(8,128)(2,1)S(1)} %bitcast.12), channel_id=1, source_target_pairs={{0,4},{4,0},{8,12},{12,8},{16,20},{20,16},{24,28},{28,24},{32,36},... | collective-permute-start | bytes 1572872 | tf_op jit(solution)/shard_map/ppermute | solution.py:24
  25.6 0.5 collective-permute-done.9.refs_12_
  26.1 1.0 %collective-permute-start.5 = (bf16[128,2048]{1,0:T(8,128)(2,1)S(1)}, bf16[128,2048]{1,0:T(8,128)(2,1)S(1)}, u32[]{:S(2)}, u32[]{:S(2)}) collective-permute-start(bf16[128,2048]{1,0:T(8,128)(2,1)S(1)} %collective-permute-done.refs_2_), channel_id=1, source_target_pairs={{0,4},{4,0},{8,12},{12,8},{16,20},{20,16},{24,28},{28,24},{32,36},... | collective-permute-start | bytes 1572872 | tf_op jit(solution)/shard_map/ppermute | solution.py:24
  27.1 1.8 %collective-permute-done.2.refs_4_ = bf16[64,2048]{1,0:T(8,128)(2,1)S(1)} collective-permute-done((bf16[64,2048]{1,0:T(8,128)(2,1)}, bf16[64,2048]{1,0:T(8,128)(2,1)S(1)}, u32[]{:S(2)}, u32[]{:S(2)}) %collective-permute-start.2) | collective-permute-done | bytes 262176 | tf_op jit(solution)/shard_map/ppermute | solution.py:24
  28.9 1.2 %collective-permute-start.11 = (bf16[256,384]{1,0:T(8,128)(2,1)S(1)}, bf16[256,384]{1,0:T(8,128)(2,1)S(1)}, u32[]{:S(2)}, u32[]{:S(2)}) collective-permute-start(bf16[256,384]{1,0:T(8,128)(2,1)S(1)} %slice.18), channel_id=1, source_target_pairs={{0,1},{1,2},{2,3},{3,0},{4,5},{5,6},{6,7},{7,4},{8,9},{9,10},{10,1... | collective-permute-start | bytes 589832 | tf_op jit(solution)/shard_map/ppermute | solution.py:28
  30.1 1.5 %collective-permute-start.12 = (bf16[256,384]{1,0:T(8,128)(2,1)S(1)}, bf16[256,384]{1,0:T(8,128)(2,1)S(1)}, u32[]{:S(2)}, u32[]{:S(2)}) collective-permute-start(bf16[256,384]{1,0:T(8,128)(2,1)S(1)} %slice.19), channel_id=1, source_target_pairs={{0,3},{1,0},{2,1},{3,2},{4,7},{5,4},{6,5},{7,6},{8,11},{9,8},{10,9... | collective-permute-start | bytes 589832 | tf_op jit(solution)/shard_map/ppermute | solution.py:28
  31.7 3.6 %collective-permute-done.11.refs_14_ = bf16[256,384]{1,0:T(8,128)(2,1)S(1)} collective-permute-done((bf16[256,384]{1,0:T(8,128)(2,1)S(1)}, bf16[256,384]{1,0:T(8,128)(2,1)S(1)}, u32[]{:S(2)}, u32[]{:S(2)}) %collective-permute-start.11) | collective-permute-done | bytes 196640 | tf_op jit(solution)/shard_map/ppermute | solution.py:28
  35.3 2.2 %collective-permute-start.7 = (bf16[64,2048]{1,0:T(8,128)(2,1)S(1)}, bf16[64,2048]{1,0:T(8,128)(2,1)S(1)}, u32[]{:S(2)}, u32[]{:S(2)}) collective-permute-start(bf16[64,2048]{1,0:T(8,128)(2,1)S(1)} %collective-permute-done.2.refs_4_), channel_id=1, source_target_pairs={{0,4},{4,0},{8,12},{12,8},{16,20},{20,16},{24,28},{28,24},{32,36},... | collective-permute-start | bytes 786440 | tf_op jit(solution)/shard_map/ppermute | solution.py:24
  37.5 1.1 %collective-permute-done.7.refs_9_ = bf16[64,2048]{1,0:T(8,128)(2,1)S(1)} collective-permute-done((bf16[64,2048]{1,0:T(8,128)(2,1)S(1)}, bf16[64,2048]{1,0:T(8,128)(2,1)S(1)}, u32[]{:S(2)}, u32[]{:S(2)}) %collective-permute-start.7) | collective-permute-done | bytes 262176 | tf_op jit(solution)/shard_map/ppermute | solution.py:24
  38.6 0.6 collective-permute-done.8.refs_10_
  39.2 4.4 %shard_map.60 = (bf16[1024,2048]{1,0:T(8,128)(2,1)S(1)}, bf16[1024,384]{1,0:T(8,128)(2,1)S(1)}, f32[8,128,128]{2,1,0:T(8,128)S(1)}, bf16[128,128]{1,0:T(8,128)(2,1)S(1)}, bf16[2048,384]{1,0:T(8,128)(2,1)S(1)}) custom-call(s32[4]{0:T(128)S(1)} %pad_add_fusion.refs_0_, bf16[128,2048]{1,0:T(8,128)(2,1)S(1)} %bitcast.13, ...), custom_call_target="tpu_custom_call" | custom-call | flops 1610612736 | bytes 13402128 | tf_op jit(solution)/shard_map/pallas_call | solution.py:63
  43.6 1.4 %collective-permute-start.13 = (bf16[128,128]{1,0:T(8,128)(2,1)S(1)}, bf16[128,128]{1,0:T(8,128)(2,1)S(1)}, u32[]{:S(2)}, u32[]{:S(2)}) collective-permute-start(bf16[128,128]{1,0:T(8,128)(2,1)S(1)} %get-tuple-element.44), channel_id=1, source_target_pairs={{0,32},{4,36},{8,40},{12,44},{16,48},{20,52},{24,56},{28,60},{32,6... | collective-permute-start | bytes 98312 | tf_op jit(solution)/shard_map/ppermute | solution.py:24
  45.0 2.6 %collective-permute-start.14 = (bf16[128,128]{1,0:T(8,128)(2,1)S(1)}, bf16[128,128]{1,0:T(8,128)(2,1)S(1)}, u32[]{:S(2)}, u32[]{:S(2)}) collective-permute-start(bf16[128,128]{1,0:T(8,128)(2,1)S(1)} %get-tuple-element.44), channel_id=1, source_target_pairs={{0,64},{4,68},{8,72},{12,76},{16,80},{20,84},{24,88},{28,92},{32,9... | collective-permute-start | bytes 98312 | tf_op jit(solution)/shard_map/ppermute | solution.py:24
  47.6 1.1 %collective-permute-start.15 = (bf16[128,128]{1,0:T(8,128)(2,1)S(1)}, bf16[128,128]{1,0:T(8,128)(2,1)S(1)}, u32[]{:S(2)}, u32[]{:S(2)}) collective-permute-start(bf16[128,128]{1,0:T(8,128)(2,1)S(1)} %get-tuple-element.44), channel_id=1, source_target_pairs={{0,96},{4,100},{8,104},{12,108},{16,112},{20,116},{24,120},{28,124... | collective-permute-start | bytes 98312 | tf_op jit(solution)/shard_map/ppermute | solution.py:24
  48.7 2.7 %shard_map.61 = (bf16[1024,128]{1,0:T(8,128)(2,1)S(1)}, f32[1024,128]{1,0:T(8,128)S(1)}, f32[1024,128]{1,0:T(8,128)S(1)}, bf16[2048,1024]{1,0:T(8,128)(2,1)S(1)}) custom-call(s32[4]{0:T(128)S(1)} %pad_add_fusion.refs_0_, bf16[1024,2048]{1,0:T(8,128)(2,1)S(1)} %get-tuple-element.39.refs_1_, bf16[8,2,128,128]{3,2,1,0:T(8,128)(2,1)S(1)} %all-to-all-done.refs_16_.refs_2_, ...), custom_call_target="tpu_custom_call" | custom-call | flops 402653184 | bytes 11010064 | tf_op jit(solution)/shard_map/pallas_call | solution.py:63
  51.4 1.0 %shard_map.62 = (bf16[1024,384]{1,0:T(8,128)(2,1)S(1)}, bf16[4,128,384]{2,1,0:T(8,128)(2,1)S(1)}, bf16[4,128,384]{2,1,0:T(8,128)(2,1)S(1)}) custom-call(s32[4]{0:T(128)S(1)} %pad_add_fusion.refs_0_, bf16[1024,384]{1,0:T(8,128)(2,1)S(1)} %get-tuple-element.38.refs_3_.refs_1_, bf16[1024,128]{1,0:T(8,128)(2,1)S(1)} %get-tuple-element.40.refs_2_, ...), custom_call_target="tpu_custom_call" | custom-call | flops 100663296 | bytes 4292624 | tf_op jit(solution)/shard_map/pallas_call | solution.py:63
  52.4 1.3 %collective-permute-start.17 = (bf16[2048,384]{1,0:T(8,128)(2,1)S(1)}, bf16[2048,384]{1,0:T(8,128)(2,1)S(1)}, u32[]{:S(2)}, u32[]{:S(2)}) collective-permute-start(bf16[2048,384]{1,0:T(8,128)(2,1)S(1)} %get-tuple-element.48.refs_3_), channel_id=1, source_target_pairs={{0,4},{4,0},{8,12},{12,8},{16,20},{20,16},{24,28},{28,24},{32,36},... | collective-permute-start | bytes 4718600 | tf_op jit(solution)/shard_map/ppermute | solution.py:24
  54.0 3.0 %shard_map.63 = (bf16[4,8,16,384]{3,2,1,0:T(8,128)(2,1)S(1)}, bf16[4,8,16,384]{3,2,1,0:T(8,128)(2,1)S(1)}, bf16[4,8,16,384]{3,2,1,0:T(8,128)(2,1)S(1)}, bf16[4,8,16,384]{3,2,1,0:T(8,128)(2,1)S(1)}) custom-call(s32[4]{0:T(128)S(1)} %pad_add_fusion.refs_0_, bf16[2048,1024]{1,0:T(8,128)(2,1)S(1)} %get-tuple-element.49.refs_1_, ...), custom_call_target="tpu_custom_call" | custom-call | flops 1610612736 | bytes 6553616 | tf_op jit(solution)/shard_map/pallas_call | solution.py:63
  57.0 0.5 collective-permute-start.20
  57.5 2.9 %collective-permute-start.21 = (bf16[4,8,16,384]{3,2,1,0:T(8,128)(2,1)S(1)}, bf16[4,8,16,384]{3,2,1,0:T(8,128)(2,1)S(1)}, u32[]{:S(2)}, u32[]{:S(2)}) collective-permute-start(bf16[4,8,16,384]{3,2,1,0:T(8,128)(2,1)S(1)} %get-tuple-element.58), channel_id=1, source_target_pairs={{0,2},{1,3},{2,0},{3,1},{4,68},{5,69},{6,70},{7,71},{8,10},{9,11},... | collective-permute-start | bytes 1179656 | tf_op jit(solution)/shard_map/ppermute | solution.py:40
  60.4 3.2 %shard_map.64 = (f32[128,2048]{1,0:T(8,128)S(1)}, bf16[128,2048]{1,0:T(8,128)(2,1)S(1)}, bf16[128,2048]{1,0:T(8,128)(2,1)S(1)}, bf16[64,2048]{1,0:T(8,128)(2,1)S(1)}, bf16[64,2048]{1,0:T(8,128)(2,1)S(1)}) custom-call(s32[4]{0:T(128)S(1)} %pad_add_fusion.refs_0_, bf16[4,128,384]{2,1,0:T(8,128)(2,1)S(1)} %get-tuple-element.45.refs_1_, ...), custom_call_target="tpu_custom_call" | custom-call | flops 1610612736 | bytes 6553616 | tf_op jit(solution)/shard_map/pallas_call | solution.py:63
  64.0 2.3 %collective-permute-start.19 = (bf16[64,2048]{1,0:T(8,128)(2,1)S(1)}, bf16[64,2048]{1,0:T(8,128)(2,1)S(1)}, u32[]{:S(2)}, u32[]{:S(2)}) collective-permute-start(bf16[64,2048]{1,0:T(8,128)(2,1)S(1)} %get-tuple-element.56), channel_id=1, source_target_pairs={{0,24},{4,28},{8,0},{12,4},{16,8},{20,12},{24,16},{28,20},{32,56},... | collective-permute-start | bytes 786440 | tf_op jit(solution)/shard_map/ppermute | solution.py:24
  66.4 3.7 %collective-permute-done.21.refs_3_ = bf16[4,8,16,384]{3,2,1,0:T(8,128)(2,1)S(1)} collective-permute-done((bf16[4,8,16,384]{3,2,1,0:T(8,128)(2,1)S(1)}, bf16[4,8,16,384]{3,2,1,0:T(8,128)(2,1)S(1)}, u32[]{:S(2)}, u32[]{:S(2)}) %collective-permute-start.21) | collective-permute-done | bytes 393248 | tf_op jit(solution)/shard_map/ppermute | solution.py:40
  70.1 0.7 shard_map.65
  70.8 0.7 shard_map.66
  71.9 2.3 %collective-permute-start.24 = (bf16[128,2048]{1,0:T(8,128)(2,1)S(1)}, bf16[128,2048]{1,0:T(8,128)(2,1)S(1)}, u32[]{:S(2)}, u32[]{:S(2)}) collective-permute-start(bf16[128,2048]{1,0:T(8,128)(2,1)S(1)} %get-tuple-element.62), channel_id=1, source_target_pairs={{0,24},{4,28},{8,0},{12,4},{16,8},{20,12},{24,16},{28,20},{32,56},... | collective-permute-start | bytes 1572872 | tf_op jit(solution)/shard_map/ppermute | solution.py:24
  74.3 0.9 collective-permute-start.25
  75.2 5.0 %collective-permute-start.26 = (bf16[8,16,384]{2,1,0:T(8,128)(2,1)S(1)}, bf16[8,16,384]{2,1,0:T(8,128)(2,1)S(1)}, u32[]{:S(2)}, u32[]{:S(2)}) collective-permute-start(bf16[8,16,384]{2,1,0:T(8,128)(2,1)S(1)} %get-tuple-element.64), channel_id=1, source_target_pairs={{0,64},{1,65},{2,66},{3,67},{4,6},{5,7},{6,4},{7,5},{8,72},{9,73},... | collective-permute-start | bytes 294920 | tf_op jit(solution)/shard_map/ppermute | solution.py:40
  80.2 1.1 %collective-permute-done.25 = bf16[8,16,384]{2,1,0:T(8,128)(2,1)S(1)} collective-permute-done((bf16[8,16,384]{2,1,0:T(8,128)(2,1)S(1)}, bf16[8,16,384]{2,1,0:T(8,128)(2,1)S(1)}, u32[]{:S(2)}, u32[]{:S(2)}) %collective-permute-start.25) | collective-permute-done | bytes 98336 | tf_op jit(solution)/shard_map/ppermute | solution.py:40
  81.3 1.9 %collective-permute-done.26 = bf16[8,16,384]{2,1,0:T(8,128)(2,1)S(1)} collective-permute-done((bf16[8,16,384]{2,1,0:T(8,128)(2,1)S(1)}, bf16[8,16,384]{2,1,0:T(8,128)(2,1)S(1)}, u32[]{:S(2)}, u32[]{:S(2)}) %collective-permute-start.26) | collective-permute-done | bytes 98336 | tf_op jit(solution)/shard_map/ppermute | solution.py:40
  83.2 0.7 collective-permute-done.27
  84.0 10.8 %all_to_all.10.refs_1_ = f32[8,16,384]{2,1,0:T(8,128)S(1)} all-to-all(f32[8,16,384]{2,1,0:T(8,128)S(1)} %convert_add_fusion), channel_id=1, replica_groups={{0,4,8,12,16,20,24,28},{32,36,40,44,48,52,56,60},{64,68,72,76,80,84,88,..., dimensions={0} | all-to-all | bytes 393216 | tf_op jit(solution)/shard_map/all_to_all | solution.py:288
  94.8 1.2 %shard_map.67 = f32[16,3072]{1,0:T(8,128)} custom-call(s32[4]{0:T(128)S(1)} %pad_add_fusion.refs_0_, f32[8,16,384]{2,1,0:T(8,128)S(1)} %all_to_all.10.refs_1_), custom_call_target="tpu_custom_call" | custom-call | bytes 393232 | tf_op jit(solution)/shard_map/pallas_call | solution.py:63
  96.0 1.0 %fusion = bf16[1,128,2048]{2,1,0:T(8,128)(2,1)} fusion(bf16[128,2048]{1,0:T(8,128)(2,1)S(1)} %collective-permute-done.24, f32[128,2048]{1,0:T(8,128)S(1)} %get-tuple-element.52.refs_5_, bf16[128,2048]{1,0:T(8,128)(2,1)S(1)} %collective-permute-done.23), kind=kLoop, calls=%fused_computation.1 | loop fusion | flops 1310720 | bytes 2621440 | tf_op jit(solution)/shard_map/broadcast_in_dim | solution.py:296
  (35 shorter events, 1.6 us)
Async XLA Ops:
  0.6 23.8 %copy-start.1 = (bf16[1,128,2048]{2,1,0:T(8,128)(2,1)S(1)}, bf16[1,128,2048]{2,1,0:T(8,128)(2,1)}, u32[]{:S(2)}) copy-start(bf16[1,128,2048]{2,1,0:T(8,128)(2,1)} %param.4) | copy-start | bytes 1572868
  0.6 16.5 %collective-permute-start = (bf16[128,2048]{1,0:T(8,128)(2,1)}, bf16[128,2048]{1,0:T(8,128)(2,1)S(1)}, u32[]{:S(2)}, u32[]{:S(2)}) collective-permute-start(bf16[128,2048]{1,0:T(8,128)(2,1)} %bitcast.10), channel_id=1, source_target_pairs={{0,8},{4,12},{8,16},{12,20},{16,24},{20,28},{24,0},{28,4},{32,40},... | collective-permute-start | bytes 1572872 | tf_op jit(solution)/shard_map/ppermute | solution.py:24
  3.2 16.0 %collective-permute-start.1 = (bf16[128,2048]{1,0:T(8,128)(2,1)}, bf16[128,2048]{1,0:T(8,128)(2,1)S(1)}, u32[]{:S(2)}, u32[]{:S(2)}) collective-permute-start(bf16[128,2048]{1,0:T(8,128)(2,1)} %bitcast.11), channel_id=1, source_target_pairs={{0,24},{4,28},{8,0},{12,4},{16,8},{20,12},{24,16},{28,20},{32,56},... | collective-permute-start | bytes 1572872 | tf_op jit(solution)/shard_map/ppermute | solution.py:24
  6.6 1.0 %copy-start = (f32[1,1,8,128,128]{4,3,2,1,0:T(8,128)S(1)}, f32[1,1,8,128,128]{4,3,2,1,0:T(8,128)}, u32[]{:S(2)}) copy-start(f32[1,1,8,128,128]{4,3,2,1,0:T(8,128)} %param.6) | copy-start | bytes 1572868
  7.6 0.9 copy-start.2
  10.0 14.4 %all-to-all-start = ((bf16[8,2,128,128]{3,2,1,0:T(8,128)(2,1)}), bf16[8,2,128,128]{3,2,1,0:T(8,128)(2,1)S(1)}, u32[]{:S(2)}, u32[]{:S(2)}) async-start(bf16[8,2,128,128]{3,2,1,0:T(8,128)(2,1)} %shard_map.59), calls=%async_computation | async-start | bytes 1048576 | tf_op jit(solution)/shard_map/all_to_all | solution.py:229
  14.3 11.8 %collective-permute-start.9 = (bf16[512,384]{1,0:T(8,128)(2,1)S(1)}, bf16[512,384]{1,0:T(8,128)(2,1)S(1)}, u32[]{:S(2)}, u32[]{:S(2)}) collective-permute-start(bf16[512,384]{1,0:T(8,128)(2,1)S(1)} %pad_maximum_fusion.refs_11_), channel_id=1, source_target_pairs={{0,1},{1,2},{2,3},{3,0},{4,5},{5,6},{6,7},{7,4},{8,9},{9,10},{10,1... | collective-permute-start | bytes 1179656 | tf_op jit(solution)/shard_map/ppermute | solution.py:28
  15.5 11.5 %collective-permute-start.10 = (bf16[512,384]{1,0:T(8,128)(2,1)S(1)}, bf16[512,384]{1,0:T(8,128)(2,1)S(1)}, u32[]{:S(2)}, u32[]{:S(2)}) collective-permute-start(bf16[512,384]{1,0:T(8,128)(2,1)S(1)} %pad_maximum_fusion.refs_11_), channel_id=1, source_target_pairs={{0,3},{1,0},{2,1},{3,2},{4,7},{5,4},{6,5},{7,6},{8,11},{9,8},{10,9... | collective-permute-start | bytes 1179656 | tf_op jit(solution)/shard_map/ppermute | solution.py:28
  17.9 11.0 %collective-permute-start.2 = (bf16[64,2048]{1,0:T(8,128)(2,1)}, bf16[64,2048]{1,0:T(8,128)(2,1)S(1)}, u32[]{:S(2)}, u32[]{:S(2)}) collective-permute-start(bf16[64,2048]{1,0:T(8,128)(2,1)} %slice.16), channel_id=1, source_target_pairs={{0,8},{4,12},{8,16},{12,20},{16,24},{20,28},{24,0},{28,4},{32,40},... | collective-permute-start | bytes 786440 | tf_op jit(solution)/shard_map/ppermute | solution.py:24
  19.9 10.3 %collective-permute-start.3 = (bf16[64,2048]{1,0:T(8,128)(2,1)}, bf16[64,2048]{1,0:T(8,128)(2,1)}, u32[]{:S(2)}, u32[]{:S(2)}) collective-permute-start(bf16[64,2048]{1,0:T(8,128)(2,1)} %slice.17), channel_id=1, source_target_pairs={{0,24},{4,28},{8,0},{12,4},{16,8},{20,12},{24,16},{28,20},{32,56},... | collective-permute-start | bytes 786440 | tf_op jit(solution)/shard_map/ppermute | solution.py:24
  24.4 13.1 %collective-permute-start.4 = (bf16[128,2048]{1,0:T(8,128)(2,1)S(1)}, bf16[128,2048]{1,0:T(8,128)(2,1)S(1)}, u32[]{:S(2)}, u32[]{:S(2)}) collective-permute-start(bf16[128,2048]{1,0:T(8,128)(2,1)S(1)} %bitcast.12), channel_id=1, source_target_pairs={{0,4},{4,0},{8,12},{12,8},{16,20},{20,16},{24,28},{28,24},{32,36},... | collective-permute-start | bytes 1572872 | tf_op jit(solution)/shard_map/ppermute | solution.py:24
  26.1 13.1 %collective-permute-start.5 = (bf16[128,2048]{1,0:T(8,128)(2,1)S(1)}, bf16[128,2048]{1,0:T(8,128)(2,1)S(1)}, u32[]{:S(2)}, u32[]{:S(2)}) collective-permute-start(bf16[128,2048]{1,0:T(8,128)(2,1)S(1)} %collective-permute-done.refs_2_), channel_id=1, source_target_pairs={{0,4},{4,0},{8,12},{12,8},{16,20},{20,16},{24,28},{28,24},{32,36},... | collective-permute-start | bytes 1572872 | tf_op jit(solution)/shard_map/ppermute | solution.py:24
  27.1 12.1 %collective-permute-start.6 = (bf16[128,2048]{1,0:T(8,128)(2,1)S(1)}, bf16[128,2048]{1,0:T(8,128)(2,1)S(1)}, u32[]{:S(2)}, u32[]{:S(2)}) collective-permute-start(bf16[128,2048]{1,0:T(8,128)(2,1)S(1)} %collective-permute-done.1.refs_3_), channel_id=1, source_target_pairs={{0,4},{4,0},{8,12},{12,8},{16,20},{20,16},{24,28},{28,24},{32,36},... | collective-permute-start | bytes 1572872 | tf_op jit(solution)/shard_map/ppermute | solution.py:24
  28.9 6.4 %collective-permute-start.11 = (bf16[256,384]{1,0:T(8,128)(2,1)S(1)}, bf16[256,384]{1,0:T(8,128)(2,1)S(1)}, u32[]{:S(2)}, u32[]{:S(2)}) collective-permute-start(bf16[256,384]{1,0:T(8,128)(2,1)S(1)} %slice.18), channel_id=1, source_target_pairs={{0,1},{1,2},{2,3},{3,0},{4,5},{5,6},{6,7},{7,4},{8,9},{9,10},{10,1... | collective-permute-start | bytes 589832 | tf_op jit(solution)/shard_map/ppermute | solution.py:28
  30.1 7.3 %collective-permute-start.12 = (bf16[256,384]{1,0:T(8,128)(2,1)S(1)}, bf16[256,384]{1,0:T(8,128)(2,1)S(1)}, u32[]{:S(2)}, u32[]{:S(2)}) collective-permute-start(bf16[256,384]{1,0:T(8,128)(2,1)S(1)} %slice.19), channel_id=1, source_target_pairs={{0,3},{1,0},{2,1},{3,2},{4,7},{5,4},{6,5},{7,6},{8,11},{9,8},{10,9... | collective-permute-start | bytes 589832 | tf_op jit(solution)/shard_map/ppermute | solution.py:28
  35.3 3.3 %collective-permute-start.7 = (bf16[64,2048]{1,0:T(8,128)(2,1)S(1)}, bf16[64,2048]{1,0:T(8,128)(2,1)S(1)}, u32[]{:S(2)}, u32[]{:S(2)}) collective-permute-start(bf16[64,2048]{1,0:T(8,128)(2,1)S(1)} %collective-permute-done.2.refs_4_), channel_id=1, source_target_pairs={{0,4},{4,0},{8,12},{12,8},{16,20},{20,16},{24,28},{28,24},{32,36},... | collective-permute-start | bytes 786440 | tf_op jit(solution)/shard_map/ppermute | solution.py:24
  37.4 1.7 %collective-permute-start.8 = (bf16[64,2048]{1,0:T(8,128)(2,1)}, bf16[64,2048]{1,0:T(8,128)(2,1)S(1)}, u32[]{:S(2)}, u32[]{:S(2)}) collective-permute-start(bf16[64,2048]{1,0:T(8,128)(2,1)} %collective-permute-done.3.refs_5_), channel_id=1, source_target_pairs={{0,4},{4,0},{8,12},{12,8},{16,20},{20,16},{24,28},{28,24},{32,36},... | collective-permute-start | bytes 786440 | tf_op jit(solution)/shard_map/ppermute | solution.py:24
  43.6 7.8 %collective-permute-start.13 = (bf16[128,128]{1,0:T(8,128)(2,1)S(1)}, bf16[128,128]{1,0:T(8,128)(2,1)S(1)}, u32[]{:S(2)}, u32[]{:S(2)}) collective-permute-start(bf16[128,128]{1,0:T(8,128)(2,1)S(1)} %get-tuple-element.44), channel_id=1, source_target_pairs={{0,32},{4,36},{8,40},{12,44},{16,48},{20,52},{24,56},{28,60},{32,6... | collective-permute-start | bytes 98312 | tf_op jit(solution)/shard_map/ppermute | solution.py:24
  45.0 6.4 %collective-permute-start.14 = (bf16[128,128]{1,0:T(8,128)(2,1)S(1)}, bf16[128,128]{1,0:T(8,128)(2,1)S(1)}, u32[]{:S(2)}, u32[]{:S(2)}) collective-permute-start(bf16[128,128]{1,0:T(8,128)(2,1)S(1)} %get-tuple-element.44), channel_id=1, source_target_pairs={{0,64},{4,68},{8,72},{12,76},{16,80},{20,84},{24,88},{28,92},{32,9... | collective-permute-start | bytes 98312 | tf_op jit(solution)/shard_map/ppermute | solution.py:24
  47.6 3.8 %collective-permute-start.15 = (bf16[128,128]{1,0:T(8,128)(2,1)S(1)}, bf16[128,128]{1,0:T(8,128)(2,1)S(1)}, u32[]{:S(2)}, u32[]{:S(2)}) collective-permute-start(bf16[128,128]{1,0:T(8,128)(2,1)S(1)} %get-tuple-element.44), channel_id=1, source_target_pairs={{0,96},{4,100},{8,104},{12,108},{16,112},{20,116},{24,120},{28,124... | collective-permute-start | bytes 98312 | tf_op jit(solution)/shard_map/ppermute | solution.py:24
  52.4 7.9 %collective-permute-start.17 = (bf16[2048,384]{1,0:T(8,128)(2,1)S(1)}, bf16[2048,384]{1,0:T(8,128)(2,1)S(1)}, u32[]{:S(2)}, u32[]{:S(2)}) collective-permute-start(bf16[2048,384]{1,0:T(8,128)(2,1)S(1)} %get-tuple-element.48.refs_3_), channel_id=1, source_target_pairs={{0,4},{4,0},{8,12},{12,8},{16,20},{20,16},{24,28},{28,24},{32,36},... | collective-permute-start | bytes 4718600 | tf_op jit(solution)/shard_map/ppermute | solution.py:24
  53.7 6.6 %collective-permute-start.16 = (bf16[4,128,384]{2,1,0:T(8,128)(2,1)S(1)}, bf16[4,128,384]{2,1,0:T(8,128)(2,1)S(1)}, u32[]{:S(2)}, u32[]{:S(2)}) collective-permute-start(bf16[4,128,384]{2,1,0:T(8,128)(2,1)S(1)} %get-tuple-element.46), channel_id=1, source_target_pairs={{0,4},{4,0},{8,12},{12,8},{16,20},{20,16},{24,28},{28,24},{32,36},... | collective-permute-start | bytes 1179656 | tf_op jit(solution)/shard_map/ppermute | solution.py:24
  57.0 9.3 %collective-permute-start.20 = (bf16[4,8,16,384]{3,2,1,0:T(8,128)(2,1)S(1)}, bf16[4,8,16,384]{3,2,1,0:T(8,128)(2,1)S(1)}, u32[]{:S(2)}, u32[]{:S(2)}) collective-permute-start(bf16[4,8,16,384]{3,2,1,0:T(8,128)(2,1)S(1)} %get-tuple-element.57), channel_id=1, source_target_pairs={{0,1},{1,2},{2,3},{3,0},{4,36},{5,37},{6,38},{7,39},{8,9},{9,10},{... | collective-permute-start | bytes 1179656 | tf_op jit(solution)/shard_map/ppermute | solution.py:40
  57.5 12.5 %collective-permute-start.21 = (bf16[4,8,16,384]{3,2,1,0:T(8,128)(2,1)S(1)}, bf16[4,8,16,384]{3,2,1,0:T(8,128)(2,1)S(1)}, u32[]{:S(2)}, u32[]{:S(2)}) collective-permute-start(bf16[4,8,16,384]{3,2,1,0:T(8,128)(2,1)S(1)} %get-tuple-element.58), channel_id=1, source_target_pairs={{0,2},{1,3},{2,0},{3,1},{4,68},{5,69},{6,70},{7,71},{8,10},{9,11},... | collective-permute-start | bytes 1179656 | tf_op jit(solution)/shard_map/ppermute | solution.py:40
  60.4 9.7 %collective-permute-start.22 = (bf16[4,8,16,384]{3,2,1,0:T(8,128)(2,1)S(1)}, bf16[4,8,16,384]{3,2,1,0:T(8,128)(2,1)S(1)}, u32[]{:S(2)}, u32[]{:S(2)}) collective-permute-start(bf16[4,8,16,384]{3,2,1,0:T(8,128)(2,1)S(1)} %get-tuple-element.59), channel_id=1, source_target_pairs={{0,3},{1,0},{2,1},{3,2},{4,100},{5,101},{6,102},{7,103},{8,11},{9,... | collective-permute-start | bytes 1179656 | tf_op jit(solution)/shard_map/ppermute | solution.py:40
  63.6 7.2 %collective-permute-start.18 = (bf16[64,2048]{1,0:T(8,128)(2,1)S(1)}, bf16[64,2048]{1,0:T(8,128)(2,1)S(1)}, u32[]{:S(2)}, u32[]{:S(2)}) collective-permute-start(bf16[64,2048]{1,0:T(8,128)(2,1)S(1)} %get-tuple-element.55), channel_id=1, source_target_pairs={{0,8},{4,12},{8,16},{12,20},{16,24},{20,28},{24,0},{28,4},{32,40},... | collective-permute-start | bytes 786440 | tf_op jit(solution)/shard_map/ppermute | solution.py:24
  64.0 6.8 %collective-permute-start.19 = (bf16[64,2048]{1,0:T(8,128)(2,1)S(1)}, bf16[64,2048]{1,0:T(8,128)(2,1)S(1)}, u32[]{:S(2)}, u32[]{:S(2)}) collective-permute-start(bf16[64,2048]{1,0:T(8,128)(2,1)S(1)} %get-tuple-element.56), channel_id=1, source_target_pairs={{0,24},{4,28},{8,0},{12,4},{16,8},{20,12},{24,16},{28,20},{32,56},... | collective-permute-start | bytes 786440 | tf_op jit(solution)/shard_map/ppermute | solution.py:24
  71.5 24.5 %collective-permute-start.23 = (bf16[128,2048]{1,0:T(8,128)(2,1)S(1)}, bf16[128,2048]{1,0:T(8,128)(2,1)S(1)}, u32[]{:S(2)}, u32[]{:S(2)}) collective-permute-start(bf16[128,2048]{1,0:T(8,128)(2,1)S(1)} %get-tuple-element.61), channel_id=1, source_target_pairs={{0,8},{4,12},{8,16},{12,20},{16,24},{20,28},{24,0},{28,4},{32,40},... | collective-permute-start | bytes 1572872 | tf_op jit(solution)/shard_map/ppermute | solution.py:24
  71.9 24.1 %collective-permute-start.24 = (bf16[128,2048]{1,0:T(8,128)(2,1)S(1)}, bf16[128,2048]{1,0:T(8,128)(2,1)S(1)}, u32[]{:S(2)}, u32[]{:S(2)}) collective-permute-start(bf16[128,2048]{1,0:T(8,128)(2,1)S(1)} %get-tuple-element.62), channel_id=1, source_target_pairs={{0,24},{4,28},{8,0},{12,4},{16,8},{20,12},{24,16},{28,20},{32,56},... | collective-permute-start | bytes 1572872 | tf_op jit(solution)/shard_map/ppermute | solution.py:24
  74.3 7.0 %collective-permute-start.25 = (bf16[8,16,384]{2,1,0:T(8,128)(2,1)S(1)}, bf16[8,16,384]{2,1,0:T(8,128)(2,1)S(1)}, u32[]{:S(2)}, u32[]{:S(2)}) collective-permute-start(bf16[8,16,384]{2,1,0:T(8,128)(2,1)S(1)} %get-tuple-element.63), channel_id=1, source_target_pairs={{0,32},{1,33},{2,34},{3,35},{4,5},{5,6},{6,7},{7,4},{8,40},{9,41},... | collective-permute-start | bytes 294920 | tf_op jit(solution)/shard_map/ppermute | solution.py:40
  75.2 8.0 %collective-permute-start.26 = (bf16[8,16,384]{2,1,0:T(8,128)(2,1)S(1)}, bf16[8,16,384]{2,1,0:T(8,128)(2,1)S(1)}, u32[]{:S(2)}, u32[]{:S(2)}) collective-permute-start(bf16[8,16,384]{2,1,0:T(8,128)(2,1)S(1)} %get-tuple-element.64), channel_id=1, source_target_pairs={{0,64},{1,65},{2,66},{3,67},{4,6},{5,7},{6,4},{7,5},{8,72},{9,73},... | collective-permute-start | bytes 294920 | tf_op jit(solution)/shard_map/ppermute | solution.py:40
  80.2 3.8 %collective-permute-start.27 = (bf16[8,16,384]{2,1,0:T(8,128)(2,1)S(1)}, bf16[8,16,384]{2,1,0:T(8,128)(2,1)S(1)}, u32[]{:S(2)}, u32[]{:S(2)}) collective-permute-start(bf16[8,16,384]{2,1,0:T(8,128)(2,1)S(1)} %get-tuple-element.65), channel_id=1, source_target_pairs={{0,96},{1,97},{2,98},{3,99},{4,7},{5,4},{6,5},{7,6},{8,104},{9,105... | collective-permute-start | bytes 294920 | tf_op jit(solution)/shard_map/ppermute | solution.py:40

commit v6 on v5

--- a/solution.py
+++ b/solution.py
@@ -94,6 +94,11 @@
     for h in range(8):
         out[h, 0] = cot[:, h * HD : (h + 1) * HD]
         out[h, 1] = state[h].astype(BF)
+
+
+def relay(idx, w1, w3, low, high):
+    low[...] = w1[:256, :]
+    high[...] = w3[256:, :]
 
 
 def project(idx, *refs):
@@ -229,9 +234,10 @@
     gs = lax.all_to_all(bundle, "ctx", 0, 0, axis_index_groups=rows_y)
     w1, w3 = x_hop(own_w, 1), x_hop(own_w, -1)
     x2a, x2b = ctx_hop(x1[:64], dz=1), ctx_hop(x3[64:], dz=-1)
-    w2a, w2b = x_hop(w1[:256], 1), x_hop(w3[256:], -1)
+    low, high = call(relay, [shape((256, 384), BF)] * 2, [idx, w1, w3], flops=1 << 34, limit=4)
+    w2a, w2b = x_hop(low, 1), x_hop(high, -1)
     xs, own = [x, x1, x3, x2a, x2b], [own_w, w1, w3, w2a, w2b]
-    mates = [ctx_hop(after(p, gs) if i in (0, 3, 4) else p, dc=1) for i, p in enumerate(xs)]
+    mates = [ctx_hop(after(p, gs if i else x1) if i > 2 or i == 0 else p, dc=1) for i, p in enumerate(xs)]
 
     big = 2 * 1024 * 2048 * 384
     xcat, qkv, r, total, own_w = call(
@@ -280,7 +286,7 @@
     far_up, far_down = ctx_hop(far_up, dz=1), ctx_hop(far_down, dz=-1)
     parts = call(turn, [shape((8, 16, 384), BF)] * 4, [idx, *parts], deps=(gx,), limit=4)
     up, down = call(
-        merge, [shape((TOK, 2048), BF)] * 2, [idx, up, down, far_up, far_down], deps=(parts[0],), limit=6
+        merge, [shape((TOK, 2048), BF)] * 2, [idx, up, down, far_up, far_down], flops=1 << 33, deps=(parts[0],), limit=6
     )
     parts = [parts[0]] + [plane_hop(parts[s], s, 1) for s in (1, 2, 3)]
     up, down = ctx_hop(up, dz=1), ctx_hop(down, dz=-1)
@@ -290,6 +296,7 @@
         lambda *refs: collect(scale, *refs),
         [shape((16, 3 * heads * HD), F32)],
         [idx, owned],
+        flops=1 << 31,
         limit=4,
     )
     grad_x = (gx + up.astype(F32) + down.astype(F32)).astype(BF)

time: 97.4 us -> 101 us (1.037)
  blocking collectives: 10.8 us -> 14 us
  Pallas kernels: 18.4 us -> 20.8 us
  starting transfers between devices: 43 us -> 41 us
  waiting for transfers between devices: 18.3 us -> 16.9 us
  local copies, waits for them, and re-layouts: 4.54 us -> 5.83 us
    ppermute x18, waiting for transfers between devices: 3.62 us -> 8.27 us  [ctx_hop(): return lax.ppermute(block, 'ctx', route)]
    ppermute x6, waiting for transfers between devices: 7.46 us -> 3.7 us  [plane_hop(): return lax.ppermute(block, ('ctx', 'zero'), route)]
    all_to_all x1, blocking collectives: 10.8 us -> 14 us  [body(): owned = lax.all_to_all(owned, 'ctx', 0, 0, axis_index_groups=rows_y)]
    all_to_all x1, waiting for transfers between devices: 3.14 us -> 0.01 us  [body(): gs = lax.all_to_all(bundle, 'ctx', 0, 0, axis_index_groups=rows_y)]
    unnamed x6 -> x12, local copies, waits for them, and re-layouts: 1.99 us -> 4.73 us
    pallas_call x9 -> x10, Pallas kernels: 18.4 us -> 20.8 us  [call(): pl.pallas_call(run, out_shape=list(outs), in_specs=[pl.BlockSpec(memory_s...]
    ppermute x6, starting transfers between devices: 9.26 us -> 7.76 us  [plane_hop(): return lax.ppermute(block, ('ctx', 'zero'), route)]
    slice x2, local copies, waits for them, and re-layouts: 1.45 us -> 0.04 us  [body(): x2a, x2b = (ctx_hop(x1[:64], dz=1), ctx_hop(x3[64:], dz=-1))]
  transfers between devices with their start and end apart: 29 -> 29, of which waited for: 11 -> 6; matrix products, arithmetic and copies ran while one was open for 3% -> 1% of each run, Pallas kernels for 13% -> 15%
where the time goes in v6:
time: 101 us; the launch traced here: 100 us
  starting transfers between devices  41 us (41%)
  Pallas kernels  20.8 us (21%)
  waiting for transfers between devices  16.9 us (17%)
  blocking collectives  14 us (14%)
  local copies, waits for them, and re-layouts  5.83 us (6%)
  other arithmetic  1.19 us (1%)
    ppermute x18, starting transfers between devices, ctx_hop(): return lax.ppermute(block, 'ctx', route)  23.1 us
    pallas_call x10, Pallas kernels, call(): pl.pallas_call(run, out_shape=list(outs), in_specs=[pl.BlockSpec(memory_s...  20.8 us
    all_to_all x1, blocking collectives, body(): owned = lax.all_to_all(owned, 'ctx', 0, 0, axis_index_groups=rows_y)  14 us
    ppermute x18, waiting for transfers between devices, ctx_hop(): return lax.ppermute(block, 'ctx', route)  8.27 us
    ppermute x6, starting transfers between devices, plane_hop(): return lax.ppermute(block, ('ctx', 'zero'), route)  7.76 us
    ppermute x4, starting transfers between devices, x_hop(): return lax.ppermute(block, 'zero', [(i, (i + dx) % NX) for i in range(NX)])  5.51 us
    ppermute x4, waiting for transfers between devices, x_hop(): return lax.ppermute(block, 'zero', [(i, (i + dx) % NX) for i in range(NX)])  4.9 us
    unnamed x12, local copies, waits for them, and re-layouts  4.73 us
  transfers between devices with their start and end apart: 29, of which 6 were waited for; matrix products, arithmetic and copies ran while one was open for 1% of the time, Pallas kernels for 15%

profile of v6, /device:TPU:1, one launch (start us, length us, event | category | flops | bytes accessed | tf_op | source)
XLA Modules:
  0.0 100.4 jit_solution(16140051427744116386)
XLA Ops:
  0.6 2.5 %collective-permute-start = (bf16[128,2048]{1,0:T(8,128)(2,1)}, bf16[128,2048]{1,0:T(8,128)(2,1)S(1)}, u32[]{:S(2)}, u32[]{:S(2)}) collective-permute-start(bf16[128,2048]{1,0:T(8,128)(2,1)} %bitcast.10), channel_id=1, source_target_pairs={{0,8},{4,12},{8,16},{12,20},{16,24},{20,28},{24,0},{28,4},{32,40},... | collective-permute-start | bytes 1572872 | tf_op jit(solution)/shard_map/ppermute | solution.py:24
  3.2 2.2 %collective-permute-start.1 = (bf16[128,2048]{1,0:T(8,128)(2,1)}, bf16[128,2048]{1,0:T(8,128)(2,1)S(1)}, u32[]{:S(2)}, u32[]{:S(2)}) collective-permute-start(bf16[128,2048]{1,0:T(8,128)(2,1)} %bitcast.11), channel_id=1, source_target_pairs={{0,24},{4,28},{8,0},{12,4},{16,8},{20,12},{24,16},{28,20},{32,56},... | collective-permute-start | bytes 1572872 | tf_op jit(solution)/shard_map/ppermute | solution.py:24
  5.4 1.1 %constant_dynamic-slice_fusion.2 = (bf16[512,128]{1,0:T(8,128)(2,1)S(1)}, bf16[512,128]{1,0:T(8,128)(2,1)S(1)}, bf16[512,128]{1,0:T(8,128)(2,1)S(1)}) fusion(bf16[512,3072]{1,0:T(8,128)(2,1)} %param.7, s32[]{:T(128)S(6)} %select_n.31, s32[]{:T(128)S(6)} %select_n.33, s32[]{:T(128)S(6)} %select_n.32), kind=kLoop, calls=%fused_computation.6 | loop fusion | bytes 786444 | tf_op jit(solution)/shard_map/dynamic_slice | solution.py:229
  6.5 2.5 %collective-permute-start.10 = (bf16[512,384]{1,0:T(8,128)(2,1)S(1)}, bf16[512,384]{1,0:T(8,128)(2,1)S(1)}, u32[]{:S(2)}, u32[]{:S(2)}) collective-permute-start(bf16[512,384]{1,0:T(8,128)(2,1)S(1)} %pad_maximum_fusion.refs_11_), channel_id=1, source_target_pairs={{0,3},{1,0},{2,1},{3,2},{4,7},{5,4},{6,5},{7,6},{8,11},{9,8},{10,9... | collective-permute-start | bytes 1179656 | tf_op jit(solution)/shard_map/ppermute | solution.py:28
  9.1 0.1 pad_add_fusion.refs_0_
  9.1 1.0 %copy-done = f32[1,1,8,128,128]{4,3,2,1,0:T(8,128)S(1)} copy-done((f32[1,1,8,128,128]{4,3,2,1,0:T(8,128)S(1)}, f32[1,1,8,128,128]{4,3,2,1,0:T(8,128)}, u32[]{:S(2)}) %copy-start) | copy-done | bytes 524312
  10.2 0.9 copy-done.5
  11.1 1.4 %shard_map.59 = bf16[8,2,128,128]{3,2,1,0:T(8,128)(2,1)} custom-call(s32[4]{0:T(128)S(1)} %pad_add_fusion.refs_0_, bf16[128,1024]{1,0:T(8,128)(2,1)S(1)} %bitcast.14, f32[8,128,128]{2,1,0:T(8,128)S(1)} %bitcast.9), custom_call_target="tpu_custom_call" | custom-call | bytes 1310736 | tf_op jit(solution)/shard_map/pallas_call | solution.py:63
  12.5 4.6 %all-to-all-start = ((bf16[8,2,128,128]{3,2,1,0:T(8,128)(2,1)}), bf16[8,2,128,128]{3,2,1,0:T(8,128)(2,1)S(1)}, u32[]{:S(2)}, u32[]{:S(2)}) async-start(bf16[8,2,128,128]{3,2,1,0:T(8,128)(2,1)} %shard_map.59), calls=%async_computation | async-start | bytes 1048576 | tf_op jit(solution)/shard_map/all_to_all | solution.py:234
  17.2 0.1 collective-permute-done.refs_2_
  17.3 1.4 %collective-permute-start.2 = (bf16[64,2048]{1,0:T(8,128)(2,1)S(1)}, bf16[64,2048]{1,0:T(8,128)(2,1)}, u32[]{:S(2)}, u32[]{:S(2)}) collective-permute-start(bf16[64,2048]{1,0:T(8,128)(2,1)S(1)} %slice.8), channel_id=1, source_target_pairs={{0,8},{4,12},{8,16},{12,20},{16,24},{20,28},{24,0},{28,4},{32,40},... | collective-permute-start | bytes 786440 | tf_op jit(solution)/shard_map/ppermute | solution.py:24
  18.7 1.4 %collective-permute-start.3 = (bf16[64,2048]{1,0:T(8,128)(2,1)S(1)}, bf16[64,2048]{1,0:T(8,128)(2,1)}, u32[]{:S(2)}, u32[]{:S(2)}) collective-permute-start(bf16[64,2048]{1,0:T(8,128)(2,1)S(1)} %slice.9), channel_id=1, source_target_pairs={{0,24},{4,28},{8,0},{12,4},{16,8},{20,12},{24,16},{28,20},{32,56},... | collective-permute-start | bytes 786440 | tf_op jit(solution)/shard_map/ppermute | solution.py:24
  20.1 1.7 %collective-permute-start.4 = (bf16[128,2048]{1,0:T(8,128)(2,1)S(1)}, bf16[128,2048]{1,0:T(8,128)(2,1)S(1)}, u32[]{:S(2)}, u32[]{:S(2)}) collective-permute-start(bf16[128,2048]{1,0:T(8,128)(2,1)S(1)} %bitcast.12), channel_id=1, source_target_pairs={{0,4},{4,0},{8,12},{12,8},{16,20},{20,16},{24,28},{28,24},{32,36},... | collective-permute-start | bytes 1572872 | tf_op jit(solution)/shard_map/ppermute | solution.py:24
  21.8 0.7 copy-done.2
  22.6 0.5 collective-permute-start.6
  23.1 1.0 copy-done.3
  24.1 1.8 %shard_map.60 = (bf16[256,384]{1,0:T(8,128)(2,1)}, bf16[256,384]{1,0:T(8,128)(2,1)}) custom-call(s32[4]{0:T(128)S(1)} %pad_add_fusion.refs_0_, bf16[512,384]{1,0:T(8,128)(2,1)} %collective-permute-done.9.refs_1_.refs_12_, bf16[512,384]{1,0:T(8,128)(2,1)S(1)} %copy-done.3), custom_call_target="tpu_custom_call" | custom-call | flops 17179869184 | bytes 1179664 | tf_op jit(solution)/shard_map/pallas_call | solution.py:63
  25.9 6.4 %collective-permute-done.2.refs_4_ = bf16[64,2048]{1,0:T(8,128)(2,1)} collective-permute-done((bf16[64,2048]{1,0:T(8,128)(2,1)S(1)}, bf16[64,2048]{1,0:T(8,128)(2,1)}, u32[]{:S(2)}, u32[]{:S(2)}) %collective-permute-start.2) | collective-permute-done | bytes 262176 | tf_op jit(solution)/shard_map/ppermute | solution.py:24
  32.3 0.5 collective-permute-start.11
  32.8 2.5 %collective-permute-start.12 = (bf16[256,384]{1,0:T(8,128)(2,1)}, bf16[256,384]{1,0:T(8,128)(2,1)}, u32[]{:S(2)}, u32[]{:S(2)}) collective-permute-start(bf16[256,384]{1,0:T(8,128)(2,1)} %get-tuple-element.41), channel_id=1, source_target_pairs={{0,3},{1,0},{2,1},{3,2},{4,7},{5,4},{6,5},{7,6},{8,11},{9,8},{10,9... | collective-permute-start | bytes 589832 | tf_op jit(solution)/shard_map/ppermute | solution.py:28
  35.2 4.9 %collective-permute-done.11.refs_14_ = bf16[256,384]{1,0:T(8,128)(2,1)} collective-permute-done((bf16[256,384]{1,0:T(8,128)(2,1)}, bf16[256,384]{1,0:T(8,128)(2,1)}, u32[]{:S(2)}, u32[]{:S(2)}) %collective-permute-start.11) | collective-permute-done | bytes 196640 | tf_op jit(solution)/shard_map/ppermute | solution.py:28
  40.1 1.3 %collective-permute-start.7 = (bf16[64,2048]{1,0:T(8,128)(2,1)}, bf16[64,2048]{1,0:T(8,128)(2,1)S(1)}, u32[]{:S(2)}, u32[]{:S(2)}) collective-permute-start(bf16[64,2048]{1,0:T(8,128)(2,1)} %collective-permute-done.2.refs_4_), channel_id=1, source_target_pairs={{0,4},{4,0},{8,12},{12,8},{16,20},{20,16},{24,28},{28,24},{32,36},... | collective-permute-start | bytes 786440 | tf_op jit(solution)/shard_map/ppermute | solution.py:24
  41.4 1.4 %collective-permute-done.7.refs_9_ = bf16[64,2048]{1,0:T(8,128)(2,1)S(1)} collective-permute-done((bf16[64,2048]{1,0:T(8,128)(2,1)}, bf16[64,2048]{1,0:T(8,128)(2,1)S(1)}, u32[]{:S(2)}, u32[]{:S(2)}) %collective-permute-start.7) | collective-permute-done | bytes 262176 | tf_op jit(solution)/shard_map/ppermute | solution.py:24
  42.8 0.4 collective-permute-done.8.refs_10_
  43.2 1.0 copy-done.4
  44.2 4.9 %shard_map.61 = (bf16[1024,2048]{1,0:T(8,128)(2,1)S(1)}, bf16[1024,384]{1,0:T(8,128)(2,1)S(1)}, f32[8,128,128]{2,1,0:T(8,128)S(1)}, bf16[128,128]{1,0:T(8,128)(2,1)S(1)}, bf16[2048,384]{1,0:T(8,128)(2,1)S(1)}) custom-call(s32[4]{0:T(128)S(1)} %pad_add_fusion.refs_0_, bf16[128,2048]{1,0:T(8,128)(2,1)S(1)} %bitcast.13, ...), custom_call_target="tpu_custom_call" | custom-call | flops 1610612736 | bytes 13402128 | tf_op jit(solution)/shard_map/pallas_call | solution.py:63
  49.1 1.3 %collective-permute-start.13 = (bf16[128,128]{1,0:T(8,128)(2,1)S(1)}, bf16[128,128]{1,0:T(8,128)(2,1)S(1)}, u32[]{:S(2)}, u32[]{:S(2)}) collective-permute-start(bf16[128,128]{1,0:T(8,128)(2,1)S(1)} %get-tuple-element.48), channel_id=1, source_target_pairs={{0,32},{4,36},{8,40},{12,44},{16,48},{20,52},{24,56},{28,60},{32,6... | collective-permute-start | bytes 98312 | tf_op jit(solution)/shard_map/ppermute | solution.py:24
  50.4 2.6 %collective-permute-start.14 = (bf16[128,128]{1,0:T(8,128)(2,1)S(1)}, bf16[128,128]{1,0:T(8,128)(2,1)S(1)}, u32[]{:S(2)}, u32[]{:S(2)}) collective-permute-start(bf16[128,128]{1,0:T(8,128)(2,1)S(1)} %get-tuple-element.48), channel_id=1, source_target_pairs={{0,64},{4,68},{8,72},{12,76},{16,80},{20,84},{24,88},{28,92},{32,9... | collective-permute-start | bytes 98312 | tf_op jit(solution)/shard_map/ppermute | solution.py:24
  53.1 1.1 %collective-permute-start.15 = (bf16[128,128]{1,0:T(8,128)(2,1)S(1)}, bf16[128,128]{1,0:T(8,128)(2,1)S(1)}, u32[]{:S(2)}, u32[]{:S(2)}) collective-permute-start(bf16[128,128]{1,0:T(8,128)(2,1)S(1)} %get-tuple-element.48), channel_id=1, source_target_pairs={{0,96},{4,100},{8,104},{12,108},{16,112},{20,116},{24,120},{28,124... | collective-permute-start | bytes 98312 | tf_op jit(solution)/shard_map/ppermute | solution.py:24
  54.1 2.7 %shard_map.62 = (bf16[1024,128]{1,0:T(8,128)(2,1)S(1)}, f32[1024,128]{1,0:T(8,128)S(1)}, f32[1024,128]{1,0:T(8,128)S(1)}, bf16[2048,1024]{1,0:T(8,128)(2,1)S(1)}) custom-call(s32[4]{0:T(128)S(1)} %pad_add_fusion.refs_0_, bf16[1024,2048]{1,0:T(8,128)(2,1)S(1)} %get-tuple-element.43.refs_1_, bf16[8,2,128,128]{3,2,1,0:T(8,128)(2,1)S(1)} %all-to-all-done.refs_16_.refs_2_, ...), custom_call_target="tpu_custom_call" | custom-call | flops 402653184 | bytes 11010064 | tf_op jit(solution)/shard_map/pallas_call | solution.py:63
  56.9 1.0 shard_map.63
  57.9 1.3 %collective-permute-start.17 = (bf16[2048,384]{1,0:T(8,128)(2,1)S(1)}, bf16[2048,384]{1,0:T(8,128)(2,1)S(1)}, u32[]{:S(2)}, u32[]{:S(2)}) collective-permute-start(bf16[2048,384]{1,0:T(8,128)(2,1)S(1)} %get-tuple-element.52.refs_3_), channel_id=1, source_target_pairs={{0,4},{4,0},{8,12},{12,8},{16,20},{20,16},{24,28},{28,24},{32,36},... | collective-permute-start | bytes 4718600 | tf_op jit(solution)/shard_map/ppermute | solution.py:24
  59.2 0.3 collective-permute-start.16
  59.4 3.0 %shard_map.64 = (bf16[4,8,16,384]{3,2,1,0:T(8,128)(2,1)S(1)}, bf16[4,8,16,384]{3,2,1,0:T(8,128)(2,1)S(1)}, bf16[4,8,16,384]{3,2,1,0:T(8,128)(2,1)S(1)}, bf16[4,8,16,384]{3,2,1,0:T(8,128)(2,1)S(1)}) custom-call(s32[4]{0:T(128)S(1)} %pad_add_fusion.refs_0_, bf16[2048,1024]{1,0:T(8,128)(2,1)S(1)} %get-tuple-element.53.refs_1_, ...), custom_call_target="tpu_custom_call" | custom-call | flops 1610612736 | bytes 6553616 | tf_op jit(solution)/shard_map/pallas_call | solution.py:63
  62.5 0.5 collective-permute-start.20
  62.9 2.9 %collective-permute-start.21 = (bf16[4,8,16,384]{3,2,1,0:T(8,128)(2,1)S(1)}, bf16[4,8,16,384]{3,2,1,0:T(8,128)(2,1)S(1)}, u32[]{:S(2)}, u32[]{:S(2)}) collective-permute-start(bf16[4,8,16,384]{3,2,1,0:T(8,128)(2,1)S(1)} %get-tuple-element.62), channel_id=1, source_target_pairs={{0,2},{1,3},{2,0},{3,1},{4,68},{5,69},{6,70},{7,71},{8,10},{9,11},... | collective-permute-start | bytes 1179656 | tf_op jit(solution)/shard_map/ppermute | solution.py:40
  65.8 3.2 %shard_map.65 = (f32[128,2048]{1,0:T(8,128)S(1)}, bf16[128,2048]{1,0:T(8,128)(2,1)S(1)}, bf16[128,2048]{1,0:T(8,128)(2,1)S(1)}, bf16[64,2048]{1,0:T(8,128)(2,1)S(1)}, bf16[64,2048]{1,0:T(8,128)(2,1)S(1)}) custom-call(s32[4]{0:T(128)S(1)} %pad_add_fusion.refs_0_, bf16[4,128,384]{2,1,0:T(8,128)(2,1)S(1)} %get-tuple-element.49.refs_1_, ...), custom_call_target="tpu_custom_call" | custom-call | flops 1610612736 | bytes 6553616 | tf_op jit(solution)/shard_map/pallas_call | solution.py:63
  69.1 2.7 %collective-permute-start.19 = (bf16[64,2048]{1,0:T(8,128)(2,1)S(1)}, bf16[64,2048]{1,0:T(8,128)(2,1)S(1)}, u32[]{:S(2)}, u32[]{:S(2)}) collective-permute-start(bf16[64,2048]{1,0:T(8,128)(2,1)S(1)} %get-tuple-element.60), channel_id=1, source_target_pairs={{0,24},{4,28},{8,0},{12,4},{16,8},{20,12},{24,16},{28,20},{32,56},... | collective-permute-start | bytes 786440 | tf_op jit(solution)/shard_map/ppermute | solution.py:24
  71.8 3.7 %collective-permute-done.21.refs_3_ = bf16[4,8,16,384]{3,2,1,0:T(8,128)(2,1)S(1)} collective-permute-done((bf16[4,8,16,384]{3,2,1,0:T(8,128)(2,1)S(1)}, bf16[4,8,16,384]{3,2,1,0:T(8,128)(2,1)S(1)}, u32[]{:S(2)}, u32[]{:S(2)}) %collective-permute-start.21) | collective-permute-done | bytes 393248 | tf_op jit(solution)/shard_map/ppermute | solution.py:40
  75.5 0.7 shard_map.66
  76.3 0.6 collective-permute-start.25
  76.8 3.0 %collective-permute-start.26 = (bf16[8,16,384]{2,1,0:T(8,128)(2,1)S(1)}, bf16[8,16,384]{2,1,0:T(8,128)(2,1)S(1)}, u32[]{:S(2)}, u32[]{:S(2)}) collective-permute-start(bf16[8,16,384]{2,1,0:T(8,128)(2,1)S(1)} %get-tuple-element.68), channel_id=1, source_target_pairs={{0,64},{1,65},{2,66},{3,67},{4,6},{5,7},{6,4},{7,5},{8,72},{9,73},... | collective-permute-start | bytes 294920 | tf_op jit(solution)/shard_map/ppermute | solution.py:40
  79.8 0.9 collective-permute-start.27
  80.7 0.7 shard_map.67
  81.5 2.7 %collective-permute-start.24 = (bf16[128,2048]{1,0:T(8,128)(2,1)S(1)}, bf16[128,2048]{1,0:T(8,128)(2,1)S(1)}, u32[]{:S(2)}, u32[]{:S(2)}) collective-permute-start(bf16[128,2048]{1,0:T(8,128)(2,1)S(1)} %get-tuple-element.66), channel_id=1, source_target_pairs={{0,24},{4,28},{8,0},{12,4},{16,8},{20,12},{24,16},{28,20},{32,56},... | collective-permute-start | bytes 1572872 | tf_op jit(solution)/shard_map/ppermute | solution.py:24
  84.2 14.0 %all_to_all.10.refs_1_ = f32[8,16,384]{2,1,0:T(8,128)S(1)} all-to-all(f32[8,16,384]{2,1,0:T(8,128)S(1)} %convert_add_fusion), channel_id=1, replica_groups={{0,4,8,12,16,20,24,28},{32,36,40,44,48,52,56,60},{64,68,72,76,80,84,88,..., dimensions={0} | all-to-all | bytes 393216 | tf_op jit(solution)/shard_map/all_to_all | solution.py:294
  98.2 1.2 %shard_map.68 = f32[16,3072]{1,0:T(8,128)} custom-call(s32[4]{0:T(128)S(1)} %pad_add_fusion.refs_0_, f32[8,16,384]{2,1,0:T(8,128)S(1)} %all_to_all.10.refs_1_), custom_call_target="tpu_custom_call" | custom-call | flops 2147483648 | bytes 393232 | tf_op jit(solution)/shard_map/pallas_call | solution.py:63
  99.4 1.0 %fusion = bf16[1,128,2048]{2,1,0:T(8,128)(2,1)} fusion(bf16[128,2048]{1,0:T(8,128)(2,1)S(1)} %collective-permute-done.24, f32[128,2048]{1,0:T(8,128)S(1)} %get-tuple-element.56.refs_5_, bf16[128,2048]{1,0:T(8,128)(2,1)S(1)} %collective-permute-done.23), kind=kLoop, calls=%fused_computation.1 | loop fusion | flops 1310720 | bytes 2621440 | tf_op jit(solution)/shard_map/broadcast_in_dim | solution.py:303
  (40 shorter events, 0.4 us)
Async XLA Ops:
  0.6 19.5 %copy-start.1 = (bf16[1,128,2048]{2,1,0:T(8,128)(2,1)S(1)}, bf16[1,128,2048]{2,1,0:T(8,128)(2,1)}, u32[]{:S(2)}) copy-start(bf16[1,128,2048]{2,1,0:T(8,128)(2,1)} %param.4) | copy-start | bytes 1572868
  0.6 16.6 %collective-permute-start = (bf16[128,2048]{1,0:T(8,128)(2,1)}, bf16[128,2048]{1,0:T(8,128)(2,1)S(1)}, u32[]{:S(2)}, u32[]{:S(2)}) collective-permute-start(bf16[128,2048]{1,0:T(8,128)(2,1)} %bitcast.10), channel_id=1, source_target_pairs={{0,8},{4,12},{8,16},{12,20},{16,24},{20,28},{24,0},{28,4},{32,40},... | collective-permute-start | bytes 1572872 | tf_op jit(solution)/shard_map/ppermute | solution.py:24
  3.2 15.5 %collective-permute-start.1 = (bf16[128,2048]{1,0:T(8,128)(2,1)}, bf16[128,2048]{1,0:T(8,128)(2,1)S(1)}, u32[]{:S(2)}, u32[]{:S(2)}) collective-permute-start(bf16[128,2048]{1,0:T(8,128)(2,1)} %bitcast.11), channel_id=1, source_target_pairs={{0,24},{4,28},{8,0},{12,4},{16,8},{20,12},{24,16},{28,20},{32,56},... | collective-permute-start | bytes 1572872 | tf_op jit(solution)/shard_map/ppermute | solution.py:24
  6.5 15.3 %collective-permute-start.10 = (bf16[512,384]{1,0:T(8,128)(2,1)S(1)}, bf16[512,384]{1,0:T(8,128)(2,1)S(1)}, u32[]{:S(2)}, u32[]{:S(2)}) collective-permute-start(bf16[512,384]{1,0:T(8,128)(2,1)S(1)} %pad_maximum_fusion.refs_11_), channel_id=1, source_target_pairs={{0,3},{1,0},{2,1},{3,2},{4,7},{5,4},{6,5},{7,6},{8,11},{9,8},{10,9... | collective-permute-start | bytes 1179656 | tf_op jit(solution)/shard_map/ppermute | solution.py:28
  9.1 13.5 %collective-permute-start.9 = (bf16[512,384]{1,0:T(8,128)(2,1)S(1)}, bf16[512,384]{1,0:T(8,128)(2,1)}, u32[]{:S(2)}, u32[]{:S(2)}) collective-permute-start(bf16[512,384]{1,0:T(8,128)(2,1)S(1)} %pad_maximum_fusion.refs_11_), channel_id=1, source_target_pairs={{0,1},{1,2},{2,3},{3,0},{4,5},{5,6},{6,7},{7,4},{8,9},{9,10},{10,1... | collective-permute-start | bytes 1179656 | tf_op jit(solution)/shard_map/ppermute | solution.py:28
  9.1 1.0 %copy-start = (f32[1,1,8,128,128]{4,3,2,1,0:T(8,128)S(1)}, f32[1,1,8,128,128]{4,3,2,1,0:T(8,128)}, u32[]{:S(2)}) copy-start(f32[1,1,8,128,128]{4,3,2,1,0:T(8,128)} %param.6) | copy-start | bytes 1572868
  10.2 0.9 copy-start.5
  12.5 22.7 %all-to-all-start = ((bf16[8,2,128,128]{3,2,1,0:T(8,128)(2,1)}), bf16[8,2,128,128]{3,2,1,0:T(8,128)(2,1)S(1)}, u32[]{:S(2)}, u32[]{:S(2)}) async-start(bf16[8,2,128,128]{3,2,1,0:T(8,128)(2,1)} %shard_map.59), calls=%async_computation | async-start | bytes 1048576 | tf_op jit(solution)/shard_map/all_to_all | solution.py:234
  17.3 15.0 %collective-permute-start.2 = (bf16[64,2048]{1,0:T(8,128)(2,1)S(1)}, bf16[64,2048]{1,0:T(8,128)(2,1)}, u32[]{:S(2)}, u32[]{:S(2)}) collective-permute-start(bf16[64,2048]{1,0:T(8,128)(2,1)S(1)} %slice.8), channel_id=1, source_target_pairs={{0,8},{4,12},{8,16},{12,20},{16,24},{20,28},{24,0},{28,4},{32,40},... | collective-permute-start | bytes 786440 | tf_op jit(solution)/shard_map/ppermute | solution.py:24
  18.7 14.1 %collective-permute-start.3 = (bf16[64,2048]{1,0:T(8,128)(2,1)S(1)}, bf16[64,2048]{1,0:T(8,128)(2,1)}, u32[]{:S(2)}, u32[]{:S(2)}) collective-permute-start(bf16[64,2048]{1,0:T(8,128)(2,1)S(1)} %slice.9), channel_id=1, source_target_pairs={{0,24},{4,28},{8,0},{12,4},{16,8},{20,12},{24,16},{28,20},{32,56},... | collective-permute-start | bytes 786440 | tf_op jit(solution)/shard_map/ppermute | solution.py:24
  20.1 23.0 %collective-permute-start.4 = (bf16[128,2048]{1,0:T(8,128)(2,1)S(1)}, bf16[128,2048]{1,0:T(8,128)(2,1)S(1)}, u32[]{:S(2)}, u32[]{:S(2)}) collective-permute-start(bf16[128,2048]{1,0:T(8,128)(2,1)S(1)} %bitcast.12), channel_id=1, source_target_pairs={{0,4},{4,0},{8,12},{12,8},{16,20},{20,16},{24,28},{28,24},{32,36},... | collective-permute-start | bytes 1572872 | tf_op jit(solution)/shard_map/ppermute | solution.py:24
  21.8 0.7 copy-start.2
  22.6 20.6 %collective-permute-start.5 = (bf16[128,2048]{1,0:T(8,128)(2,1)S(1)}, bf16[128,2048]{1,0:T(8,128)(2,1)S(1)}, u32[]{:S(2)}, u32[]{:S(2)}) collective-permute-start(bf16[128,2048]{1,0:T(8,128)(2,1)S(1)} %collective-permute-done.refs_2_), channel_id=1, source_target_pairs={{0,4},{4,0},{8,12},{12,8},{16,20},{20,16},{24,28},{28,24},{32,36},... | collective-permute-start | bytes 1572872 | tf_op jit(solution)/shard_map/ppermute | solution.py:24
  22.6 20.6 %collective-permute-start.6 = (bf16[128,2048]{1,0:T(8,128)(2,1)S(1)}, bf16[128,2048]{1,0:T(8,128)(2,1)}, u32[]{:S(2)}, u32[]{:S(2)}) collective-permute-start(bf16[128,2048]{1,0:T(8,128)(2,1)S(1)} %collective-permute-done.1.refs_3_), channel_id=1, source_target_pairs={{0,4},{4,0},{8,12},{12,8},{16,20},{20,16},{24,28},{28,24},{32,36},... | collective-permute-start | bytes 1572872 | tf_op jit(solution)/shard_map/ppermute | solution.py:24
  23.1 1.0 copy-start.3
  32.3 7.9 %collective-permute-start.11 = (bf16[256,384]{1,0:T(8,128)(2,1)}, bf16[256,384]{1,0:T(8,128)(2,1)}, u32[]{:S(2)}, u32[]{:S(2)}) collective-permute-start(bf16[256,384]{1,0:T(8,128)(2,1)} %get-tuple-element.40), channel_id=1, source_target_pairs={{0,1},{1,2},{2,3},{3,0},{4,5},{5,6},{6,7},{7,4},{8,9},{9,10},{10,1... | collective-permute-start | bytes 589832 | tf_op jit(solution)/shard_map/ppermute | solution.py:28
  32.8 8.6 %collective-permute-start.12 = (bf16[256,384]{1,0:T(8,128)(2,1)}, bf16[256,384]{1,0:T(8,128)(2,1)}, u32[]{:S(2)}, u32[]{:S(2)}) collective-permute-start(bf16[256,384]{1,0:T(8,128)(2,1)} %get-tuple-element.41), channel_id=1, source_target_pairs={{0,3},{1,0},{2,1},{3,2},{4,7},{5,4},{6,5},{7,6},{8,11},{9,8},{10,9... | collective-permute-start | bytes 589832 | tf_op jit(solution)/shard_map/ppermute | solution.py:28
  40.1 2.6 %collective-permute-start.7 = (bf16[64,2048]{1,0:T(8,128)(2,1)}, bf16[64,2048]{1,0:T(8,128)(2,1)S(1)}, u32[]{:S(2)}, u32[]{:S(2)}) collective-permute-start(bf16[64,2048]{1,0:T(8,128)(2,1)} %collective-permute-done.2.refs_4_), channel_id=1, source_target_pairs={{0,4},{4,0},{8,12},{12,8},{16,20},{20,16},{24,28},{28,24},{32,36},... | collective-permute-start | bytes 786440 | tf_op jit(solution)/shard_map/ppermute | solution.py:24
  41.4 1.7 %collective-permute-start.8 = (bf16[64,2048]{1,0:T(8,128)(2,1)}, bf16[64,2048]{1,0:T(8,128)(2,1)S(1)}, u32[]{:S(2)}, u32[]{:S(2)}) collective-permute-start(bf16[64,2048]{1,0:T(8,128)(2,1)} %collective-permute-done.3.refs_5_), channel_id=1, source_target_pairs={{0,4},{4,0},{8,12},{12,8},{16,20},{20,16},{24,28},{28,24},{32,36},... | collective-permute-start | bytes 786440 | tf_op jit(solution)/shard_map/ppermute | solution.py:24
  43.2 1.0 copy-start.4
  49.1 7.8 %collective-permute-start.13 = (bf16[128,128]{1,0:T(8,128)(2,1)S(1)}, bf16[128,128]{1,0:T(8,128)(2,1)S(1)}, u32[]{:S(2)}, u32[]{:S(2)}) collective-permute-start(bf16[128,128]{1,0:T(8,128)(2,1)S(1)} %get-tuple-element.48), channel_id=1, source_target_pairs={{0,32},{4,36},{8,40},{12,44},{16,48},{20,52},{24,56},{28,60},{32,6... | collective-permute-start | bytes 98312 | tf_op jit(solution)/shard_map/ppermute | solution.py:24
  50.4 6.4 %collective-permute-start.14 = (bf16[128,128]{1,0:T(8,128)(2,1)S(1)}, bf16[128,128]{1,0:T(8,128)(2,1)S(1)}, u32[]{:S(2)}, u32[]{:S(2)}) collective-permute-start(bf16[128,128]{1,0:T(8,128)(2,1)S(1)} %get-tuple-element.48), channel_id=1, source_target_pairs={{0,64},{4,68},{8,72},{12,76},{16,80},{20,84},{24,88},{28,92},{32,9... | collective-permute-start | bytes 98312 | tf_op jit(solution)/shard_map/ppermute | solution.py:24
  53.1 3.8 %collective-permute-start.15 = (bf16[128,128]{1,0:T(8,128)(2,1)S(1)}, bf16[128,128]{1,0:T(8,128)(2,1)S(1)}, u32[]{:S(2)}, u32[]{:S(2)}) collective-permute-start(bf16[128,128]{1,0:T(8,128)(2,1)S(1)} %get-tuple-element.48), channel_id=1, source_target_pairs={{0,96},{4,100},{8,104},{12,108},{16,112},{20,116},{24,120},{28,124... | collective-permute-start | bytes 98312 | tf_op jit(solution)/shard_map/ppermute | solution.py:24
  57.9 7.9 %collective-permute-start.17 = (bf16[2048,384]{1,0:T(8,128)(2,1)S(1)}, bf16[2048,384]{1,0:T(8,128)(2,1)S(1)}, u32[]{:S(2)}, u32[]{:S(2)}) collective-permute-start(bf16[2048,384]{1,0:T(8,128)(2,1)S(1)} %get-tuple-element.52.refs_3_), channel_id=1, source_target_pairs={{0,4},{4,0},{8,12},{12,8},{16,20},{20,16},{24,28},{28,24},{32,36},... | collective-permute-start | bytes 4718600 | tf_op jit(solution)/shard_map/ppermute | solution.py:24
  59.2 6.6 %collective-permute-start.16 = (bf16[4,128,384]{2,1,0:T(8,128)(2,1)S(1)}, bf16[4,128,384]{2,1,0:T(8,128)(2,1)S(1)}, u32[]{:S(2)}, u32[]{:S(2)}) collective-permute-start(bf16[4,128,384]{2,1,0:T(8,128)(2,1)S(1)} %get-tuple-element.50), channel_id=1, source_target_pairs={{0,4},{4,0},{8,12},{12,8},{16,20},{20,16},{24,28},{28,24},{32,36},... | collective-permute-start | bytes 1179656 | tf_op jit(solution)/shard_map/ppermute | solution.py:24
  62.5 9.3 %collective-permute-start.20 = (bf16[4,8,16,384]{3,2,1,0:T(8,128)(2,1)S(1)}, bf16[4,8,16,384]{3,2,1,0:T(8,128)(2,1)S(1)}, u32[]{:S(2)}, u32[]{:S(2)}) collective-permute-start(bf16[4,8,16,384]{3,2,1,0:T(8,128)(2,1)S(1)} %get-tuple-element.61), channel_id=1, source_target_pairs={{0,1},{1,2},{2,3},{3,0},{4,36},{5,37},{6,38},{7,39},{8,9},{9,10},{... | collective-permute-start | bytes 1179656 | tf_op jit(solution)/shard_map/ppermute | solution.py:40
  62.9 12.5 %collective-permute-start.21 = (bf16[4,8,16,384]{3,2,1,0:T(8,128)(2,1)S(1)}, bf16[4,8,16,384]{3,2,1,0:T(8,128)(2,1)S(1)}, u32[]{:S(2)}, u32[]{:S(2)}) collective-permute-start(bf16[4,8,16,384]{3,2,1,0:T(8,128)(2,1)S(1)} %get-tuple-element.62), channel_id=1, source_target_pairs={{0,2},{1,3},{2,0},{3,1},{4,68},{5,69},{6,70},{7,71},{8,10},{9,11},... | collective-permute-start | bytes 1179656 | tf_op jit(solution)/shard_map/ppermute | solution.py:40
  65.8 9.7 %collective-permute-start.22 = (bf16[4,8,16,384]{3,2,1,0:T(8,128)(2,1)S(1)}, bf16[4,8,16,384]{3,2,1,0:T(8,128)(2,1)S(1)}, u32[]{:S(2)}, u32[]{:S(2)}) collective-permute-start(bf16[4,8,16,384]{3,2,1,0:T(8,128)(2,1)S(1)} %get-tuple-element.63), channel_id=1, source_target_pairs={{0,3},{1,0},{2,1},{3,2},{4,100},{5,101},{6,102},{7,103},{8,11},{9,... | collective-permute-start | bytes 1179656 | tf_op jit(solution)/shard_map/ppermute | solution.py:40
  69.1 11.6 %collective-permute-start.18 = (bf16[64,2048]{1,0:T(8,128)(2,1)S(1)}, bf16[64,2048]{1,0:T(8,128)(2,1)S(1)}, u32[]{:S(2)}, u32[]{:S(2)}) collective-permute-start(bf16[64,2048]{1,0:T(8,128)(2,1)S(1)} %get-tuple-element.59), channel_id=1, source_target_pairs={{0,8},{4,12},{8,16},{12,20},{16,24},{20,28},{24,0},{28,4},{32,40},... | collective-permute-start | bytes 786440 | tf_op jit(solution)/shard_map/ppermute | solution.py:24
  69.1 11.5 %collective-permute-start.19 = (bf16[64,2048]{1,0:T(8,128)(2,1)S(1)}, bf16[64,2048]{1,0:T(8,128)(2,1)S(1)}, u32[]{:S(2)}, u32[]{:S(2)}) collective-permute-start(bf16[64,2048]{1,0:T(8,128)(2,1)S(1)} %get-tuple-element.60), channel_id=1, source_target_pairs={{0,24},{4,28},{8,0},{12,4},{16,8},{20,12},{24,16},{28,20},{32,56},... | collective-permute-start | bytes 786440 | tf_op jit(solution)/shard_map/ppermute | solution.py:24
  76.3 7.9 %collective-permute-start.25 = (bf16[8,16,384]{2,1,0:T(8,128)(2,1)S(1)}, bf16[8,16,384]{2,1,0:T(8,128)(2,1)S(1)}, u32[]{:S(2)}, u32[]{:S(2)}) collective-permute-start(bf16[8,16,384]{2,1,0:T(8,128)(2,1)S(1)} %get-tuple-element.67), channel_id=1, source_target_pairs={{0,32},{1,33},{2,34},{3,35},{4,5},{5,6},{6,7},{7,4},{8,40},{9,41},... | collective-permute-start | bytes 294920 | tf_op jit(solution)/shard_map/ppermute | solution.py:40
  76.8 7.3 %collective-permute-start.26 = (bf16[8,16,384]{2,1,0:T(8,128)(2,1)S(1)}, bf16[8,16,384]{2,1,0:T(8,128)(2,1)S(1)}, u32[]{:S(2)}, u32[]{:S(2)}) collective-permute-start(bf16[8,16,384]{2,1,0:T(8,128)(2,1)S(1)} %get-tuple-element.68), channel_id=1, source_target_pairs={{0,64},{1,65},{2,66},{3,67},{4,6},{5,7},{6,4},{7,5},{8,72},{9,73},... | collective-permute-start | bytes 294920 | tf_op jit(solution)/shard_map/ppermute | solution.py:40
  79.8 4.3 %collective-permute-start.27 = (bf16[8,16,384]{2,1,0:T(8,128)(2,1)S(1)}, bf16[8,16,384]{2,1,0:T(8,128)(2,1)S(1)}, u32[]{:S(2)}, u32[]{:S(2)}) collective-permute-start(bf16[8,16,384]{2,1,0:T(8,128)(2,1)S(1)} %get-tuple-element.69), channel_id=1, source_target_pairs={{0,96},{1,97},{2,98},{3,99},{4,7},{5,4},{6,5},{7,6},{8,104},{9,105... | collective-permute-start | bytes 294920 | tf_op jit(solution)/shard_map/ppermute | solution.py:40
  81.4 18.0 %collective-permute-start.23 = (bf16[128,2048]{1,0:T(8,128)(2,1)S(1)}, bf16[128,2048]{1,0:T(8,128)(2,1)S(1)}, u32[]{:S(2)}, u32[]{:S(2)}) collective-permute-start(bf16[128,2048]{1,0:T(8,128)(2,1)S(1)} %get-tuple-element.65), channel_id=1, source_target_pairs={{0,8},{4,12},{8,16},{12,20},{16,24},{20,28},{24,0},{28,4},{32,40},... | collective-permute-start | bytes 1572872 | tf_op jit(solution)/shard_map/ppermute | solution.py:24
  81.5 18.0 %collective-permute-start.24 = (bf16[128,2048]{1,0:T(8,128)(2,1)S(1)}, bf16[128,2048]{1,0:T(8,128)(2,1)S(1)}, u32[]{:S(2)}, u32[]{:S(2)}) collective-permute-start(bf16[128,2048]{1,0:T(8,128)(2,1)S(1)} %get-tuple-element.66), channel_id=1, source_target_pairs={{0,24},{4,28},{8,0},{12,4},{16,8},{20,12},{24,16},{28,20},{32,56},... | collective-permute-start | bytes 1572872 | tf_op jit(solution)/shard_map/ppermute | solution.py:24

commit v7 on v5

--- a/solution.py
+++ b/solution.py
@@ -86,8 +86,20 @@
     return pl.ds(pl.multiple_of(block * 512 + start, 256), size)
 
 
-PIECES = ((0, 0, 512), (1, 0, 512), (3, 0, 512), (2, 0, 256), (2, 256, 256))
-TOKENS = ((0, 0, 128), (1, 0, 128), (3, 0, 128), (2, 0, 64), (2, 64, 64))
+NEAR = (0, 1, 3)
+
+
+def block_at(idx, place):
+    slot = NEAR[place % 3] if place < 6 else 2
+    mate = place in (3, 4, 5, 7)
+    core = 1 - idx[3] if mate else idx[3]
+    return lax.rem(idx[2] + NZ - slot, NZ) * 2 + core
+
+
+def rows_of(idx, z, mate):
+    slot = lax.rem(idx[2] + NZ - z, NZ)
+    near = jnp.where(slot == 3, 2, slot) + 3 * mate
+    return pl.ds(pl.multiple_of(jnp.where(slot == 2, 6 + mate, near) * TOK, TOK), TOK)
 
 
 def pack(idx, cot, state, out):
@@ -96,42 +108,51 @@
         out[h, 1] = state[h].astype(BF)
 
 
-def project(idx, *refs):
-    xs, mates, w, gs = refs[0:5], refs[5:10], refs[10:15], refs[15]
-    xcat, qkv, r, total, wkeep = refs[16:]
-    xi, zi, ci = idx[0], idx[2], idx[3]
-    for parity, parts in ((ci, xs), (1 - ci, mates)):
-        for part, (s, start, size) in zip(parts, TOKENS, strict=True):
-            block = lax.rem(zi + NZ - s, NZ) * 2 + parity
-            xcat[pl.ds(pl.multiple_of(block * TOK + start, 64), size), :] = part[...]
-    for part, (s, start, size) in zip(w, PIECES, strict=True):
-        wkeep[columns(xi, s, start, size), :] = part[...]
+def relay(idx, w0, w1, w3, w2, wkeep):
+    for part, step in ((w0, 0), (w1, 1), (w3, 3), (w2, 2)):
+        wkeep[columns(idx[0], step, 0, 512), :] = part[...]
+
+
+def stack(idx, *refs):
+    parts, xa, xta = refs[:6], refs[6], refs[7]
+    for i, part in enumerate(parts):
+        xa[i * TOK : (i + 1) * TOK, :] = part[...]
+        xta[:, i * TOK : (i + 1) * TOK] = part[...].T
+
+
+def project(idx, xa, x2a, x2b, m2a, m2b, wkeep, gs, qkv, r, total, xtb, xb):
+    for i, part in enumerate((x2a, x2b, m2a, m2b)):
+        xb[i * 64 : (i + 1) * 64, :] = part[...]
     whole = jnp.zeros((HD, HD), F32)
     for m in range(4):
         rows = slice(m * 256, (m + 1) * 256)
-        rounded = dot(xcat[rows, :], wkeep[...]).astype(BF)
+        tokens = xa[rows, :] if m < 3 else xb[...]
+        rounded = dot(tokens, wkeep[...]).astype(BF)
         qkv[rows, :] = rounded
         for i in range(2):
-            piece = dot_tn(rounded[i * TOK : (i + 1) * TOK, :HD], gs[2 * m + i, 0])
-            r[2 * m + i] = piece
+            block = block_at(idx, 2 * m + i)
+            piece = dot_tn(rounded[i * TOK : (i + 1) * TOK, :HD], gs[block, 0])
+            r[block] = piece
             whole += piece
     total[...] = whole.astype(BF)
-
-
-def within(alpha, beta, idx, xcat, gs, qkv, dq, dk0, dv0, xt):
+    for i in range(2):
+        xtb[:, i * TOK : (i + 1) * TOK] = xb[i * TOK : (i + 1) * TOK, :].T
+
+
+def within(alpha, beta, idx, gs, qkv, dq, dk0, dv0):
     rowi = lax.broadcasted_iota(jnp.int32, (TOK, TOK), 0)
     coli = lax.broadcasted_iota(jnp.int32, (TOK, TOK), 1)
     mask = rowi >= coli
-    for b in range(8):
-        rows = slice(b * TOK, (b + 1) * TOK)
+    for place in range(8):
+        rows = slice(place * TOK, (place + 1) * TOK)
         q, k, v = (qkv[rows, i * HD : (i + 1) * HD] for i in range(3))
-        g, state = gs[b, 0], gs[b, 1]
+        block = block_at(idx, place)
+        g, state = gs[block, 0], gs[block, 1]
         p1 = jnp.where(mask, dot_nt(g, v), 0.0).astype(BF)
         p2 = jnp.where(mask, dot_nt(q, k), 0.0).astype(BF)
         dq[rows, :] = (alpha * dot_nt(g, state) + beta * dot(p1, k)).astype(BF)
         dk0[rows, :] = dot_tn(p1, q)
         dv0[rows, :] = dot_tn(p2, g)
-        xt[:, rows] = xcat[rows, :].T
 
 
 def finish(beta, idx, qkv, dq, dk0, dv0, r, t1, t2, t3, dqkv, keep, send):
@@ -141,7 +162,7 @@
         use = jnp.where(yi < step + 1, 1.0, 0.0).astype(F32)
         acc += use * total[...].astype(F32)
     for b in range(7, -1, -1):
-        rows = slice(b * TOK, (b + 1) * TOK)
+        rows = rows_of(idx, b // 2, jnp.where(ci == b % 2, 0, 1))
         k, v = qkv[rows, HD : 2 * HD], qkv[rows, 2 * HD :]
         later = acc.astype(BF)
         dqkv[rows, :HD] = dq[rows, :]
@@ -149,15 +170,16 @@
         dqkv[rows, 2 * HD :] = (beta * (dv0[rows, :] + dot(k, later))).astype(BF)
         acc += r[b]
     for z in range(NZ):
-        keep[z] = dqkv[pl.ds(pl.multiple_of((2 * z + ci) * TOK, TOK), TOK), :]
-        send[z] = dqkv[pl.ds(pl.multiple_of((2 * z + 1 - ci) * TOK, TOK), TOK), :]
-
-
-def weights(idx, xt, dqkv, *refs):
+        keep[z] = dqkv[rows_of(idx, z, 0), :]
+        send[z] = dqkv[rows_of(idx, z, 1), :]
+
+
+def weights(idx, xta, xtb, dqkv, *refs):
     outs, buf = refs[:4], refs[4]
     xi, yi, ci = idx[0], idx[1], idx[3]
     for m in range(4):
-        tile = dot(xt[m * 512 : (m + 1) * 512, :], dqkv[...]).astype(BF)
+        rows = slice(m * 512, (m + 1) * 512)
+        tile = (dot(xta[rows, :], dqkv[:768, :]) + dot(xtb[rows, :], dqkv[768:, :])).astype(BF)
         buf[m] = tile.reshape(8, NX, 16, 384)
     for s in range(4):
         for j in range(4):
@@ -227,30 +249,35 @@
         pack, [shape((8, 2, HD, HD), BF)], [after(idx, own_w), grad_out[0], saved[0, 0]]
     )
     gs = lax.all_to_all(bundle, "ctx", 0, 0, axis_index_groups=rows_y)
-    w1, w3 = x_hop(own_w, 1), x_hop(own_w, -1)
+    w2, w1, w3 = (x_hop(own_w, s) for s in (2, 1, -1))
     x2a, x2b = ctx_hop(x1[:64], dz=1), ctx_hop(x3[64:], dz=-1)
-    w2a, w2b = x_hop(w1[:256], 1), x_hop(w3[256:], -1)
-    xs, own = [x, x1, x3, x2a, x2b], [own_w, w1, w3, w2a, w2b]
-    mates = [ctx_hop(after(p, gs) if i in (0, 3, 4) else p, dc=1) for i, p in enumerate(xs)]
+    (own_w,) = call(relay, [shape((2048, 384), BF)], [idx, own_w, w1, w3, w2], flops=1 << 33, limit=6)
+    first = [x, x1, x3]
+    first += [ctx_hop(p, dc=1) for p in first]
+    xa, xta = call(
+        stack, [shape((768, 2048), BF), shape((2048, 768), BF)], [idx, *first], flops=1 << 33, limit=10
+    )
+    last = [x2a, x2b]
+    last += [ctx_hop(after(p, gs), dc=1) for p in last]
 
     big = 2 * 1024 * 2048 * 384
-    xcat, qkv, r, total, own_w = call(
+    qkv, r, total, xtb = call(
         project,
         [
-            shape((1024, 2048), BF),
             shape((1024, 384), BF),
             shape((8, HD, HD), F32),
             shape((HD, HD), BF),
-            shape((2048, 384), BF),
+            shape((2048, 256), BF),
         ],
-        [idx, *xs, *mates, *own, gs],
+        [idx, xa, *last, own_w, gs],
+        [pltpu.VMEM((256, 2048), BF)],
         flops=big,
     )
     totals = [ctx_hop(total, dy=s) for s in (1, 2, 3)]
-    dq, dk0, dv0, xt = call(
+    dq, dk0, dv0 = call(
         lambda *refs: within(alpha, beta, *refs),
-        [shape((1024, HD), BF), shape((1024, HD), F32), shape((1024, HD), F32), shape((2048, 1024), BF)],
-        [idx, xcat, gs, qkv],
+        [shape((1024, HD), BF), shape((1024, HD), F32), shape((1024, HD), F32)],
+        [idx, gs, qkv],
         flops=big // 4,
     )
     dqkv, keep, send = call(
@@ -264,7 +291,7 @@
     parts = call(
         weights,
         [shape((4, 8, 16, 384), BF)] * 4,
-        [idx, xt, dqkv],
+        [idx, xta, xtb, dqkv],
         [pltpu.VMEM((NY, 8, NX, 16, 384), BF)],
         flops=big,
     )
@@ -280,7 +307,7 @@
     far_up, far_down = ctx_hop(far_up, dz=1), ctx_hop(far_down, dz=-1)
     parts = call(turn, [shape((8, 16, 384), BF)] * 4, [idx, *parts], deps=(gx,), limit=4)
     up, down = call(
-        merge, [shape((TOK, 2048), BF)] * 2, [idx, up, down, far_up, far_down], deps=(parts[0],), limit=6
+        merge, [shape((TOK, 2048), BF)] * 2, [idx, up, down, far_up, far_down], flops=1 << 33, deps=(parts[0],), limit=6
     )
     parts = [parts[0]] + [plane_hop(parts[s], s, 1) for s in (1, 2, 3)]
     up, down = ctx_hop(up, dz=1), ctx_hop(down, dz=-1)
@@ -290,6 +317,7 @@
         lambda *refs: collect(scale, *refs),
         [shape((16, 3 * heads * HD), F32)],
         [idx, owned],
+        flops=1 << 31,
         limit=4,
     )
     grad_x = (gx + up.astype(F32) + down.astype(F32)).astype(BF)

time: 97.4 us -> 93.2 us (0.957)
  waiting for transfers between devices: 18.3 us -> 3.74 us
  local copies, waits for them, and re-layouts: 4.54 us -> 10.7 us
  blocking collectives: 10.8 us -> 13.8 us
  Pallas kernels: 18.4 us -> 20.8 us
  starting transfers between devices: 43 us -> 41.8 us
    unnamed x6 -> x16, local copies, waits for them, and re-layouts: 1.99 us -> 7.21 us
    ppermute x4 -> x3, waiting for transfers between devices: 4.06 us -> 0.01 us  [x_hop(): return lax.ppermute(block, 'zero', [(i, (i + dx) % NX) for i in range(NX)])]
    ppermute x6, waiting for transfers between devices: 7.46 us -> 3.68 us  [plane_hop(): return lax.ppermute(block, ('ctx', 'zero'), route)]
    ppermute x18, waiting for transfers between devices: 3.62 us -> 0.05 us  [ctx_hop(): return lax.ppermute(block, 'ctx', route)]
    all_to_all x1, waiting for transfers between devices: 3.14 us -> 0.01 us  [body(): gs = lax.all_to_all(bundle, 'ctx', 0, 0, axis_index_groups=rows_y)]
    all_to_all x1, blocking collectives: 10.8 us -> 13.8 us  [body(): owned = lax.all_to_all(owned, 'ctx', 0, 0, axis_index_groups=rows_y)]
    pallas_call x9 -> x11, Pallas kernels: 18.4 us -> 20.8 us  [call(): pl.pallas_call(run, out_shape=list(outs), in_specs=[pl.BlockSpec(memory_s...]
    ppermute x4 -> x3, starting transfers between devices: 5.42 us -> 3.67 us  [x_hop(): return lax.ppermute(block, 'zero', [(i, (i + dx) % NX) for i in range(NX)])]
  transfers between devices with their start and end apart: 29 -> 28, of which waited for: 11 -> 1; matrix products, arithmetic and copies ran while one was open for 3% -> 4% of each run, Pallas kernels for 13% -> 17%
where the time goes in v7:
time: 93.2 us; the launch traced here: 92.7 us
  starting transfers between devices  41.8 us (45%)
  Pallas kernels  20.8 us (22%)
  blocking collectives  13.8 us (15%)
  local copies, waits for them, and re-layouts  10.7 us (11%)
  waiting for transfers between devices  3.74 us (4%)
  other arithmetic  1.16 us (1%)
    ppermute x18, starting transfers between devices, ctx_hop(): return lax.ppermute(block, 'ctx', route)  25 us
    pallas_call x11, Pallas kernels, call(): pl.pallas_call(run, out_shape=list(outs), in_specs=[pl.BlockSpec(memory_s...  20.8 us
    all_to_all x1, blocking collectives, body(): owned = lax.all_to_all(owned, 'ctx', 0, 0, axis_index_groups=rows_y)  13.8 us
    ppermute x6, starting transfers between devices, plane_hop(): return lax.ppermute(block, ('ctx', 'zero'), route)  7.92 us
    unnamed x16, local copies, waits for them, and re-layouts  7.21 us
    all_to_all x1, starting transfers between devices, body(): gs = lax.all_to_all(bundle, 'ctx', 0, 0, axis_index_groups=rows_y)  5.19 us
    ppermute x6, waiting for transfers between devices, plane_hop(): return lax.ppermute(block, ('ctx', 'zero'), route)  3.68 us
    ppermute x3, starting transfers between devices, x_hop(): return lax.ppermute(block, 'zero', [(i, (i + dx) % NX) for i in range(NX)])  3.67 us
  transfers between devices with their start and end apart: 28, of which 1 were waited for; matrix products, arithmetic and copies ran while one was open for 4% of the time, Pallas kernels for 17%

profile of v7, /device:TPU:1, one launch (start us, length us, event | category | flops | bytes accessed | tf_op | source)
XLA Modules:
  0.0 92.7 jit_solution(9459183102305894284)
XLA Ops:
  0.6 2.5 %collective-permute-start = (bf16[128,2048]{1,0:T(8,128)(2,1)}, bf16[128,2048]{1,0:T(8,128)(2,1)S(1)}, u32[]{:S(2)}, u32[]{:S(2)}) collective-permute-start(bf16[128,2048]{1,0:T(8,128)(2,1)} %bitcast.4.refs_1_), channel_id=1, source_target_pairs={{0,8},{4,12},{8,16},{12,20},{16,24},{20,28},{24,0},{28,4},{32,40},... | collective-permute-start | bytes 1572872 | tf_op jit(solution)/shard_map/ppermute | solution.py:24
  3.2 2.2 %collective-permute-start.1 = (bf16[128,2048]{1,0:T(8,128)(2,1)}, bf16[128,2048]{1,0:T(8,128)(2,1)}, u32[]{:S(2)}, u32[]{:S(2)}) collective-permute-start(bf16[128,2048]{1,0:T(8,128)(2,1)} %bitcast.4.refs_1_), channel_id=1, source_target_pairs={{0,24},{4,28},{8,0},{12,4},{16,8},{20,12},{24,16},{28,20},{32,56},... | collective-permute-start | bytes 1572872 | tf_op jit(solution)/shard_map/ppermute | solution.py:24
  5.4 1.1 %constant_dynamic-slice_fusion.2 = (bf16[512,128]{1,0:T(8,128)(2,1)S(1)}, bf16[512,128]{1,0:T(8,128)(2,1)S(1)}, bf16[512,128]{1,0:T(8,128)(2,1)S(1)}) fusion(bf16[512,3072]{1,0:T(8,128)(2,1)} %param.7, s32[]{:T(128)S(6)} %select_n.31, s32[]{:T(128)S(6)} %select_n.33, s32[]{:T(128)S(6)} %select_n.32), kind=kLoop, calls=%fused_computation.6 | loop fusion | bytes 786444 | tf_op jit(solution)/shard_map/dynamic_slice | solution.py:246
  6.5 2.5 %collective-permute-start.10 = (bf16[512,384]{1,0:T(8,128)(2,1)S(1)}, bf16[512,384]{1,0:T(8,128)(2,1)S(1)}, u32[]{:S(2)}, u32[]{:S(2)}) collective-permute-start(bf16[512,384]{1,0:T(8,128)(2,1)S(1)} %pad_maximum_fusion.refs_1_), channel_id=1, source_target_pairs={{0,3},{1,0},{2,1},{3,2},{4,7},{5,4},{6,5},{7,6},{8,11},{9,8},{10,9... | collective-permute-start | bytes 1179656 | tf_op jit(solution)/shard_map/ppermute | solution.py:28
  9.0 0.5 collective-permute-start.11
  9.6 0.6 collective-permute-start.9
  10.3 1.0 %copy-done = f32[1,1,8,128,128]{4,3,2,1,0:T(8,128)S(1)} copy-done((f32[1,1,8,128,128]{4,3,2,1,0:T(8,128)S(1)}, f32[1,1,8,128,128]{4,3,2,1,0:T(8,128)}, u32[]{:S(2)}) %copy-start) | copy-done | bytes 524312
  11.3 0.9 %copy-done.1 = bf16[1,128,1024]{2,1,0:T(8,128)(2,1)S(1)} copy-done((bf16[1,128,1024]{2,1,0:T(8,128)(2,1)S(1)}, bf16[1,128,1024]{2,1,0:T(8,128)(2,1)}, u32[]{:S(2)}) %copy-start.1) | copy-done | bytes 262168
  12.2 1.4 %shard_map.60 = bf16[8,2,128,128]{3,2,1,0:T(8,128)(2,1)} custom-call(s32[4]{0:T(128)S(1)} %pad_add_fusion.refs_0_, bf16[128,1024]{1,0:T(8,128)(2,1)S(1)} %bitcast.10, f32[8,128,128]{2,1,0:T(8,128)S(1)} %bitcast.9), custom_call_target="tpu_custom_call" | custom-call | bytes 1310736 | tf_op jit(solution)/shard_map/pallas_call | solution.py:63
  13.7 5.2 %all-to-all-start = ((bf16[8,2,128,128]{3,2,1,0:T(8,128)(2,1)}), bf16[8,2,128,128]{3,2,1,0:T(8,128)(2,1)S(1)}, u32[]{:S(2)}, u32[]{:S(2)}) async-start(bf16[8,2,128,128]{3,2,1,0:T(8,128)(2,1)} %shard_map.60), calls=%async_computation | async-start | bytes 1048576 | tf_op jit(solution)/shard_map/all_to_all | solution.py:251
  18.9 0.2 collective-permute-start.2
  19.0 0.7 slice.8
  19.8 1.6 %collective-permute-start.5 = (bf16[64,2048]{1,0:T(8,128)(2,1)}, bf16[64,2048]{1,0:T(8,128)(2,1)S(1)}, u32[]{:S(2)}, u32[]{:S(2)}) collective-permute-start(bf16[64,2048]{1,0:T(8,128)(2,1)} %slice.8), channel_id=1, source_target_pairs={{0,8},{4,12},{8,16},{12,20},{16,24},{20,28},{24,0},{28,4},{32,40},... | collective-permute-start | bytes 786440 | tf_op jit(solution)/shard_map/ppermute | solution.py:24
  21.3 1.7 %slice.9 = bf16[64,2048]{1,0:T(8,128)(2,1)} slice(bf16[128,2048]{1,0:T(8,128)(2,1)} %collective-permute-done.1.refs_3_), slice={[64:128], [0:2048]} | slice | bytes 524288 | tf_op jit(solution)/shard_map/slice | solution.py:253
  23.0 0.8 copy-done.2
  23.8 1.2 %collective-permute-start.6 = (bf16[64,2048]{1,0:T(8,128)(2,1)}, bf16[64,2048]{1,0:T(8,128)(2,1)S(1)}, u32[]{:S(2)}, u32[]{:S(2)}) collective-permute-start(bf16[64,2048]{1,0:T(8,128)(2,1)} %slice.9), channel_id=1, source_target_pairs={{0,24},{4,28},{8,0},{12,4},{16,8},{20,12},{24,16},{28,20},{32,56},... | collective-permute-start | bytes 786440 | tf_op jit(solution)/shard_map/ppermute | solution.py:24
  25.0 0.7 copy-done.4
  25.7 4.3 %collective-permute-start.3 = (bf16[128,2048]{1,0:T(8,128)(2,1)S(1)}, bf16[128,2048]{1,0:T(8,128)(2,1)}, u32[]{:S(2)}, u32[]{:S(2)}) collective-permute-start(bf16[128,2048]{1,0:T(8,128)(2,1)S(1)} %collective-permute-done.refs_2_), channel_id=1, source_target_pairs={{0,4},{4,0},{8,12},{12,8},{16,20},{20,16},{24,28},{28,24},{32,36},... | collective-permute-start | bytes 1572872 | tf_op jit(solution)/shard_map/ppermute | solution.py:24
  30.0 0.7 copy-done.6
  30.7 0.5 collective-permute-start.4
  31.2 1.0 %copy-done.3 = bf16[512,384]{1,0:T(8,128)(2,1)S(1)} copy-done((bf16[512,384]{1,0:T(8,128)(2,1)S(1)}, bf16[512,384]{1,0:T(8,128)(2,1)}, u32[]{:S(2)}) %copy-start.3) | copy-done | bytes 393240
  32.2 1.0 %copy-done.5 = bf16[512,384]{1,0:T(8,128)(2,1)S(1)} copy-done((bf16[512,384]{1,0:T(8,128)(2,1)S(1)}, bf16[512,384]{1,0:T(8,128)(2,1)}, u32[]{:S(2)}) %copy-start.5) | copy-done | bytes 393240
  33.2 1.0 %copy-done.7 = bf16[512,384]{1,0:T(8,128)(2,1)S(1)} copy-done((bf16[512,384]{1,0:T(8,128)(2,1)S(1)}, bf16[512,384]{1,0:T(8,128)(2,1)}, u32[]{:S(2)}) %copy-start.7) | copy-done | bytes 393240
  34.2 0.7 shard_map.61.refs_6_.refs_3_
  35.0 0.5 collective-permute-start.8
  35.5 2.7 %shard_map.59 = (bf16[768,2048]{1,0:T(8,128)(2,1)S(1)}, bf16[2048,768]{1,0:T(8,128)(2,1)S(1)}) custom-call(s32[4]{0:T(128)S(1)} %pad_add_fusion.refs_0_, bf16[128,2048]{1,0:T(8,128)(2,1)} %bitcast.4.refs_1_, bf16[128,2048]{1,0:T(8,128)(2,1)S(1)} %collective-permute-done.refs_2_, bf16[128,2048]{1,0:T(8,128)(2,1)} %collective-permute-done.1.refs_3_, ...), custom_call_target="tpu_custom_call" | custom-call | flops 8589934592 | bytes 9437200 | tf_op jit(solution)/shard_map/pallas_call | solution.py:63
  38.3 3.6 %shard_map.62 = (bf16[1024,384]{1,0:T(8,128)(2,1)S(1)}, f32[8,128,128]{2,1,0:T(8,128)S(1)}, bf16[128,128]{1,0:T(8,128)(2,1)S(1)}, bf16[2048,256]{1,0:T(8,128)(2,1)S(1)}) custom-call(s32[4]{0:T(128)S(1)} %pad_add_fusion.refs_0_, bf16[768,2048]{1,0:T(8,128)(2,1)S(1)} %get-tuple-element.33.refs_1_, bf16[64,2048]{1,0:T(8,128)(2,1)S(1)} %collective-permute-done.5.refs_2_, ...), custom_call_target="tpu_custom_call" | custom-call | flops 1610612736 | bytes 8683536 | tf_op jit(solution)/shard_map/pallas_call | solution.py:63
  41.9 1.4 %collective-permute-start.12 = (bf16[128,128]{1,0:T(8,128)(2,1)S(1)}, bf16[128,128]{1,0:T(8,128)(2,1)S(1)}, u32[]{:S(2)}, u32[]{:S(2)}) collective-permute-start(bf16[128,128]{1,0:T(8,128)(2,1)S(1)} %get-tuple-element.42), channel_id=1, source_target_pairs={{0,32},{4,36},{8,40},{12,44},{16,48},{20,52},{24,56},{28,60},{32,6... | collective-permute-start | bytes 98312 | tf_op jit(solution)/shard_map/ppermute | solution.py:24
  43.3 2.6 %collective-permute-start.13 = (bf16[128,128]{1,0:T(8,128)(2,1)S(1)}, bf16[128,128]{1,0:T(8,128)(2,1)S(1)}, u32[]{:S(2)}, u32[]{:S(2)}) collective-permute-start(bf16[128,128]{1,0:T(8,128)(2,1)S(1)} %get-tuple-element.42), channel_id=1, source_target_pairs={{0,64},{4,68},{8,72},{12,76},{16,80},{20,84},{24,88},{28,92},{32,9... | collective-permute-start | bytes 98312 | tf_op jit(solution)/shard_map/ppermute | solution.py:24
  45.9 1.1 %collective-permute-start.14 = (bf16[128,128]{1,0:T(8,128)(2,1)S(1)}, bf16[128,128]{1,0:T(8,128)(2,1)S(1)}, u32[]{:S(2)}, u32[]{:S(2)}) collective-permute-start(bf16[128,128]{1,0:T(8,128)(2,1)S(1)} %get-tuple-element.42), channel_id=1, source_target_pairs={{0,96},{4,100},{8,104},{12,108},{16,112},{20,116},{24,120},{28,124... | collective-permute-start | bytes 98312 | tf_op jit(solution)/shard_map/ppermute | solution.py:24
  47.0 2.4 %shard_map.63 = (bf16[1024,128]{1,0:T(8,128)(2,1)S(1)}, f32[1024,128]{1,0:T(8,128)S(1)}, f32[1024,128]{1,0:T(8,128)S(1)}) custom-call(s32[4]{0:T(128)S(1)} %pad_add_fusion.refs_0_, bf16[8,2,128,128]{3,2,1,0:T(8,128)(2,1)S(1)} %all-to-all-done.refs_7_.refs_1_, bf16[1024,384]{1,0:T(8,128)(2,1)S(1)} %get-tuple-element.37.refs_2_.refs_1_), custom_call_target="tpu_custom_call" | custom-call | flops 402653184 | bytes 2621456 | tf_op jit(solution)/shard_map/pallas_call | solution.py:63
  49.4 1.0 %shard_map.64 = (bf16[1024,384]{1,0:T(8,128)(2,1)S(1)}, bf16[4,128,384]{2,1,0:T(8,128)(2,1)S(1)}, bf16[4,128,384]{2,1,0:T(8,128)(2,1)S(1)}) custom-call(s32[4]{0:T(128)S(1)} %pad_add_fusion.refs_0_, bf16[1024,384]{1,0:T(8,128)(2,1)S(1)} %get-tuple-element.37.refs_2_.refs_1_, bf16[1024,128]{1,0:T(8,128)(2,1)S(1)} %get-tuple-element.38.refs_2_, ...), custom_call_target="tpu_custom_call" | custom-call | flops 100663296 | bytes 4292624 | tf_op jit(solution)/shard_map/pallas_call | solution.py:63
  50.4 1.1 %collective-permute-start.16 = (bf16[2048,384]{1,0:T(8,128)(2,1)S(1)}, bf16[2048,384]{1,0:T(8,128)(2,1)S(1)}, u32[]{:S(2)}, u32[]{:S(2)}) collective-permute-start(bf16[2048,384]{1,0:T(8,128)(2,1)S(1)} %shard_map.61.refs_6_.refs_3_), channel_id=1, source_target_pairs={{0,4},{4,0},{8,12},{12,8},{16,20},{20,16},{24,28},{28,24},{32,36},... | collective-permute-start | bytes 4718600 | tf_op jit(solution)/shard_map/ppermute | solution.py:24
  51.5 0.3 collective-permute-start.15
  51.8 3.0 %shard_map.65 = (bf16[4,8,16,384]{3,2,1,0:T(8,128)(2,1)S(1)}, bf16[4,8,16,384]{3,2,1,0:T(8,128)(2,1)S(1)}, bf16[4,8,16,384]{3,2,1,0:T(8,128)(2,1)S(1)}, bf16[4,8,16,384]{3,2,1,0:T(8,128)(2,1)S(1)}) custom-call(s32[4]{0:T(128)S(1)} %pad_add_fusion.refs_0_, bf16[2048,768]{1,0:T(8,128)(2,1)S(1)} %get-tuple-element.46.refs_1_, ...), custom_call_target="tpu_custom_call" | custom-call | flops 1610612736 | bytes 6553616 | tf_op jit(solution)/shard_map/pallas_call | solution.py:63
  54.8 0.4 collective-permute-start.19
  55.2 3.2 %collective-permute-start.20 = (bf16[4,8,16,384]{3,2,1,0:T(8,128)(2,1)S(1)}, bf16[4,8,16,384]{3,2,1,0:T(8,128)(2,1)S(1)}, u32[]{:S(2)}, u32[]{:S(2)}) collective-permute-start(bf16[4,8,16,384]{3,2,1,0:T(8,128)(2,1)S(1)} %get-tuple-element.56), channel_id=1, source_target_pairs={{0,2},{1,3},{2,0},{3,1},{4,68},{5,69},{6,70},{7,71},{8,10},{9,11},... | collective-permute-start | bytes 1179656 | tf_op jit(solution)/shard_map/ppermute | solution.py:40
  58.4 3.2 %shard_map.66 = (f32[128,2048]{1,0:T(8,128)S(1)}, bf16[128,2048]{1,0:T(8,128)(2,1)S(1)}, bf16[128,2048]{1,0:T(8,128)(2,1)S(1)}, bf16[64,2048]{1,0:T(8,128)(2,1)S(1)}, bf16[64,2048]{1,0:T(8,128)(2,1)S(1)}) custom-call(s32[4]{0:T(128)S(1)} %pad_add_fusion.refs_0_, bf16[4,128,384]{2,1,0:T(8,128)(2,1)S(1)} %get-tuple-element.43.refs_1_, ...), custom_call_target="tpu_custom_call" | custom-call | flops 1610612736 | bytes 6553616 | tf_op jit(solution)/shard_map/pallas_call | solution.py:63
  61.7 2.7 %collective-permute-start.18 = (bf16[64,2048]{1,0:T(8,128)(2,1)S(1)}, bf16[64,2048]{1,0:T(8,128)(2,1)S(1)}, u32[]{:S(2)}, u32[]{:S(2)}) collective-permute-start(bf16[64,2048]{1,0:T(8,128)(2,1)S(1)} %get-tuple-element.54), channel_id=1, source_target_pairs={{0,24},{4,28},{8,0},{12,4},{16,8},{20,12},{24,16},{28,20},{32,56},... | collective-permute-start | bytes 786440 | tf_op jit(solution)/shard_map/ppermute | solution.py:24
  64.4 3.7 %collective-permute-done.20.refs_3_ = bf16[4,8,16,384]{3,2,1,0:T(8,128)(2,1)S(1)} collective-permute-done((bf16[4,8,16,384]{3,2,1,0:T(8,128)(2,1)S(1)}, bf16[4,8,16,384]{3,2,1,0:T(8,128)(2,1)S(1)}, u32[]{:S(2)}, u32[]{:S(2)}) %collective-permute-start.20) | collective-permute-done | bytes 393248 | tf_op jit(solution)/shard_map/ppermute | solution.py:40
  68.0 0.7 shard_map.67
  68.8 0.9 collective-permute-start.24
  69.7 3.5 %collective-permute-start.25 = (bf16[8,16,384]{2,1,0:T(8,128)(2,1)S(1)}, bf16[8,16,384]{2,1,0:T(8,128)(2,1)S(1)}, u32[]{:S(2)}, u32[]{:S(2)}) collective-permute-start(bf16[8,16,384]{2,1,0:T(8,128)(2,1)S(1)} %get-tuple-element.62), channel_id=1, source_target_pairs={{0,64},{1,65},{2,66},{3,67},{4,6},{5,7},{6,4},{7,5},{8,72},{9,73},... | collective-permute-start | bytes 294920 | tf_op jit(solution)/shard_map/ppermute | solution.py:40
  73.2 0.7 shard_map.68
  74.0 2.6 %collective-permute-start.23 = (bf16[128,2048]{1,0:T(8,128)(2,1)S(1)}, bf16[128,2048]{1,0:T(8,128)(2,1)S(1)}, u32[]{:S(2)}, u32[]{:S(2)}) collective-permute-start(bf16[128,2048]{1,0:T(8,128)(2,1)S(1)} %get-tuple-element.60), channel_id=1, source_target_pairs={{0,24},{4,28},{8,0},{12,4},{16,8},{20,12},{24,16},{28,20},{32,56},... | collective-permute-start | bytes 1572872 | tf_op jit(solution)/shard_map/ppermute | solution.py:24
  76.7 13.8 %all_to_all.10.refs_1_ = f32[8,16,384]{2,1,0:T(8,128)S(1)} all-to-all(f32[8,16,384]{2,1,0:T(8,128)S(1)} %convert_add_fusion), channel_id=1, replica_groups={{0,4,8,12,16,20,24,28},{32,36,40,44,48,52,56,60},{64,68,72,76,80,84,88,..., dimensions={0} | all-to-all | bytes 393216 | tf_op jit(solution)/shard_map/all_to_all | solution.py:315
  90.5 1.2 %shard_map.69 = f32[16,3072]{1,0:T(8,128)} custom-call(s32[4]{0:T(128)S(1)} %pad_add_fusion.refs_0_, f32[8,16,384]{2,1,0:T(8,128)S(1)} %all_to_all.10.refs_1_), custom_call_target="tpu_custom_call" | custom-call | flops 2147483648 | bytes 393232 | tf_op jit(solution)/shard_map/pallas_call | solution.py:63
  91.7 1.0 %fusion = bf16[1,128,2048]{2,1,0:T(8,128)(2,1)} fusion(bf16[128,2048]{1,0:T(8,128)(2,1)S(1)} %collective-permute-done.23, f32[128,2048]{1,0:T(8,128)S(1)} %get-tuple-element.50.refs_5_, bf16[128,2048]{1,0:T(8,128)(2,1)S(1)} %collective-permute-done.22), kind=kLoop, calls=%fused_computation.1 | loop fusion | flops 1310720 | bytes 2621440 | tf_op jit(solution)/shard_map/broadcast_in_dim | solution.py:324
  (43 shorter events, 0.6 us)
Async XLA Ops:
  0.6 18.2 %collective-permute-start = (bf16[128,2048]{1,0:T(8,128)(2,1)}, bf16[128,2048]{1,0:T(8,128)(2,1)S(1)}, u32[]{:S(2)}, u32[]{:S(2)}) collective-permute-start(bf16[128,2048]{1,0:T(8,128)(2,1)} %bitcast.4.refs_1_), channel_id=1, source_target_pairs={{0,8},{4,12},{8,16},{12,20},{16,24},{20,28},{24,0},{28,4},{32,40},... | collective-permute-start | bytes 1572872 | tf_op jit(solution)/shard_map/ppermute | solution.py:24
  3.2 16.6 %collective-permute-start.1 = (bf16[128,2048]{1,0:T(8,128)(2,1)}, bf16[128,2048]{1,0:T(8,128)(2,1)}, u32[]{:S(2)}, u32[]{:S(2)}) collective-permute-start(bf16[128,2048]{1,0:T(8,128)(2,1)} %bitcast.4.refs_1_), channel_id=1, source_target_pairs={{0,24},{4,28},{8,0},{12,4},{16,8},{20,12},{24,16},{28,20},{32,56},... | collective-permute-start | bytes 1572872 | tf_op jit(solution)/shard_map/ppermute | solution.py:24
  6.5 16.5 %collective-permute-start.10 = (bf16[512,384]{1,0:T(8,128)(2,1)S(1)}, bf16[512,384]{1,0:T(8,128)(2,1)S(1)}, u32[]{:S(2)}, u32[]{:S(2)}) collective-permute-start(bf16[512,384]{1,0:T(8,128)(2,1)S(1)} %pad_maximum_fusion.refs_1_), channel_id=1, source_target_pairs={{0,3},{1,0},{2,1},{3,2},{4,7},{5,4},{6,5},{7,6},{8,11},{9,8},{10,9... | collective-permute-start | bytes 1179656 | tf_op jit(solution)/shard_map/ppermute | solution.py:28
  9.0 16.0 %collective-permute-start.11 = (bf16[512,384]{1,0:T(8,128)(2,1)S(1)}, bf16[512,384]{1,0:T(8,128)(2,1)S(1)}, u32[]{:S(2)}, u32[]{:S(2)}) collective-permute-start(bf16[512,384]{1,0:T(8,128)(2,1)S(1)} %pad_maximum_fusion.refs_1_), channel_id=1, source_target_pairs={{0,2},{1,3},{2,0},{3,1},{4,6},{5,7},{6,4},{7,5},{8,10},{9,11},{10,... | collective-permute-start | bytes 1179656 | tf_op jit(solution)/shard_map/ppermute | solution.py:28
  9.6 20.4 %collective-permute-start.9 = (bf16[512,384]{1,0:T(8,128)(2,1)S(1)}, bf16[512,384]{1,0:T(8,128)(2,1)S(1)}, u32[]{:S(2)}, u32[]{:S(2)}) collective-permute-start(bf16[512,384]{1,0:T(8,128)(2,1)S(1)} %pad_maximum_fusion.refs_1_), channel_id=1, source_target_pairs={{0,1},{1,2},{2,3},{3,0},{4,5},{5,6},{6,7},{7,4},{8,9},{9,10},{10,1... | collective-permute-start | bytes 1179656 | tf_op jit(solution)/shard_map/ppermute | solution.py:28
  10.2 1.0 %copy-start = (f32[1,1,8,128,128]{4,3,2,1,0:T(8,128)S(1)}, f32[1,1,8,128,128]{4,3,2,1,0:T(8,128)}, u32[]{:S(2)}) copy-start(f32[1,1,8,128,128]{4,3,2,1,0:T(8,128)} %param.6) | copy-start | bytes 1572868
  11.3 0.9 %copy-start.1 = (bf16[1,128,1024]{2,1,0:T(8,128)(2,1)S(1)}, bf16[1,128,1024]{2,1,0:T(8,128)(2,1)}, u32[]{:S(2)}) copy-start(bf16[1,128,1024]{2,1,0:T(8,128)(2,1)} %param.5) | copy-start | bytes 786436
  13.7 21.3 %all-to-all-start = ((bf16[8,2,128,128]{3,2,1,0:T(8,128)(2,1)}), bf16[8,2,128,128]{3,2,1,0:T(8,128)(2,1)S(1)}, u32[]{:S(2)}, u32[]{:S(2)}) async-start(bf16[8,2,128,128]{3,2,1,0:T(8,128)(2,1)} %shard_map.60), calls=%async_computation | async-start | bytes 1048576 | tf_op jit(solution)/shard_map/all_to_all | solution.py:251
  18.9 16.7 %collective-permute-start.2 = (bf16[128,2048]{1,0:T(8,128)(2,1)}, bf16[128,2048]{1,0:T(8,128)(2,1)}, u32[]{:S(2)}, u32[]{:S(2)}) collective-permute-start(bf16[128,2048]{1,0:T(8,128)(2,1)} %bitcast.4.refs_1_), channel_id=1, source_target_pairs={{0,4},{4,0},{8,12},{12,8},{16,20},{20,16},{24,28},{28,24},{32,36},... | collective-permute-start | bytes 1572872 | tf_op jit(solution)/shard_map/ppermute | solution.py:24
  19.8 15.2 %collective-permute-start.5 = (bf16[64,2048]{1,0:T(8,128)(2,1)}, bf16[64,2048]{1,0:T(8,128)(2,1)S(1)}, u32[]{:S(2)}, u32[]{:S(2)}) collective-permute-start(bf16[64,2048]{1,0:T(8,128)(2,1)} %slice.8), channel_id=1, source_target_pairs={{0,8},{4,12},{8,16},{12,20},{16,24},{20,28},{24,0},{28,4},{32,40},... | collective-permute-start | bytes 786440 | tf_op jit(solution)/shard_map/ppermute | solution.py:24
  23.0 0.8 copy-start.2
  23.8 11.3 %collective-permute-start.6 = (bf16[64,2048]{1,0:T(8,128)(2,1)}, bf16[64,2048]{1,0:T(8,128)(2,1)S(1)}, u32[]{:S(2)}, u32[]{:S(2)}) collective-permute-start(bf16[64,2048]{1,0:T(8,128)(2,1)} %slice.9), channel_id=1, source_target_pairs={{0,24},{4,28},{8,0},{12,4},{16,8},{20,12},{24,16},{28,20},{32,56},... | collective-permute-start | bytes 786440 | tf_op jit(solution)/shard_map/ppermute | solution.py:24
  25.0 0.7 copy-start.4
  25.7 9.8 %collective-permute-start.3 = (bf16[128,2048]{1,0:T(8,128)(2,1)S(1)}, bf16[128,2048]{1,0:T(8,128)(2,1)}, u32[]{:S(2)}, u32[]{:S(2)}) collective-permute-start(bf16[128,2048]{1,0:T(8,128)(2,1)S(1)} %collective-permute-done.refs_2_), channel_id=1, source_target_pairs={{0,4},{4,0},{8,12},{12,8},{16,20},{20,16},{24,28},{28,24},{32,36},... | collective-permute-start | bytes 1572872 | tf_op jit(solution)/shard_map/ppermute | solution.py:24
  30.0 0.7 copy-start.6
  30.7 4.8 %collective-permute-start.4 = (bf16[128,2048]{1,0:T(8,128)(2,1)}, bf16[128,2048]{1,0:T(8,128)(2,1)}, u32[]{:S(2)}, u32[]{:S(2)}) collective-permute-start(bf16[128,2048]{1,0:T(8,128)(2,1)} %collective-permute-done.1.refs_3_), channel_id=1, source_target_pairs={{0,4},{4,0},{8,12},{12,8},{16,20},{20,16},{24,28},{28,24},{32,36},... | collective-permute-start | bytes 1572872 | tf_op jit(solution)/shard_map/ppermute | solution.py:24
  31.2 1.0 %copy-start.3 = (bf16[512,384]{1,0:T(8,128)(2,1)S(1)}, bf16[512,384]{1,0:T(8,128)(2,1)}, u32[]{:S(2)}) copy-start(bf16[512,384]{1,0:T(8,128)(2,1)} %copy-done.2) | copy-start | bytes 1179652
  32.2 1.0 %copy-start.5 = (bf16[512,384]{1,0:T(8,128)(2,1)S(1)}, bf16[512,384]{1,0:T(8,128)(2,1)}, u32[]{:S(2)}) copy-start(bf16[512,384]{1,0:T(8,128)(2,1)} %copy-done.4) | copy-start | bytes 1179652
  33.2 1.0 %copy-start.7 = (bf16[512,384]{1,0:T(8,128)(2,1)S(1)}, bf16[512,384]{1,0:T(8,128)(2,1)}, u32[]{:S(2)}) copy-start(bf16[512,384]{1,0:T(8,128)(2,1)} %copy-done.6) | copy-start | bytes 1179652
  34.9 3.3 %collective-permute-start.7 = (bf16[64,2048]{1,0:T(8,128)(2,1)S(1)}, bf16[64,2048]{1,0:T(8,128)(2,1)S(1)}, u32[]{:S(2)}, u32[]{:S(2)}) collective-permute-start(bf16[64,2048]{1,0:T(8,128)(2,1)S(1)} %collective-permute-done.5.refs_2_), channel_id=1, source_target_pairs={{0,4},{4,0},{8,12},{12,8},{16,20},{20,16},{24,28},{28,24},{32,36},... | collective-permute-start | bytes 786440 | tf_op jit(solution)/shard_map/ppermute | solution.py:24
  35.0 3.2 %collective-permute-start.8 = (bf16[64,2048]{1,0:T(8,128)(2,1)S(1)}, bf16[64,2048]{1,0:T(8,128)(2,1)S(1)}, u32[]{:S(2)}, u32[]{:S(2)}) collective-permute-start(bf16[64,2048]{1,0:T(8,128)(2,1)S(1)} %collective-permute-done.6.refs_3_), channel_id=1, source_target_pairs={{0,4},{4,0},{8,12},{12,8},{16,20},{20,16},{24,28},{28,24},{32,36},... | collective-permute-start | bytes 786440 | tf_op jit(solution)/shard_map/ppermute | solution.py:24
  41.9 7.5 %collective-permute-start.12 = (bf16[128,128]{1,0:T(8,128)(2,1)S(1)}, bf16[128,128]{1,0:T(8,128)(2,1)S(1)}, u32[]{:S(2)}, u32[]{:S(2)}) collective-permute-start(bf16[128,128]{1,0:T(8,128)(2,1)S(1)} %get-tuple-element.42), channel_id=1, source_target_pairs={{0,32},{4,36},{8,40},{12,44},{16,48},{20,52},{24,56},{28,60},{32,6... | collective-permute-start | bytes 98312 | tf_op jit(solution)/shard_map/ppermute | solution.py:24
  43.3 6.1 %collective-permute-start.13 = (bf16[128,128]{1,0:T(8,128)(2,1)S(1)}, bf16[128,128]{1,0:T(8,128)(2,1)S(1)}, u32[]{:S(2)}, u32[]{:S(2)}) collective-permute-start(bf16[128,128]{1,0:T(8,128)(2,1)S(1)} %get-tuple-element.42), channel_id=1, source_target_pairs={{0,64},{4,68},{8,72},{12,76},{16,80},{20,84},{24,88},{28,92},{32,9... | collective-permute-start | bytes 98312 | tf_op jit(solution)/shard_map/ppermute | solution.py:24
  45.9 3.5 %collective-permute-start.14 = (bf16[128,128]{1,0:T(8,128)(2,1)S(1)}, bf16[128,128]{1,0:T(8,128)(2,1)S(1)}, u32[]{:S(2)}, u32[]{:S(2)}) collective-permute-start(bf16[128,128]{1,0:T(8,128)(2,1)S(1)} %get-tuple-element.42), channel_id=1, source_target_pairs={{0,96},{4,100},{8,104},{12,108},{16,112},{20,116},{24,120},{28,124... | collective-permute-start | bytes 98312 | tf_op jit(solution)/shard_map/ppermute | solution.py:24
  50.4 7.9 %collective-permute-start.16 = (bf16[2048,384]{1,0:T(8,128)(2,1)S(1)}, bf16[2048,384]{1,0:T(8,128)(2,1)S(1)}, u32[]{:S(2)}, u32[]{:S(2)}) collective-permute-start(bf16[2048,384]{1,0:T(8,128)(2,1)S(1)} %shard_map.61.refs_6_.refs_3_), channel_id=1, source_target_pairs={{0,4},{4,0},{8,12},{12,8},{16,20},{20,16},{24,28},{28,24},{32,36},... | collective-permute-start | bytes 4718600 | tf_op jit(solution)/shard_map/ppermute | solution.py:24
  51.5 6.8 %collective-permute-start.15 = (bf16[4,128,384]{2,1,0:T(8,128)(2,1)S(1)}, bf16[4,128,384]{2,1,0:T(8,128)(2,1)S(1)}, u32[]{:S(2)}, u32[]{:S(2)}) collective-permute-start(bf16[4,128,384]{2,1,0:T(8,128)(2,1)S(1)} %get-tuple-element.44), channel_id=1, source_target_pairs={{0,4},{4,0},{8,12},{12,8},{16,20},{20,16},{24,28},{28,24},{32,36},... | collective-permute-start | bytes 1179656 | tf_op jit(solution)/shard_map/ppermute | solution.py:24
  54.8 9.5 %collective-permute-start.19 = (bf16[4,8,16,384]{3,2,1,0:T(8,128)(2,1)S(1)}, bf16[4,8,16,384]{3,2,1,0:T(8,128)(2,1)S(1)}, u32[]{:S(2)}, u32[]{:S(2)}) collective-permute-start(bf16[4,8,16,384]{3,2,1,0:T(8,128)(2,1)S(1)} %get-tuple-element.55), channel_id=1, source_target_pairs={{0,1},{1,2},{2,3},{3,0},{4,36},{5,37},{6,38},{7,39},{8,9},{9,10},{... | collective-permute-start | bytes 1179656 | tf_op jit(solution)/shard_map/ppermute | solution.py:40
  55.2 12.8 %collective-permute-start.20 = (bf16[4,8,16,384]{3,2,1,0:T(8,128)(2,1)S(1)}, bf16[4,8,16,384]{3,2,1,0:T(8,128)(2,1)S(1)}, u32[]{:S(2)}, u32[]{:S(2)}) collective-permute-start(bf16[4,8,16,384]{3,2,1,0:T(8,128)(2,1)S(1)} %get-tuple-element.56), channel_id=1, source_target_pairs={{0,2},{1,3},{2,0},{3,1},{4,68},{5,69},{6,70},{7,71},{8,10},{9,11},... | collective-permute-start | bytes 1179656 | tf_op jit(solution)/shard_map/ppermute | solution.py:40
  58.4 9.7 %collective-permute-start.21 = (bf16[4,8,16,384]{3,2,1,0:T(8,128)(2,1)S(1)}, bf16[4,8,16,384]{3,2,1,0:T(8,128)(2,1)S(1)}, u32[]{:S(2)}, u32[]{:S(2)}) collective-permute-start(bf16[4,8,16,384]{3,2,1,0:T(8,128)(2,1)S(1)} %get-tuple-element.57), channel_id=1, source_target_pairs={{0,3},{1,0},{2,1},{3,2},{4,100},{5,101},{6,102},{7,103},{8,11},{9,... | collective-permute-start | bytes 1179656 | tf_op jit(solution)/shard_map/ppermute | solution.py:40
  61.6 11.5 %collective-permute-start.17 = (bf16[64,2048]{1,0:T(8,128)(2,1)S(1)}, bf16[64,2048]{1,0:T(8,128)(2,1)S(1)}, u32[]{:S(2)}, u32[]{:S(2)}) collective-permute-start(bf16[64,2048]{1,0:T(8,128)(2,1)S(1)} %get-tuple-element.53), channel_id=1, source_target_pairs={{0,8},{4,12},{8,16},{12,20},{16,24},{20,28},{24,0},{28,4},{32,40},... | collective-permute-start | bytes 786440 | tf_op jit(solution)/shard_map/ppermute | solution.py:24
  61.7 11.5 %collective-permute-start.18 = (bf16[64,2048]{1,0:T(8,128)(2,1)S(1)}, bf16[64,2048]{1,0:T(8,128)(2,1)S(1)}, u32[]{:S(2)}, u32[]{:S(2)}) collective-permute-start(bf16[64,2048]{1,0:T(8,128)(2,1)S(1)} %get-tuple-element.54), channel_id=1, source_target_pairs={{0,24},{4,28},{8,0},{12,4},{16,8},{20,12},{24,16},{28,20},{32,56},... | collective-permute-start | bytes 786440 | tf_op jit(solution)/shard_map/ppermute | solution.py:24
  68.8 7.8 %collective-permute-start.24 = (bf16[8,16,384]{2,1,0:T(8,128)(2,1)S(1)}, bf16[8,16,384]{2,1,0:T(8,128)(2,1)S(1)}, u32[]{:S(2)}, u32[]{:S(2)}) collective-permute-start(bf16[8,16,384]{2,1,0:T(8,128)(2,1)S(1)} %get-tuple-element.61), channel_id=1, source_target_pairs={{0,32},{1,33},{2,34},{3,35},{4,5},{5,6},{6,7},{7,4},{8,40},{9,41},... | collective-permute-start | bytes 294920 | tf_op jit(solution)/shard_map/ppermute | solution.py:40
  69.7 7.0 %collective-permute-start.25 = (bf16[8,16,384]{2,1,0:T(8,128)(2,1)S(1)}, bf16[8,16,384]{2,1,0:T(8,128)(2,1)S(1)}, u32[]{:S(2)}, u32[]{:S(2)}) collective-permute-start(bf16[8,16,384]{2,1,0:T(8,128)(2,1)S(1)} %get-tuple-element.62), channel_id=1, source_target_pairs={{0,64},{1,65},{2,66},{3,67},{4,6},{5,7},{6,4},{7,5},{8,72},{9,73},... | collective-permute-start | bytes 294920 | tf_op jit(solution)/shard_map/ppermute | solution.py:40
  73.2 3.5 %collective-permute-start.26 = (bf16[8,16,384]{2,1,0:T(8,128)(2,1)S(1)}, bf16[8,16,384]{2,1,0:T(8,128)(2,1)S(1)}, u32[]{:S(2)}, u32[]{:S(2)}) collective-permute-start(bf16[8,16,384]{2,1,0:T(8,128)(2,1)S(1)} %get-tuple-element.63), channel_id=1, source_target_pairs={{0,96},{1,97},{2,98},{3,99},{4,7},{5,4},{6,5},{7,6},{8,104},{9,105... | collective-permute-start | bytes 294920 | tf_op jit(solution)/shard_map/ppermute | solution.py:40
  73.9 17.9 %collective-permute-start.22 = (bf16[128,2048]{1,0:T(8,128)(2,1)S(1)}, bf16[128,2048]{1,0:T(8,128)(2,1)S(1)}, u32[]{:S(2)}, u32[]{:S(2)}) collective-permute-start(bf16[128,2048]{1,0:T(8,128)(2,1)S(1)} %get-tuple-element.59), channel_id=1, source_target_pairs={{0,8},{4,12},{8,16},{12,20},{16,24},{20,28},{24,0},{28,4},{32,40},... | collective-permute-start | bytes 1572872 | tf_op jit(solution)/shard_map/ppermute | solution.py:24
  74.0 17.7 %collective-permute-start.23 = (bf16[128,2048]{1,0:T(8,128)(2,1)S(1)}, bf16[128,2048]{1,0:T(8,128)(2,1)S(1)}, u32[]{:S(2)}, u32[]{:S(2)}) collective-permute-start(bf16[128,2048]{1,0:T(8,128)(2,1)S(1)} %get-tuple-element.60), channel_id=1, source_target_pairs={{0,24},{4,28},{8,0},{12,4},{16,8},{20,12},{24,16},{28,20},{32,56},... | collective-permute-start | bytes 1572872 | tf_op jit(solution)/shard_map/ppermute | solution.py:24

commit v8 on v7

--- a/solution.py
+++ b/solution.py
@@ -114,13 +114,12 @@
 
 
 def stack(idx, *refs):
-    parts, xa, xta = refs[:6], refs[6], refs[7]
+    parts, xa = refs[:6], refs[6]
     for i, part in enumerate(parts):
         xa[i * TOK : (i + 1) * TOK, :] = part[...]
-        xta[:, i * TOK : (i + 1) * TOK] = part[...].T
-
-
-def project(idx, xa, x2a, x2b, m2a, m2b, wkeep, gs, qkv, r, total, xtb, xb):
+
+
+def project(idx, xa, x2a, x2b, m2a, m2b, wkeep, gs, qkv, r, total, xb):
     for i, part in enumerate((x2a, x2b, m2a, m2b)):
         xb[i * 64 : (i + 1) * 64, :] = part[...]
     whole = jnp.zeros((HD, HD), F32)
@@ -135,11 +134,9 @@
             r[block] = piece
             whole += piece
     total[...] = whole.astype(BF)
-    for i in range(2):
-        xtb[:, i * TOK : (i + 1) * TOK] = xb[i * TOK : (i + 1) * TOK, :].T
-
-
-def within(alpha, beta, idx, gs, qkv, dq, dk0, dv0):
+
+
+def within(alpha, beta, idx, xa, xb, gs, qkv, dq, dk0, dv0, xt):
     rowi = lax.broadcasted_iota(jnp.int32, (TOK, TOK), 0)
     coli = lax.broadcasted_iota(jnp.int32, (TOK, TOK), 1)
     mask = rowi >= coli
@@ -153,6 +150,7 @@
         dq[rows, :] = (alpha * dot_nt(g, state) + beta * dot(p1, k)).astype(BF)
         dk0[rows, :] = dot_tn(p1, q)
         dv0[rows, :] = dot_tn(p2, g)
+        xt[:, rows] = xa[rows, :].T if place < 6 else xb[place * TOK - 768 : place * TOK - 640, :].T
 
 
 def finish(beta, idx, qkv, dq, dk0, dv0, r, t1, t2, t3, dqkv, keep, send):
@@ -174,12 +172,12 @@
         send[z] = dqkv[rows_of(idx, z, 1), :]
 
 
-def weights(idx, xta, xtb, dqkv, *refs):
+def weights(idx, xt, dqkv, *refs):
     outs, buf = refs[:4], refs[4]
     xi, yi, ci = idx[0], idx[1], idx[3]
     for m in range(4):
         rows = slice(m * 512, (m + 1) * 512)
-        tile = (dot(xta[rows, :], dqkv[:768, :]) + dot(xtb[rows, :], dqkv[768:, :])).astype(BF)
+        tile = dot(xt[rows, :], dqkv[...]).astype(BF)
         buf[m] = tile.reshape(8, NX, 16, 384)
     for s in range(4):
         for j in range(4):
@@ -254,30 +252,27 @@
     (own_w,) = call(relay, [shape((2048, 384), BF)], [idx, own_w, w1, w3, w2], flops=1 << 33, limit=6)
     first = [x, x1, x3]
     first += [ctx_hop(p, dc=1) for p in first]
-    xa, xta = call(
-        stack, [shape((768, 2048), BF), shape((2048, 768), BF)], [idx, *first], flops=1 << 33, limit=10
-    )
+    (xa,) = call(stack, [shape((768, 2048), BF)], [idx, *first], flops=1 << 33, limit=10)
     last = [x2a, x2b]
     last += [ctx_hop(after(p, gs), dc=1) for p in last]
 
     big = 2 * 1024 * 2048 * 384
-    qkv, r, total, xtb = call(
+    qkv, r, total, xb = call(
         project,
         [
             shape((1024, 384), BF),
             shape((8, HD, HD), F32),
             shape((HD, HD), BF),
-            shape((2048, 256), BF),
+            shape((256, 2048), BF),
         ],
         [idx, xa, *last, own_w, gs],
-        [pltpu.VMEM((256, 2048), BF)],
         flops=big,
     )
     totals = [ctx_hop(total, dy=s) for s in (1, 2, 3)]
-    dq, dk0, dv0 = call(
+    dq, dk0, dv0, xt = call(
         lambda *refs: within(alpha, beta, *refs),
-        [shape((1024, HD), BF), shape((1024, HD), F32), shape((1024, HD), F32)],
-        [idx, gs, qkv],
+        [shape((1024, HD), BF), shape((1024, HD), F32), shape((1024, HD), F32), shape((2048, 1024), BF)],
+        [idx, xa, xb, gs, qkv],
         flops=big // 4,
     )
     dqkv, keep, send = call(
@@ -291,7 +286,7 @@
     parts = call(
         weights,
         [shape((4, 8, 16, 384), BF)] * 4,
-        [idx, xta, xtb, dqkv],
+        [idx, xt, dqkv],
         [pltpu.VMEM((NY, 8, NX, 16, 384), BF)],
         flops=big,
     )

time: 93.2 us -> 92.6 us (level)
  no operation moved by 1% of the time
where the time goes in v8:
time: 92.6 us; the launch traced here: 92.1 us
  starting transfers between devices  41.7 us (45%)
  Pallas kernels  20.2 us (22%)
  blocking collectives  13.8 us (15%)
  local copies, waits for them, and re-layouts  10.7 us (12%)
  waiting for transfers between devices  3.77 us (4%)
  other arithmetic  1.17 us (1%)
    ppermute x18, starting transfers between devices, ctx_hop(): return lax.ppermute(block, 'ctx', route)  24.9 us
    pallas_call x11, Pallas kernels, call(): pl.pallas_call(run, out_shape=list(outs), in_specs=[pl.BlockSpec(memory_s...  20.2 us
    all_to_all x1, blocking collectives, body(): owned = lax.all_to_all(owned, 'ctx', 0, 0, axis_index_groups=rows_y)  13.8 us
    ppermute x6, starting transfers between devices, plane_hop(): return lax.ppermute(block, ('ctx', 'zero'), route)  7.89 us
    unnamed x16, local copies, waits for them, and re-layouts  7.23 us
    all_to_all x1, starting transfers between devices, body(): gs = lax.all_to_all(bundle, 'ctx', 0, 0, axis_index_groups=rows_y)  5.19 us
    ppermute x6, waiting for transfers between devices, plane_hop(): return lax.ppermute(block, ('ctx', 'zero'), route)  3.71 us
    ppermute x3, starting transfers between devices, x_hop(): return lax.ppermute(block, 'zero', [(i, (i + dx) % NX) for i in range(NX)])  3.67 us
  transfers between devices with their start and end apart: 28, of which 1 were waited for; matrix products, arithmetic and copies ran while one was open for 4% of the time, Pallas kernels for 17%

profile of v8, /device:TPU:1, one launch (start us, length us, event | category | flops | bytes accessed | tf_op | source)
XLA Modules:
  0.0 92.1 jit_solution(17838191148783965207)
XLA Ops:
  0.6 2.5 %collective-permute-start = (bf16[128,2048]{1,0:T(8,128)(2,1)}, bf16[128,2048]{1,0:T(8,128)(2,1)S(1)}, u32[]{:S(2)}, u32[]{:S(2)}) collective-permute-start(bf16[128,2048]{1,0:T(8,128)(2,1)} %bitcast.4.refs_1_), channel_id=1, source_target_pairs={{0,8},{4,12},{8,16},{12,20},{16,24},{20,28},{24,0},{28,4},{32,40},... | collective-permute-start | bytes 1572872 | tf_op jit(solution)/shard_map/ppermute | solution.py:24
  3.2 2.2 %collective-permute-start.1 = (bf16[128,2048]{1,0:T(8,128)(2,1)}, bf16[128,2048]{1,0:T(8,128)(2,1)}, u32[]{:S(2)}, u32[]{:S(2)}) collective-permute-start(bf16[128,2048]{1,0:T(8,128)(2,1)} %bitcast.4.refs_1_), channel_id=1, source_target_pairs={{0,24},{4,28},{8,0},{12,4},{16,8},{20,12},{24,16},{28,20},{32,56},... | collective-permute-start | bytes 1572872 | tf_op jit(solution)/shard_map/ppermute | solution.py:24
  5.4 1.1 %constant_dynamic-slice_fusion.2 = (bf16[512,128]{1,0:T(8,128)(2,1)S(1)}, bf16[512,128]{1,0:T(8,128)(2,1)S(1)}, bf16[512,128]{1,0:T(8,128)(2,1)S(1)}) fusion(bf16[512,3072]{1,0:T(8,128)(2,1)} %param.7, s32[]{:T(128)S(6)} %select_n.31, s32[]{:T(128)S(6)} %select_n.33, s32[]{:T(128)S(6)} %select_n.32), kind=kLoop, calls=%fused_computation.6 | loop fusion | bytes 786444 | tf_op jit(solution)/shard_map/dynamic_slice | solution.py:244
  6.5 2.5 %collective-permute-start.10 = (bf16[512,384]{1,0:T(8,128)(2,1)S(1)}, bf16[512,384]{1,0:T(8,128)(2,1)S(1)}, u32[]{:S(2)}, u32[]{:S(2)}) collective-permute-start(bf16[512,384]{1,0:T(8,128)(2,1)S(1)} %pad_maximum_fusion.refs_1_), channel_id=1, source_target_pairs={{0,3},{1,0},{2,1},{3,2},{4,7},{5,4},{6,5},{7,6},{8,11},{9,8},{10,9... | collective-permute-start | bytes 1179656 | tf_op jit(solution)/shard_map/ppermute | solution.py:28
  9.0 0.5 collective-permute-start.11
  9.6 0.6 collective-permute-start.9
  10.3 1.0 %copy-done = f32[1,1,8,128,128]{4,3,2,1,0:T(8,128)S(1)} copy-done((f32[1,1,8,128,128]{4,3,2,1,0:T(8,128)S(1)}, f32[1,1,8,128,128]{4,3,2,1,0:T(8,128)}, u32[]{:S(2)}) %copy-start) | copy-done | bytes 524312
  11.3 0.9 %copy-done.1 = bf16[1,128,1024]{2,1,0:T(8,128)(2,1)S(1)} copy-done((bf16[1,128,1024]{2,1,0:T(8,128)(2,1)S(1)}, bf16[1,128,1024]{2,1,0:T(8,128)(2,1)}, u32[]{:S(2)}) %copy-start.1) | copy-done | bytes 262168
  12.2 1.4 %shard_map.60 = bf16[8,2,128,128]{3,2,1,0:T(8,128)(2,1)} custom-call(s32[4]{0:T(128)S(1)} %pad_add_fusion.refs_0_, bf16[128,1024]{1,0:T(8,128)(2,1)S(1)} %bitcast.10, f32[8,128,128]{2,1,0:T(8,128)S(1)} %bitcast.9), custom_call_target="tpu_custom_call" | custom-call | bytes 1310736 | tf_op jit(solution)/shard_map/pallas_call | solution.py:63
  13.7 5.2 %all-to-all-start = ((bf16[8,2,128,128]{3,2,1,0:T(8,128)(2,1)}), bf16[8,2,128,128]{3,2,1,0:T(8,128)(2,1)S(1)}, u32[]{:S(2)}, u32[]{:S(2)}) async-start(bf16[8,2,128,128]{3,2,1,0:T(8,128)(2,1)} %shard_map.60), calls=%async_computation | async-start | bytes 1048576 | tf_op jit(solution)/shard_map/all_to_all | solution.py:249
  18.9 0.2 collective-permute-start.2
  19.0 0.7 slice.8
  19.8 1.6 %collective-permute-start.5 = (bf16[64,2048]{1,0:T(8,128)(2,1)}, bf16[64,2048]{1,0:T(8,128)(2,1)S(1)}, u32[]{:S(2)}, u32[]{:S(2)}) collective-permute-start(bf16[64,2048]{1,0:T(8,128)(2,1)} %slice.8), channel_id=1, source_target_pairs={{0,8},{4,12},{8,16},{12,20},{16,24},{20,28},{24,0},{28,4},{32,40},... | collective-permute-start | bytes 786440 | tf_op jit(solution)/shard_map/ppermute | solution.py:24
  21.3 1.7 %slice.9 = bf16[64,2048]{1,0:T(8,128)(2,1)} slice(bf16[128,2048]{1,0:T(8,128)(2,1)} %collective-permute-done.1.refs_3_), slice={[64:128], [0:2048]} | slice | bytes 524288 | tf_op jit(solution)/shard_map/slice | solution.py:251
  23.0 0.8 copy-done.2
  23.8 1.2 %collective-permute-start.6 = (bf16[64,2048]{1,0:T(8,128)(2,1)}, bf16[64,2048]{1,0:T(8,128)(2,1)S(1)}, u32[]{:S(2)}, u32[]{:S(2)}) collective-permute-start(bf16[64,2048]{1,0:T(8,128)(2,1)} %slice.9), channel_id=1, source_target_pairs={{0,24},{4,28},{8,0},{12,4},{16,8},{20,12},{24,16},{28,20},{32,56},... | collective-permute-start | bytes 786440 | tf_op jit(solution)/shard_map/ppermute | solution.py:24
  25.0 0.7 copy-done.4
  25.8 4.3 %collective-permute-start.3 = (bf16[128,2048]{1,0:T(8,128)(2,1)S(1)}, bf16[128,2048]{1,0:T(8,128)(2,1)}, u32[]{:S(2)}, u32[]{:S(2)}) collective-permute-start(bf16[128,2048]{1,0:T(8,128)(2,1)S(1)} %collective-permute-done.refs_2_), channel_id=1, source_target_pairs={{0,4},{4,0},{8,12},{12,8},{16,20},{20,16},{24,28},{28,24},{32,36},... | collective-permute-start | bytes 1572872 | tf_op jit(solution)/shard_map/ppermute | solution.py:24
  30.0 0.7 copy-done.6
  30.8 0.5 collective-permute-start.4
  31.2 1.0 %copy-done.3 = bf16[512,384]{1,0:T(8,128)(2,1)S(1)} copy-done((bf16[512,384]{1,0:T(8,128)(2,1)S(1)}, bf16[512,384]{1,0:T(8,128)(2,1)}, u32[]{:S(2)}) %copy-start.3) | copy-done | bytes 393240
  32.2 1.0 %copy-done.5 = bf16[512,384]{1,0:T(8,128)(2,1)S(1)} copy-done((bf16[512,384]{1,0:T(8,128)(2,1)S(1)}, bf16[512,384]{1,0:T(8,128)(2,1)}, u32[]{:S(2)}) %copy-start.5) | copy-done | bytes 393240
  33.2 1.0 %copy-done.7 = bf16[512,384]{1,0:T(8,128)(2,1)S(1)} copy-done((bf16[512,384]{1,0:T(8,128)(2,1)S(1)}, bf16[512,384]{1,0:T(8,128)(2,1)}, u32[]{:S(2)}) %copy-start.7) | copy-done | bytes 393240
  34.2 0.7 shard_map.61.refs_6_.refs_3_
  35.1 0.5 collective-permute-start.8
  35.6 1.9 %shard_map.59.refs_1_ = bf16[768,2048]{1,0:T(8,128)(2,1)S(1)} custom-call(s32[4]{0:T(128)S(1)} %pad_add_fusion.refs_0_, bf16[128,2048]{1,0:T(8,128)(2,1)} %bitcast.4.refs_1_, bf16[128,2048]{1,0:T(8,128)(2,1)S(1)} %collective-permute-done.refs_2_, bf16[128,2048]{1,0:T(8,128)(2,1)} %collective-permute-done.1.refs_3_, ...), custom_call_target="tpu_custom_call" | custom-call | flops 8589934592 | bytes 6291472 | tf_op jit(solution)/shard_map/pallas_call | solution.py:63
  37.5 3.6 %shard_map.62 = (bf16[1024,384]{1,0:T(8,128)(2,1)S(1)}, f32[8,128,128]{2,1,0:T(8,128)S(1)}, bf16[128,128]{1,0:T(8,128)(2,1)S(1)}, bf16[256,2048]{1,0:T(8,128)(2,1)S(1)}) custom-call(s32[4]{0:T(128)S(1)} %pad_add_fusion.refs_0_, bf16[768,2048]{1,0:T(8,128)(2,1)S(1)} %shard_map.59.refs_1_, bf16[64,2048]{1,0:T(8,128)(2,1)S(1)} %collective-permute-done.5.refs_2_, ...), custom_call_target="tpu_custom_call" | custom-call | flops 1610612736 | bytes 8683536 | tf_op jit(solution)/shard_map/pallas_call | solution.py:63
  41.1 1.4 %collective-permute-start.12 = (bf16[128,128]{1,0:T(8,128)(2,1)S(1)}, bf16[128,128]{1,0:T(8,128)(2,1)S(1)}, u32[]{:S(2)}, u32[]{:S(2)}) collective-permute-start(bf16[128,128]{1,0:T(8,128)(2,1)S(1)} %get-tuple-element.41), channel_id=1, source_target_pairs={{0,32},{4,36},{8,40},{12,44},{16,48},{20,52},{24,56},{28,60},{32,6... | collective-permute-start | bytes 98312 | tf_op jit(solution)/shard_map/ppermute | solution.py:24
  42.5 2.6 %collective-permute-start.13 = (bf16[128,128]{1,0:T(8,128)(2,1)S(1)}, bf16[128,128]{1,0:T(8,128)(2,1)S(1)}, u32[]{:S(2)}, u32[]{:S(2)}) collective-permute-start(bf16[128,128]{1,0:T(8,128)(2,1)S(1)} %get-tuple-element.41), channel_id=1, source_target_pairs={{0,64},{4,68},{8,72},{12,76},{16,80},{20,84},{24,88},{28,92},{32,9... | collective-permute-start | bytes 98312 | tf_op jit(solution)/shard_map/ppermute | solution.py:24
  45.1 1.1 %collective-permute-start.14 = (bf16[128,128]{1,0:T(8,128)(2,1)S(1)}, bf16[128,128]{1,0:T(8,128)(2,1)S(1)}, u32[]{:S(2)}, u32[]{:S(2)}) collective-permute-start(bf16[128,128]{1,0:T(8,128)(2,1)S(1)} %get-tuple-element.41), channel_id=1, source_target_pairs={{0,96},{4,100},{8,104},{12,108},{16,112},{20,116},{24,120},{28,124... | collective-permute-start | bytes 98312 | tf_op jit(solution)/shard_map/ppermute | solution.py:24
  46.2 2.7 %shard_map.63 = (bf16[1024,128]{1,0:T(8,128)(2,1)S(1)}, f32[1024,128]{1,0:T(8,128)S(1)}, f32[1024,128]{1,0:T(8,128)S(1)}, bf16[2048,1024]{1,0:T(8,128)(2,1)S(1)}) custom-call(s32[4]{0:T(128)S(1)} %pad_add_fusion.refs_0_, bf16[768,2048]{1,0:T(8,128)(2,1)S(1)} %shard_map.59.refs_1_, bf16[256,2048]{1,0:T(8,128)(2,1)S(1)} %get-tuple-element.36.refs_2_, ...), custom_call_target="tpu_custom_call" | custom-call | flops 402653184 | bytes 11010064 | tf_op jit(solution)/shard_map/pallas_call | solution.py:63
  48.9 1.0 %shard_map.64 = (bf16[1024,384]{1,0:T(8,128)(2,1)S(1)}, bf16[4,128,384]{2,1,0:T(8,128)(2,1)S(1)}, bf16[4,128,384]{2,1,0:T(8,128)(2,1)S(1)}) custom-call(s32[4]{0:T(128)S(1)} %pad_add_fusion.refs_0_, bf16[1024,384]{1,0:T(8,128)(2,1)S(1)} %get-tuple-element.35.refs_4_.refs_1_, bf16[1024,128]{1,0:T(8,128)(2,1)S(1)} %get-tuple-element.37.refs_2_, ...), custom_call_target="tpu_custom_call" | custom-call | flops 100663296 | bytes 4292624 | tf_op jit(solution)/shard_map/pallas_call | solution.py:63
  49.9 1.0 %collective-permute-start.16 = (bf16[2048,384]{1,0:T(8,128)(2,1)S(1)}, bf16[2048,384]{1,0:T(8,128)(2,1)S(1)}, u32[]{:S(2)}, u32[]{:S(2)}) collective-permute-start(bf16[2048,384]{1,0:T(8,128)(2,1)S(1)} %shard_map.61.refs_6_.refs_3_), channel_id=1, source_target_pairs={{0,4},{4,0},{8,12},{12,8},{16,20},{20,16},{24,28},{28,24},{32,36},... | collective-permute-start | bytes 4718600 | tf_op jit(solution)/shard_map/ppermute | solution.py:24
  50.9 0.3 collective-permute-start.15
  51.2 3.0 %shard_map.65 = (bf16[4,8,16,384]{3,2,1,0:T(8,128)(2,1)S(1)}, bf16[4,8,16,384]{3,2,1,0:T(8,128)(2,1)S(1)}, bf16[4,8,16,384]{3,2,1,0:T(8,128)(2,1)S(1)}, bf16[4,8,16,384]{3,2,1,0:T(8,128)(2,1)S(1)}) custom-call(s32[4]{0:T(128)S(1)} %pad_add_fusion.refs_0_, bf16[2048,1024]{1,0:T(8,128)(2,1)S(1)} %get-tuple-element.45.refs_1_, ...), custom_call_target="tpu_custom_call" | custom-call | flops 1610612736 | bytes 6553616 | tf_op jit(solution)/shard_map/pallas_call | solution.py:63
  54.2 0.5 collective-permute-start.19
  54.7 2.9 %collective-permute-start.20 = (bf16[4,8,16,384]{3,2,1,0:T(8,128)(2,1)S(1)}, bf16[4,8,16,384]{3,2,1,0:T(8,128)(2,1)S(1)}, u32[]{:S(2)}, u32[]{:S(2)}) collective-permute-start(bf16[4,8,16,384]{3,2,1,0:T(8,128)(2,1)S(1)} %get-tuple-element.54), channel_id=1, source_target_pairs={{0,2},{1,3},{2,0},{3,1},{4,68},{5,69},{6,70},{7,71},{8,10},{9,11},... | collective-permute-start | bytes 1179656 | tf_op jit(solution)/shard_map/ppermute | solution.py:40
  57.5 3.2 %shard_map.66 = (f32[128,2048]{1,0:T(8,128)S(1)}, bf16[128,2048]{1,0:T(8,128)(2,1)S(1)}, bf16[128,2048]{1,0:T(8,128)(2,1)S(1)}, bf16[64,2048]{1,0:T(8,128)(2,1)S(1)}, bf16[64,2048]{1,0:T(8,128)(2,1)S(1)}) custom-call(s32[4]{0:T(128)S(1)} %pad_add_fusion.refs_0_, bf16[4,128,384]{2,1,0:T(8,128)(2,1)S(1)} %get-tuple-element.42.refs_1_, ...), custom_call_target="tpu_custom_call" | custom-call | flops 1610612736 | bytes 6553616 | tf_op jit(solution)/shard_map/pallas_call | solution.py:63
  60.9 2.7 %collective-permute-start.18 = (bf16[64,2048]{1,0:T(8,128)(2,1)S(1)}, bf16[64,2048]{1,0:T(8,128)(2,1)S(1)}, u32[]{:S(2)}, u32[]{:S(2)}) collective-permute-start(bf16[64,2048]{1,0:T(8,128)(2,1)S(1)} %get-tuple-element.52), channel_id=1, source_target_pairs={{0,24},{4,28},{8,0},{12,4},{16,8},{20,12},{24,16},{28,20},{32,56},... | collective-permute-start | bytes 786440 | tf_op jit(solution)/shard_map/ppermute | solution.py:24
  63.5 3.7 %collective-permute-done.20.refs_3_ = bf16[4,8,16,384]{3,2,1,0:T(8,128)(2,1)S(1)} collective-permute-done((bf16[4,8,16,384]{3,2,1,0:T(8,128)(2,1)S(1)}, bf16[4,8,16,384]{3,2,1,0:T(8,128)(2,1)S(1)}, u32[]{:S(2)}, u32[]{:S(2)}) %collective-permute-start.20) | collective-permute-done | bytes 393248 | tf_op jit(solution)/shard_map/ppermute | solution.py:40
  67.2 0.7 shard_map.67
  68.0 1.0 %collective-permute-start.24 = (bf16[8,16,384]{2,1,0:T(8,128)(2,1)S(1)}, bf16[8,16,384]{2,1,0:T(8,128)(2,1)S(1)}, u32[]{:S(2)}, u32[]{:S(2)}) collective-permute-start(bf16[8,16,384]{2,1,0:T(8,128)(2,1)S(1)} %get-tuple-element.59), channel_id=1, source_target_pairs={{0,32},{1,33},{2,34},{3,35},{4,5},{5,6},{6,7},{7,4},{8,40},{9,41},... | collective-permute-start | bytes 294920 | tf_op jit(solution)/shard_map/ppermute | solution.py:40
  69.0 3.5 %collective-permute-start.25 = (bf16[8,16,384]{2,1,0:T(8,128)(2,1)S(1)}, bf16[8,16,384]{2,1,0:T(8,128)(2,1)S(1)}, u32[]{:S(2)}, u32[]{:S(2)}) collective-permute-start(bf16[8,16,384]{2,1,0:T(8,128)(2,1)S(1)} %get-tuple-element.60), channel_id=1, source_target_pairs={{0,64},{1,65},{2,66},{3,67},{4,6},{5,7},{6,4},{7,5},{8,72},{9,73},... | collective-permute-start | bytes 294920 | tf_op jit(solution)/shard_map/ppermute | solution.py:40
  72.5 0.7 shard_map.68
  73.4 2.6 %collective-permute-start.23 = (bf16[128,2048]{1,0:T(8,128)(2,1)S(1)}, bf16[128,2048]{1,0:T(8,128)(2,1)S(1)}, u32[]{:S(2)}, u32[]{:S(2)}) collective-permute-start(bf16[128,2048]{1,0:T(8,128)(2,1)S(1)} %get-tuple-element.58), channel_id=1, source_target_pairs={{0,24},{4,28},{8,0},{12,4},{16,8},{20,12},{24,16},{28,20},{32,56},... | collective-permute-start | bytes 1572872 | tf_op jit(solution)/shard_map/ppermute | solution.py:24
  76.1 13.8 %all_to_all.10.refs_1_ = f32[8,16,384]{2,1,0:T(8,128)S(1)} all-to-all(f32[8,16,384]{2,1,0:T(8,128)S(1)} %convert_add_fusion), channel_id=1, replica_groups={{0,4,8,12,16,20,24,28},{32,36,40,44,48,52,56,60},{64,68,72,76,80,84,88,..., dimensions={0} | all-to-all | bytes 393216 | tf_op jit(solution)/shard_map/all_to_all | solution.py:310
  89.8 1.2 %shard_map.69 = f32[16,3072]{1,0:T(8,128)} custom-call(s32[4]{0:T(128)S(1)} %pad_add_fusion.refs_0_, f32[8,16,384]{2,1,0:T(8,128)S(1)} %all_to_all.10.refs_1_), custom_call_target="tpu_custom_call" | custom-call | flops 2147483648 | bytes 393232 | tf_op jit(solution)/shard_map/pallas_call | solution.py:63
  91.1 1.0 %fusion = bf16[1,128,2048]{2,1,0:T(8,128)(2,1)} fusion(bf16[128,2048]{1,0:T(8,128)(2,1)S(1)} %collective-permute-done.23, f32[128,2048]{1,0:T(8,128)S(1)} %get-tuple-element.48.refs_5_, bf16[128,2048]{1,0:T(8,128)(2,1)S(1)} %collective-permute-done.22), kind=kLoop, calls=%fused_computation.1 | loop fusion | flops 1310720 | bytes 2621440 | tf_op jit(solution)/shard_map/broadcast_in_dim | solution.py:319
  (43 shorter events, 0.6 us)
Async XLA Ops:
  0.6 18.2 %collective-permute-start = (bf16[128,2048]{1,0:T(8,128)(2,1)}, bf16[128,2048]{1,0:T(8,128)(2,1)S(1)}, u32[]{:S(2)}, u32[]{:S(2)}) collective-permute-start(bf16[128,2048]{1,0:T(8,128)(2,1)} %bitcast.4.refs_1_), channel_id=1, source_target_pairs={{0,8},{4,12},{8,16},{12,20},{16,24},{20,28},{24,0},{28,4},{32,40},... | collective-permute-start | bytes 1572872 | tf_op jit(solution)/shard_map/ppermute | solution.py:24
  3.2 16.6 %collective-permute-start.1 = (bf16[128,2048]{1,0:T(8,128)(2,1)}, bf16[128,2048]{1,0:T(8,128)(2,1)}, u32[]{:S(2)}, u32[]{:S(2)}) collective-permute-start(bf16[128,2048]{1,0:T(8,128)(2,1)} %bitcast.4.refs_1_), channel_id=1, source_target_pairs={{0,24},{4,28},{8,0},{12,4},{16,8},{20,12},{24,16},{28,20},{32,56},... | collective-permute-start | bytes 1572872 | tf_op jit(solution)/shard_map/ppermute | solution.py:24
  6.5 16.5 %collective-permute-start.10 = (bf16[512,384]{1,0:T(8,128)(2,1)S(1)}, bf16[512,384]{1,0:T(8,128)(2,1)S(1)}, u32[]{:S(2)}, u32[]{:S(2)}) collective-permute-start(bf16[512,384]{1,0:T(8,128)(2,1)S(1)} %pad_maximum_fusion.refs_1_), channel_id=1, source_target_pairs={{0,3},{1,0},{2,1},{3,2},{4,7},{5,4},{6,5},{7,6},{8,11},{9,8},{10,9... | collective-permute-start | bytes 1179656 | tf_op jit(solution)/shard_map/ppermute | solution.py:28
  9.0 16.0 %collective-permute-start.11 = (bf16[512,384]{1,0:T(8,128)(2,1)S(1)}, bf16[512,384]{1,0:T(8,128)(2,1)S(1)}, u32[]{:S(2)}, u32[]{:S(2)}) collective-permute-start(bf16[512,384]{1,0:T(8,128)(2,1)S(1)} %pad_maximum_fusion.refs_1_), channel_id=1, source_target_pairs={{0,2},{1,3},{2,0},{3,1},{4,6},{5,7},{6,4},{7,5},{8,10},{9,11},{10,... | collective-permute-start | bytes 1179656 | tf_op jit(solution)/shard_map/ppermute | solution.py:28
  9.6 20.5 %collective-permute-start.9 = (bf16[512,384]{1,0:T(8,128)(2,1)S(1)}, bf16[512,384]{1,0:T(8,128)(2,1)S(1)}, u32[]{:S(2)}, u32[]{:S(2)}) collective-permute-start(bf16[512,384]{1,0:T(8,128)(2,1)S(1)} %pad_maximum_fusion.refs_1_), channel_id=1, source_target_pairs={{0,1},{1,2},{2,3},{3,0},{4,5},{5,6},{6,7},{7,4},{8,9},{9,10},{10,1... | collective-permute-start | bytes 1179656 | tf_op jit(solution)/shard_map/ppermute | solution.py:28
  10.2 1.0 %copy-start = (f32[1,1,8,128,128]{4,3,2,1,0:T(8,128)S(1)}, f32[1,1,8,128,128]{4,3,2,1,0:T(8,128)}, u32[]{:S(2)}) copy-start(f32[1,1,8,128,128]{4,3,2,1,0:T(8,128)} %param.6) | copy-start | bytes 1572868
  11.3 0.9 %copy-start.1 = (bf16[1,128,1024]{2,1,0:T(8,128)(2,1)S(1)}, bf16[1,128,1024]{2,1,0:T(8,128)(2,1)}, u32[]{:S(2)}) copy-start(bf16[1,128,1024]{2,1,0:T(8,128)(2,1)} %param.5) | copy-start | bytes 786436
  13.7 21.3 %all-to-all-start = ((bf16[8,2,128,128]{3,2,1,0:T(8,128)(2,1)}), bf16[8,2,128,128]{3,2,1,0:T(8,128)(2,1)S(1)}, u32[]{:S(2)}, u32[]{:S(2)}) async-start(bf16[8,2,128,128]{3,2,1,0:T(8,128)(2,1)} %shard_map.60), calls=%async_computation | async-start | bytes 1048576 | tf_op jit(solution)/shard_map/all_to_all | solution.py:249
  18.9 16.7 %collective-permute-start.2 = (bf16[128,2048]{1,0:T(8,128)(2,1)}, bf16[128,2048]{1,0:T(8,128)(2,1)}, u32[]{:S(2)}, u32[]{:S(2)}) collective-permute-start(bf16[128,2048]{1,0:T(8,128)(2,1)} %bitcast.4.refs_1_), channel_id=1, source_target_pairs={{0,4},{4,0},{8,12},{12,8},{16,20},{20,16},{24,28},{28,24},{32,36},... | collective-permute-start | bytes 1572872 | tf_op jit(solution)/shard_map/ppermute | solution.py:24
  19.8 15.2 %collective-permute-start.5 = (bf16[64,2048]{1,0:T(8,128)(2,1)}, bf16[64,2048]{1,0:T(8,128)(2,1)S(1)}, u32[]{:S(2)}, u32[]{:S(2)}) collective-permute-start(bf16[64,2048]{1,0:T(8,128)(2,1)} %slice.8), channel_id=1, source_target_pairs={{0,8},{4,12},{8,16},{12,20},{16,24},{20,28},{24,0},{28,4},{32,40},... | collective-permute-start | bytes 786440 | tf_op jit(solution)/shard_map/ppermute | solution.py:24
  23.0 0.8 copy-start.2
  23.8 11.3 %collective-permute-start.6 = (bf16[64,2048]{1,0:T(8,128)(2,1)}, bf16[64,2048]{1,0:T(8,128)(2,1)S(1)}, u32[]{:S(2)}, u32[]{:S(2)}) collective-permute-start(bf16[64,2048]{1,0:T(8,128)(2,1)} %slice.9), channel_id=1, source_target_pairs={{0,24},{4,28},{8,0},{12,4},{16,8},{20,12},{24,16},{28,20},{32,56},... | collective-permute-start | bytes 786440 | tf_op jit(solution)/shard_map/ppermute | solution.py:24
  25.0 0.7 copy-start.4
  25.8 9.8 %collective-permute-start.3 = (bf16[128,2048]{1,0:T(8,128)(2,1)S(1)}, bf16[128,2048]{1,0:T(8,128)(2,1)}, u32[]{:S(2)}, u32[]{:S(2)}) collective-permute-start(bf16[128,2048]{1,0:T(8,128)(2,1)S(1)} %collective-permute-done.refs_2_), channel_id=1, source_target_pairs={{0,4},{4,0},{8,12},{12,8},{16,20},{20,16},{24,28},{28,24},{32,36},... | collective-permute-start | bytes 1572872 | tf_op jit(solution)/shard_map/ppermute | solution.py:24
  30.0 0.7 copy-start.6
  30.8 4.8 %collective-permute-start.4 = (bf16[128,2048]{1,0:T(8,128)(2,1)}, bf16[128,2048]{1,0:T(8,128)(2,1)}, u32[]{:S(2)}, u32[]{:S(2)}) collective-permute-start(bf16[128,2048]{1,0:T(8,128)(2,1)} %collective-permute-done.1.refs_3_), channel_id=1, source_target_pairs={{0,4},{4,0},{8,12},{12,8},{16,20},{20,16},{24,28},{28,24},{32,36},... | collective-permute-start | bytes 1572872 | tf_op jit(solution)/shard_map/ppermute | solution.py:24
  31.2 1.0 %copy-start.3 = (bf16[512,384]{1,0:T(8,128)(2,1)S(1)}, bf16[512,384]{1,0:T(8,128)(2,1)}, u32[]{:S(2)}) copy-start(bf16[512,384]{1,0:T(8,128)(2,1)} %copy-done.2) | copy-start | bytes 1179652
  32.2 1.0 %copy-start.5 = (bf16[512,384]{1,0:T(8,128)(2,1)S(1)}, bf16[512,384]{1,0:T(8,128)(2,1)}, u32[]{:S(2)}) copy-start(bf16[512,384]{1,0:T(8,128)(2,1)} %copy-done.4) | copy-start | bytes 1179652
  33.2 1.0 %copy-start.7 = (bf16[512,384]{1,0:T(8,128)(2,1)S(1)}, bf16[512,384]{1,0:T(8,128)(2,1)}, u32[]{:S(2)}) copy-start(bf16[512,384]{1,0:T(8,128)(2,1)} %copy-done.6) | copy-start | bytes 1179652
  34.9 2.5 %collective-permute-start.7 = (bf16[64,2048]{1,0:T(8,128)(2,1)S(1)}, bf16[64,2048]{1,0:T(8,128)(2,1)S(1)}, u32[]{:S(2)}, u32[]{:S(2)}) collective-permute-start(bf16[64,2048]{1,0:T(8,128)(2,1)S(1)} %collective-permute-done.5.refs_2_), channel_id=1, source_target_pairs={{0,4},{4,0},{8,12},{12,8},{16,20},{20,16},{24,28},{28,24},{32,36},... | collective-permute-start | bytes 786440 | tf_op jit(solution)/shard_map/ppermute | solution.py:24
  35.1 2.4 %collective-permute-start.8 = (bf16[64,2048]{1,0:T(8,128)(2,1)S(1)}, bf16[64,2048]{1,0:T(8,128)(2,1)S(1)}, u32[]{:S(2)}, u32[]{:S(2)}) collective-permute-start(bf16[64,2048]{1,0:T(8,128)(2,1)S(1)} %collective-permute-done.6.refs_3_), channel_id=1, source_target_pairs={{0,4},{4,0},{8,12},{12,8},{16,20},{20,16},{24,28},{28,24},{32,36},... | collective-permute-start | bytes 786440 | tf_op jit(solution)/shard_map/ppermute | solution.py:24
  41.1 7.8 %collective-permute-start.12 = (bf16[128,128]{1,0:T(8,128)(2,1)S(1)}, bf16[128,128]{1,0:T(8,128)(2,1)S(1)}, u32[]{:S(2)}, u32[]{:S(2)}) collective-permute-start(bf16[128,128]{1,0:T(8,128)(2,1)S(1)} %get-tuple-element.41), channel_id=1, source_target_pairs={{0,32},{4,36},{8,40},{12,44},{16,48},{20,52},{24,56},{28,60},{32,6... | collective-permute-start | bytes 98312 | tf_op jit(solution)/shard_map/ppermute | solution.py:24
  42.5 6.4 %collective-permute-start.13 = (bf16[128,128]{1,0:T(8,128)(2,1)S(1)}, bf16[128,128]{1,0:T(8,128)(2,1)S(1)}, u32[]{:S(2)}, u32[]{:S(2)}) collective-permute-start(bf16[128,128]{1,0:T(8,128)(2,1)S(1)} %get-tuple-element.41), channel_id=1, source_target_pairs={{0,64},{4,68},{8,72},{12,76},{16,80},{20,84},{24,88},{28,92},{32,9... | collective-permute-start | bytes 98312 | tf_op jit(solution)/shard_map/ppermute | solution.py:24
  45.1 3.8 %collective-permute-start.14 = (bf16[128,128]{1,0:T(8,128)(2,1)S(1)}, bf16[128,128]{1,0:T(8,128)(2,1)S(1)}, u32[]{:S(2)}, u32[]{:S(2)}) collective-permute-start(bf16[128,128]{1,0:T(8,128)(2,1)S(1)} %get-tuple-element.41), channel_id=1, source_target_pairs={{0,96},{4,100},{8,104},{12,108},{16,112},{20,116},{24,120},{28,124... | collective-permute-start | bytes 98312 | tf_op jit(solution)/shard_map/ppermute | solution.py:24
  49.9 7.6 %collective-permute-start.16 = (bf16[2048,384]{1,0:T(8,128)(2,1)S(1)}, bf16[2048,384]{1,0:T(8,128)(2,1)S(1)}, u32[]{:S(2)}, u32[]{:S(2)}) collective-permute-start(bf16[2048,384]{1,0:T(8,128)(2,1)S(1)} %shard_map.61.refs_6_.refs_3_), channel_id=1, source_target_pairs={{0,4},{4,0},{8,12},{12,8},{16,20},{20,16},{24,28},{28,24},{32,36},... | collective-permute-start | bytes 4718600 | tf_op jit(solution)/shard_map/ppermute | solution.py:24
  50.9 6.6 %collective-permute-start.15 = (bf16[4,128,384]{2,1,0:T(8,128)(2,1)S(1)}, bf16[4,128,384]{2,1,0:T(8,128)(2,1)S(1)}, u32[]{:S(2)}, u32[]{:S(2)}) collective-permute-start(bf16[4,128,384]{2,1,0:T(8,128)(2,1)S(1)} %get-tuple-element.43), channel_id=1, source_target_pairs={{0,4},{4,0},{8,12},{12,8},{16,20},{20,16},{24,28},{28,24},{32,36},... | collective-permute-start | bytes 1179656 | tf_op jit(solution)/shard_map/ppermute | solution.py:24
  54.2 9.3 %collective-permute-start.19 = (bf16[4,8,16,384]{3,2,1,0:T(8,128)(2,1)S(1)}, bf16[4,8,16,384]{3,2,1,0:T(8,128)(2,1)S(1)}, u32[]{:S(2)}, u32[]{:S(2)}) collective-permute-start(bf16[4,8,16,384]{3,2,1,0:T(8,128)(2,1)S(1)} %get-tuple-element.53), channel_id=1, source_target_pairs={{0,1},{1,2},{2,3},{3,0},{4,36},{5,37},{6,38},{7,39},{8,9},{9,10},{... | collective-permute-start | bytes 1179656 | tf_op jit(solution)/shard_map/ppermute | solution.py:40
  54.7 12.5 %collective-permute-start.20 = (bf16[4,8,16,384]{3,2,1,0:T(8,128)(2,1)S(1)}, bf16[4,8,16,384]{3,2,1,0:T(8,128)(2,1)S(1)}, u32[]{:S(2)}, u32[]{:S(2)}) collective-permute-start(bf16[4,8,16,384]{3,2,1,0:T(8,128)(2,1)S(1)} %get-tuple-element.54), channel_id=1, source_target_pairs={{0,2},{1,3},{2,0},{3,1},{4,68},{5,69},{6,70},{7,71},{8,10},{9,11},... | collective-permute-start | bytes 1179656 | tf_op jit(solution)/shard_map/ppermute | solution.py:40
  57.5 9.7 %collective-permute-start.21 = (bf16[4,8,16,384]{3,2,1,0:T(8,128)(2,1)S(1)}, bf16[4,8,16,384]{3,2,1,0:T(8,128)(2,1)S(1)}, u32[]{:S(2)}, u32[]{:S(2)}) collective-permute-start(bf16[4,8,16,384]{3,2,1,0:T(8,128)(2,1)S(1)} %get-tuple-element.55), channel_id=1, source_target_pairs={{0,3},{1,0},{2,1},{3,2},{4,100},{5,101},{6,102},{7,103},{8,11},{9,... | collective-permute-start | bytes 1179656 | tf_op jit(solution)/shard_map/ppermute | solution.py:40
  60.8 11.7 %collective-permute-start.17 = (bf16[64,2048]{1,0:T(8,128)(2,1)S(1)}, bf16[64,2048]{1,0:T(8,128)(2,1)S(1)}, u32[]{:S(2)}, u32[]{:S(2)}) collective-permute-start(bf16[64,2048]{1,0:T(8,128)(2,1)S(1)} %get-tuple-element.51), channel_id=1, source_target_pairs={{0,8},{4,12},{8,16},{12,20},{16,24},{20,28},{24,0},{28,4},{32,40},... | collective-permute-start | bytes 786440 | tf_op jit(solution)/shard_map/ppermute | solution.py:24
  60.9 11.7 %collective-permute-start.18 = (bf16[64,2048]{1,0:T(8,128)(2,1)S(1)}, bf16[64,2048]{1,0:T(8,128)(2,1)S(1)}, u32[]{:S(2)}, u32[]{:S(2)}) collective-permute-start(bf16[64,2048]{1,0:T(8,128)(2,1)S(1)} %get-tuple-element.52), channel_id=1, source_target_pairs={{0,24},{4,28},{8,0},{12,4},{16,8},{20,12},{24,16},{28,20},{32,56},... | collective-permute-start | bytes 786440 | tf_op jit(solution)/shard_map/ppermute | solution.py:24
  68.0 8.0 %collective-permute-start.24 = (bf16[8,16,384]{2,1,0:T(8,128)(2,1)S(1)}, bf16[8,16,384]{2,1,0:T(8,128)(2,1)S(1)}, u32[]{:S(2)}, u32[]{:S(2)}) collective-permute-start(bf16[8,16,384]{2,1,0:T(8,128)(2,1)S(1)} %get-tuple-element.59), channel_id=1, source_target_pairs={{0,32},{1,33},{2,34},{3,35},{4,5},{5,6},{6,7},{7,4},{8,40},{9,41},... | collective-permute-start | bytes 294920 | tf_op jit(solution)/shard_map/ppermute | solution.py:40
  69.0 7.0 %collective-permute-start.25 = (bf16[8,16,384]{2,1,0:T(8,128)(2,1)S(1)}, bf16[8,16,384]{2,1,0:T(8,128)(2,1)S(1)}, u32[]{:S(2)}, u32[]{:S(2)}) collective-permute-start(bf16[8,16,384]{2,1,0:T(8,128)(2,1)S(1)} %get-tuple-element.60), channel_id=1, source_target_pairs={{0,64},{1,65},{2,66},{3,67},{4,6},{5,7},{6,4},{7,5},{8,72},{9,73},... | collective-permute-start | bytes 294920 | tf_op jit(solution)/shard_map/ppermute | solution.py:40
  72.5 3.5 %collective-permute-start.26 = (bf16[8,16,384]{2,1,0:T(8,128)(2,1)S(1)}, bf16[8,16,384]{2,1,0:T(8,128)(2,1)S(1)}, u32[]{:S(2)}, u32[]{:S(2)}) collective-permute-start(bf16[8,16,384]{2,1,0:T(8,128)(2,1)S(1)} %get-tuple-element.61), channel_id=1, source_target_pairs={{0,96},{1,97},{2,98},{3,99},{4,7},{5,4},{6,5},{7,6},{8,104},{9,105... | collective-permute-start | bytes 294920 | tf_op jit(solution)/shard_map/ppermute | solution.py:40
  73.2 17.8 %collective-permute-start.22 = (bf16[128,2048]{1,0:T(8,128)(2,1)S(1)}, bf16[128,2048]{1,0:T(8,128)(2,1)S(1)}, u32[]{:S(2)}, u32[]{:S(2)}) collective-permute-start(bf16[128,2048]{1,0:T(8,128)(2,1)S(1)} %get-tuple-element.57), channel_id=1, source_target_pairs={{0,8},{4,12},{8,16},{12,20},{16,24},{20,28},{24,0},{28,4},{32,40},... | collective-permute-start | bytes 1572872 | tf_op jit(solution)/shard_map/ppermute | solution.py:24
  73.4 17.7 %collective-permute-start.23 = (bf16[128,2048]{1,0:T(8,128)(2,1)S(1)}, bf16[128,2048]{1,0:T(8,128)(2,1)S(1)}, u32[]{:S(2)}, u32[]{:S(2)}) collective-permute-start(bf16[128,2048]{1,0:T(8,128)(2,1)S(1)} %get-tuple-element.58), channel_id=1, source_target_pairs={{0,24},{4,28},{8,0},{12,4},{16,8},{20,12},{24,16},{28,20},{32,56},... | collective-permute-start | bytes 1572872 | tf_op jit(solution)/shard_map/ppermute | solution.py:24

commit v9 on v8

--- a/solution.py
+++ b/solution.py
@@ -196,20 +196,27 @@
             outs[s][g] = sum(p[j, g].astype(F32) for p in parts).astype(BF)
 
 
-def back(idx, keep, got, own, other, mine_gx, up, down, far_up, far_down, gx):
-    zi = idx[2]
-    mine = keep[...].reshape(512, 384)
-    theirs = got[...].reshape(512, 384)
+def far_back(idx, keep, got, own, other, far_up, far_down):
+    far = lax.rem(idx[2] + 2, NZ)
     for n in range(4):
         cols = slice(n * 512, (n + 1) * 512)
-        part = dot_nt(mine, own[cols, :]) + dot_nt(theirs, other[cols, :])
-        gx[:, :, cols] = part.reshape(NZ, TOK, 512)
-    mine_gx[...] = gx[zi]
-    up[...] = gx[lax.rem(zi + 1, NZ)].astype(BF)
-    down[...] = gx[lax.rem(zi + 3, NZ)].astype(BF)
-    far = lax.rem(zi + 2, NZ)
-    far_up[...] = gx[far, :64, :].astype(BF)
-    far_down[...] = gx[far, 64:, :].astype(BF)
+        part = (dot_nt(keep[far], own[cols, :]) + dot_nt(got[far], other[cols, :])).astype(BF)
+        far_up[:, cols] = part[:64, :]
+        far_down[:, cols] = part[64:, :]
+
+
+def near_back(idx, keep, got, own, other, mine_gx, up, down, mine, theirs):
+    for i, step in enumerate((0, 1, 3)):
+        z = lax.rem(idx[2] + step, NZ)
+        rows = slice(i * TOK, (i + 1) * TOK)
+        mine[rows, :] = keep[z]
+        theirs[rows, :] = got[z]
+    for n in range(4):
+        cols = slice(n * 512, (n + 1) * 512)
+        part = dot_nt(mine[...], own[cols, :]) + dot_nt(theirs[...], other[cols, :])
+        mine_gx[:, cols] = part[:TOK, :]
+        up[:, cols] = part[TOK : 2 * TOK, :].astype(BF)
+        down[:, cols] = part[2 * TOK :, :].astype(BF)
 
 
 def merge(idx, up, down, from_low, from_high, new_up, new_down):
@@ -223,7 +230,7 @@
     for head in range(8):
         for i in range(3):
             at = i * 1024 + head * HD
-            out[:, at : at + HD] = parts[head, :, i * HD : (i + 1) * HD] * scale
+            out[:, at : at + HD] = parts[head, :, i * HD : (i + 1) * HD].astype(F32) * scale
 
 
 def body(inputs, grad_out, saved, w_qkv):
@@ -283,36 +290,45 @@
     )
     got = ctx_hop(send, dc=1)
     other_w = ctx_hop(after(own_w, send), dc=1)
+    far_up, far_down = call(
+        far_back,
+        [shape((64, 2048), BF)] * 2,
+        [idx, keep, got, own_w, other_w],
+        flops=big // 4,
+        limit=8,
+    )
     parts = call(
         weights,
         [shape((4, 8, 16, 384), BF)] * 4,
         [idx, xt, dqkv],
         [pltpu.VMEM((NY, 8, NX, 16, 384), BF)],
         flops=big,
-    )
-    gx, up, down, far_up, far_down = call(
-        back,
-        [shape((TOK, 2048), F32)] + [shape((TOK, 2048), BF)] * 2 + [shape((64, 2048), BF)] * 2,
+        deps=(far_up,),
+    )
+    gx, up, down = call(
+        near_back,
+        [shape((TOK, 2048), F32)] + [shape((TOK, 2048), BF)] * 2,
         [idx, keep, got, own_w, other_w],
-        [pltpu.VMEM((NZ, TOK, 2048), F32)],
+        [pltpu.VMEM((384, 384), BF)] * 2,
         flops=big,
         deps=(parts[0],),
+        limit=12,
     )
     parts = [parts[0]] + [plane_hop(parts[s], s, 0) for s in (1, 2, 3)]
     far_up, far_down = ctx_hop(far_up, dz=1), ctx_hop(far_down, dz=-1)
     parts = call(turn, [shape((8, 16, 384), BF)] * 4, [idx, *parts], deps=(gx,), limit=4)
     up, down = call(
-        merge, [shape((TOK, 2048), BF)] * 2, [idx, up, down, far_up, far_down], flops=1 << 33, deps=(parts[0],), limit=6
+        merge, [shape((TOK, 2048), BF)] * 2, [idx, up, down, far_up, far_down], flops=1 << 34, deps=(gx,), limit=6
     )
     parts = [parts[0]] + [plane_hop(parts[s], s, 1) for s in (1, 2, 3)]
     up, down = ctx_hop(up, dz=1), ctx_hop(down, dz=-1)
-    owned = sum(p.astype(F32) for p in parts)
+    owned = sum(p.astype(F32) for p in parts).astype(BF)
     owned = lax.all_to_all(owned, "ctx", 0, 0, axis_index_groups=rows_y)
     (grad_w,) = call(
         lambda *refs: collect(scale, *refs),
         [shape((16, 3 * heads * HD), F32)],
         [idx, owned],
-        flops=1 << 31,
+        flops=0,
         limit=4,
     )
     grad_x = (gx + up.astype(F32) + down.astype(F32)).astype(BF)

time: 92.6 us -> 97.5 us (1.053)
  waiting for transfers between devices: 3.77 us -> 11.2 us
  blocking collectives: 13.8 us -> 10.5 us
    ppermute x6, waiting for transfers between devices: 3.71 us -> 7.6 us  [plane_hop(): return lax.ppermute(block, ('ctx', 'zero'), route)]
    ppermute x18, waiting for transfers between devices: 0.05 us -> 3.55 us  [ctx_hop(): return lax.ppermute(block, 'ctx', route)]
    all_to_all x1, blocking collectives: 13.8 us -> 10.5 us  [body(): owned = lax.all_to_all(owned, 'ctx', 0, 0, axis_index_groups=rows_y)]
    pallas_call x11 -> x12, Pallas kernels: 20.2 us -> 21 us  [call(): pl.pallas_call(run, out_shape=list(outs), in_specs=[pl.BlockSpec(memory_s...]
  transfers between devices with their start and end apart: 28 -> 28, of which waited for: 1 -> 5; matrix products, arithmetic and copies ran while one was open for 4% -> 4% of each run, Pallas kernels for 17% -> 15%
where the time goes in v9:
time: 97.5 us; the launch traced here: 97 us
  starting transfers between devices  41.7 us (43%)
  Pallas kernels  21 us (22%)
  waiting for transfers between devices  11.2 us (11%)
  local copies, waits for them, and re-layouts  10.7 us (11%)
  blocking collectives  10.5 us (11%)
  other arithmetic  1.17 us (1%)
    ppermute x18, starting transfers between devices, ctx_hop(): return lax.ppermute(block, 'ctx', route)  24.9 us
    pallas_call x12, Pallas kernels, call(): pl.pallas_call(run, out_shape=list(outs), in_specs=[pl.BlockSpec(memory_s...  21 us
    all_to_all x1, blocking collectives, body(): owned = lax.all_to_all(owned, 'ctx', 0, 0, axis_index_groups=rows_y)  10.5 us
    ppermute x6, starting transfers between devices, plane_hop(): return lax.ppermute(block, ('ctx', 'zero'), route)  7.88 us
    ppermute x6, waiting for transfers between devices, plane_hop(): return lax.ppermute(block, ('ctx', 'zero'), route)  7.6 us
    unnamed x16, local copies, waits for them, and re-layouts  7.21 us
    all_to_all x1, starting transfers between devices, body(): gs = lax.all_to_all(bundle, 'ctx', 0, 0, axis_index_groups=rows_y)  5.19 us
    ppermute x3, starting transfers between devices, x_hop(): return lax.ppermute(block, 'zero', [(i, (i + dx) % NX) for i in range(NX)])  3.67 us
  transfers between devices with their start and end apart: 28, of which 5 were waited for; matrix products, arithmetic and copies ran while one was open for 4% of the time, Pallas kernels for 15%

profile of v9, /device:TPU:1, one launch (start us, length us, event | category | flops | bytes accessed | tf_op | source)
XLA Modules:
  0.0 97.0 jit_solution(12956700819044496110)
XLA Ops:
  0.6 2.5 %collective-permute-start = (bf16[128,2048]{1,0:T(8,128)(2,1)}, bf16[128,2048]{1,0:T(8,128)(2,1)S(1)}, u32[]{:S(2)}, u32[]{:S(2)}) collective-permute-start(bf16[128,2048]{1,0:T(8,128)(2,1)} %bitcast.4.refs_1_), channel_id=1, source_target_pairs={{0,8},{4,12},{8,16},{12,20},{16,24},{20,28},{24,0},{28,4},{32,40},... | collective-permute-start | bytes 1572872 | tf_op jit(solution)/shard_map/ppermute | solution.py:24
  3.2 2.2 %collective-permute-start.1 = (bf16[128,2048]{1,0:T(8,128)(2,1)}, bf16[128,2048]{1,0:T(8,128)(2,1)}, u32[]{:S(2)}, u32[]{:S(2)}) collective-permute-start(bf16[128,2048]{1,0:T(8,128)(2,1)} %bitcast.4.refs_1_), channel_id=1, source_target_pairs={{0,24},{4,28},{8,0},{12,4},{16,8},{20,12},{24,16},{28,20},{32,56},... | collective-permute-start | bytes 1572872 | tf_op jit(solution)/shard_map/ppermute | solution.py:24
  5.4 1.1 %constant_dynamic-slice_fusion.2 = (bf16[512,128]{1,0:T(8,128)(2,1)S(1)}, bf16[512,128]{1,0:T(8,128)(2,1)S(1)}, bf16[512,128]{1,0:T(8,128)(2,1)S(1)}) fusion(bf16[512,3072]{1,0:T(8,128)(2,1)} %param.7, s32[]{:T(128)S(6)} %select_n.31, s32[]{:T(128)S(6)} %select_n.33, s32[]{:T(128)S(6)} %select_n.32), kind=kLoop, calls=%fused_computation.6 | loop fusion | bytes 786444 | tf_op jit(solution)/shard_map/dynamic_slice | solution.py:251
  6.5 2.5 %collective-permute-start.10 = (bf16[512,384]{1,0:T(8,128)(2,1)S(1)}, bf16[512,384]{1,0:T(8,128)(2,1)S(1)}, u32[]{:S(2)}, u32[]{:S(2)}) collective-permute-start(bf16[512,384]{1,0:T(8,128)(2,1)S(1)} %pad_maximum_fusion.refs_1_), channel_id=1, source_target_pairs={{0,3},{1,0},{2,1},{3,2},{4,7},{5,4},{6,5},{7,6},{8,11},{9,8},{10,9... | collective-permute-start | bytes 1179656 | tf_op jit(solution)/shard_map/ppermute | solution.py:28
  9.0 0.5 collective-permute-start.11
  9.6 0.6 collective-permute-start.9
  10.3 1.0 %copy-done = f32[1,1,8,128,128]{4,3,2,1,0:T(8,128)S(1)} copy-done((f32[1,1,8,128,128]{4,3,2,1,0:T(8,128)S(1)}, f32[1,1,8,128,128]{4,3,2,1,0:T(8,128)}, u32[]{:S(2)}) %copy-start) | copy-done | bytes 524312
  11.3 0.9 copy-done.1
  12.2 1.4 %shard_map.60 = bf16[8,2,128,128]{3,2,1,0:T(8,128)(2,1)} custom-call(s32[4]{0:T(128)S(1)} %pad_add_fusion.refs_0_, bf16[128,1024]{1,0:T(8,128)(2,1)S(1)} %bitcast.10, f32[8,128,128]{2,1,0:T(8,128)S(1)} %bitcast.9), custom_call_target="tpu_custom_call" | custom-call | bytes 1310736 | tf_op jit(solution)/shard_map/pallas_call | solution.py:63
  13.7 5.2 %all-to-all-start = ((bf16[8,2,128,128]{3,2,1,0:T(8,128)(2,1)}), bf16[8,2,128,128]{3,2,1,0:T(8,128)(2,1)S(1)}, u32[]{:S(2)}, u32[]{:S(2)}) async-start(bf16[8,2,128,128]{3,2,1,0:T(8,128)(2,1)} %shard_map.60), calls=%async_computation | async-start | bytes 1048576 | tf_op jit(solution)/shard_map/all_to_all | solution.py:256
  19.0 0.7 slice.8
  19.8 1.6 %collective-permute-start.5 = (bf16[64,2048]{1,0:T(8,128)(2,1)}, bf16[64,2048]{1,0:T(8,128)(2,1)S(1)}, u32[]{:S(2)}, u32[]{:S(2)}) collective-permute-start(bf16[64,2048]{1,0:T(8,128)(2,1)} %slice.8), channel_id=1, source_target_pairs={{0,8},{4,12},{8,16},{12,20},{16,24},{20,28},{24,0},{28,4},{32,40},... | collective-permute-start | bytes 786440 | tf_op jit(solution)/shard_map/ppermute | solution.py:24
  21.3 1.7 %slice.9 = bf16[64,2048]{1,0:T(8,128)(2,1)} slice(bf16[128,2048]{1,0:T(8,128)(2,1)} %collective-permute-done.1.refs_3_), slice={[64:128], [0:2048]} | slice | bytes 524288 | tf_op jit(solution)/shard_map/slice | solution.py:258
  23.0 0.8 copy-done.2
  23.8 1.2 %collective-permute-start.6 = (bf16[64,2048]{1,0:T(8,128)(2,1)}, bf16[64,2048]{1,0:T(8,128)(2,1)S(1)}, u32[]{:S(2)}, u32[]{:S(2)}) collective-permute-start(bf16[64,2048]{1,0:T(8,128)(2,1)} %slice.9), channel_id=1, source_target_pairs={{0,24},{4,28},{8,0},{12,4},{16,8},{20,12},{24,16},{28,20},{32,56},... | collective-permute-start | bytes 786440 | tf_op jit(solution)/shard_map/ppermute | solution.py:24
  25.0 0.7 copy-done.4
  25.7 4.3 %collective-permute-start.3 = (bf16[128,2048]{1,0:T(8,128)(2,1)S(1)}, bf16[128,2048]{1,0:T(8,128)(2,1)}, u32[]{:S(2)}, u32[]{:S(2)}) collective-permute-start(bf16[128,2048]{1,0:T(8,128)(2,1)S(1)} %collective-permute-done.refs_2_), channel_id=1, source_target_pairs={{0,4},{4,0},{8,12},{12,8},{16,20},{20,16},{24,28},{28,24},{32,36},... | collective-permute-start | bytes 1572872 | tf_op jit(solution)/shard_map/ppermute | solution.py:24
  30.0 0.7 copy-done.6
  31.2 1.0 %copy-done.3 = bf16[512,384]{1,0:T(8,128)(2,1)S(1)} copy-done((bf16[512,384]{1,0:T(8,128)(2,1)S(1)}, bf16[512,384]{1,0:T(8,128)(2,1)}, u32[]{:S(2)}) %copy-start.3) | copy-done | bytes 393240
  32.2 1.0 %copy-done.5 = bf16[512,384]{1,0:T(8,128)(2,1)S(1)} copy-done((bf16[512,384]{1,0:T(8,128)(2,1)S(1)}, bf16[512,384]{1,0:T(8,128)(2,1)}, u32[]{:S(2)}) %copy-start.5) | copy-done | bytes 393240
  33.2 1.0 %copy-done.7 = bf16[512,384]{1,0:T(8,128)(2,1)S(1)} copy-done((bf16[512,384]{1,0:T(8,128)(2,1)S(1)}, bf16[512,384]{1,0:T(8,128)(2,1)}, u32[]{:S(2)}) %copy-start.7) | copy-done | bytes 393240
  34.2 0.7 shard_map.61.refs_6_.refs_3_
  35.5 1.9 %shard_map.59.refs_1_ = bf16[768,2048]{1,0:T(8,128)(2,1)S(1)} custom-call(s32[4]{0:T(128)S(1)} %pad_add_fusion.refs_0_, bf16[128,2048]{1,0:T(8,128)(2,1)} %bitcast.4.refs_1_, bf16[128,2048]{1,0:T(8,128)(2,1)S(1)} %collective-permute-done.refs_2_, bf16[128,2048]{1,0:T(8,128)(2,1)} %collective-permute-done.1.refs_3_, ...), custom_call_target="tpu_custom_call" | custom-call | flops 8589934592 | bytes 6291472 | tf_op jit(solution)/shard_map/pallas_call | solution.py:63
  37.5 3.6 %shard_map.62 = (bf16[1024,384]{1,0:T(8,128)(2,1)S(1)}, f32[8,128,128]{2,1,0:T(8,128)S(1)}, bf16[128,128]{1,0:T(8,128)(2,1)S(1)}, bf16[256,2048]{1,0:T(8,128)(2,1)S(1)}) custom-call(s32[4]{0:T(128)S(1)} %pad_add_fusion.refs_0_, bf16[768,2048]{1,0:T(8,128)(2,1)S(1)} %shard_map.59.refs_1_, bf16[64,2048]{1,0:T(8,128)(2,1)S(1)} %collective-permute-done.5.refs_2_, ...), custom_call_target="tpu_custom_call" | custom-call | flops 1610612736 | bytes 8683536 | tf_op jit(solution)/shard_map/pallas_call | solution.py:63
  41.1 1.4 %collective-permute-start.12 = (bf16[128,128]{1,0:T(8,128)(2,1)S(1)}, bf16[128,128]{1,0:T(8,128)(2,1)S(1)}, u32[]{:S(2)}, u32[]{:S(2)}) collective-permute-start(bf16[128,128]{1,0:T(8,128)(2,1)S(1)} %get-tuple-element.41), channel_id=1, source_target_pairs={{0,32},{4,36},{8,40},{12,44},{16,48},{20,52},{24,56},{28,60},{32,6... | collective-permute-start | bytes 98312 | tf_op jit(solution)/shard_map/ppermute | solution.py:24
  42.5 2.6 %collective-permute-start.13 = (bf16[128,128]{1,0:T(8,128)(2,1)S(1)}, bf16[128,128]{1,0:T(8,128)(2,1)S(1)}, u32[]{:S(2)}, u32[]{:S(2)}) collective-permute-start(bf16[128,128]{1,0:T(8,128)(2,1)S(1)} %get-tuple-element.41), channel_id=1, source_target_pairs={{0,64},{4,68},{8,72},{12,76},{16,80},{20,84},{24,88},{28,92},{32,9... | collective-permute-start | bytes 98312 | tf_op jit(solution)/shard_map/ppermute | solution.py:24
  45.1 1.1 %collective-permute-start.14 = (bf16[128,128]{1,0:T(8,128)(2,1)S(1)}, bf16[128,128]{1,0:T(8,128)(2,1)S(1)}, u32[]{:S(2)}, u32[]{:S(2)}) collective-permute-start(bf16[128,128]{1,0:T(8,128)(2,1)S(1)} %get-tuple-element.41), channel_id=1, source_target_pairs={{0,96},{4,100},{8,104},{12,108},{16,112},{20,116},{24,120},{28,124... | collective-permute-start | bytes 98312 | tf_op jit(solution)/shard_map/ppermute | solution.py:24
  46.1 2.7 %shard_map.63 = (bf16[1024,128]{1,0:T(8,128)(2,1)S(1)}, f32[1024,128]{1,0:T(8,128)S(1)}, f32[1024,128]{1,0:T(8,128)S(1)}, bf16[2048,1024]{1,0:T(8,128)(2,1)S(1)}) custom-call(s32[4]{0:T(128)S(1)} %pad_add_fusion.refs_0_, bf16[768,2048]{1,0:T(8,128)(2,1)S(1)} %shard_map.59.refs_1_, bf16[256,2048]{1,0:T(8,128)(2,1)S(1)} %get-tuple-element.36.refs_2_, ...), custom_call_target="tpu_custom_call" | custom-call | flops 402653184 | bytes 11010064 | tf_op jit(solution)/shard_map/pallas_call | solution.py:63
  48.9 1.0 %shard_map.64 = (bf16[1024,384]{1,0:T(8,128)(2,1)S(1)}, bf16[4,128,384]{2,1,0:T(8,128)(2,1)S(1)}, bf16[4,128,384]{2,1,0:T(8,128)(2,1)S(1)}) custom-call(s32[4]{0:T(128)S(1)} %pad_add_fusion.refs_0_, bf16[1024,384]{1,0:T(8,128)(2,1)S(1)} %get-tuple-element.35.refs_4_.refs_1_, bf16[1024,128]{1,0:T(8,128)(2,1)S(1)} %get-tuple-element.37.refs_2_, ...), custom_call_target="tpu_custom_call" | custom-call | flops 100663296 | bytes 4292624 | tf_op jit(solution)/shard_map/pallas_call | solution.py:63
  49.9 1.0 %collective-permute-start.16 = (bf16[2048,384]{1,0:T(8,128)(2,1)S(1)}, bf16[2048,384]{1,0:T(8,128)(2,1)S(1)}, u32[]{:S(2)}, u32[]{:S(2)}) collective-permute-start(bf16[2048,384]{1,0:T(8,128)(2,1)S(1)} %shard_map.61.refs_6_.refs_3_), channel_id=1, source_target_pairs={{0,4},{4,0},{8,12},{12,8},{16,20},{20,16},{24,28},{28,24},{32,36},... | collective-permute-start | bytes 4718600 | tf_op jit(solution)/shard_map/ppermute | solution.py:24
  51.0 3.5 %collective-permute-done.15.refs_2_ = bf16[4,128,384]{2,1,0:T(8,128)(2,1)S(1)} collective-permute-done((bf16[4,128,384]{2,1,0:T(8,128)(2,1)S(1)}, bf16[4,128,384]{2,1,0:T(8,128)(2,1)S(1)}, u32[]{:S(2)}, u32[]{:S(2)}) %collective-permute-start.15) | collective-permute-done | bytes 393248 | tf_op jit(solution)/shard_map/ppermute | solution.py:24
  54.5 1.6 %shard_map.65 = (bf16[64,2048]{1,0:T(8,128)(2,1)S(1)}, bf16[64,2048]{1,0:T(8,128)(2,1)S(1)}) custom-call(s32[4]{0:T(128)S(1)} %pad_add_fusion.refs_0_, bf16[4,128,384]{2,1,0:T(8,128)(2,1)S(1)} %get-tuple-element.42.refs_1_, bf16[4,128,384]{2,1,0:T(8,128)(2,1)S(1)} %collective-permute-done.15.refs_2_, bf16[2048,384]{1,0:T(8,128)(2,1)S(1)} %shard_map.61.refs_6_.refs_3_, ...), custom_call_target="tpu_custom_call" | custom-call | flops 402653184 | bytes 4456464 | tf_op jit(solution)/shard_map/pallas_call | solution.py:63
  56.4 2.7 %collective-permute-start.18 = (bf16[64,2048]{1,0:T(8,128)(2,1)S(1)}, bf16[64,2048]{1,0:T(8,128)(2,1)S(1)}, u32[]{:S(2)}, u32[]{:S(2)}) collective-permute-start(bf16[64,2048]{1,0:T(8,128)(2,1)S(1)} %get-tuple-element.52), channel_id=1, source_target_pairs={{0,24},{4,28},{8,0},{12,4},{16,8},{20,12},{24,16},{28,20},{32,56},... | collective-permute-start | bytes 786440 | tf_op jit(solution)/shard_map/ppermute | solution.py:24
  59.1 3.0 %shard_map.66 = (bf16[4,8,16,384]{3,2,1,0:T(8,128)(2,1)S(1)}, bf16[4,8,16,384]{3,2,1,0:T(8,128)(2,1)S(1)}, bf16[4,8,16,384]{3,2,1,0:T(8,128)(2,1)S(1)}, bf16[4,8,16,384]{3,2,1,0:T(8,128)(2,1)S(1)}) custom-call(s32[4]{0:T(128)S(1)} %pad_add_fusion.refs_0_, bf16[2048,1024]{1,0:T(8,128)(2,1)S(1)} %get-tuple-element.45.refs_1_, ...), custom_call_target="tpu_custom_call" | custom-call | flops 1610612736 | bytes 6553616 | tf_op jit(solution)/shard_map/pallas_call | solution.py:63
  62.5 2.9 %collective-permute-start.22 = (bf16[4,8,16,384]{3,2,1,0:T(8,128)(2,1)S(1)}, bf16[4,8,16,384]{3,2,1,0:T(8,128)(2,1)S(1)}, u32[]{:S(2)}, u32[]{:S(2)}) collective-permute-start(bf16[4,8,16,384]{3,2,1,0:T(8,128)(2,1)S(1)} %get-tuple-element.56), channel_id=1, source_target_pairs={{0,2},{1,3},{2,0},{3,1},{4,68},{5,69},{6,70},{7,71},{8,10},{9,11},... | collective-permute-start | bytes 1179656 | tf_op jit(solution)/shard_map/ppermute | solution.py:40
  65.4 2.4 %shard_map.67 = (f32[128,2048]{1,0:T(8,128)S(1)}, bf16[128,2048]{1,0:T(8,128)(2,1)S(1)}, bf16[128,2048]{1,0:T(8,128)(2,1)S(1)}) custom-call(s32[4]{0:T(128)S(1)} %pad_add_fusion.refs_0_, bf16[4,128,384]{2,1,0:T(8,128)(2,1)S(1)} %get-tuple-element.42.refs_1_, bf16[4,128,384]{2,1,0:T(8,128)(2,1)S(1)} %collective-permute-done.15.refs_2_, ...), custom_call_target="tpu_custom_call" | custom-call | flops 1610612736 | bytes 6029328 | tf_op jit(solution)/shard_map/pallas_call | solution.py:63
  67.8 0.7 shard_map.68
  68.6 2.7 %collective-permute-start.20 = (bf16[128,2048]{1,0:T(8,128)(2,1)S(1)}, bf16[128,2048]{1,0:T(8,128)(2,1)S(1)}, u32[]{:S(2)}, u32[]{:S(2)}) collective-permute-start(bf16[128,2048]{1,0:T(8,128)(2,1)S(1)} %get-tuple-element.54), channel_id=1, source_target_pairs={{0,24},{4,28},{8,0},{12,4},{16,8},{20,12},{24,16},{28,20},{32,56},... | collective-permute-start | bytes 1572872 | tf_op jit(solution)/shard_map/ppermute | solution.py:24
  71.3 3.8 %collective-permute-done.22.refs_3_ = bf16[4,8,16,384]{3,2,1,0:T(8,128)(2,1)S(1)} collective-permute-done((bf16[4,8,16,384]{3,2,1,0:T(8,128)(2,1)S(1)}, bf16[4,8,16,384]{3,2,1,0:T(8,128)(2,1)S(1)}, u32[]{:S(2)}, u32[]{:S(2)}) %collective-permute-start.22) | collective-permute-done | bytes 393248 | tf_op jit(solution)/shard_map/ppermute | solution.py:40
  75.1 0.7 shard_map.69
  75.9 1.0 %collective-permute-start.24 = (bf16[8,16,384]{2,1,0:T(8,128)(2,1)S(1)}, bf16[8,16,384]{2,1,0:T(8,128)(2,1)S(1)}, u32[]{:S(2)}, u32[]{:S(2)}) collective-permute-start(bf16[8,16,384]{2,1,0:T(8,128)(2,1)S(1)} %get-tuple-element.59), channel_id=1, source_target_pairs={{0,32},{1,33},{2,34},{3,35},{4,5},{5,6},{6,7},{7,4},{8,40},{9,41},... | collective-permute-start | bytes 294920 | tf_op jit(solution)/shard_map/ppermute | solution.py:40
  76.9 3.5 %collective-permute-start.25 = (bf16[8,16,384]{2,1,0:T(8,128)(2,1)S(1)}, bf16[8,16,384]{2,1,0:T(8,128)(2,1)S(1)}, u32[]{:S(2)}, u32[]{:S(2)}) collective-permute-start(bf16[8,16,384]{2,1,0:T(8,128)(2,1)S(1)} %get-tuple-element.60), channel_id=1, source_target_pairs={{0,64},{1,65},{2,66},{3,67},{4,6},{5,7},{6,4},{7,5},{8,72},{9,73},... | collective-permute-start | bytes 294920 | tf_op jit(solution)/shard_map/ppermute | solution.py:40
  80.4 1.1 %collective-permute-done.24 = bf16[8,16,384]{2,1,0:T(8,128)(2,1)S(1)} collective-permute-done((bf16[8,16,384]{2,1,0:T(8,128)(2,1)S(1)}, bf16[8,16,384]{2,1,0:T(8,128)(2,1)S(1)}, u32[]{:S(2)}, u32[]{:S(2)}) %collective-permute-start.24) | collective-permute-done | bytes 98336 | tf_op jit(solution)/shard_map/ppermute | solution.py:40
  81.5 1.9 %collective-permute-done.25 = bf16[8,16,384]{2,1,0:T(8,128)(2,1)S(1)} collective-permute-done((bf16[8,16,384]{2,1,0:T(8,128)(2,1)S(1)}, bf16[8,16,384]{2,1,0:T(8,128)(2,1)S(1)}, u32[]{:S(2)}, u32[]{:S(2)}) %collective-permute-start.25) | collective-permute-done | bytes 98336 | tf_op jit(solution)/shard_map/ppermute | solution.py:40
  83.5 0.7 collective-permute-done.26
  84.2 10.5 %all_to_all.10.refs_1_ = bf16[8,16,384]{2,1,0:T(8,128)(2,1)S(1)} all-to-all(bf16[8,16,384]{2,1,0:T(8,128)(2,1)S(1)} %add_convert_fusion.1), channel_id=1, replica_groups={{0,4,8,12,16,20,24,28},{32,36,40,44,48,52,56,60},{64,68,72,76,80,84,88,..., dimensions={0} | all-to-all | bytes 196608 | tf_op jit(solution)/shard_map/all_to_all | solution.py:326
  94.8 1.2 %shard_map.70 = f32[16,3072]{1,0:T(8,128)} custom-call(s32[4]{0:T(128)S(1)} %pad_add_fusion.refs_0_, bf16[8,16,384]{2,1,0:T(8,128)(2,1)S(1)} %all_to_all.10.refs_1_), custom_call_target="tpu_custom_call" | custom-call | bytes 294928 | tf_op jit(solution)/shard_map/pallas_call | solution.py:63
  96.0 1.0 %fusion = bf16[1,128,2048]{2,1,0:T(8,128)(2,1)} fusion(bf16[128,2048]{1,0:T(8,128)(2,1)S(1)} %collective-permute-done.20, f32[128,2048]{1,0:T(8,128)S(1)} %get-tuple-element.49.refs_5_, bf16[128,2048]{1,0:T(8,128)(2,1)S(1)} %collective-permute-done.19), kind=kLoop, calls=%fused_computation.1 | loop fusion | flops 1310720 | bytes 2621440 | tf_op jit(solution)/shard_map/broadcast_in_dim | solution.py:335
  (44 shorter events, 2.5 us)
Async XLA Ops:
  0.6 18.2 %collective-permute-start = (bf16[128,2048]{1,0:T(8,128)(2,1)}, bf16[128,2048]{1,0:T(8,128)(2,1)S(1)}, u32[]{:S(2)}, u32[]{:S(2)}) collective-permute-start(bf16[128,2048]{1,0:T(8,128)(2,1)} %bitcast.4.refs_1_), channel_id=1, source_target_pairs={{0,8},{4,12},{8,16},{12,20},{16,24},{20,28},{24,0},{28,4},{32,40},... | collective-permute-start | bytes 1572872 | tf_op jit(solution)/shard_map/ppermute | solution.py:24
  3.2 16.6 %collective-permute-start.1 = (bf16[128,2048]{1,0:T(8,128)(2,1)}, bf16[128,2048]{1,0:T(8,128)(2,1)}, u32[]{:S(2)}, u32[]{:S(2)}) collective-permute-start(bf16[128,2048]{1,0:T(8,128)(2,1)} %bitcast.4.refs_1_), channel_id=1, source_target_pairs={{0,24},{4,28},{8,0},{12,4},{16,8},{20,12},{24,16},{28,20},{32,56},... | collective-permute-start | bytes 1572872 | tf_op jit(solution)/shard_map/ppermute | solution.py:24
  6.5 16.5 %collective-permute-start.10 = (bf16[512,384]{1,0:T(8,128)(2,1)S(1)}, bf16[512,384]{1,0:T(8,128)(2,1)S(1)}, u32[]{:S(2)}, u32[]{:S(2)}) collective-permute-start(bf16[512,384]{1,0:T(8,128)(2,1)S(1)} %pad_maximum_fusion.refs_1_), channel_id=1, source_target_pairs={{0,3},{1,0},{2,1},{3,2},{4,7},{5,4},{6,5},{7,6},{8,11},{9,8},{10,9... | collective-permute-start | bytes 1179656 | tf_op jit(solution)/shard_map/ppermute | solution.py:28
  9.0 16.0 %collective-permute-start.11 = (bf16[512,384]{1,0:T(8,128)(2,1)S(1)}, bf16[512,384]{1,0:T(8,128)(2,1)S(1)}, u32[]{:S(2)}, u32[]{:S(2)}) collective-permute-start(bf16[512,384]{1,0:T(8,128)(2,1)S(1)} %pad_maximum_fusion.refs_1_), channel_id=1, source_target_pairs={{0,2},{1,3},{2,0},{3,1},{4,6},{5,7},{6,4},{7,5},{8,10},{9,11},{10,... | collective-permute-start | bytes 1179656 | tf_op jit(solution)/shard_map/ppermute | solution.py:28
  9.6 20.4 %collective-permute-start.9 = (bf16[512,384]{1,0:T(8,128)(2,1)S(1)}, bf16[512,384]{1,0:T(8,128)(2,1)S(1)}, u32[]{:S(2)}, u32[]{:S(2)}) collective-permute-start(bf16[512,384]{1,0:T(8,128)(2,1)S(1)} %pad_maximum_fusion.refs_1_), channel_id=1, source_target_pairs={{0,1},{1,2},{2,3},{3,0},{4,5},{5,6},{6,7},{7,4},{8,9},{9,10},{10,1... | collective-permute-start | bytes 1179656 | tf_op jit(solution)/shard_map/ppermute | solution.py:28
  10.2 1.0 %copy-start = (f32[1,1,8,128,128]{4,3,2,1,0:T(8,128)S(1)}, f32[1,1,8,128,128]{4,3,2,1,0:T(8,128)}, u32[]{:S(2)}) copy-start(f32[1,1,8,128,128]{4,3,2,1,0:T(8,128)} %param.6) | copy-start | bytes 1572868
  11.3 0.9 copy-start.1
  13.7 21.3 %all-to-all-start = ((bf16[8,2,128,128]{3,2,1,0:T(8,128)(2,1)}), bf16[8,2,128,128]{3,2,1,0:T(8,128)(2,1)S(1)}, u32[]{:S(2)}, u32[]{:S(2)}) async-start(bf16[8,2,128,128]{3,2,1,0:T(8,128)(2,1)} %shard_map.60), calls=%async_computation | async-start | bytes 1048576 | tf_op jit(solution)/shard_map/all_to_all | solution.py:256
  18.9 16.7 %collective-permute-start.2 = (bf16[128,2048]{1,0:T(8,128)(2,1)}, bf16[128,2048]{1,0:T(8,128)(2,1)}, u32[]{:S(2)}, u32[]{:S(2)}) collective-permute-start(bf16[128,2048]{1,0:T(8,128)(2,1)} %bitcast.4.refs_1_), channel_id=1, source_target_pairs={{0,4},{4,0},{8,12},{12,8},{16,20},{20,16},{24,28},{28,24},{32,36},... | collective-permute-start | bytes 1572872 | tf_op jit(solution)/shard_map/ppermute | solution.py:24
  19.8 15.2 %collective-permute-start.5 = (bf16[64,2048]{1,0:T(8,128)(2,1)}, bf16[64,2048]{1,0:T(8,128)(2,1)S(1)}, u32[]{:S(2)}, u32[]{:S(2)}) collective-permute-start(bf16[64,2048]{1,0:T(8,128)(2,1)} %slice.8), channel_id=1, source_target_pairs={{0,8},{4,12},{8,16},{12,20},{16,24},{20,28},{24,0},{28,4},{32,40},... | collective-permute-start | bytes 786440 | tf_op jit(solution)/shard_map/ppermute | solution.py:24
  23.0 0.8 copy-start.2
  23.8 11.3 %collective-permute-start.6 = (bf16[64,2048]{1,0:T(8,128)(2,1)}, bf16[64,2048]{1,0:T(8,128)(2,1)S(1)}, u32[]{:S(2)}, u32[]{:S(2)}) collective-permute-start(bf16[64,2048]{1,0:T(8,128)(2,1)} %slice.9), channel_id=1, source_target_pairs={{0,24},{4,28},{8,0},{12,4},{16,8},{20,12},{24,16},{28,20},{32,56},... | collective-permute-start | bytes 786440 | tf_op jit(solution)/shard_map/ppermute | solution.py:24
  25.0 0.7 copy-start.4
  25.7 9.8 %collective-permute-start.3 = (bf16[128,2048]{1,0:T(8,128)(2,1)S(1)}, bf16[128,2048]{1,0:T(8,128)(2,1)}, u32[]{:S(2)}, u32[]{:S(2)}) collective-permute-start(bf16[128,2048]{1,0:T(8,128)(2,1)S(1)} %collective-permute-done.refs_2_), channel_id=1, source_target_pairs={{0,4},{4,0},{8,12},{12,8},{16,20},{20,16},{24,28},{28,24},{32,36},... | collective-permute-start | bytes 1572872 | tf_op jit(solution)/shard_map/ppermute | solution.py:24
  30.0 0.7 copy-start.6
  30.7 4.8 %collective-permute-start.4 = (bf16[128,2048]{1,0:T(8,128)(2,1)}, bf16[128,2048]{1,0:T(8,128)(2,1)}, u32[]{:S(2)}, u32[]{:S(2)}) collective-permute-start(bf16[128,2048]{1,0:T(8,128)(2,1)} %collective-permute-done.1.refs_3_), channel_id=1, source_target_pairs={{0,4},{4,0},{8,12},{12,8},{16,20},{20,16},{24,28},{28,24},{32,36},... | collective-permute-start | bytes 1572872 | tf_op jit(solution)/shard_map/ppermute | solution.py:24
  31.2 1.0 %copy-start.3 = (bf16[512,384]{1,0:T(8,128)(2,1)S(1)}, bf16[512,384]{1,0:T(8,128)(2,1)}, u32[]{:S(2)}) copy-start(bf16[512,384]{1,0:T(8,128)(2,1)} %copy-done.2) | copy-start | bytes 1179652
  32.2 1.0 %copy-start.5 = (bf16[512,384]{1,0:T(8,128)(2,1)S(1)}, bf16[512,384]{1,0:T(8,128)(2,1)}, u32[]{:S(2)}) copy-start(bf16[512,384]{1,0:T(8,128)(2,1)} %copy-done.4) | copy-start | bytes 1179652
  33.2 1.0 %copy-start.7 = (bf16[512,384]{1,0:T(8,128)(2,1)S(1)}, bf16[512,384]{1,0:T(8,128)(2,1)}, u32[]{:S(2)}) copy-start(bf16[512,384]{1,0:T(8,128)(2,1)} %copy-done.6) | copy-start | bytes 1179652
  34.9 2.5 %collective-permute-start.7 = (bf16[64,2048]{1,0:T(8,128)(2,1)S(1)}, bf16[64,2048]{1,0:T(8,128)(2,1)S(1)}, u32[]{:S(2)}, u32[]{:S(2)}) collective-permute-start(bf16[64,2048]{1,0:T(8,128)(2,1)S(1)} %collective-permute-done.5.refs_2_), channel_id=1, source_target_pairs={{0,4},{4,0},{8,12},{12,8},{16,20},{20,16},{24,28},{28,24},{32,36},... | collective-permute-start | bytes 786440 | tf_op jit(solution)/shard_map/ppermute | solution.py:24
  35.0 2.4 %collective-permute-start.8 = (bf16[64,2048]{1,0:T(8,128)(2,1)S(1)}, bf16[64,2048]{1,0:T(8,128)(2,1)S(1)}, u32[]{:S(2)}, u32[]{:S(2)}) collective-permute-start(bf16[64,2048]{1,0:T(8,128)(2,1)S(1)} %collective-permute-done.6.refs_3_), channel_id=1, source_target_pairs={{0,4},{4,0},{8,12},{12,8},{16,20},{20,16},{24,28},{28,24},{32,36},... | collective-permute-start | bytes 786440 | tf_op jit(solution)/shard_map/ppermute | solution.py:24
  41.1 7.8 %collective-permute-start.12 = (bf16[128,128]{1,0:T(8,128)(2,1)S(1)}, bf16[128,128]{1,0:T(8,128)(2,1)S(1)}, u32[]{:S(2)}, u32[]{:S(2)}) collective-permute-start(bf16[128,128]{1,0:T(8,128)(2,1)S(1)} %get-tuple-element.41), channel_id=1, source_target_pairs={{0,32},{4,36},{8,40},{12,44},{16,48},{20,52},{24,56},{28,60},{32,6... | collective-permute-start | bytes 98312 | tf_op jit(solution)/shard_map/ppermute | solution.py:24
  42.5 6.4 %collective-permute-start.13 = (bf16[128,128]{1,0:T(8,128)(2,1)S(1)}, bf16[128,128]{1,0:T(8,128)(2,1)S(1)}, u32[]{:S(2)}, u32[]{:S(2)}) collective-permute-start(bf16[128,128]{1,0:T(8,128)(2,1)S(1)} %get-tuple-element.41), channel_id=1, source_target_pairs={{0,64},{4,68},{8,72},{12,76},{16,80},{20,84},{24,88},{28,92},{32,9... | collective-permute-start | bytes 98312 | tf_op jit(solution)/shard_map/ppermute | solution.py:24
  45.1 3.8 %collective-permute-start.14 = (bf16[128,128]{1,0:T(8,128)(2,1)S(1)}, bf16[128,128]{1,0:T(8,128)(2,1)S(1)}, u32[]{:S(2)}, u32[]{:S(2)}) collective-permute-start(bf16[128,128]{1,0:T(8,128)(2,1)S(1)} %get-tuple-element.41), channel_id=1, source_target_pairs={{0,96},{4,100},{8,104},{12,108},{16,112},{20,116},{24,120},{28,124... | collective-permute-start | bytes 98312 | tf_op jit(solution)/shard_map/ppermute | solution.py:24
  49.9 4.6 %collective-permute-start.16 = (bf16[2048,384]{1,0:T(8,128)(2,1)S(1)}, bf16[2048,384]{1,0:T(8,128)(2,1)S(1)}, u32[]{:S(2)}, u32[]{:S(2)}) collective-permute-start(bf16[2048,384]{1,0:T(8,128)(2,1)S(1)} %shard_map.61.refs_6_.refs_3_), channel_id=1, source_target_pairs={{0,4},{4,0},{8,12},{12,8},{16,20},{20,16},{24,28},{28,24},{32,36},... | collective-permute-start | bytes 4718600 | tf_op jit(solution)/shard_map/ppermute | solution.py:24
  50.9 3.6 %collective-permute-start.15 = (bf16[4,128,384]{2,1,0:T(8,128)(2,1)S(1)}, bf16[4,128,384]{2,1,0:T(8,128)(2,1)S(1)}, u32[]{:S(2)}, u32[]{:S(2)}) collective-permute-start(bf16[4,128,384]{2,1,0:T(8,128)(2,1)S(1)} %get-tuple-element.43), channel_id=1, source_target_pairs={{0,4},{4,0},{8,12},{12,8},{16,20},{20,16},{24,28},{28,24},{32,36},... | collective-permute-start | bytes 1179656 | tf_op jit(solution)/shard_map/ppermute | solution.py:24
  56.1 11.7 %collective-permute-start.17 = (bf16[64,2048]{1,0:T(8,128)(2,1)S(1)}, bf16[64,2048]{1,0:T(8,128)(2,1)S(1)}, u32[]{:S(2)}, u32[]{:S(2)}) collective-permute-start(bf16[64,2048]{1,0:T(8,128)(2,1)S(1)} %get-tuple-element.47.refs_3_), channel_id=1, source_target_pairs={{0,8},{4,12},{8,16},{12,20},{16,24},{20,28},{24,0},{28,4},{32,40},... | collective-permute-start | bytes 786440 | tf_op jit(solution)/shard_map/ppermute | solution.py:24
  56.4 11.4 %collective-permute-start.18 = (bf16[64,2048]{1,0:T(8,128)(2,1)S(1)}, bf16[64,2048]{1,0:T(8,128)(2,1)S(1)}, u32[]{:S(2)}, u32[]{:S(2)}) collective-permute-start(bf16[64,2048]{1,0:T(8,128)(2,1)S(1)} %get-tuple-element.52), channel_id=1, source_target_pairs={{0,24},{4,28},{8,0},{12,4},{16,8},{20,12},{24,16},{28,20},{32,56},... | collective-permute-start | bytes 786440 | tf_op jit(solution)/shard_map/ppermute | solution.py:24
  62.1 9.2 %collective-permute-start.21 = (bf16[4,8,16,384]{3,2,1,0:T(8,128)(2,1)S(1)}, bf16[4,8,16,384]{3,2,1,0:T(8,128)(2,1)S(1)}, u32[]{:S(2)}, u32[]{:S(2)}) collective-permute-start(bf16[4,8,16,384]{3,2,1,0:T(8,128)(2,1)S(1)} %get-tuple-element.55), channel_id=1, source_target_pairs={{0,1},{1,2},{2,3},{3,0},{4,36},{5,37},{6,38},{7,39},{8,9},{9,10},{... | collective-permute-start | bytes 1179656 | tf_op jit(solution)/shard_map/ppermute | solution.py:40
  62.5 12.5 %collective-permute-start.22 = (bf16[4,8,16,384]{3,2,1,0:T(8,128)(2,1)S(1)}, bf16[4,8,16,384]{3,2,1,0:T(8,128)(2,1)S(1)}, u32[]{:S(2)}, u32[]{:S(2)}) collective-permute-start(bf16[4,8,16,384]{3,2,1,0:T(8,128)(2,1)S(1)} %get-tuple-element.56), channel_id=1, source_target_pairs={{0,2},{1,3},{2,0},{3,1},{4,68},{5,69},{6,70},{7,71},{8,10},{9,11},... | collective-permute-start | bytes 1179656 | tf_op jit(solution)/shard_map/ppermute | solution.py:40
  65.4 9.7 %collective-permute-start.23 = (bf16[4,8,16,384]{3,2,1,0:T(8,128)(2,1)S(1)}, bf16[4,8,16,384]{3,2,1,0:T(8,128)(2,1)S(1)}, u32[]{:S(2)}, u32[]{:S(2)}) collective-permute-start(bf16[4,8,16,384]{3,2,1,0:T(8,128)(2,1)S(1)} %get-tuple-element.57), channel_id=1, source_target_pairs={{0,3},{1,0},{2,1},{3,2},{4,100},{5,101},{6,102},{7,103},{8,11},{9,... | collective-permute-start | bytes 1179656 | tf_op jit(solution)/shard_map/ppermute | solution.py:40
  68.5 27.5 %collective-permute-start.19 = (bf16[128,2048]{1,0:T(8,128)(2,1)S(1)}, bf16[128,2048]{1,0:T(8,128)(2,1)S(1)}, u32[]{:S(2)}, u32[]{:S(2)}) collective-permute-start(bf16[128,2048]{1,0:T(8,128)(2,1)S(1)} %get-tuple-element.53), channel_id=1, source_target_pairs={{0,8},{4,12},{8,16},{12,20},{16,24},{20,28},{24,0},{28,4},{32,40},... | collective-permute-start | bytes 1572872 | tf_op jit(solution)/shard_map/ppermute | solution.py:24
  68.6 27.4 %collective-permute-start.20 = (bf16[128,2048]{1,0:T(8,128)(2,1)S(1)}, bf16[128,2048]{1,0:T(8,128)(2,1)S(1)}, u32[]{:S(2)}, u32[]{:S(2)}) collective-permute-start(bf16[128,2048]{1,0:T(8,128)(2,1)S(1)} %get-tuple-element.54), channel_id=1, source_target_pairs={{0,24},{4,28},{8,0},{12,4},{16,8},{20,12},{24,16},{28,20},{32,56},... | collective-permute-start | bytes 1572872 | tf_op jit(solution)/shard_map/ppermute | solution.py:24
  75.9 5.7 %collective-permute-start.24 = (bf16[8,16,384]{2,1,0:T(8,128)(2,1)S(1)}, bf16[8,16,384]{2,1,0:T(8,128)(2,1)S(1)}, u32[]{:S(2)}, u32[]{:S(2)}) collective-permute-start(bf16[8,16,384]{2,1,0:T(8,128)(2,1)S(1)} %get-tuple-element.59), channel_id=1, source_target_pairs={{0,32},{1,33},{2,34},{3,35},{4,5},{5,6},{6,7},{7,4},{8,40},{9,41},... | collective-permute-start | bytes 294920 | tf_op jit(solution)/shard_map/ppermute | solution.py:40
  76.9 6.6 %collective-permute-start.25 = (bf16[8,16,384]{2,1,0:T(8,128)(2,1)S(1)}, bf16[8,16,384]{2,1,0:T(8,128)(2,1)S(1)}, u32[]{:S(2)}, u32[]{:S(2)}) collective-permute-start(bf16[8,16,384]{2,1,0:T(8,128)(2,1)S(1)} %get-tuple-element.60), channel_id=1, source_target_pairs={{0,64},{1,65},{2,66},{3,67},{4,6},{5,7},{6,4},{7,5},{8,72},{9,73},... | collective-permute-start | bytes 294920 | tf_op jit(solution)/shard_map/ppermute | solution.py:40
  80.4 3.8 %collective-permute-start.26 = (bf16[8,16,384]{2,1,0:T(8,128)(2,1)S(1)}, bf16[8,16,384]{2,1,0:T(8,128)(2,1)S(1)}, u32[]{:S(2)}, u32[]{:S(2)}) collective-permute-start(bf16[8,16,384]{2,1,0:T(8,128)(2,1)S(1)} %get-tuple-element.61), channel_id=1, source_target_pairs={{0,96},{1,97},{2,98},{3,99},{4,7},{5,4},{6,5},{7,6},{8,104},{9,105... | collective-permute-start | bytes 294920 | tf_op jit(solution)/shard_map/ppermute | solution.py:40

commit v10 on v9

--- a/solution.py
+++ b/solution.py
@@ -226,11 +226,12 @@
     new_down[64:, :] = (down[64:, :].astype(F32) + from_high[...].astype(F32)).astype(BF)
 
 
-def collect(scale, idx, parts, out):
+def close(scale, idx, parts, mine, up, down, grad_w, grad_x):
     for head in range(8):
         for i in range(3):
             at = i * 1024 + head * HD
-            out[:, at : at + HD] = parts[head, :, i * HD : (i + 1) * HD].astype(F32) * scale
+            grad_w[:, at : at + HD] = parts[head, :, i * HD : (i + 1) * HD].astype(F32) * scale
+    grad_x[...] = (mine[...] + up[...].astype(F32) + down[...].astype(F32)).astype(BF)
 
 
 def body(inputs, grad_out, saved, w_qkv):
@@ -290,20 +291,20 @@
     )
     got = ctx_hop(send, dc=1)
     other_w = ctx_hop(after(own_w, send), dc=1)
-    far_up, far_down = call(
-        far_back,
-        [shape((64, 2048), BF)] * 2,
-        [idx, keep, got, own_w, other_w],
-        flops=big // 4,
-        limit=8,
-    )
     parts = call(
         weights,
         [shape((4, 8, 16, 384), BF)] * 4,
         [idx, xt, dqkv],
         [pltpu.VMEM((NY, 8, NX, 16, 384), BF)],
         flops=big,
-        deps=(far_up,),
+    )
+    far_up, far_down = call(
+        far_back,
+        [shape((64, 2048), BF)] * 2,
+        [idx, keep, got, own_w, other_w],
+        flops=big // 4,
+        deps=(parts[0],),
+        limit=8,
     )
     gx, up, down = call(
         near_back,
@@ -311,27 +312,26 @@
         [idx, keep, got, own_w, other_w],
         [pltpu.VMEM((384, 384), BF)] * 2,
         flops=big,
-        deps=(parts[0],),
+        deps=(far_up,),
         limit=12,
     )
     parts = [parts[0]] + [plane_hop(parts[s], s, 0) for s in (1, 2, 3)]
     far_up, far_down = ctx_hop(far_up, dz=1), ctx_hop(far_down, dz=-1)
     parts = call(turn, [shape((8, 16, 384), BF)] * 4, [idx, *parts], deps=(gx,), limit=4)
     up, down = call(
-        merge, [shape((TOK, 2048), BF)] * 2, [idx, up, down, far_up, far_down], flops=1 << 34, deps=(gx,), limit=6
+        merge, [shape((TOK, 2048), BF)] * 2, [idx, up, down, far_up, far_down], flops=1 << 34, deps=(parts[0],), limit=6
     )
     parts = [parts[0]] + [plane_hop(parts[s], s, 1) for s in (1, 2, 3)]
     up, down = ctx_hop(up, dz=1), ctx_hop(down, dz=-1)
     owned = sum(p.astype(F32) for p in parts).astype(BF)
     owned = lax.all_to_all(owned, "ctx", 0, 0, axis_index_groups=rows_y)
-    (grad_w,) = call(
-        lambda *refs: collect(scale, *refs),
-        [shape((16, 3 * heads * HD), F32)],
-        [idx, owned],
+    grad_w, grad_x = call(
+        lambda *refs: close(scale, *refs),
+        [shape((16, 3 * heads * HD), F32), shape((TOK, 2048), BF)],
+        [idx, owned, gx, up, down],
         flops=0,
-        limit=4,
-    )
-    grad_x = (gx + up.astype(F32) + down.astype(F32)).astype(BF)
+        limit=8,
+    )
     return (grad_x[None], grad_w)
 
 

time: 97.5 us -> 92.2 us (0.946)
  waiting for transfers between devices: 11.2 us -> 6.71 us
  other arithmetic: 1.17 us -> 0.19 us
    ppermute x18, waiting for transfers between devices: 3.55 us -> 0.05 us  [ctx_hop(): return lax.ppermute(block, 'ctx', route)]
    broadcast_in_dim x1 -> x0, other arithmetic: 0.98 us -> none  [body(): return (grad_x[None], grad_w)]
  transfers between devices with their start and end apart: 28 -> 28, of which waited for: 5 -> 4; matrix products, arithmetic and copies ran while one was open for 4% -> 4% of each run, Pallas kernels for 15% -> 16%
where the time goes in v10:
time: 92.2 us; the launch traced here: 91.7 us
  starting transfers between devices  41.9 us (45%)
  Pallas kernels  21.2 us (23%)
  local copies, waits for them, and re-layouts  10.7 us (12%)
  blocking collectives  10.1 us (11%)
  waiting for transfers between devices  6.71 us (7%)
    ppermute x18, starting transfers between devices, ctx_hop(): return lax.ppermute(block, 'ctx', route)  24.9 us
    pallas_call x12, Pallas kernels, call(): pl.pallas_call(run, out_shape=list(outs), in_specs=[pl.BlockSpec(memory_s...  21.2 us
    all_to_all x1, blocking collectives, body(): owned = lax.all_to_all(owned, 'ctx', 0, 0, axis_index_groups=rows_y)  10.1 us
    ppermute x6, starting transfers between devices, plane_hop(): return lax.ppermute(block, ('ctx', 'zero'), route)  8.15 us
    unnamed x16, local copies, waits for them, and re-layouts  7.24 us
    ppermute x6, waiting for transfers between devices, plane_hop(): return lax.ppermute(block, ('ctx', 'zero'), route)  6.65 us
    all_to_all x1, starting transfers between devices, body(): gs = lax.all_to_all(bundle, 'ctx', 0, 0, axis_index_groups=rows_y)  5.19 us
    ppermute x3, starting transfers between devices, x_hop(): return lax.ppermute(block, 'zero', [(i, (i + dx) % NX) for i in range(NX)])  3.67 us
  transfers between devices with their start and end apart: 28, of which 4 were waited for; matrix products, arithmetic and copies ran while one was open for 4% of the time, Pallas kernels for 16%

profile of v10, /device:TPU:1, one launch (start us, length us, event | category | flops | bytes accessed | tf_op | source)
XLA Modules:
  0.0 91.7 jit_solution(6680826019847675701)
XLA Ops:
  0.6 2.5 %collective-permute-start = (bf16[128,2048]{1,0:T(8,128)(2,1)}, bf16[128,2048]{1,0:T(8,128)(2,1)S(1)}, u32[]{:S(2)}, u32[]{:S(2)}) collective-permute-start(bf16[128,2048]{1,0:T(8,128)(2,1)} %bitcast.4.refs_1_), channel_id=1, source_target_pairs={{0,8},{4,12},{8,16},{12,20},{16,24},{20,28},{24,0},{28,4},{32,40},... | collective-permute-start | bytes 1572872 | tf_op jit(solution)/shard_map/ppermute | solution.py:24
  3.2 2.2 %collective-permute-start.1 = (bf16[128,2048]{1,0:T(8,128)(2,1)}, bf16[128,2048]{1,0:T(8,128)(2,1)}, u32[]{:S(2)}, u32[]{:S(2)}) collective-permute-start(bf16[128,2048]{1,0:T(8,128)(2,1)} %bitcast.4.refs_1_), channel_id=1, source_target_pairs={{0,24},{4,28},{8,0},{12,4},{16,8},{20,12},{24,16},{28,20},{32,56},... | collective-permute-start | bytes 1572872 | tf_op jit(solution)/shard_map/ppermute | solution.py:24
  5.4 1.1 %constant_dynamic-slice_fusion.2 = (bf16[512,128]{1,0:T(8,128)(2,1)S(1)}, bf16[512,128]{1,0:T(8,128)(2,1)S(1)}, bf16[512,128]{1,0:T(8,128)(2,1)S(1)}) fusion(bf16[512,3072]{1,0:T(8,128)(2,1)} %param.7, s32[]{:T(128)S(6)} %select_n.31, s32[]{:T(128)S(6)} %select_n.33, s32[]{:T(128)S(6)} %select_n.32), kind=kLoop, calls=%fused_computation.4 | loop fusion | bytes 786444 | tf_op jit(solution)/shard_map/dynamic_slice | solution.py:252
  6.5 2.5 %collective-permute-start.10 = (bf16[512,384]{1,0:T(8,128)(2,1)S(1)}, bf16[512,384]{1,0:T(8,128)(2,1)S(1)}, u32[]{:S(2)}, u32[]{:S(2)}) collective-permute-start(bf16[512,384]{1,0:T(8,128)(2,1)S(1)} %pad_maximum_fusion.refs_1_), channel_id=1, source_target_pairs={{0,3},{1,0},{2,1},{3,2},{4,7},{5,4},{6,5},{7,6},{8,11},{9,8},{10,9... | collective-permute-start | bytes 1179656 | tf_op jit(solution)/shard_map/ppermute | solution.py:28
  9.0 0.5 collective-permute-start.11
  9.6 0.6 collective-permute-start.9
  10.3 1.0 %copy-done = f32[1,1,8,128,128]{4,3,2,1,0:T(8,128)S(1)} copy-done((f32[1,1,8,128,128]{4,3,2,1,0:T(8,128)S(1)}, f32[1,1,8,128,128]{4,3,2,1,0:T(8,128)}, u32[]{:S(2)}) %copy-start) | copy-done | bytes 524312
  11.3 0.9 %copy-done.1 = bf16[1,128,1024]{2,1,0:T(8,128)(2,1)S(1)} copy-done((bf16[1,128,1024]{2,1,0:T(8,128)(2,1)S(1)}, bf16[1,128,1024]{2,1,0:T(8,128)(2,1)}, u32[]{:S(2)}) %copy-start.1) | copy-done | bytes 262168
  12.2 1.4 %shard_map.60 = bf16[8,2,128,128]{3,2,1,0:T(8,128)(2,1)} custom-call(s32[4]{0:T(128)S(1)} %pad_add_fusion.refs_0_, bf16[128,1024]{1,0:T(8,128)(2,1)S(1)} %bitcast.9, f32[8,128,128]{2,1,0:T(8,128)S(1)} %bitcast.8), custom_call_target="tpu_custom_call" | custom-call | bytes 1310736 | tf_op jit(solution)/shard_map/pallas_call | solution.py:63
  13.6 5.2 %all-to-all-start = ((bf16[8,2,128,128]{3,2,1,0:T(8,128)(2,1)}), bf16[8,2,128,128]{3,2,1,0:T(8,128)(2,1)S(1)}, u32[]{:S(2)}, u32[]{:S(2)}) async-start(bf16[8,2,128,128]{3,2,1,0:T(8,128)(2,1)} %shard_map.60), calls=%async_computation | async-start | bytes 1048576 | tf_op jit(solution)/shard_map/all_to_all | solution.py:257
  19.0 0.7 slice.8
  19.7 1.6 %collective-permute-start.5 = (bf16[64,2048]{1,0:T(8,128)(2,1)}, bf16[64,2048]{1,0:T(8,128)(2,1)S(1)}, u32[]{:S(2)}, u32[]{:S(2)}) collective-permute-start(bf16[64,2048]{1,0:T(8,128)(2,1)} %slice.8), channel_id=1, source_target_pairs={{0,8},{4,12},{8,16},{12,20},{16,24},{20,28},{24,0},{28,4},{32,40},... | collective-permute-start | bytes 786440 | tf_op jit(solution)/shard_map/ppermute | solution.py:24
  21.3 1.7 %slice.9 = bf16[64,2048]{1,0:T(8,128)(2,1)} slice(bf16[128,2048]{1,0:T(8,128)(2,1)} %collective-permute-done.1.refs_3_), slice={[64:128], [0:2048]} | slice | bytes 524288 | tf_op jit(solution)/shard_map/slice | solution.py:259
  23.0 0.8 copy-done.2
  23.8 1.2 %collective-permute-start.6 = (bf16[64,2048]{1,0:T(8,128)(2,1)}, bf16[64,2048]{1,0:T(8,128)(2,1)S(1)}, u32[]{:S(2)}, u32[]{:S(2)}) collective-permute-start(bf16[64,2048]{1,0:T(8,128)(2,1)} %slice.9), channel_id=1, source_target_pairs={{0,24},{4,28},{8,0},{12,4},{16,8},{20,12},{24,16},{28,20},{32,56},... | collective-permute-start | bytes 786440 | tf_op jit(solution)/shard_map/ppermute | solution.py:24
  25.0 0.7 copy-done.4
  25.7 4.3 %collective-permute-start.3 = (bf16[128,2048]{1,0:T(8,128)(2,1)S(1)}, bf16[128,2048]{1,0:T(8,128)(2,1)}, u32[]{:S(2)}, u32[]{:S(2)}) collective-permute-start(bf16[128,2048]{1,0:T(8,128)(2,1)S(1)} %collective-permute-done.refs_2_), channel_id=1, source_target_pairs={{0,4},{4,0},{8,12},{12,8},{16,20},{20,16},{24,28},{28,24},{32,36},... | collective-permute-start | bytes 1572872 | tf_op jit(solution)/shard_map/ppermute | solution.py:24
  30.0 0.8 copy-done.6
  30.8 0.5 collective-permute-start.4
  31.3 1.0 %copy-done.3 = bf16[512,384]{1,0:T(8,128)(2,1)S(1)} copy-done((bf16[512,384]{1,0:T(8,128)(2,1)S(1)}, bf16[512,384]{1,0:T(8,128)(2,1)}, u32[]{:S(2)}) %copy-start.3) | copy-done | bytes 393240
  32.3 1.0 %copy-done.5 = bf16[512,384]{1,0:T(8,128)(2,1)S(1)} copy-done((bf16[512,384]{1,0:T(8,128)(2,1)S(1)}, bf16[512,384]{1,0:T(8,128)(2,1)}, u32[]{:S(2)}) %copy-start.5) | copy-done | bytes 393240
  33.3 1.0 %copy-done.7 = bf16[512,384]{1,0:T(8,128)(2,1)S(1)} copy-done((bf16[512,384]{1,0:T(8,128)(2,1)S(1)}, bf16[512,384]{1,0:T(8,128)(2,1)}, u32[]{:S(2)}) %copy-start.7) | copy-done | bytes 393240
  34.3 0.7 shard_map.61.refs_6_.refs_3_
  35.1 0.5 collective-permute-start.8
  35.6 1.9 %shard_map.59.refs_1_ = bf16[768,2048]{1,0:T(8,128)(2,1)S(1)} custom-call(s32[4]{0:T(128)S(1)} %pad_add_fusion.refs_0_, bf16[128,2048]{1,0:T(8,128)(2,1)} %bitcast.4.refs_1_, bf16[128,2048]{1,0:T(8,128)(2,1)S(1)} %collective-permute-done.refs_2_, bf16[128,2048]{1,0:T(8,128)(2,1)} %collective-permute-done.1.refs_3_, ...), custom_call_target="tpu_custom_call" | custom-call | flops 8589934592 | bytes 6291472 | tf_op jit(solution)/shard_map/pallas_call | solution.py:63
  37.5 3.6 %shard_map.62 = (bf16[1024,384]{1,0:T(8,128)(2,1)S(1)}, f32[8,128,128]{2,1,0:T(8,128)S(1)}, bf16[128,128]{1,0:T(8,128)(2,1)S(1)}, bf16[256,2048]{1,0:T(8,128)(2,1)S(1)}) custom-call(s32[4]{0:T(128)S(1)} %pad_add_fusion.refs_0_, bf16[768,2048]{1,0:T(8,128)(2,1)S(1)} %shard_map.59.refs_1_, bf16[64,2048]{1,0:T(8,128)(2,1)S(1)} %collective-permute-done.5.refs_2_, ...), custom_call_target="tpu_custom_call" | custom-call | flops 1610612736 | bytes 8683536 | tf_op jit(solution)/shard_map/pallas_call | solution.py:63
  41.1 1.4 %collective-permute-start.12 = (bf16[128,128]{1,0:T(8,128)(2,1)S(1)}, bf16[128,128]{1,0:T(8,128)(2,1)S(1)}, u32[]{:S(2)}, u32[]{:S(2)}) collective-permute-start(bf16[128,128]{1,0:T(8,128)(2,1)S(1)} %get-tuple-element.44), channel_id=1, source_target_pairs={{0,32},{4,36},{8,40},{12,44},{16,48},{20,52},{24,56},{28,60},{32,6... | collective-permute-start | bytes 98312 | tf_op jit(solution)/shard_map/ppermute | solution.py:24
  42.5 2.6 %collective-permute-start.13 = (bf16[128,128]{1,0:T(8,128)(2,1)S(1)}, bf16[128,128]{1,0:T(8,128)(2,1)S(1)}, u32[]{:S(2)}, u32[]{:S(2)}) collective-permute-start(bf16[128,128]{1,0:T(8,128)(2,1)S(1)} %get-tuple-element.44), channel_id=1, source_target_pairs={{0,64},{4,68},{8,72},{12,76},{16,80},{20,84},{24,88},{28,92},{32,9... | collective-permute-start | bytes 98312 | tf_op jit(solution)/shard_map/ppermute | solution.py:24
  45.1 1.1 %collective-permute-start.14 = (bf16[128,128]{1,0:T(8,128)(2,1)S(1)}, bf16[128,128]{1,0:T(8,128)(2,1)S(1)}, u32[]{:S(2)}, u32[]{:S(2)}) collective-permute-start(bf16[128,128]{1,0:T(8,128)(2,1)S(1)} %get-tuple-element.44), channel_id=1, source_target_pairs={{0,96},{4,100},{8,104},{12,108},{16,112},{20,116},{24,120},{28,124... | collective-permute-start | bytes 98312 | tf_op jit(solution)/shard_map/ppermute | solution.py:24
  46.1 2.7 %shard_map.63 = (bf16[1024,128]{1,0:T(8,128)(2,1)S(1)}, f32[1024,128]{1,0:T(8,128)S(1)}, f32[1024,128]{1,0:T(8,128)S(1)}, bf16[2048,1024]{1,0:T(8,128)(2,1)S(1)}) custom-call(s32[4]{0:T(128)S(1)} %pad_add_fusion.refs_0_, bf16[768,2048]{1,0:T(8,128)(2,1)S(1)} %shard_map.59.refs_1_, bf16[256,2048]{1,0:T(8,128)(2,1)S(1)} %get-tuple-element.37.refs_2_, ...), custom_call_target="tpu_custom_call" | custom-call | flops 402653184 | bytes 11010064 | tf_op jit(solution)/shard_map/pallas_call | solution.py:63
  48.9 1.0 %shard_map.64 = (bf16[1024,384]{1,0:T(8,128)(2,1)S(1)}, bf16[4,128,384]{2,1,0:T(8,128)(2,1)S(1)}, bf16[4,128,384]{2,1,0:T(8,128)(2,1)S(1)}) custom-call(s32[4]{0:T(128)S(1)} %pad_add_fusion.refs_0_, bf16[1024,384]{1,0:T(8,128)(2,1)S(1)} %get-tuple-element.38.refs_4_.refs_1_, bf16[1024,128]{1,0:T(8,128)(2,1)S(1)} %get-tuple-element.40.refs_2_, ...), custom_call_target="tpu_custom_call" | custom-call | flops 100663296 | bytes 4292624 | tf_op jit(solution)/shard_map/pallas_call | solution.py:63
  49.9 1.0 %collective-permute-start.19 = (bf16[2048,384]{1,0:T(8,128)(2,1)S(1)}, bf16[2048,384]{1,0:T(8,128)(2,1)S(1)}, u32[]{:S(2)}, u32[]{:S(2)}) collective-permute-start(bf16[2048,384]{1,0:T(8,128)(2,1)S(1)} %shard_map.61.refs_6_.refs_3_), channel_id=1, source_target_pairs={{0,4},{4,0},{8,12},{12,8},{16,20},{20,16},{24,28},{28,24},{32,36},... | collective-permute-start | bytes 4718600 | tf_op jit(solution)/shard_map/ppermute | solution.py:24
  51.2 3.0 %shard_map.65 = (bf16[4,8,16,384]{3,2,1,0:T(8,128)(2,1)S(1)}, bf16[4,8,16,384]{3,2,1,0:T(8,128)(2,1)S(1)}, bf16[4,8,16,384]{3,2,1,0:T(8,128)(2,1)S(1)}, bf16[4,8,16,384]{3,2,1,0:T(8,128)(2,1)S(1)}) custom-call(s32[4]{0:T(128)S(1)} %pad_add_fusion.refs_0_, bf16[2048,1024]{1,0:T(8,128)(2,1)S(1)} %get-tuple-element.39.refs_1_, ...), custom_call_target="tpu_custom_call" | custom-call | flops 1610612736 | bytes 6553616 | tf_op jit(solution)/shard_map/pallas_call | solution.py:63
  54.7 2.9 %collective-permute-start.16 = (bf16[4,8,16,384]{3,2,1,0:T(8,128)(2,1)S(1)}, bf16[4,8,16,384]{3,2,1,0:T(8,128)(2,1)S(1)}, u32[]{:S(2)}, u32[]{:S(2)}) collective-permute-start(bf16[4,8,16,384]{3,2,1,0:T(8,128)(2,1)S(1)} %get-tuple-element.48), channel_id=1, source_target_pairs={{0,2},{1,3},{2,0},{3,1},{4,68},{5,69},{6,70},{7,71},{8,10},{9,11},... | collective-permute-start | bytes 1179656 | tf_op jit(solution)/shard_map/ppermute | solution.py:40
  57.5 1.6 %shard_map.66 = (bf16[64,2048]{1,0:T(8,128)(2,1)S(1)}, bf16[64,2048]{1,0:T(8,128)(2,1)S(1)}) custom-call(s32[4]{0:T(128)S(1)} %pad_add_fusion.refs_0_, bf16[4,128,384]{2,1,0:T(8,128)(2,1)S(1)} %get-tuple-element.50.refs_1_, bf16[4,128,384]{2,1,0:T(8,128)(2,1)S(1)} %collective-permute-done.18.refs_2_, bf16[2048,384]{1,0:T(8,128)(2,1)S(1)} %shard_map.61.refs_6_.refs_3_, ...), custom_call_target="tpu_custom_call" | custom-call | flops 402653184 | bytes 4456464 | tf_op jit(solution)/shard_map/pallas_call | solution.py:63
  59.3 2.7 %collective-permute-start.24 = (bf16[64,2048]{1,0:T(8,128)(2,1)S(1)}, bf16[64,2048]{1,0:T(8,128)(2,1)S(1)}, u32[]{:S(2)}, u32[]{:S(2)}) collective-permute-start(bf16[64,2048]{1,0:T(8,128)(2,1)S(1)} %get-tuple-element.61), channel_id=1, source_target_pairs={{0,24},{4,28},{8,0},{12,4},{16,8},{20,12},{24,16},{28,20},{32,56},... | collective-permute-start | bytes 786440 | tf_op jit(solution)/shard_map/ppermute | solution.py:24
  61.9 2.4 %shard_map.67 = (f32[128,2048]{1,0:T(8,128)S(1)}, bf16[128,2048]{1,0:T(8,128)(2,1)S(1)}, bf16[128,2048]{1,0:T(8,128)(2,1)S(1)}) custom-call(s32[4]{0:T(128)S(1)} %pad_add_fusion.refs_0_, bf16[4,128,384]{2,1,0:T(8,128)(2,1)S(1)} %get-tuple-element.50.refs_1_, bf16[4,128,384]{2,1,0:T(8,128)(2,1)S(1)} %collective-permute-done.18.refs_2_, ...), custom_call_target="tpu_custom_call" | custom-call | flops 1610612736 | bytes 6029328 | tf_op jit(solution)/shard_map/pallas_call | solution.py:63
  64.3 2.9 %collective-permute-done.16.refs_3_ = bf16[4,8,16,384]{3,2,1,0:T(8,128)(2,1)S(1)} collective-permute-done((bf16[4,8,16,384]{3,2,1,0:T(8,128)(2,1)S(1)}, bf16[4,8,16,384]{3,2,1,0:T(8,128)(2,1)S(1)}, u32[]{:S(2)}, u32[]{:S(2)}) %collective-permute-start.16) | collective-permute-done | bytes 393248 | tf_op jit(solution)/shard_map/ppermute | solution.py:40
  67.2 0.7 shard_map.68
  68.0 0.7 shard_map.69
  68.8 2.7 %collective-permute-start.26 = (bf16[128,2048]{1,0:T(8,128)(2,1)S(1)}, bf16[128,2048]{1,0:T(8,128)(2,1)S(1)}, u32[]{:S(2)}, u32[]{:S(2)}) collective-permute-start(bf16[128,2048]{1,0:T(8,128)(2,1)S(1)} %get-tuple-element.63), channel_id=1, source_target_pairs={{0,24},{4,28},{8,0},{12,4},{16,8},{20,12},{24,16},{28,20},{32,56},... | collective-permute-start | bytes 1572872 | tf_op jit(solution)/shard_map/ppermute | solution.py:24
  71.4 0.9 %collective-permute-start.20 = (bf16[8,16,384]{2,1,0:T(8,128)(2,1)S(1)}, bf16[8,16,384]{2,1,0:T(8,128)(2,1)S(1)}, u32[]{:S(2)}, u32[]{:S(2)}) collective-permute-start(bf16[8,16,384]{2,1,0:T(8,128)(2,1)S(1)} %get-tuple-element.56), channel_id=1, source_target_pairs={{0,32},{1,33},{2,34},{3,35},{4,5},{5,6},{6,7},{7,4},{8,40},{9,41},... | collective-permute-start | bytes 294920 | tf_op jit(solution)/shard_map/ppermute | solution.py:40
  72.4 3.9 %collective-permute-start.21 = (bf16[8,16,384]{2,1,0:T(8,128)(2,1)S(1)}, bf16[8,16,384]{2,1,0:T(8,128)(2,1)S(1)}, u32[]{:S(2)}, u32[]{:S(2)}) collective-permute-start(bf16[8,16,384]{2,1,0:T(8,128)(2,1)S(1)} %get-tuple-element.57), channel_id=1, source_target_pairs={{0,64},{1,65},{2,66},{3,67},{4,6},{5,7},{6,4},{7,5},{8,72},{9,73},... | collective-permute-start | bytes 294920 | tf_op jit(solution)/shard_map/ppermute | solution.py:40
  76.2 1.1 %collective-permute-done.20 = bf16[8,16,384]{2,1,0:T(8,128)(2,1)S(1)} collective-permute-done((bf16[8,16,384]{2,1,0:T(8,128)(2,1)S(1)}, bf16[8,16,384]{2,1,0:T(8,128)(2,1)S(1)}, u32[]{:S(2)}, u32[]{:S(2)}) %collective-permute-start.20) | collective-permute-done | bytes 98336 | tf_op jit(solution)/shard_map/ppermute | solution.py:40
  77.4 1.9 %collective-permute-done.21 = bf16[8,16,384]{2,1,0:T(8,128)(2,1)S(1)} collective-permute-done((bf16[8,16,384]{2,1,0:T(8,128)(2,1)S(1)}, bf16[8,16,384]{2,1,0:T(8,128)(2,1)S(1)}, u32[]{:S(2)}, u32[]{:S(2)}) %collective-permute-start.21) | collective-permute-done | bytes 98336 | tf_op jit(solution)/shard_map/ppermute | solution.py:40
  79.3 0.7 collective-permute-done.22
  80.1 10.1 %all_to_all.10.refs_1_ = bf16[8,16,384]{2,1,0:T(8,128)(2,1)S(1)} all-to-all(bf16[8,16,384]{2,1,0:T(8,128)(2,1)S(1)} %add_convert_fusion), channel_id=1, replica_groups={{0,4,8,12,16,20,24,28},{32,36,40,44,48,52,56,60},{64,68,72,76,80,84,88,..., dimensions={0} | all-to-all | bytes 196608 | tf_op jit(solution)/shard_map/all_to_all | solution.py:327
  90.1 1.5 %shard_map.70 = (f32[16,3072]{1,0:T(8,128)}, bf16[128,2048]{1,0:T(8,128)(2,1)}) custom-call(s32[4]{0:T(128)S(1)} %pad_add_fusion.refs_0_, bf16[8,16,384]{2,1,0:T(8,128)(2,1)S(1)} %all_to_all.10.refs_1_, f32[128,2048]{1,0:T(8,128)S(1)} %get-tuple-element.54.refs_5_.refs_2_, bf16[128,2048]{1,0:T(8,128)(2,1)S(1)} %collective-permute-done.25.refs_3_, ...), custom_call_target="tpu_custom_call" | custom-call | bytes 2916368 | tf_op jit(solution)/shard_map/pallas_call | solution.py:63
  (43 shorter events, 1.5 us)
Async XLA Ops:
  0.6 18.2 %collective-permute-start = (bf16[128,2048]{1,0:T(8,128)(2,1)}, bf16[128,2048]{1,0:T(8,128)(2,1)S(1)}, u32[]{:S(2)}, u32[]{:S(2)}) collective-permute-start(bf16[128,2048]{1,0:T(8,128)(2,1)} %bitcast.4.refs_1_), channel_id=1, source_target_pairs={{0,8},{4,12},{8,16},{12,20},{16,24},{20,28},{24,0},{28,4},{32,40},... | collective-permute-start | bytes 1572872 | tf_op jit(solution)/shard_map/ppermute | solution.py:24
  3.2 16.6 %collective-permute-start.1 = (bf16[128,2048]{1,0:T(8,128)(2,1)}, bf16[128,2048]{1,0:T(8,128)(2,1)}, u32[]{:S(2)}, u32[]{:S(2)}) collective-permute-start(bf16[128,2048]{1,0:T(8,128)(2,1)} %bitcast.4.refs_1_), channel_id=1, source_target_pairs={{0,24},{4,28},{8,0},{12,4},{16,8},{20,12},{24,16},{28,20},{32,56},... | collective-permute-start | bytes 1572872 | tf_op jit(solution)/shard_map/ppermute | solution.py:24
  6.5 16.5 %collective-permute-start.10 = (bf16[512,384]{1,0:T(8,128)(2,1)S(1)}, bf16[512,384]{1,0:T(8,128)(2,1)S(1)}, u32[]{:S(2)}, u32[]{:S(2)}) collective-permute-start(bf16[512,384]{1,0:T(8,128)(2,1)S(1)} %pad_maximum_fusion.refs_1_), channel_id=1, source_target_pairs={{0,3},{1,0},{2,1},{3,2},{4,7},{5,4},{6,5},{7,6},{8,11},{9,8},{10,9... | collective-permute-start | bytes 1179656 | tf_op jit(solution)/shard_map/ppermute | solution.py:28
  9.0 16.0 %collective-permute-start.11 = (bf16[512,384]{1,0:T(8,128)(2,1)S(1)}, bf16[512,384]{1,0:T(8,128)(2,1)S(1)}, u32[]{:S(2)}, u32[]{:S(2)}) collective-permute-start(bf16[512,384]{1,0:T(8,128)(2,1)S(1)} %pad_maximum_fusion.refs_1_), channel_id=1, source_target_pairs={{0,2},{1,3},{2,0},{3,1},{4,6},{5,7},{6,4},{7,5},{8,10},{9,11},{10,... | collective-permute-start | bytes 1179656 | tf_op jit(solution)/shard_map/ppermute | solution.py:28
  9.6 20.4 %collective-permute-start.9 = (bf16[512,384]{1,0:T(8,128)(2,1)S(1)}, bf16[512,384]{1,0:T(8,128)(2,1)S(1)}, u32[]{:S(2)}, u32[]{:S(2)}) collective-permute-start(bf16[512,384]{1,0:T(8,128)(2,1)S(1)} %pad_maximum_fusion.refs_1_), channel_id=1, source_target_pairs={{0,1},{1,2},{2,3},{3,0},{4,5},{5,6},{6,7},{7,4},{8,9},{9,10},{10,1... | collective-permute-start | bytes 1179656 | tf_op jit(solution)/shard_map/ppermute | solution.py:28
  10.2 1.0 %copy-start = (f32[1,1,8,128,128]{4,3,2,1,0:T(8,128)S(1)}, f32[1,1,8,128,128]{4,3,2,1,0:T(8,128)}, u32[]{:S(2)}) copy-start(f32[1,1,8,128,128]{4,3,2,1,0:T(8,128)} %param.6) | copy-start | bytes 1572868
  11.3 0.9 %copy-start.1 = (bf16[1,128,1024]{2,1,0:T(8,128)(2,1)S(1)}, bf16[1,128,1024]{2,1,0:T(8,128)(2,1)}, u32[]{:S(2)}) copy-start(bf16[1,128,1024]{2,1,0:T(8,128)(2,1)} %param.5) | copy-start | bytes 786436
  13.6 21.3 %all-to-all-start = ((bf16[8,2,128,128]{3,2,1,0:T(8,128)(2,1)}), bf16[8,2,128,128]{3,2,1,0:T(8,128)(2,1)S(1)}, u32[]{:S(2)}, u32[]{:S(2)}) async-start(bf16[8,2,128,128]{3,2,1,0:T(8,128)(2,1)} %shard_map.60), calls=%async_computation | async-start | bytes 1048576 | tf_op jit(solution)/shard_map/all_to_all | solution.py:257
  18.8 16.7 %collective-permute-start.2 = (bf16[128,2048]{1,0:T(8,128)(2,1)}, bf16[128,2048]{1,0:T(8,128)(2,1)}, u32[]{:S(2)}, u32[]{:S(2)}) collective-permute-start(bf16[128,2048]{1,0:T(8,128)(2,1)} %bitcast.4.refs_1_), channel_id=1, source_target_pairs={{0,4},{4,0},{8,12},{12,8},{16,20},{20,16},{24,28},{28,24},{32,36},... | collective-permute-start | bytes 1572872 | tf_op jit(solution)/shard_map/ppermute | solution.py:24
  19.7 15.2 %collective-permute-start.5 = (bf16[64,2048]{1,0:T(8,128)(2,1)}, bf16[64,2048]{1,0:T(8,128)(2,1)S(1)}, u32[]{:S(2)}, u32[]{:S(2)}) collective-permute-start(bf16[64,2048]{1,0:T(8,128)(2,1)} %slice.8), channel_id=1, source_target_pairs={{0,8},{4,12},{8,16},{12,20},{16,24},{20,28},{24,0},{28,4},{32,40},... | collective-permute-start | bytes 786440 | tf_op jit(solution)/shard_map/ppermute | solution.py:24
  23.0 0.8 copy-start.2
  23.8 11.3 %collective-permute-start.6 = (bf16[64,2048]{1,0:T(8,128)(2,1)}, bf16[64,2048]{1,0:T(8,128)(2,1)S(1)}, u32[]{:S(2)}, u32[]{:S(2)}) collective-permute-start(bf16[64,2048]{1,0:T(8,128)(2,1)} %slice.9), channel_id=1, source_target_pairs={{0,24},{4,28},{8,0},{12,4},{16,8},{20,12},{24,16},{28,20},{32,56},... | collective-permute-start | bytes 786440 | tf_op jit(solution)/shard_map/ppermute | solution.py:24
  25.0 0.7 copy-start.4
  25.7 9.8 %collective-permute-start.3 = (bf16[128,2048]{1,0:T(8,128)(2,1)S(1)}, bf16[128,2048]{1,0:T(8,128)(2,1)}, u32[]{:S(2)}, u32[]{:S(2)}) collective-permute-start(bf16[128,2048]{1,0:T(8,128)(2,1)S(1)} %collective-permute-done.refs_2_), channel_id=1, source_target_pairs={{0,4},{4,0},{8,12},{12,8},{16,20},{20,16},{24,28},{28,24},{32,36},... | collective-permute-start | bytes 1572872 | tf_op jit(solution)/shard_map/ppermute | solution.py:24
  30.0 0.8 copy-start.6
  30.8 4.8 %collective-permute-start.4 = (bf16[128,2048]{1,0:T(8,128)(2,1)}, bf16[128,2048]{1,0:T(8,128)(2,1)}, u32[]{:S(2)}, u32[]{:S(2)}) collective-permute-start(bf16[128,2048]{1,0:T(8,128)(2,1)} %collective-permute-done.1.refs_3_), channel_id=1, source_target_pairs={{0,4},{4,0},{8,12},{12,8},{16,20},{20,16},{24,28},{28,24},{32,36},... | collective-permute-start | bytes 1572872 | tf_op jit(solution)/shard_map/ppermute | solution.py:24
  31.3 1.0 %copy-start.3 = (bf16[512,384]{1,0:T(8,128)(2,1)S(1)}, bf16[512,384]{1,0:T(8,128)(2,1)}, u32[]{:S(2)}) copy-start(bf16[512,384]{1,0:T(8,128)(2,1)} %copy-done.2) | copy-start | bytes 1179652
  32.3 1.0 %copy-start.5 = (bf16[512,384]{1,0:T(8,128)(2,1)S(1)}, bf16[512,384]{1,0:T(8,128)(2,1)}, u32[]{:S(2)}) copy-start(bf16[512,384]{1,0:T(8,128)(2,1)} %copy-done.4) | copy-start | bytes 1179652
  33.3 1.0 %copy-start.7 = (bf16[512,384]{1,0:T(8,128)(2,1)S(1)}, bf16[512,384]{1,0:T(8,128)(2,1)}, u32[]{:S(2)}) copy-start(bf16[512,384]{1,0:T(8,128)(2,1)} %copy-done.6) | copy-start | bytes 1179652
  35.0 2.5 %collective-permute-start.7 = (bf16[64,2048]{1,0:T(8,128)(2,1)S(1)}, bf16[64,2048]{1,0:T(8,128)(2,1)S(1)}, u32[]{:S(2)}, u32[]{:S(2)}) collective-permute-start(bf16[64,2048]{1,0:T(8,128)(2,1)S(1)} %collective-permute-done.5.refs_2_), channel_id=1, source_target_pairs={{0,4},{4,0},{8,12},{12,8},{16,20},{20,16},{24,28},{28,24},{32,36},... | collective-permute-start | bytes 786440 | tf_op jit(solution)/shard_map/ppermute | solution.py:24
  35.1 2.4 %collective-permute-start.8 = (bf16[64,2048]{1,0:T(8,128)(2,1)S(1)}, bf16[64,2048]{1,0:T(8,128)(2,1)S(1)}, u32[]{:S(2)}, u32[]{:S(2)}) collective-permute-start(bf16[64,2048]{1,0:T(8,128)(2,1)S(1)} %collective-permute-done.6.refs_3_), channel_id=1, source_target_pairs={{0,4},{4,0},{8,12},{12,8},{16,20},{20,16},{24,28},{28,24},{32,36},... | collective-permute-start | bytes 786440 | tf_op jit(solution)/shard_map/ppermute | solution.py:24
  41.1 7.8 %collective-permute-start.12 = (bf16[128,128]{1,0:T(8,128)(2,1)S(1)}, bf16[128,128]{1,0:T(8,128)(2,1)S(1)}, u32[]{:S(2)}, u32[]{:S(2)}) collective-permute-start(bf16[128,128]{1,0:T(8,128)(2,1)S(1)} %get-tuple-element.44), channel_id=1, source_target_pairs={{0,32},{4,36},{8,40},{12,44},{16,48},{20,52},{24,56},{28,60},{32,6... | collective-permute-start | bytes 98312 | tf_op jit(solution)/shard_map/ppermute | solution.py:24
  42.5 6.4 %collective-permute-start.13 = (bf16[128,128]{1,0:T(8,128)(2,1)S(1)}, bf16[128,128]{1,0:T(8,128)(2,1)S(1)}, u32[]{:S(2)}, u32[]{:S(2)}) collective-permute-start(bf16[128,128]{1,0:T(8,128)(2,1)S(1)} %get-tuple-element.44), channel_id=1, source_target_pairs={{0,64},{4,68},{8,72},{12,76},{16,80},{20,84},{24,88},{28,92},{32,9... | collective-permute-start | bytes 98312 | tf_op jit(solution)/shard_map/ppermute | solution.py:24
  45.1 3.8 %collective-permute-start.14 = (bf16[128,128]{1,0:T(8,128)(2,1)S(1)}, bf16[128,128]{1,0:T(8,128)(2,1)S(1)}, u32[]{:S(2)}, u32[]{:S(2)}) collective-permute-start(bf16[128,128]{1,0:T(8,128)(2,1)S(1)} %get-tuple-element.44), channel_id=1, source_target_pairs={{0,96},{4,100},{8,104},{12,108},{16,112},{20,116},{24,120},{28,124... | collective-permute-start | bytes 98312 | tf_op jit(solution)/shard_map/ppermute | solution.py:24
  49.9 7.6 %collective-permute-start.19 = (bf16[2048,384]{1,0:T(8,128)(2,1)S(1)}, bf16[2048,384]{1,0:T(8,128)(2,1)S(1)}, u32[]{:S(2)}, u32[]{:S(2)}) collective-permute-start(bf16[2048,384]{1,0:T(8,128)(2,1)S(1)} %shard_map.61.refs_6_.refs_3_), channel_id=1, source_target_pairs={{0,4},{4,0},{8,12},{12,8},{16,20},{20,16},{24,28},{28,24},{32,36},... | collective-permute-start | bytes 4718600 | tf_op jit(solution)/shard_map/ppermute | solution.py:24
  50.9 6.6 %collective-permute-start.18 = (bf16[4,128,384]{2,1,0:T(8,128)(2,1)S(1)}, bf16[4,128,384]{2,1,0:T(8,128)(2,1)S(1)}, u32[]{:S(2)}, u32[]{:S(2)}) collective-permute-start(bf16[4,128,384]{2,1,0:T(8,128)(2,1)S(1)} %get-tuple-element.51), channel_id=1, source_target_pairs={{0,4},{4,0},{8,12},{12,8},{16,20},{20,16},{24,28},{28,24},{32,36},... | collective-permute-start | bytes 1179656 | tf_op jit(solution)/shard_map/ppermute | solution.py:24
  54.2 10.1 %collective-permute-start.15 = (bf16[4,8,16,384]{3,2,1,0:T(8,128)(2,1)S(1)}, bf16[4,8,16,384]{3,2,1,0:T(8,128)(2,1)S(1)}, u32[]{:S(2)}, u32[]{:S(2)}) collective-permute-start(bf16[4,8,16,384]{3,2,1,0:T(8,128)(2,1)S(1)} %get-tuple-element.47), channel_id=1, source_target_pairs={{0,1},{1,2},{2,3},{3,0},{4,36},{5,37},{6,38},{7,39},{8,9},{9,10},{... | collective-permute-start | bytes 1179656 | tf_op jit(solution)/shard_map/ppermute | solution.py:40
  54.7 12.5 %collective-permute-start.16 = (bf16[4,8,16,384]{3,2,1,0:T(8,128)(2,1)S(1)}, bf16[4,8,16,384]{3,2,1,0:T(8,128)(2,1)S(1)}, u32[]{:S(2)}, u32[]{:S(2)}) collective-permute-start(bf16[4,8,16,384]{3,2,1,0:T(8,128)(2,1)S(1)} %get-tuple-element.48), channel_id=1, source_target_pairs={{0,2},{1,3},{2,0},{3,1},{4,68},{5,69},{6,70},{7,71},{8,10},{9,11},... | collective-permute-start | bytes 1179656 | tf_op jit(solution)/shard_map/ppermute | solution.py:40
  57.5 9.7 %collective-permute-start.17 = (bf16[4,8,16,384]{3,2,1,0:T(8,128)(2,1)S(1)}, bf16[4,8,16,384]{3,2,1,0:T(8,128)(2,1)S(1)}, u32[]{:S(2)}, u32[]{:S(2)}) collective-permute-start(bf16[4,8,16,384]{3,2,1,0:T(8,128)(2,1)S(1)} %get-tuple-element.49), channel_id=1, source_target_pairs={{0,3},{1,0},{2,1},{3,2},{4,100},{5,101},{6,102},{7,103},{8,11},{9,... | collective-permute-start | bytes 1179656 | tf_op jit(solution)/shard_map/ppermute | solution.py:40
  59.2 8.8 %collective-permute-start.23 = (bf16[64,2048]{1,0:T(8,128)(2,1)S(1)}, bf16[64,2048]{1,0:T(8,128)(2,1)S(1)}, u32[]{:S(2)}, u32[]{:S(2)}) collective-permute-start(bf16[64,2048]{1,0:T(8,128)(2,1)S(1)} %get-tuple-element.53.refs_5_), channel_id=1, source_target_pairs={{0,8},{4,12},{8,16},{12,20},{16,24},{20,28},{24,0},{28,4},{32,40},... | collective-permute-start | bytes 786440 | tf_op jit(solution)/shard_map/ppermute | solution.py:24
  59.3 8.7 %collective-permute-start.24 = (bf16[64,2048]{1,0:T(8,128)(2,1)S(1)}, bf16[64,2048]{1,0:T(8,128)(2,1)S(1)}, u32[]{:S(2)}, u32[]{:S(2)}) collective-permute-start(bf16[64,2048]{1,0:T(8,128)(2,1)S(1)} %get-tuple-element.61), channel_id=1, source_target_pairs={{0,24},{4,28},{8,0},{12,4},{16,8},{20,12},{24,16},{28,20},{32,56},... | collective-permute-start | bytes 786440 | tf_op jit(solution)/shard_map/ppermute | solution.py:24
  68.7 21.5 %collective-permute-start.25 = (bf16[128,2048]{1,0:T(8,128)(2,1)S(1)}, bf16[128,2048]{1,0:T(8,128)(2,1)S(1)}, u32[]{:S(2)}, u32[]{:S(2)}) collective-permute-start(bf16[128,2048]{1,0:T(8,128)(2,1)S(1)} %get-tuple-element.62), channel_id=1, source_target_pairs={{0,8},{4,12},{8,16},{12,20},{16,24},{20,28},{24,0},{28,4},{32,40},... | collective-permute-start | bytes 1572872 | tf_op jit(solution)/shard_map/ppermute | solution.py:24
  68.8 21.4 %collective-permute-start.26 = (bf16[128,2048]{1,0:T(8,128)(2,1)S(1)}, bf16[128,2048]{1,0:T(8,128)(2,1)S(1)}, u32[]{:S(2)}, u32[]{:S(2)}) collective-permute-start(bf16[128,2048]{1,0:T(8,128)(2,1)S(1)} %get-tuple-element.63), channel_id=1, source_target_pairs={{0,24},{4,28},{8,0},{12,4},{16,8},{20,12},{24,16},{28,20},{32,56},... | collective-permute-start | bytes 1572872 | tf_op jit(solution)/shard_map/ppermute | solution.py:24
  71.4 5.9 %collective-permute-start.20 = (bf16[8,16,384]{2,1,0:T(8,128)(2,1)S(1)}, bf16[8,16,384]{2,1,0:T(8,128)(2,1)S(1)}, u32[]{:S(2)}, u32[]{:S(2)}) collective-permute-start(bf16[8,16,384]{2,1,0:T(8,128)(2,1)S(1)} %get-tuple-element.56), channel_id=1, source_target_pairs={{0,32},{1,33},{2,34},{3,35},{4,5},{5,6},{6,7},{7,4},{8,40},{9,41},... | collective-permute-start | bytes 294920 | tf_op jit(solution)/shard_map/ppermute | solution.py:40
  72.4 6.9 %collective-permute-start.21 = (bf16[8,16,384]{2,1,0:T(8,128)(2,1)S(1)}, bf16[8,16,384]{2,1,0:T(8,128)(2,1)S(1)}, u32[]{:S(2)}, u32[]{:S(2)}) collective-permute-start(bf16[8,16,384]{2,1,0:T(8,128)(2,1)S(1)} %get-tuple-element.57), channel_id=1, source_target_pairs={{0,64},{1,65},{2,66},{3,67},{4,6},{5,7},{6,4},{7,5},{8,72},{9,73},... | collective-permute-start | bytes 294920 | tf_op jit(solution)/shard_map/ppermute | solution.py:40
  76.2 3.8 %collective-permute-start.22 = (bf16[8,16,384]{2,1,0:T(8,128)(2,1)S(1)}, bf16[8,16,384]{2,1,0:T(8,128)(2,1)S(1)}, u32[]{:S(2)}, u32[]{:S(2)}) collective-permute-start(bf16[8,16,384]{2,1,0:T(8,128)(2,1)S(1)} %get-tuple-element.58), channel_id=1, source_target_pairs={{0,96},{1,97},{2,98},{3,99},{4,7},{5,4},{6,5},{7,6},{8,104},{9,105... | collective-permute-start | bytes 294920 | tf_op jit(solution)/shard_map/ppermute | solution.py:40

commit v11 on v10

--- a/solution.py
+++ b/solution.py
@@ -117,6 +117,11 @@
     parts, xa = refs[:6], refs[6]
     for i, part in enumerate(parts):
         xa[i * TOK : (i + 1) * TOK, :] = part[...]
+
+
+def halve(idx, x1, x3, low, high):
+    low[...] = x1[:64, :]
+    high[...] = x3[64:, :]
 
 
 def project(idx, xa, x2a, x2b, m2a, m2b, wkeep, gs, qkv, r, total, xb):
@@ -256,7 +261,8 @@
     )
     gs = lax.all_to_all(bundle, "ctx", 0, 0, axis_index_groups=rows_y)
     w2, w1, w3 = (x_hop(own_w, s) for s in (2, 1, -1))
-    x2a, x2b = ctx_hop(x1[:64], dz=1), ctx_hop(x3[64:], dz=-1)
+    low, high = call(halve, [shape((64, 2048), BF)] * 2, [idx, x1, x3], limit=6, deps=())
+    x2a, x2b = ctx_hop(low, dz=1), ctx_hop(high, dz=-1)
     (own_w,) = call(relay, [shape((2048, 384), BF)], [idx, own_w, w1, w3, w2], flops=1 << 33, limit=6)
     first = [x, x1, x3]
     first += [ctx_hop(p, dc=1) for p in first]

time: 92.2 us -> 92.5 us (level)
  local copies, waits for them, and re-layouts: 10.7 us -> 8.28 us
  Pallas kernels: 21.2 us -> 23 us
    slice x2 -> x0, local copies, waits for them, and re-layouts: 2.38 us -> none  [body(): x2a, x2b = (ctx_hop(x1[:64], dz=1), ctx_hop(x3[64:], dz=-1))]
    pallas_call x12 -> x13, Pallas kernels: 21.2 us -> 23 us  [call(): pl.pallas_call(run, out_shape=list(outs), in_specs=[pl.BlockSpec(memory_s...]
    ppermute x18, starting transfers between devices: 24.9 us -> 25.9 us  [ctx_hop(): return lax.ppermute(block, 'ctx', route)]
  transfers between devices with their start and end apart: 28 -> 28, of which waited for: 4 -> 5; matrix products, arithmetic and copies ran while one was open for 4% -> 1% of each run, Pallas kernels for 16% -> 17%
where the time goes in v11:
time: 92.5 us; the launch traced here: 92 us
  starting transfers between devices  42.8 us (46%)
  Pallas kernels  23 us (25%)
  blocking collectives  10.1 us (11%)
  local copies, waits for them, and re-layouts  8.28 us (9%)
  waiting for transfers between devices  6.82 us (7%)
    ppermute x18, starting transfers between devices, ctx_hop(): return lax.ppermute(block, 'ctx', route)  25.9 us
    pallas_call x13, Pallas kernels, call(): pl.pallas_call(run, out_shape=list(outs), in_specs=[pl.BlockSpec(memory_s...  23 us
    all_to_all x1, blocking collectives, body(): owned = lax.all_to_all(owned, 'ctx', 0, 0, axis_index_groups=rows_y)  10.1 us
    ppermute x6, starting transfers between devices, plane_hop(): return lax.ppermute(block, ('ctx', 'zero'), route)  8.09 us
    unnamed x16, local copies, waits for them, and re-layouts  7.22 us
    ppermute x6, waiting for transfers between devices, plane_hop(): return lax.ppermute(block, ('ctx', 'zero'), route)  6.65 us
    all_to_all x1, starting transfers between devices, body(): gs = lax.all_to_all(bundle, 'ctx', 0, 0, axis_index_groups=rows_y)  5.19 us
    ppermute x3, starting transfers between devices, x_hop(): return lax.ppermute(block, 'zero', [(i, (i + dx) % NX) for i in range(NX)])  3.67 us
  transfers between devices with their start and end apart: 28, of which 5 were waited for; matrix products, arithmetic and copies ran while one was open for 1% of the time, Pallas kernels for 17%

profile of v11, /device:TPU:1, one launch (start us, length us, event | category | flops | bytes accessed | tf_op | source)
XLA Modules:
  0.0 92.0 jit_solution(11207863689131610797)
XLA Ops:
  0.6 2.5 %collective-permute-start = (bf16[128,2048]{1,0:T(8,128)(2,1)}, bf16[128,2048]{1,0:T(8,128)(2,1)S(1)}, u32[]{:S(2)}, u32[]{:S(2)}) collective-permute-start(bf16[128,2048]{1,0:T(8,128)(2,1)} %bitcast.4.refs_1_), channel_id=1, source_target_pairs={{0,8},{4,12},{8,16},{12,20},{16,24},{20,28},{24,0},{28,4},{32,40},... | collective-permute-start | bytes 1572872 | tf_op jit(solution)/shard_map/ppermute | solution.py:24
  3.2 2.2 %collective-permute-start.1 = (bf16[128,2048]{1,0:T(8,128)(2,1)}, bf16[128,2048]{1,0:T(8,128)(2,1)S(1)}, u32[]{:S(2)}, u32[]{:S(2)}) collective-permute-start(bf16[128,2048]{1,0:T(8,128)(2,1)} %bitcast.4.refs_1_), channel_id=1, source_target_pairs={{0,24},{4,28},{8,0},{12,4},{16,8},{20,12},{24,16},{28,20},{32,56},... | collective-permute-start | bytes 1572872 | tf_op jit(solution)/shard_map/ppermute | solution.py:24
  5.4 1.1 %constant_dynamic-slice_fusion.2 = (bf16[512,128]{1,0:T(8,128)(2,1)S(1)}, bf16[512,128]{1,0:T(8,128)(2,1)S(1)}, bf16[512,128]{1,0:T(8,128)(2,1)S(1)}) fusion(bf16[512,3072]{1,0:T(8,128)(2,1)} %param.7, s32[]{:T(128)S(6)} %select_n.31, s32[]{:T(128)S(6)} %select_n.33, s32[]{:T(128)S(6)} %select_n.32), kind=kLoop, calls=%fused_computation.4 | loop fusion | bytes 786444 | tf_op jit(solution)/shard_map/dynamic_slice | solution.py:257
  6.5 2.5 %collective-permute-start.10 = (bf16[512,384]{1,0:T(8,128)(2,1)S(1)}, bf16[512,384]{1,0:T(8,128)(2,1)S(1)}, u32[]{:S(2)}, u32[]{:S(2)}) collective-permute-start(bf16[512,384]{1,0:T(8,128)(2,1)S(1)} %pad_maximum_fusion.refs_1_), channel_id=1, source_target_pairs={{0,3},{1,0},{2,1},{3,2},{4,7},{5,4},{6,5},{7,6},{8,11},{9,8},{10,9... | collective-permute-start | bytes 1179656 | tf_op jit(solution)/shard_map/ppermute | solution.py:28
  9.0 0.5 collective-permute-start.11
  9.6 0.6 collective-permute-start.9
  10.3 1.0 %copy-done = f32[1,1,8,128,128]{4,3,2,1,0:T(8,128)S(1)} copy-done((f32[1,1,8,128,128]{4,3,2,1,0:T(8,128)S(1)}, f32[1,1,8,128,128]{4,3,2,1,0:T(8,128)}, u32[]{:S(2)}) %copy-start) | copy-done | bytes 524312
  11.3 0.9 %copy-done.1 = bf16[1,128,1024]{2,1,0:T(8,128)(2,1)S(1)} copy-done((bf16[1,128,1024]{2,1,0:T(8,128)(2,1)S(1)}, bf16[1,128,1024]{2,1,0:T(8,128)(2,1)}, u32[]{:S(2)}) %copy-start.1) | copy-done | bytes 262168
  12.2 1.4 %shard_map.61 = bf16[8,2,128,128]{3,2,1,0:T(8,128)(2,1)} custom-call(s32[4]{0:T(128)S(1)} %pad_add_fusion.refs_0_, bf16[128,1024]{1,0:T(8,128)(2,1)S(1)} %bitcast.9, f32[8,128,128]{2,1,0:T(8,128)S(1)} %bitcast.8), custom_call_target="tpu_custom_call" | custom-call | bytes 1310736 | tf_op jit(solution)/shard_map/pallas_call | solution.py:63
  13.6 5.2 %all-to-all-start = ((bf16[8,2,128,128]{3,2,1,0:T(8,128)(2,1)}), bf16[8,2,128,128]{3,2,1,0:T(8,128)(2,1)S(1)}, u32[]{:S(2)}, u32[]{:S(2)}) async-start(bf16[8,2,128,128]{3,2,1,0:T(8,128)(2,1)} %shard_map.61), calls=%async_computation | async-start | bytes 1048576 | tf_op jit(solution)/shard_map/all_to_all | solution.py:262
  19.0 1.4 %shard_map.60 = (bf16[64,2048]{1,0:T(8,128)(2,1)}, bf16[64,2048]{1,0:T(8,128)(2,1)}) custom-call(s32[4]{0:T(128)S(1)} %pad_add_fusion.refs_0_, bf16[128,2048]{1,0:T(8,128)(2,1)S(1)} %collective-permute-done.refs_2_.refs_1_, bf16[128,2048]{1,0:T(8,128)(2,1)S(1)} %collective-permute-done.1.refs_3_.refs_2_), custom_call_target="tpu_custom_call" | custom-call | bytes 1572880 | tf_op jit(solution)/shard_map/pallas_call | solution.py:63
  20.4 1.6 %collective-permute-start.5 = (bf16[64,2048]{1,0:T(8,128)(2,1)}, bf16[64,2048]{1,0:T(8,128)(2,1)}, u32[]{:S(2)}, u32[]{:S(2)}) collective-permute-start(bf16[64,2048]{1,0:T(8,128)(2,1)} %get-tuple-element.36), channel_id=1, source_target_pairs={{0,8},{4,12},{8,16},{12,20},{16,24},{20,28},{24,0},{28,4},{32,40},... | collective-permute-start | bytes 786440 | tf_op jit(solution)/shard_map/ppermute | solution.py:24
  22.0 0.7 copy-done.2
  22.7 1.2 %collective-permute-start.6 = (bf16[64,2048]{1,0:T(8,128)(2,1)}, bf16[64,2048]{1,0:T(8,128)(2,1)}, u32[]{:S(2)}, u32[]{:S(2)}) collective-permute-start(bf16[64,2048]{1,0:T(8,128)(2,1)} %get-tuple-element.37), channel_id=1, source_target_pairs={{0,24},{4,28},{8,0},{12,4},{16,8},{20,12},{24,16},{28,20},{32,56},... | collective-permute-start | bytes 786440 | tf_op jit(solution)/shard_map/ppermute | solution.py:24
  24.0 0.8 copy-done.4
  24.7 5.3 %collective-permute-start.3 = (bf16[128,2048]{1,0:T(8,128)(2,1)S(1)}, bf16[128,2048]{1,0:T(8,128)(2,1)}, u32[]{:S(2)}, u32[]{:S(2)}) collective-permute-start(bf16[128,2048]{1,0:T(8,128)(2,1)S(1)} %collective-permute-done.refs_2_.refs_1_), channel_id=1, source_target_pairs={{0,4},{4,0},{8,12},{12,8},{16,20},{20,16},{24,28},{28,24},{32,36},... | collective-permute-start | bytes 1572872 | tf_op jit(solution)/shard_map/ppermute | solution.py:24
  30.1 0.7 copy-done.6
  30.9 0.4 collective-permute-start.4
  31.3 1.0 %copy-done.3 = bf16[512,384]{1,0:T(8,128)(2,1)S(1)} copy-done((bf16[512,384]{1,0:T(8,128)(2,1)S(1)}, bf16[512,384]{1,0:T(8,128)(2,1)}, u32[]{:S(2)}) %copy-start.3) | copy-done | bytes 393240
  32.2 1.0 %copy-done.5 = bf16[512,384]{1,0:T(8,128)(2,1)S(1)} copy-done((bf16[512,384]{1,0:T(8,128)(2,1)S(1)}, bf16[512,384]{1,0:T(8,128)(2,1)}, u32[]{:S(2)}) %copy-start.5) | copy-done | bytes 393240
  33.2 1.0 %copy-done.7 = bf16[512,384]{1,0:T(8,128)(2,1)S(1)} copy-done((bf16[512,384]{1,0:T(8,128)(2,1)S(1)}, bf16[512,384]{1,0:T(8,128)(2,1)}, u32[]{:S(2)}) %copy-start.7) | copy-done | bytes 393240
  34.2 0.7 shard_map.62.refs_6_.refs_3_
  35.2 0.4 collective-permute-start.8
  35.6 1.7 %shard_map.59.refs_1_ = bf16[768,2048]{1,0:T(8,128)(2,1)S(1)} custom-call(s32[4]{0:T(128)S(1)} %pad_add_fusion.refs_0_, bf16[128,2048]{1,0:T(8,128)(2,1)} %bitcast.4.refs_1_, bf16[128,2048]{1,0:T(8,128)(2,1)S(1)} %collective-permute-done.refs_2_.refs_1_, bf16[128,2048]{1,0:T(8,128)(2,1)S(1)} %collective-permute-done.1.refs_3_.refs_2_, ...), custom_call_target="tpu_custom_call" | custom-call | flops 8589934592 | bytes 6291472 | tf_op jit(solution)/shard_map/pallas_call | solution.py:63
  37.3 4.1 %shard_map.63 = (bf16[1024,384]{1,0:T(8,128)(2,1)S(1)}, f32[8,128,128]{2,1,0:T(8,128)S(1)}, bf16[128,128]{1,0:T(8,128)(2,1)S(1)}, bf16[256,2048]{1,0:T(8,128)(2,1)S(1)}) custom-call(s32[4]{0:T(128)S(1)} %pad_add_fusion.refs_0_, bf16[768,2048]{1,0:T(8,128)(2,1)S(1)} %shard_map.59.refs_1_, bf16[64,2048]{1,0:T(8,128)(2,1)} %collective-permute-done.5.refs_2_, ...), custom_call_target="tpu_custom_call" | custom-call | flops 1610612736 | bytes 8683536 | tf_op jit(solution)/shard_map/pallas_call | solution.py:63
  41.4 1.4 %collective-permute-start.12 = (bf16[128,128]{1,0:T(8,128)(2,1)S(1)}, bf16[128,128]{1,0:T(8,128)(2,1)S(1)}, u32[]{:S(2)}, u32[]{:S(2)}) collective-permute-start(bf16[128,128]{1,0:T(8,128)(2,1)S(1)} %get-tuple-element.48), channel_id=1, source_target_pairs={{0,32},{4,36},{8,40},{12,44},{16,48},{20,52},{24,56},{28,60},{32,6... | collective-permute-start | bytes 98312 | tf_op jit(solution)/shard_map/ppermute | solution.py:24
  42.8 2.6 %collective-permute-start.13 = (bf16[128,128]{1,0:T(8,128)(2,1)S(1)}, bf16[128,128]{1,0:T(8,128)(2,1)S(1)}, u32[]{:S(2)}, u32[]{:S(2)}) collective-permute-start(bf16[128,128]{1,0:T(8,128)(2,1)S(1)} %get-tuple-element.48), channel_id=1, source_target_pairs={{0,64},{4,68},{8,72},{12,76},{16,80},{20,84},{24,88},{28,92},{32,9... | collective-permute-start | bytes 98312 | tf_op jit(solution)/shard_map/ppermute | solution.py:24
  45.4 1.1 %collective-permute-start.14 = (bf16[128,128]{1,0:T(8,128)(2,1)S(1)}, bf16[128,128]{1,0:T(8,128)(2,1)S(1)}, u32[]{:S(2)}, u32[]{:S(2)}) collective-permute-start(bf16[128,128]{1,0:T(8,128)(2,1)S(1)} %get-tuple-element.48), channel_id=1, source_target_pairs={{0,96},{4,100},{8,104},{12,108},{16,112},{20,116},{24,120},{28,124... | collective-permute-start | bytes 98312 | tf_op jit(solution)/shard_map/ppermute | solution.py:24
  46.5 2.7 %shard_map.64 = (bf16[1024,128]{1,0:T(8,128)(2,1)S(1)}, f32[1024,128]{1,0:T(8,128)S(1)}, f32[1024,128]{1,0:T(8,128)S(1)}, bf16[2048,1024]{1,0:T(8,128)(2,1)S(1)}) custom-call(s32[4]{0:T(128)S(1)} %pad_add_fusion.refs_0_, bf16[768,2048]{1,0:T(8,128)(2,1)S(1)} %shard_map.59.refs_1_, bf16[256,2048]{1,0:T(8,128)(2,1)S(1)} %get-tuple-element.41.refs_2_, ...), custom_call_target="tpu_custom_call" | custom-call | flops 402653184 | bytes 11010064 | tf_op jit(solution)/shard_map/pallas_call | solution.py:63
  49.2 1.0 %shard_map.65 = (bf16[1024,384]{1,0:T(8,128)(2,1)S(1)}, bf16[4,128,384]{2,1,0:T(8,128)(2,1)S(1)}, bf16[4,128,384]{2,1,0:T(8,128)(2,1)S(1)}) custom-call(s32[4]{0:T(128)S(1)} %pad_add_fusion.refs_0_, bf16[1024,384]{1,0:T(8,128)(2,1)S(1)} %get-tuple-element.42.refs_4_.refs_1_, bf16[1024,128]{1,0:T(8,128)(2,1)S(1)} %get-tuple-element.44.refs_2_, ...), custom_call_target="tpu_custom_call" | custom-call | flops 100663296 | bytes 4292624 | tf_op jit(solution)/shard_map/pallas_call | solution.py:63
  50.2 1.1 %collective-permute-start.19 = (bf16[2048,384]{1,0:T(8,128)(2,1)S(1)}, bf16[2048,384]{1,0:T(8,128)(2,1)S(1)}, u32[]{:S(2)}, u32[]{:S(2)}) collective-permute-start(bf16[2048,384]{1,0:T(8,128)(2,1)S(1)} %shard_map.62.refs_6_.refs_3_), channel_id=1, source_target_pairs={{0,4},{4,0},{8,12},{12,8},{16,20},{20,16},{24,28},{28,24},{32,36},... | collective-permute-start | bytes 4718600 | tf_op jit(solution)/shard_map/ppermute | solution.py:24
  51.6 3.0 %shard_map.66 = (bf16[4,8,16,384]{3,2,1,0:T(8,128)(2,1)S(1)}, bf16[4,8,16,384]{3,2,1,0:T(8,128)(2,1)S(1)}, bf16[4,8,16,384]{3,2,1,0:T(8,128)(2,1)S(1)}, bf16[4,8,16,384]{3,2,1,0:T(8,128)(2,1)S(1)}) custom-call(s32[4]{0:T(128)S(1)} %pad_add_fusion.refs_0_, bf16[2048,1024]{1,0:T(8,128)(2,1)S(1)} %get-tuple-element.43.refs_1_, ...), custom_call_target="tpu_custom_call" | custom-call | flops 1610612736 | bytes 6553616 | tf_op jit(solution)/shard_map/pallas_call | solution.py:63
  54.6 0.5 collective-permute-start.15
  55.0 2.9 %collective-permute-start.16 = (bf16[4,8,16,384]{3,2,1,0:T(8,128)(2,1)S(1)}, bf16[4,8,16,384]{3,2,1,0:T(8,128)(2,1)S(1)}, u32[]{:S(2)}, u32[]{:S(2)}) collective-permute-start(bf16[4,8,16,384]{3,2,1,0:T(8,128)(2,1)S(1)} %get-tuple-element.52), channel_id=1, source_target_pairs={{0,2},{1,3},{2,0},{3,1},{4,68},{5,69},{6,70},{7,71},{8,10},{9,11},... | collective-permute-start | bytes 1179656 | tf_op jit(solution)/shard_map/ppermute | solution.py:40
  57.9 1.6 %shard_map.67 = (bf16[64,2048]{1,0:T(8,128)(2,1)S(1)}, bf16[64,2048]{1,0:T(8,128)(2,1)S(1)}) custom-call(s32[4]{0:T(128)S(1)} %pad_add_fusion.refs_0_, bf16[4,128,384]{2,1,0:T(8,128)(2,1)S(1)} %get-tuple-element.54.refs_1_, bf16[4,128,384]{2,1,0:T(8,128)(2,1)S(1)} %collective-permute-done.18.refs_2_, bf16[2048,384]{1,0:T(8,128)(2,1)S(1)} %shard_map.62.refs_6_.refs_3_, ...), custom_call_target="tpu_custom_call" | custom-call | flops 402653184 | bytes 4456464 | tf_op jit(solution)/shard_map/pallas_call | solution.py:63
  59.7 2.7 %collective-permute-start.24 = (bf16[64,2048]{1,0:T(8,128)(2,1)S(1)}, bf16[64,2048]{1,0:T(8,128)(2,1)S(1)}, u32[]{:S(2)}, u32[]{:S(2)}) collective-permute-start(bf16[64,2048]{1,0:T(8,128)(2,1)S(1)} %get-tuple-element.65), channel_id=1, source_target_pairs={{0,24},{4,28},{8,0},{12,4},{16,8},{20,12},{24,16},{28,20},{32,56},... | collective-permute-start | bytes 786440 | tf_op jit(solution)/shard_map/ppermute | solution.py:24
  62.3 2.4 %shard_map.68 = (f32[128,2048]{1,0:T(8,128)S(1)}, bf16[128,2048]{1,0:T(8,128)(2,1)S(1)}, bf16[128,2048]{1,0:T(8,128)(2,1)S(1)}) custom-call(s32[4]{0:T(128)S(1)} %pad_add_fusion.refs_0_, bf16[4,128,384]{2,1,0:T(8,128)(2,1)S(1)} %get-tuple-element.54.refs_1_, bf16[4,128,384]{2,1,0:T(8,128)(2,1)S(1)} %collective-permute-done.18.refs_2_, ...), custom_call_target="tpu_custom_call" | custom-call | flops 1610612736 | bytes 6029328 | tf_op jit(solution)/shard_map/pallas_call | solution.py:63
  64.7 2.9 %collective-permute-done.16.refs_3_ = bf16[4,8,16,384]{3,2,1,0:T(8,128)(2,1)S(1)} collective-permute-done((bf16[4,8,16,384]{3,2,1,0:T(8,128)(2,1)S(1)}, bf16[4,8,16,384]{3,2,1,0:T(8,128)(2,1)S(1)}, u32[]{:S(2)}, u32[]{:S(2)}) %collective-permute-start.16) | collective-permute-done | bytes 393248 | tf_op jit(solution)/shard_map/ppermute | solution.py:40
  67.6 0.7 shard_map.69
  68.4 0.7 shard_map.70
  69.2 2.7 %collective-permute-start.26 = (bf16[128,2048]{1,0:T(8,128)(2,1)S(1)}, bf16[128,2048]{1,0:T(8,128)(2,1)S(1)}, u32[]{:S(2)}, u32[]{:S(2)}) collective-permute-start(bf16[128,2048]{1,0:T(8,128)(2,1)S(1)} %get-tuple-element.67), channel_id=1, source_target_pairs={{0,24},{4,28},{8,0},{12,4},{16,8},{20,12},{24,16},{28,20},{32,56},... | collective-permute-start | bytes 1572872 | tf_op jit(solution)/shard_map/ppermute | solution.py:24
  71.8 1.0 %collective-permute-start.20 = (bf16[8,16,384]{2,1,0:T(8,128)(2,1)S(1)}, bf16[8,16,384]{2,1,0:T(8,128)(2,1)S(1)}, u32[]{:S(2)}, u32[]{:S(2)}) collective-permute-start(bf16[8,16,384]{2,1,0:T(8,128)(2,1)S(1)} %get-tuple-element.60), channel_id=1, source_target_pairs={{0,32},{1,33},{2,34},{3,35},{4,5},{5,6},{6,7},{7,4},{8,40},{9,41},... | collective-permute-start | bytes 294920 | tf_op jit(solution)/shard_map/ppermute | solution.py:40
  72.8 3.8 %collective-permute-start.21 = (bf16[8,16,384]{2,1,0:T(8,128)(2,1)S(1)}, bf16[8,16,384]{2,1,0:T(8,128)(2,1)S(1)}, u32[]{:S(2)}, u32[]{:S(2)}) collective-permute-start(bf16[8,16,384]{2,1,0:T(8,128)(2,1)S(1)} %get-tuple-element.61), channel_id=1, source_target_pairs={{0,64},{1,65},{2,66},{3,67},{4,6},{5,7},{6,4},{7,5},{8,72},{9,73},... | collective-permute-start | bytes 294920 | tf_op jit(solution)/shard_map/ppermute | solution.py:40
  76.6 1.1 %collective-permute-done.20 = bf16[8,16,384]{2,1,0:T(8,128)(2,1)S(1)} collective-permute-done((bf16[8,16,384]{2,1,0:T(8,128)(2,1)S(1)}, bf16[8,16,384]{2,1,0:T(8,128)(2,1)S(1)}, u32[]{:S(2)}, u32[]{:S(2)}) %collective-permute-start.20) | collective-permute-done | bytes 98336 | tf_op jit(solution)/shard_map/ppermute | solution.py:40
  77.7 1.9 %collective-permute-done.21 = bf16[8,16,384]{2,1,0:T(8,128)(2,1)S(1)} collective-permute-done((bf16[8,16,384]{2,1,0:T(8,128)(2,1)S(1)}, bf16[8,16,384]{2,1,0:T(8,128)(2,1)S(1)}, u32[]{:S(2)}, u32[]{:S(2)}) %collective-permute-start.21) | collective-permute-done | bytes 98336 | tf_op jit(solution)/shard_map/ppermute | solution.py:40
  79.6 0.7 collective-permute-done.22
  80.4 10.1 %all_to_all.10.refs_1_ = bf16[8,16,384]{2,1,0:T(8,128)(2,1)S(1)} all-to-all(bf16[8,16,384]{2,1,0:T(8,128)(2,1)S(1)} %add_convert_fusion), channel_id=1, replica_groups={{0,4,8,12,16,20,24,28},{32,36,40,44,48,52,56,60},{64,68,72,76,80,84,88,..., dimensions={0} | all-to-all | bytes 196608 | tf_op jit(solution)/shard_map/all_to_all | solution.py:333
  90.5 1.5 %shard_map.71 = (f32[16,3072]{1,0:T(8,128)}, bf16[128,2048]{1,0:T(8,128)(2,1)}) custom-call(s32[4]{0:T(128)S(1)} %pad_add_fusion.refs_0_, bf16[8,16,384]{2,1,0:T(8,128)(2,1)S(1)} %all_to_all.10.refs_1_, f32[128,2048]{1,0:T(8,128)S(1)} %get-tuple-element.58.refs_5_.refs_2_, bf16[128,2048]{1,0:T(8,128)(2,1)S(1)} %collective-permute-done.25.refs_3_, ...), custom_call_target="tpu_custom_call" | custom-call | bytes 2916368 | tf_op jit(solution)/shard_map/pallas_call | solution.py:63
  (42 shorter events, 1.2 us)
Async XLA Ops:
  0.6 18.2 %collective-permute-start = (bf16[128,2048]{1,0:T(8,128)(2,1)}, bf16[128,2048]{1,0:T(8,128)(2,1)S(1)}, u32[]{:S(2)}, u32[]{:S(2)}) collective-permute-start(bf16[128,2048]{1,0:T(8,128)(2,1)} %bitcast.4.refs_1_), channel_id=1, source_target_pairs={{0,8},{4,12},{8,16},{12,20},{16,24},{20,28},{24,0},{28,4},{32,40},... | collective-permute-start | bytes 1572872 | tf_op jit(solution)/shard_map/ppermute | solution.py:24
  3.2 15.9 %collective-permute-start.1 = (bf16[128,2048]{1,0:T(8,128)(2,1)}, bf16[128,2048]{1,0:T(8,128)(2,1)S(1)}, u32[]{:S(2)}, u32[]{:S(2)}) collective-permute-start(bf16[128,2048]{1,0:T(8,128)(2,1)} %bitcast.4.refs_1_), channel_id=1, source_target_pairs={{0,24},{4,28},{8,0},{12,4},{16,8},{20,12},{24,16},{28,20},{32,56},... | collective-permute-start | bytes 1572872 | tf_op jit(solution)/shard_map/ppermute | solution.py:24
  6.5 15.5 %collective-permute-start.10 = (bf16[512,384]{1,0:T(8,128)(2,1)S(1)}, bf16[512,384]{1,0:T(8,128)(2,1)S(1)}, u32[]{:S(2)}, u32[]{:S(2)}) collective-permute-start(bf16[512,384]{1,0:T(8,128)(2,1)S(1)} %pad_maximum_fusion.refs_1_), channel_id=1, source_target_pairs={{0,3},{1,0},{2,1},{3,2},{4,7},{5,4},{6,5},{7,6},{8,11},{9,8},{10,9... | collective-permute-start | bytes 1179656 | tf_op jit(solution)/shard_map/ppermute | solution.py:28
  9.0 14.9 %collective-permute-start.11 = (bf16[512,384]{1,0:T(8,128)(2,1)S(1)}, bf16[512,384]{1,0:T(8,128)(2,1)S(1)}, u32[]{:S(2)}, u32[]{:S(2)}) collective-permute-start(bf16[512,384]{1,0:T(8,128)(2,1)S(1)} %pad_maximum_fusion.refs_1_), channel_id=1, source_target_pairs={{0,2},{1,3},{2,0},{3,1},{4,6},{5,7},{6,4},{7,5},{8,10},{9,11},{10,... | collective-permute-start | bytes 1179656 | tf_op jit(solution)/shard_map/ppermute | solution.py:28
  9.6 20.6 %collective-permute-start.9 = (bf16[512,384]{1,0:T(8,128)(2,1)S(1)}, bf16[512,384]{1,0:T(8,128)(2,1)S(1)}, u32[]{:S(2)}, u32[]{:S(2)}) collective-permute-start(bf16[512,384]{1,0:T(8,128)(2,1)S(1)} %pad_maximum_fusion.refs_1_), channel_id=1, source_target_pairs={{0,1},{1,2},{2,3},{3,0},{4,5},{5,6},{6,7},{7,4},{8,9},{9,10},{10,1... | collective-permute-start | bytes 1179656 | tf_op jit(solution)/shard_map/ppermute | solution.py:28
  10.2 1.0 %copy-start = (f32[1,1,8,128,128]{4,3,2,1,0:T(8,128)S(1)}, f32[1,1,8,128,128]{4,3,2,1,0:T(8,128)}, u32[]{:S(2)}) copy-start(f32[1,1,8,128,128]{4,3,2,1,0:T(8,128)} %param.6) | copy-start | bytes 1572868
  11.3 0.9 %copy-start.1 = (bf16[1,128,1024]{2,1,0:T(8,128)(2,1)S(1)}, bf16[1,128,1024]{2,1,0:T(8,128)(2,1)}, u32[]{:S(2)}) copy-start(bf16[1,128,1024]{2,1,0:T(8,128)(2,1)} %param.5) | copy-start | bytes 786436
  13.6 21.3 %all-to-all-start = ((bf16[8,2,128,128]{3,2,1,0:T(8,128)(2,1)}), bf16[8,2,128,128]{3,2,1,0:T(8,128)(2,1)S(1)}, u32[]{:S(2)}, u32[]{:S(2)}) async-start(bf16[8,2,128,128]{3,2,1,0:T(8,128)(2,1)} %shard_map.61), calls=%async_computation | async-start | bytes 1048576 | tf_op jit(solution)/shard_map/all_to_all | solution.py:262
  18.8 16.7 %collective-permute-start.2 = (bf16[128,2048]{1,0:T(8,128)(2,1)}, bf16[128,2048]{1,0:T(8,128)(2,1)}, u32[]{:S(2)}, u32[]{:S(2)}) collective-permute-start(bf16[128,2048]{1,0:T(8,128)(2,1)} %bitcast.4.refs_1_), channel_id=1, source_target_pairs={{0,4},{4,0},{8,12},{12,8},{16,20},{20,16},{24,28},{28,24},{32,36},... | collective-permute-start | bytes 1572872 | tf_op jit(solution)/shard_map/ppermute | solution.py:24
  20.4 14.5 %collective-permute-start.5 = (bf16[64,2048]{1,0:T(8,128)(2,1)}, bf16[64,2048]{1,0:T(8,128)(2,1)}, u32[]{:S(2)}, u32[]{:S(2)}) collective-permute-start(bf16[64,2048]{1,0:T(8,128)(2,1)} %get-tuple-element.36), channel_id=1, source_target_pairs={{0,8},{4,12},{8,16},{12,20},{16,24},{20,28},{24,0},{28,4},{32,40},... | collective-permute-start | bytes 786440 | tf_op jit(solution)/shard_map/ppermute | solution.py:24
  22.0 0.7 copy-start.2
  22.7 12.4 %collective-permute-start.6 = (bf16[64,2048]{1,0:T(8,128)(2,1)}, bf16[64,2048]{1,0:T(8,128)(2,1)}, u32[]{:S(2)}, u32[]{:S(2)}) collective-permute-start(bf16[64,2048]{1,0:T(8,128)(2,1)} %get-tuple-element.37), channel_id=1, source_target_pairs={{0,24},{4,28},{8,0},{12,4},{16,8},{20,12},{24,16},{28,20},{32,56},... | collective-permute-start | bytes 786440 | tf_op jit(solution)/shard_map/ppermute | solution.py:24
  24.0 0.8 copy-start.4
  24.7 10.8 %collective-permute-start.3 = (bf16[128,2048]{1,0:T(8,128)(2,1)S(1)}, bf16[128,2048]{1,0:T(8,128)(2,1)}, u32[]{:S(2)}, u32[]{:S(2)}) collective-permute-start(bf16[128,2048]{1,0:T(8,128)(2,1)S(1)} %collective-permute-done.refs_2_.refs_1_), channel_id=1, source_target_pairs={{0,4},{4,0},{8,12},{12,8},{16,20},{20,16},{24,28},{28,24},{32,36},... | collective-permute-start | bytes 1572872 | tf_op jit(solution)/shard_map/ppermute | solution.py:24
  30.1 0.7 copy-start.6
  30.9 4.7 %collective-permute-start.4 = (bf16[128,2048]{1,0:T(8,128)(2,1)S(1)}, bf16[128,2048]{1,0:T(8,128)(2,1)}, u32[]{:S(2)}, u32[]{:S(2)}) collective-permute-start(bf16[128,2048]{1,0:T(8,128)(2,1)S(1)} %collective-permute-done.1.refs_3_.refs_2_), channel_id=1, source_target_pairs={{0,4},{4,0},{8,12},{12,8},{16,20},{20,16},{24,28},{28,24},{32,36},... | collective-permute-start | bytes 1572872 | tf_op jit(solution)/shard_map/ppermute | solution.py:24
  31.3 1.0 %copy-start.3 = (bf16[512,384]{1,0:T(8,128)(2,1)S(1)}, bf16[512,384]{1,0:T(8,128)(2,1)}, u32[]{:S(2)}) copy-start(bf16[512,384]{1,0:T(8,128)(2,1)} %copy-done.2) | copy-start | bytes 1179652
  32.2 1.0 %copy-start.5 = (bf16[512,384]{1,0:T(8,128)(2,1)S(1)}, bf16[512,384]{1,0:T(8,128)(2,1)}, u32[]{:S(2)}) copy-start(bf16[512,384]{1,0:T(8,128)(2,1)} %copy-done.4) | copy-start | bytes 1179652
  33.2 1.0 %copy-start.7 = (bf16[512,384]{1,0:T(8,128)(2,1)S(1)}, bf16[512,384]{1,0:T(8,128)(2,1)}, u32[]{:S(2)}) copy-start(bf16[512,384]{1,0:T(8,128)(2,1)} %copy-done.6) | copy-start | bytes 1179652
  35.0 2.3 %collective-permute-start.7 = (bf16[64,2048]{1,0:T(8,128)(2,1)}, bf16[64,2048]{1,0:T(8,128)(2,1)S(1)}, u32[]{:S(2)}, u32[]{:S(2)}) collective-permute-start(bf16[64,2048]{1,0:T(8,128)(2,1)} %collective-permute-done.5.refs_2_), channel_id=1, source_target_pairs={{0,4},{4,0},{8,12},{12,8},{16,20},{20,16},{24,28},{28,24},{32,36},... | collective-permute-start | bytes 786440 | tf_op jit(solution)/shard_map/ppermute | solution.py:24
  35.2 2.2 %collective-permute-start.8 = (bf16[64,2048]{1,0:T(8,128)(2,1)}, bf16[64,2048]{1,0:T(8,128)(2,1)S(1)}, u32[]{:S(2)}, u32[]{:S(2)}) collective-permute-start(bf16[64,2048]{1,0:T(8,128)(2,1)} %collective-permute-done.6.refs_3_), channel_id=1, source_target_pairs={{0,4},{4,0},{8,12},{12,8},{16,20},{20,16},{24,28},{28,24},{32,36},... | collective-permute-start | bytes 786440 | tf_op jit(solution)/shard_map/ppermute | solution.py:24
  41.4 7.8 %collective-permute-start.12 = (bf16[128,128]{1,0:T(8,128)(2,1)S(1)}, bf16[128,128]{1,0:T(8,128)(2,1)S(1)}, u32[]{:S(2)}, u32[]{:S(2)}) collective-permute-start(bf16[128,128]{1,0:T(8,128)(2,1)S(1)} %get-tuple-element.48), channel_id=1, source_target_pairs={{0,32},{4,36},{8,40},{12,44},{16,48},{20,52},{24,56},{28,60},{32,6... | collective-permute-start | bytes 98312 | tf_op jit(solution)/shard_map/ppermute | solution.py:24
  42.8 6.4 %collective-permute-start.13 = (bf16[128,128]{1,0:T(8,128)(2,1)S(1)}, bf16[128,128]{1,0:T(8,128)(2,1)S(1)}, u32[]{:S(2)}, u32[]{:S(2)}) collective-permute-start(bf16[128,128]{1,0:T(8,128)(2,1)S(1)} %get-tuple-element.48), channel_id=1, source_target_pairs={{0,64},{4,68},{8,72},{12,76},{16,80},{20,84},{24,88},{28,92},{32,9... | collective-permute-start | bytes 98312 | tf_op jit(solution)/shard_map/ppermute | solution.py:24
  45.4 3.8 %collective-permute-start.14 = (bf16[128,128]{1,0:T(8,128)(2,1)S(1)}, bf16[128,128]{1,0:T(8,128)(2,1)S(1)}, u32[]{:S(2)}, u32[]{:S(2)}) collective-permute-start(bf16[128,128]{1,0:T(8,128)(2,1)S(1)} %get-tuple-element.48), channel_id=1, source_target_pairs={{0,96},{4,100},{8,104},{12,108},{16,112},{20,116},{24,120},{28,124... | collective-permute-start | bytes 98312 | tf_op jit(solution)/shard_map/ppermute | solution.py:24
  50.2 7.7 %collective-permute-start.19 = (bf16[2048,384]{1,0:T(8,128)(2,1)S(1)}, bf16[2048,384]{1,0:T(8,128)(2,1)S(1)}, u32[]{:S(2)}, u32[]{:S(2)}) collective-permute-start(bf16[2048,384]{1,0:T(8,128)(2,1)S(1)} %shard_map.62.refs_6_.refs_3_), channel_id=1, source_target_pairs={{0,4},{4,0},{8,12},{12,8},{16,20},{20,16},{24,28},{28,24},{32,36},... | collective-permute-start | bytes 4718600 | tf_op jit(solution)/shard_map/ppermute | solution.py:24
  51.3 6.6 %collective-permute-start.18 = (bf16[4,128,384]{2,1,0:T(8,128)(2,1)S(1)}, bf16[4,128,384]{2,1,0:T(8,128)(2,1)S(1)}, u32[]{:S(2)}, u32[]{:S(2)}) collective-permute-start(bf16[4,128,384]{2,1,0:T(8,128)(2,1)S(1)} %get-tuple-element.55), channel_id=1, source_target_pairs={{0,4},{4,0},{8,12},{12,8},{16,20},{20,16},{24,28},{28,24},{32,36},... | collective-permute-start | bytes 1179656 | tf_op jit(solution)/shard_map/ppermute | solution.py:24
  54.6 10.1 %collective-permute-start.15 = (bf16[4,8,16,384]{3,2,1,0:T(8,128)(2,1)S(1)}, bf16[4,8,16,384]{3,2,1,0:T(8,128)(2,1)S(1)}, u32[]{:S(2)}, u32[]{:S(2)}) collective-permute-start(bf16[4,8,16,384]{3,2,1,0:T(8,128)(2,1)S(1)} %get-tuple-element.51), channel_id=1, source_target_pairs={{0,1},{1,2},{2,3},{3,0},{4,36},{5,37},{6,38},{7,39},{8,9},{9,10},{... | collective-permute-start | bytes 1179656 | tf_op jit(solution)/shard_map/ppermute | solution.py:40
  55.0 12.5 %collective-permute-start.16 = (bf16[4,8,16,384]{3,2,1,0:T(8,128)(2,1)S(1)}, bf16[4,8,16,384]{3,2,1,0:T(8,128)(2,1)S(1)}, u32[]{:S(2)}, u32[]{:S(2)}) collective-permute-start(bf16[4,8,16,384]{3,2,1,0:T(8,128)(2,1)S(1)} %get-tuple-element.52), channel_id=1, source_target_pairs={{0,2},{1,3},{2,0},{3,1},{4,68},{5,69},{6,70},{7,71},{8,10},{9,11},... | collective-permute-start | bytes 1179656 | tf_op jit(solution)/shard_map/ppermute | solution.py:40
  57.9 9.7 %collective-permute-start.17 = (bf16[4,8,16,384]{3,2,1,0:T(8,128)(2,1)S(1)}, bf16[4,8,16,384]{3,2,1,0:T(8,128)(2,1)S(1)}, u32[]{:S(2)}, u32[]{:S(2)}) collective-permute-start(bf16[4,8,16,384]{3,2,1,0:T(8,128)(2,1)S(1)} %get-tuple-element.53), channel_id=1, source_target_pairs={{0,3},{1,0},{2,1},{3,2},{4,100},{5,101},{6,102},{7,103},{8,11},{9,... | collective-permute-start | bytes 1179656 | tf_op jit(solution)/shard_map/ppermute | solution.py:40
  59.6 8.8 %collective-permute-start.23 = (bf16[64,2048]{1,0:T(8,128)(2,1)S(1)}, bf16[64,2048]{1,0:T(8,128)(2,1)S(1)}, u32[]{:S(2)}, u32[]{:S(2)}) collective-permute-start(bf16[64,2048]{1,0:T(8,128)(2,1)S(1)} %get-tuple-element.57.refs_5_), channel_id=1, source_target_pairs={{0,8},{4,12},{8,16},{12,20},{16,24},{20,28},{24,0},{28,4},{32,40},... | collective-permute-start | bytes 786440 | tf_op jit(solution)/shard_map/ppermute | solution.py:24
  59.7 8.7 %collective-permute-start.24 = (bf16[64,2048]{1,0:T(8,128)(2,1)S(1)}, bf16[64,2048]{1,0:T(8,128)(2,1)S(1)}, u32[]{:S(2)}, u32[]{:S(2)}) collective-permute-start(bf16[64,2048]{1,0:T(8,128)(2,1)S(1)} %get-tuple-element.65), channel_id=1, source_target_pairs={{0,24},{4,28},{8,0},{12,4},{16,8},{20,12},{24,16},{28,20},{32,56},... | collective-permute-start | bytes 786440 | tf_op jit(solution)/shard_map/ppermute | solution.py:24
  69.1 21.4 %collective-permute-start.25 = (bf16[128,2048]{1,0:T(8,128)(2,1)S(1)}, bf16[128,2048]{1,0:T(8,128)(2,1)S(1)}, u32[]{:S(2)}, u32[]{:S(2)}) collective-permute-start(bf16[128,2048]{1,0:T(8,128)(2,1)S(1)} %get-tuple-element.66), channel_id=1, source_target_pairs={{0,8},{4,12},{8,16},{12,20},{16,24},{20,28},{24,0},{28,4},{32,40},... | collective-permute-start | bytes 1572872 | tf_op jit(solution)/shard_map/ppermute | solution.py:24
  69.2 21.3 %collective-permute-start.26 = (bf16[128,2048]{1,0:T(8,128)(2,1)S(1)}, bf16[128,2048]{1,0:T(8,128)(2,1)S(1)}, u32[]{:S(2)}, u32[]{:S(2)}) collective-permute-start(bf16[128,2048]{1,0:T(8,128)(2,1)S(1)} %get-tuple-element.67), channel_id=1, source_target_pairs={{0,24},{4,28},{8,0},{12,4},{16,8},{20,12},{24,16},{28,20},{32,56},... | collective-permute-start | bytes 1572872 | tf_op jit(solution)/shard_map/ppermute | solution.py:24
  71.8 5.9 %collective-permute-start.20 = (bf16[8,16,384]{2,1,0:T(8,128)(2,1)S(1)}, bf16[8,16,384]{2,1,0:T(8,128)(2,1)S(1)}, u32[]{:S(2)}, u32[]{:S(2)}) collective-permute-start(bf16[8,16,384]{2,1,0:T(8,128)(2,1)S(1)} %get-tuple-element.60), channel_id=1, source_target_pairs={{0,32},{1,33},{2,34},{3,35},{4,5},{5,6},{6,7},{7,4},{8,40},{9,41},... | collective-permute-start | bytes 294920 | tf_op jit(solution)/shard_map/ppermute | solution.py:40
  72.8 6.8 %collective-permute-start.21 = (bf16[8,16,384]{2,1,0:T(8,128)(2,1)S(1)}, bf16[8,16,384]{2,1,0:T(8,128)(2,1)S(1)}, u32[]{:S(2)}, u32[]{:S(2)}) collective-permute-start(bf16[8,16,384]{2,1,0:T(8,128)(2,1)S(1)} %get-tuple-element.61), channel_id=1, source_target_pairs={{0,64},{1,65},{2,66},{3,67},{4,6},{5,7},{6,4},{7,5},{8,72},{9,73},... | collective-permute-start | bytes 294920 | tf_op jit(solution)/shard_map/ppermute | solution.py:40
  76.6 3.8 %collective-permute-start.22 = (bf16[8,16,384]{2,1,0:T(8,128)(2,1)S(1)}, bf16[8,16,384]{2,1,0:T(8,128)(2,1)S(1)}, u32[]{:S(2)}, u32[]{:S(2)}) collective-permute-start(bf16[8,16,384]{2,1,0:T(8,128)(2,1)S(1)} %get-tuple-element.62), channel_id=1, source_target_pairs={{0,96},{1,97},{2,98},{3,99},{4,7},{5,4},{6,5},{7,6},{8,104},{9,105... | collective-permute-start | bytes 294920 | tf_op jit(solution)/shard_map/ppermute | solution.py:40

commit v12 on v10

--- a/solution.py
+++ b/solution.py
@@ -108,9 +108,8 @@
         out[h, 1] = state[h].astype(BF)
 
 
-def relay(idx, w0, w1, w3, w2, wkeep):
-    for part, step in ((w0, 0), (w1, 1), (w3, 3), (w2, 2)):
-        wkeep[columns(idx[0], step, 0, 512), :] = part[...]
+def gate(idx, w1, w3, w2, out):
+    out[...] = w1[:16, :HD] + w3[:16, :HD] + w2[:16, :HD]
 
 
 def stack(idx, *refs):
@@ -119,9 +118,11 @@
         xa[i * TOK : (i + 1) * TOK, :] = part[...]
 
 
-def project(idx, xa, x2a, x2b, m2a, m2b, wkeep, gs, qkv, r, total, xb):
+def project(idx, xa, x2a, x2b, m2a, m2b, w0, w1, w3, w2, gs, qkv, r, total, xb, wkeep):
     for i, part in enumerate((x2a, x2b, m2a, m2b)):
         xb[i * 64 : (i + 1) * 64, :] = part[...]
+    for part, step in ((w0, 0), (w1, 1), (w3, 3), (w2, 2)):
+        wkeep[columns(idx[0], step, 0, 512), :] = part[...]
     whole = jnp.zeros((HD, HD), F32)
     for m in range(4):
         rows = slice(m * 256, (m + 1) * 256)
@@ -257,25 +258,27 @@
     gs = lax.all_to_all(bundle, "ctx", 0, 0, axis_index_groups=rows_y)
     w2, w1, w3 = (x_hop(own_w, s) for s in (2, 1, -1))
     x2a, x2b = ctx_hop(x1[:64], dz=1), ctx_hop(x3[64:], dz=-1)
-    (own_w,) = call(relay, [shape((2048, 384), BF)], [idx, own_w, w1, w3, w2], flops=1 << 33, limit=6)
     first = [x, x1, x3]
     first += [ctx_hop(p, dc=1) for p in first]
-    (xa,) = call(stack, [shape((768, 2048), BF)], [idx, *first], flops=1 << 33, limit=10)
+    (token,) = call(gate, [shape((16, HD), BF)], [idx, w1, w3, w2], flops=1 << 33, limit=4)
+    (xa,) = call(stack, [shape((768, 2048), BF)], [idx, *first], flops=1 << 33, limit=10, deps=(token,))
     last = [x2a, x2b]
     last += [ctx_hop(after(p, gs), dc=1) for p in last]
 
     big = 2 * 1024 * 2048 * 384
-    qkv, r, total, xb = call(
+    qkv, r, total, xb, whole_w = call(
         project,
         [
             shape((1024, 384), BF),
             shape((8, HD, HD), F32),
             shape((HD, HD), BF),
             shape((256, 2048), BF),
+            shape((2048, 384), BF),
         ],
-        [idx, xa, *last, own_w, gs],
+        [idx, xa, *last, own_w, w1, w3, w2, gs],
         flops=big,
     )
+    own_w = whole_w
     totals = [ctx_hop(total, dy=s) for s in (1, 2, 3)]
     dq, dk0, dv0, xt = call(
         lambda *refs: within(alpha, beta, *refs),

time: 92.2 us -> 91.4 us (level)
  local copies, waits for them, and re-layouts: 10.7 us -> 4.74 us
  waiting for transfers between devices: 6.71 us -> 11.2 us
  blocking collectives: 10.1 us -> 11.1 us
    unnamed x16 -> x4, local copies, waits for them, and re-layouts: 7.24 us -> 1.99 us
    ppermute x18, waiting for transfers between devices: 0.05 us -> 5.21 us  [ctx_hop(): return lax.ppermute(block, 'ctx', route)]
    ppermute x6, starting transfers between devices: 8.15 us -> 6.86 us  [plane_hop(): return lax.ppermute(block, ('ctx', 'zero'), route)]
    all_to_all x1, blocking collectives: 10.1 us -> 11.1 us  [body(): owned = lax.all_to_all(owned, 'ctx', 0, 0, axis_index_groups=rows_y)]
  transfers between devices with their start and end apart: 28 -> 28, of which waited for: 4 -> 5; matrix products, arithmetic and copies ran while one was open for 4% -> 3% of each run, Pallas kernels for 16% -> 16%
where the time goes in v12:
time: 91.4 us; the launch traced here: 91 us
  starting transfers between devices  41.6 us (46%)
  Pallas kernels  21.3 us (23%)
  waiting for transfers between devices  11.2 us (12%)
  blocking collectives  11.1 us (12%)
  local copies, waits for them, and re-layouts  4.74 us (5%)
    ppermute x18, starting transfers between devices, ctx_hop(): return lax.ppermute(block, 'ctx', route)  25.2 us
    pallas_call x12, Pallas kernels, call(): pl.pallas_call(run, out_shape=list(outs), in_specs=[pl.BlockSpec(memory_s...  21.3 us
    all_to_all x1, blocking collectives, body(): owned = lax.all_to_all(owned, 'ctx', 0, 0, axis_index_groups=rows_y)  11.1 us
    ppermute x6, starting transfers between devices, plane_hop(): return lax.ppermute(block, ('ctx', 'zero'), route)  6.86 us
    ppermute x6, waiting for transfers between devices, plane_hop(): return lax.ppermute(block, ('ctx', 'zero'), route)  5.97 us
    ppermute x18, waiting for transfers between devices, ctx_hop(): return lax.ppermute(block, 'ctx', route)  5.21 us
    all_to_all x1, starting transfers between devices, body(): gs = lax.all_to_all(bundle, 'ctx', 0, 0, axis_index_groups=rows_y)  5.19 us
    ppermute x3, starting transfers between devices, x_hop(): return lax.ppermute(block, 'zero', [(i, (i + dx) % NX) for i in range(NX)])  4.28 us
  transfers between devices with their start and end apart: 28, of which 5 were waited for; matrix products, arithmetic and copies ran while one was open for 3% of the time, Pallas kernels for 16%

profile of v12, /device:TPU:1, one launch (start us, length us, event | category | flops | bytes accessed | tf_op | source)
XLA Modules:
  0.0 91.0 jit_solution(1399254711297062359)
XLA Ops:
  0.6 2.5 %collective-permute-start = (bf16[128,2048]{1,0:T(8,128)(2,1)}, bf16[128,2048]{1,0:T(8,128)(2,1)S(1)}, u32[]{:S(2)}, u32[]{:S(2)}) collective-permute-start(bf16[128,2048]{1,0:T(8,128)(2,1)} %bitcast.4.refs_1_), channel_id=1, source_target_pairs={{0,8},{4,12},{8,16},{12,20},{16,24},{20,28},{24,0},{28,4},{32,40},... | collective-permute-start | bytes 1572872 | tf_op jit(solution)/shard_map/ppermute | solution.py:24
  3.2 2.2 %collective-permute-start.1 = (bf16[128,2048]{1,0:T(8,128)(2,1)}, bf16[128,2048]{1,0:T(8,128)(2,1)}, u32[]{:S(2)}, u32[]{:S(2)}) collective-permute-start(bf16[128,2048]{1,0:T(8,128)(2,1)} %bitcast.4.refs_1_), channel_id=1, source_target_pairs={{0,24},{4,28},{8,0},{12,4},{16,8},{20,12},{24,16},{28,20},{32,56},... | collective-permute-start | bytes 1572872 | tf_op jit(solution)/shard_map/ppermute | solution.py:24
  5.4 1.1 %constant_dynamic-slice_fusion.2 = (bf16[512,128]{1,0:T(8,128)(2,1)S(1)}, bf16[512,128]{1,0:T(8,128)(2,1)S(1)}, bf16[512,128]{1,0:T(8,128)(2,1)S(1)}) fusion(bf16[512,3072]{1,0:T(8,128)(2,1)} %param.7, s32[]{:T(128)S(6)} %select_n.31, s32[]{:T(128)S(6)} %select_n.33, s32[]{:T(128)S(6)} %select_n.32), kind=kLoop, calls=%fused_computation.4 | loop fusion | bytes 786444 | tf_op jit(solution)/shard_map/dynamic_slice | solution.py:253
  6.5 1.3 %collective-permute-start.5 = (bf16[512,384]{1,0:T(8,128)(2,1)S(1)}, bf16[512,384]{1,0:T(8,128)(2,1)S(1)}, u32[]{:S(2)}, u32[]{:S(2)}) collective-permute-start(bf16[512,384]{1,0:T(8,128)(2,1)S(1)} %pad_maximum_fusion.refs_6_), channel_id=1, source_target_pairs={{0,1},{1,2},{2,3},{3,0},{4,5},{5,6},{6,7},{7,4},{8,9},{9,10},{10,1... | collective-permute-start | bytes 1179656 | tf_op jit(solution)/shard_map/ppermute | solution.py:28
  7.8 1.5 %collective-permute-start.6 = (bf16[512,384]{1,0:T(8,128)(2,1)S(1)}, bf16[512,384]{1,0:T(8,128)(2,1)S(1)}, u32[]{:S(2)}, u32[]{:S(2)}) collective-permute-start(bf16[512,384]{1,0:T(8,128)(2,1)S(1)} %pad_maximum_fusion.refs_6_), channel_id=1, source_target_pairs={{0,3},{1,0},{2,1},{3,2},{4,7},{5,4},{6,5},{7,6},{8,11},{9,8},{10,9... | collective-permute-start | bytes 1179656 | tf_op jit(solution)/shard_map/ppermute | solution.py:28
  9.2 1.5 %collective-permute-start.7 = (bf16[512,384]{1,0:T(8,128)(2,1)S(1)}, bf16[512,384]{1,0:T(8,128)(2,1)S(1)}, u32[]{:S(2)}, u32[]{:S(2)}) collective-permute-start(bf16[512,384]{1,0:T(8,128)(2,1)S(1)} %pad_maximum_fusion.refs_6_), channel_id=1, source_target_pairs={{0,2},{1,3},{2,0},{3,1},{4,6},{5,7},{6,4},{7,5},{8,10},{9,11},{10,... | collective-permute-start | bytes 1179656 | tf_op jit(solution)/shard_map/ppermute | solution.py:28
  10.8 0.1 pad_add_fusion.refs_0_
  10.9 1.0 %copy-done = f32[1,1,8,128,128]{4,3,2,1,0:T(8,128)S(1)} copy-done((f32[1,1,8,128,128]{4,3,2,1,0:T(8,128)S(1)}, f32[1,1,8,128,128]{4,3,2,1,0:T(8,128)}, u32[]{:S(2)}) %copy-start) | copy-done | bytes 524312
  11.9 0.9 %copy-done.1 = bf16[1,128,1024]{2,1,0:T(8,128)(2,1)S(1)} copy-done((bf16[1,128,1024]{2,1,0:T(8,128)(2,1)S(1)}, bf16[1,128,1024]{2,1,0:T(8,128)(2,1)}, u32[]{:S(2)}) %copy-start.1) | copy-done | bytes 262168
  12.8 1.4 %shard_map.61 = bf16[8,2,128,128]{3,2,1,0:T(8,128)(2,1)} custom-call(s32[4]{0:T(128)S(1)} %pad_add_fusion.refs_0_, bf16[128,1024]{1,0:T(8,128)(2,1)S(1)} %bitcast.9, f32[8,128,128]{2,1,0:T(8,128)S(1)} %bitcast.8), custom_call_target="tpu_custom_call" | custom-call | bytes 1310736 | tf_op jit(solution)/shard_map/pallas_call | solution.py:63
  14.3 5.2 %all-to-all-start = ((bf16[8,2,128,128]{3,2,1,0:T(8,128)(2,1)}), bf16[8,2,128,128]{3,2,1,0:T(8,128)(2,1)S(1)}, u32[]{:S(2)}, u32[]{:S(2)}) async-start(bf16[8,2,128,128]{3,2,1,0:T(8,128)(2,1)} %shard_map.61), calls=%async_computation | async-start | bytes 1048576 | tf_op jit(solution)/shard_map/all_to_all | solution.py:258
  19.4 0.2 collective-permute-start.2
  19.7 1.6 %collective-permute-start.8 = (bf16[64,2048]{1,0:T(8,128)(2,1)S(1)}, bf16[64,2048]{1,0:T(8,128)(2,1)S(1)}, u32[]{:S(2)}, u32[]{:S(2)}) collective-permute-start(bf16[64,2048]{1,0:T(8,128)(2,1)S(1)} %slice.8), channel_id=1, source_target_pairs={{0,8},{4,12},{8,16},{12,20},{16,24},{20,28},{24,0},{28,4},{32,40},... | collective-permute-start | bytes 786440 | tf_op jit(solution)/shard_map/ppermute | solution.py:24
  21.3 1.7 %slice.9 = bf16[64,2048]{1,0:T(8,128)(2,1)} slice(bf16[128,2048]{1,0:T(8,128)(2,1)} %collective-permute-done.1.refs_3_), slice={[64:128], [0:2048]} | slice | bytes 524288 | tf_op jit(solution)/shard_map/slice | solution.py:260
  23.0 1.3 %collective-permute-start.9 = (bf16[64,2048]{1,0:T(8,128)(2,1)}, bf16[64,2048]{1,0:T(8,128)(2,1)S(1)}, u32[]{:S(2)}, u32[]{:S(2)}) collective-permute-start(bf16[64,2048]{1,0:T(8,128)(2,1)} %slice.9), channel_id=1, source_target_pairs={{0,24},{4,28},{8,0},{12,4},{16,8},{20,12},{24,16},{28,20},{32,56},... | collective-permute-start | bytes 786440 | tf_op jit(solution)/shard_map/ppermute | solution.py:24
  24.2 2.8 %collective-permute-start.3 = (bf16[128,2048]{1,0:T(8,128)(2,1)S(1)}, bf16[128,2048]{1,0:T(8,128)(2,1)}, u32[]{:S(2)}, u32[]{:S(2)}) collective-permute-start(bf16[128,2048]{1,0:T(8,128)(2,1)S(1)} %collective-permute-done.refs_2_), channel_id=1, source_target_pairs={{0,4},{4,0},{8,12},{12,8},{16,20},{20,16},{24,28},{28,24},{32,36},... | collective-permute-start | bytes 1572872 | tf_op jit(solution)/shard_map/ppermute | solution.py:24
  27.0 1.7 %collective-permute-start.4 = (bf16[128,2048]{1,0:T(8,128)(2,1)}, bf16[128,2048]{1,0:T(8,128)(2,1)}, u32[]{:S(2)}, u32[]{:S(2)}) collective-permute-start(bf16[128,2048]{1,0:T(8,128)(2,1)} %collective-permute-done.1.refs_3_), channel_id=1, source_target_pairs={{0,4},{4,0},{8,12},{12,8},{16,20},{20,16},{24,28},{28,24},{32,36},... | collective-permute-start | bytes 1572872 | tf_op jit(solution)/shard_map/ppermute | solution.py:24
  28.7 0.5 shard_map.59.refs_7_
  29.3 5.2 %collective-permute-done.8.refs_2_ = bf16[64,2048]{1,0:T(8,128)(2,1)S(1)} collective-permute-done((bf16[64,2048]{1,0:T(8,128)(2,1)S(1)}, bf16[64,2048]{1,0:T(8,128)(2,1)S(1)}, u32[]{:S(2)}, u32[]{:S(2)}) %collective-permute-start.8) | collective-permute-done | bytes 262176 | tf_op jit(solution)/shard_map/ppermute | solution.py:24
  34.4 0.7 collective-permute-start.10
  35.2 1.9 %shard_map.60.refs_1_ = bf16[768,2048]{1,0:T(8,128)(2,1)S(1)} custom-call(s32[4]{0:T(128)S(1)} %pad_add_fusion.refs_0_, bf16[128,2048]{1,0:T(8,128)(2,1)} %bitcast.4.refs_1_, bf16[128,2048]{1,0:T(8,128)(2,1)S(1)} %collective-permute-done.refs_2_, bf16[128,2048]{1,0:T(8,128)(2,1)} %collective-permute-done.1.refs_3_, ...), custom_call_target="tpu_custom_call" | custom-call | flops 8589934592 | bytes 6291472 | tf_op jit(solution)/shard_map/pallas_call | solution.py:63
  37.1 3.8 %shard_map.62 = (bf16[1024,384]{1,0:T(8,128)(2,1)S(1)}, f32[8,128,128]{2,1,0:T(8,128)S(1)}, bf16[128,128]{1,0:T(8,128)(2,1)S(1)}, bf16[256,2048]{1,0:T(8,128)(2,1)S(1)}, bf16[2048,384]{1,0:T(8,128)(2,1)S(1)}) custom-call(s32[4]{0:T(128)S(1)} %pad_add_fusion.refs_0_, bf16[768,2048]{1,0:T(8,128)(2,1)S(1)} %shard_map.60.refs_1_, ...), custom_call_target="tpu_custom_call" | custom-call | flops 1610612736 | bytes 10256400 | tf_op jit(solution)/shard_map/pallas_call | solution.py:63
  40.9 1.4 %collective-permute-start.12 = (bf16[128,128]{1,0:T(8,128)(2,1)S(1)}, bf16[128,128]{1,0:T(8,128)(2,1)S(1)}, u32[]{:S(2)}, u32[]{:S(2)}) collective-permute-start(bf16[128,128]{1,0:T(8,128)(2,1)S(1)} %get-tuple-element.45), channel_id=1, source_target_pairs={{0,32},{4,36},{8,40},{12,44},{16,48},{20,52},{24,56},{28,60},{32,6... | collective-permute-start | bytes 98312 | tf_op jit(solution)/shard_map/ppermute | solution.py:24
  42.3 2.6 %collective-permute-start.13 = (bf16[128,128]{1,0:T(8,128)(2,1)S(1)}, bf16[128,128]{1,0:T(8,128)(2,1)S(1)}, u32[]{:S(2)}, u32[]{:S(2)}) collective-permute-start(bf16[128,128]{1,0:T(8,128)(2,1)S(1)} %get-tuple-element.45), channel_id=1, source_target_pairs={{0,64},{4,68},{8,72},{12,76},{16,80},{20,84},{24,88},{28,92},{32,9... | collective-permute-start | bytes 98312 | tf_op jit(solution)/shard_map/ppermute | solution.py:24
  44.9 1.1 %collective-permute-start.14 = (bf16[128,128]{1,0:T(8,128)(2,1)S(1)}, bf16[128,128]{1,0:T(8,128)(2,1)S(1)}, u32[]{:S(2)}, u32[]{:S(2)}) collective-permute-start(bf16[128,128]{1,0:T(8,128)(2,1)S(1)} %get-tuple-element.45), channel_id=1, source_target_pairs={{0,96},{4,100},{8,104},{12,108},{16,112},{20,116},{24,120},{28,124... | collective-permute-start | bytes 98312 | tf_op jit(solution)/shard_map/ppermute | solution.py:24
  45.9 2.7 %shard_map.63 = (bf16[1024,128]{1,0:T(8,128)(2,1)S(1)}, f32[1024,128]{1,0:T(8,128)S(1)}, f32[1024,128]{1,0:T(8,128)S(1)}, bf16[2048,1024]{1,0:T(8,128)(2,1)S(1)}) custom-call(s32[4]{0:T(128)S(1)} %pad_add_fusion.refs_0_, bf16[768,2048]{1,0:T(8,128)(2,1)S(1)} %shard_map.60.refs_1_, bf16[256,2048]{1,0:T(8,128)(2,1)S(1)} %get-tuple-element.38.refs_2_, ...), custom_call_target="tpu_custom_call" | custom-call | flops 402653184 | bytes 11010064 | tf_op jit(solution)/shard_map/pallas_call | solution.py:63
  48.7 1.0 %shard_map.64 = (bf16[1024,384]{1,0:T(8,128)(2,1)S(1)}, bf16[4,128,384]{2,1,0:T(8,128)(2,1)S(1)}, bf16[4,128,384]{2,1,0:T(8,128)(2,1)S(1)}) custom-call(s32[4]{0:T(128)S(1)} %pad_add_fusion.refs_0_, bf16[1024,384]{1,0:T(8,128)(2,1)S(1)} %get-tuple-element.39.refs_4_.refs_1_, bf16[1024,128]{1,0:T(8,128)(2,1)S(1)} %get-tuple-element.41.refs_2_, ...), custom_call_target="tpu_custom_call" | custom-call | flops 100663296 | bytes 4292624 | tf_op jit(solution)/shard_map/pallas_call | solution.py:63
  49.7 1.4 %collective-permute-start.19 = (bf16[2048,384]{1,0:T(8,128)(2,1)S(1)}, bf16[2048,384]{1,0:T(8,128)(2,1)S(1)}, u32[]{:S(2)}, u32[]{:S(2)}) collective-permute-start(bf16[2048,384]{1,0:T(8,128)(2,1)S(1)} %get-tuple-element.54.refs_3_), channel_id=1, source_target_pairs={{0,4},{4,0},{8,12},{12,8},{16,20},{20,16},{24,28},{28,24},{32,36},... | collective-permute-start | bytes 4718600 | tf_op jit(solution)/shard_map/ppermute | solution.py:24
  51.1 0.3 collective-permute-start.18
  51.4 3.0 %shard_map.65 = (bf16[4,8,16,384]{3,2,1,0:T(8,128)(2,1)S(1)}, bf16[4,8,16,384]{3,2,1,0:T(8,128)(2,1)S(1)}, bf16[4,8,16,384]{3,2,1,0:T(8,128)(2,1)S(1)}, bf16[4,8,16,384]{3,2,1,0:T(8,128)(2,1)S(1)}) custom-call(s32[4]{0:T(128)S(1)} %pad_add_fusion.refs_0_, bf16[2048,1024]{1,0:T(8,128)(2,1)S(1)} %get-tuple-element.40.refs_1_, ...), custom_call_target="tpu_custom_call" | custom-call | flops 1610612736 | bytes 6553616 | tf_op jit(solution)/shard_map/pallas_call | solution.py:63
  54.4 0.5 collective-permute-start.15
  54.9 2.9 %collective-permute-start.16 = (bf16[4,8,16,384]{3,2,1,0:T(8,128)(2,1)S(1)}, bf16[4,8,16,384]{3,2,1,0:T(8,128)(2,1)S(1)}, u32[]{:S(2)}, u32[]{:S(2)}) collective-permute-start(bf16[4,8,16,384]{3,2,1,0:T(8,128)(2,1)S(1)} %get-tuple-element.49), channel_id=1, source_target_pairs={{0,2},{1,3},{2,0},{3,1},{4,68},{5,69},{6,70},{7,71},{8,10},{9,11},... | collective-permute-start | bytes 1179656 | tf_op jit(solution)/shard_map/ppermute | solution.py:40
  57.7 1.6 %shard_map.66 = (bf16[64,2048]{1,0:T(8,128)(2,1)S(1)}, bf16[64,2048]{1,0:T(8,128)(2,1)S(1)}) custom-call(s32[4]{0:T(128)S(1)} %pad_add_fusion.refs_0_, bf16[4,128,384]{2,1,0:T(8,128)(2,1)S(1)} %get-tuple-element.51.refs_1_, bf16[4,128,384]{2,1,0:T(8,128)(2,1)S(1)} %collective-permute-done.18.refs_2_, bf16[2048,384]{1,0:T(8,128)(2,1)S(1)} %get-tuple-element.54.refs_3_, ...), custom_call_target="tpu_custom_call" | custom-call | flops 402653184 | bytes 4456464 | tf_op jit(solution)/shard_map/pallas_call | solution.py:63
  59.4 0.1 collective-permute-start.23
  59.5 2.7 %collective-permute-start.24 = (bf16[64,2048]{1,0:T(8,128)(2,1)S(1)}, bf16[64,2048]{1,0:T(8,128)(2,1)S(1)}, u32[]{:S(2)}, u32[]{:S(2)}) collective-permute-start(bf16[64,2048]{1,0:T(8,128)(2,1)S(1)} %get-tuple-element.63), channel_id=1, source_target_pairs={{0,24},{4,28},{8,0},{12,4},{16,8},{20,12},{24,16},{28,20},{32,56},... | collective-permute-start | bytes 786440 | tf_op jit(solution)/shard_map/ppermute | solution.py:24
  62.1 2.4 %shard_map.67 = (f32[128,2048]{1,0:T(8,128)S(1)}, bf16[128,2048]{1,0:T(8,128)(2,1)S(1)}, bf16[128,2048]{1,0:T(8,128)(2,1)S(1)}) custom-call(s32[4]{0:T(128)S(1)} %pad_add_fusion.refs_0_, bf16[4,128,384]{2,1,0:T(8,128)(2,1)S(1)} %get-tuple-element.51.refs_1_, bf16[4,128,384]{2,1,0:T(8,128)(2,1)S(1)} %collective-permute-done.18.refs_2_, ...), custom_call_target="tpu_custom_call" | custom-call | flops 1610612736 | bytes 6029328 | tf_op jit(solution)/shard_map/pallas_call | solution.py:63
  64.5 2.6 %collective-permute-done.16.refs_3_ = bf16[4,8,16,384]{3,2,1,0:T(8,128)(2,1)S(1)} collective-permute-done((bf16[4,8,16,384]{3,2,1,0:T(8,128)(2,1)S(1)}, bf16[4,8,16,384]{3,2,1,0:T(8,128)(2,1)S(1)}, u32[]{:S(2)}, u32[]{:S(2)}) %collective-permute-start.16) | collective-permute-done | bytes 393248 | tf_op jit(solution)/shard_map/ppermute | solution.py:40
  67.1 0.3 collective-permute-done.17.refs_4_
  67.4 0.7 shard_map.68
  68.2 0.7 shard_map.69
  69.0 2.7 %collective-permute-start.26 = (bf16[128,2048]{1,0:T(8,128)(2,1)S(1)}, bf16[128,2048]{1,0:T(8,128)(2,1)S(1)}, u32[]{:S(2)}, u32[]{:S(2)}) collective-permute-start(bf16[128,2048]{1,0:T(8,128)(2,1)S(1)} %get-tuple-element.65), channel_id=1, source_target_pairs={{0,24},{4,28},{8,0},{12,4},{16,8},{20,12},{24,16},{28,20},{32,56},... | collective-permute-start | bytes 1572872 | tf_op jit(solution)/shard_map/ppermute | solution.py:24
  71.6 0.3 collective-permute-start.20
  71.9 1.7 %collective-permute-start.21 = (bf16[8,16,384]{2,1,0:T(8,128)(2,1)S(1)}, bf16[8,16,384]{2,1,0:T(8,128)(2,1)S(1)}, u32[]{:S(2)}, u32[]{:S(2)}) collective-permute-start(bf16[8,16,384]{2,1,0:T(8,128)(2,1)S(1)} %get-tuple-element.59), channel_id=1, source_target_pairs={{0,64},{1,65},{2,66},{3,67},{4,6},{5,7},{6,4},{7,5},{8,72},{9,73},... | collective-permute-start | bytes 294920 | tf_op jit(solution)/shard_map/ppermute | solution.py:40
  73.7 1.5 %collective-permute-start.22 = (bf16[8,16,384]{2,1,0:T(8,128)(2,1)S(1)}, bf16[8,16,384]{2,1,0:T(8,128)(2,1)S(1)}, u32[]{:S(2)}, u32[]{:S(2)}) collective-permute-start(bf16[8,16,384]{2,1,0:T(8,128)(2,1)S(1)} %get-tuple-element.60), channel_id=1, source_target_pairs={{0,96},{1,97},{2,98},{3,99},{4,7},{5,4},{6,5},{7,6},{8,104},{9,105... | collective-permute-start | bytes 294920 | tf_op jit(solution)/shard_map/ppermute | solution.py:40
  75.2 2.5 %collective-permute-done.20 = bf16[8,16,384]{2,1,0:T(8,128)(2,1)S(1)} collective-permute-done((bf16[8,16,384]{2,1,0:T(8,128)(2,1)S(1)}, bf16[8,16,384]{2,1,0:T(8,128)(2,1)S(1)}, u32[]{:S(2)}, u32[]{:S(2)}) %collective-permute-start.20) | collective-permute-done | bytes 98336 | tf_op jit(solution)/shard_map/ppermute | solution.py:40
  77.7 0.6 collective-permute-done.22
  78.3 11.1 %all_to_all.10.refs_1_ = bf16[8,16,384]{2,1,0:T(8,128)(2,1)S(1)} all-to-all(bf16[8,16,384]{2,1,0:T(8,128)(2,1)S(1)} %add_convert_fusion), channel_id=1, replica_groups={{0,4,8,12,16,20,24,28},{32,36,40,44,48,52,56,60},{64,68,72,76,80,84,88,..., dimensions={0} | all-to-all | bytes 196608 | tf_op jit(solution)/shard_map/all_to_all | solution.py:330
  89.4 1.5 %shard_map.70 = (f32[16,3072]{1,0:T(8,128)}, bf16[128,2048]{1,0:T(8,128)(2,1)}) custom-call(s32[4]{0:T(128)S(1)} %pad_add_fusion.refs_0_, bf16[8,16,384]{2,1,0:T(8,128)(2,1)S(1)} %all_to_all.10.refs_1_, f32[128,2048]{1,0:T(8,128)S(1)} %get-tuple-element.56.refs_5_.refs_2_, bf16[128,2048]{1,0:T(8,128)(2,1)S(1)} %collective-permute-done.25.refs_3_, ...), custom_call_target="tpu_custom_call" | custom-call | bytes 2916368 | tf_op jit(solution)/shard_map/pallas_call | solution.py:63
  (31 shorter events, 0.3 us)
Async XLA Ops:
  0.6 18.8 %collective-permute-start = (bf16[128,2048]{1,0:T(8,128)(2,1)}, bf16[128,2048]{1,0:T(8,128)(2,1)S(1)}, u32[]{:S(2)}, u32[]{:S(2)}) collective-permute-start(bf16[128,2048]{1,0:T(8,128)(2,1)} %bitcast.4.refs_1_), channel_id=1, source_target_pairs={{0,8},{4,12},{8,16},{12,20},{16,24},{20,28},{24,0},{28,4},{32,40},... | collective-permute-start | bytes 1572872 | tf_op jit(solution)/shard_map/ppermute | solution.py:24
  3.2 16.5 %collective-permute-start.1 = (bf16[128,2048]{1,0:T(8,128)(2,1)}, bf16[128,2048]{1,0:T(8,128)(2,1)}, u32[]{:S(2)}, u32[]{:S(2)}) collective-permute-start(bf16[128,2048]{1,0:T(8,128)(2,1)} %bitcast.4.refs_1_), channel_id=1, source_target_pairs={{0,24},{4,28},{8,0},{12,4},{16,8},{20,12},{24,16},{28,20},{32,56},... | collective-permute-start | bytes 1572872 | tf_op jit(solution)/shard_map/ppermute | solution.py:24
  6.5 16.5 %collective-permute-start.5 = (bf16[512,384]{1,0:T(8,128)(2,1)S(1)}, bf16[512,384]{1,0:T(8,128)(2,1)S(1)}, u32[]{:S(2)}, u32[]{:S(2)}) collective-permute-start(bf16[512,384]{1,0:T(8,128)(2,1)S(1)} %pad_maximum_fusion.refs_6_), channel_id=1, source_target_pairs={{0,1},{1,2},{2,3},{3,0},{4,5},{5,6},{6,7},{7,4},{8,9},{9,10},{10,1... | collective-permute-start | bytes 1179656 | tf_op jit(solution)/shard_map/ppermute | solution.py:28
  7.8 16.5 %collective-permute-start.6 = (bf16[512,384]{1,0:T(8,128)(2,1)S(1)}, bf16[512,384]{1,0:T(8,128)(2,1)S(1)}, u32[]{:S(2)}, u32[]{:S(2)}) collective-permute-start(bf16[512,384]{1,0:T(8,128)(2,1)S(1)} %pad_maximum_fusion.refs_6_), channel_id=1, source_target_pairs={{0,3},{1,0},{2,1},{3,2},{4,7},{5,4},{6,5},{7,6},{8,11},{9,8},{10,9... | collective-permute-start | bytes 1179656 | tf_op jit(solution)/shard_map/ppermute | solution.py:28
  9.2 17.8 %collective-permute-start.7 = (bf16[512,384]{1,0:T(8,128)(2,1)S(1)}, bf16[512,384]{1,0:T(8,128)(2,1)S(1)}, u32[]{:S(2)}, u32[]{:S(2)}) collective-permute-start(bf16[512,384]{1,0:T(8,128)(2,1)S(1)} %pad_maximum_fusion.refs_6_), channel_id=1, source_target_pairs={{0,2},{1,3},{2,0},{3,1},{4,6},{5,7},{6,4},{7,5},{8,10},{9,11},{10,... | collective-permute-start | bytes 1179656 | tf_op jit(solution)/shard_map/ppermute | solution.py:28
  10.9 1.0 %copy-start = (f32[1,1,8,128,128]{4,3,2,1,0:T(8,128)S(1)}, f32[1,1,8,128,128]{4,3,2,1,0:T(8,128)}, u32[]{:S(2)}) copy-start(f32[1,1,8,128,128]{4,3,2,1,0:T(8,128)} %param.6) | copy-start | bytes 1572868
  11.9 0.9 %copy-start.1 = (bf16[1,128,1024]{2,1,0:T(8,128)(2,1)S(1)}, bf16[1,128,1024]{2,1,0:T(8,128)(2,1)}, u32[]{:S(2)}) copy-start(bf16[1,128,1024]{2,1,0:T(8,128)(2,1)} %param.5) | copy-start | bytes 786436
  14.3 15.0 %all-to-all-start = ((bf16[8,2,128,128]{3,2,1,0:T(8,128)(2,1)}), bf16[8,2,128,128]{3,2,1,0:T(8,128)(2,1)S(1)}, u32[]{:S(2)}, u32[]{:S(2)}) async-start(bf16[8,2,128,128]{3,2,1,0:T(8,128)(2,1)} %shard_map.61), calls=%async_computation | async-start | bytes 1048576 | tf_op jit(solution)/shard_map/all_to_all | solution.py:258
  19.4 15.7 %collective-permute-start.2 = (bf16[128,2048]{1,0:T(8,128)(2,1)}, bf16[128,2048]{1,0:T(8,128)(2,1)}, u32[]{:S(2)}, u32[]{:S(2)}) collective-permute-start(bf16[128,2048]{1,0:T(8,128)(2,1)} %bitcast.4.refs_1_), channel_id=1, source_target_pairs={{0,4},{4,0},{8,12},{12,8},{16,20},{20,16},{24,28},{28,24},{32,36},... | collective-permute-start | bytes 1572872 | tf_op jit(solution)/shard_map/ppermute | solution.py:24
  19.7 14.8 %collective-permute-start.8 = (bf16[64,2048]{1,0:T(8,128)(2,1)S(1)}, bf16[64,2048]{1,0:T(8,128)(2,1)S(1)}, u32[]{:S(2)}, u32[]{:S(2)}) collective-permute-start(bf16[64,2048]{1,0:T(8,128)(2,1)S(1)} %slice.8), channel_id=1, source_target_pairs={{0,8},{4,12},{8,16},{12,20},{16,24},{20,28},{24,0},{28,4},{32,40},... | collective-permute-start | bytes 786440 | tf_op jit(solution)/shard_map/ppermute | solution.py:24
  23.0 12.2 %collective-permute-start.9 = (bf16[64,2048]{1,0:T(8,128)(2,1)}, bf16[64,2048]{1,0:T(8,128)(2,1)S(1)}, u32[]{:S(2)}, u32[]{:S(2)}) collective-permute-start(bf16[64,2048]{1,0:T(8,128)(2,1)} %slice.9), channel_id=1, source_target_pairs={{0,24},{4,28},{8,0},{12,4},{16,8},{20,12},{24,16},{28,20},{32,56},... | collective-permute-start | bytes 786440 | tf_op jit(solution)/shard_map/ppermute | solution.py:24
  24.2 10.9 %collective-permute-start.3 = (bf16[128,2048]{1,0:T(8,128)(2,1)S(1)}, bf16[128,2048]{1,0:T(8,128)(2,1)}, u32[]{:S(2)}, u32[]{:S(2)}) collective-permute-start(bf16[128,2048]{1,0:T(8,128)(2,1)S(1)} %collective-permute-done.refs_2_), channel_id=1, source_target_pairs={{0,4},{4,0},{8,12},{12,8},{16,20},{20,16},{24,28},{28,24},{32,36},... | collective-permute-start | bytes 1572872 | tf_op jit(solution)/shard_map/ppermute | solution.py:24
  27.0 8.1 %collective-permute-start.4 = (bf16[128,2048]{1,0:T(8,128)(2,1)}, bf16[128,2048]{1,0:T(8,128)(2,1)}, u32[]{:S(2)}, u32[]{:S(2)}) collective-permute-start(bf16[128,2048]{1,0:T(8,128)(2,1)} %collective-permute-done.1.refs_3_), channel_id=1, source_target_pairs={{0,4},{4,0},{8,12},{12,8},{16,20},{20,16},{24,28},{28,24},{32,36},... | collective-permute-start | bytes 1572872 | tf_op jit(solution)/shard_map/ppermute | solution.py:24
  34.4 2.6 %collective-permute-start.10 = (bf16[64,2048]{1,0:T(8,128)(2,1)S(1)}, bf16[64,2048]{1,0:T(8,128)(2,1)S(1)}, u32[]{:S(2)}, u32[]{:S(2)}) collective-permute-start(bf16[64,2048]{1,0:T(8,128)(2,1)S(1)} %collective-permute-done.8.refs_2_), channel_id=1, source_target_pairs={{0,4},{4,0},{8,12},{12,8},{16,20},{20,16},{24,28},{28,24},{32,36},... | collective-permute-start | bytes 786440 | tf_op jit(solution)/shard_map/ppermute | solution.py:24
  35.2 1.9 %collective-permute-start.11 = (bf16[64,2048]{1,0:T(8,128)(2,1)S(1)}, bf16[64,2048]{1,0:T(8,128)(2,1)S(1)}, u32[]{:S(2)}, u32[]{:S(2)}) collective-permute-start(bf16[64,2048]{1,0:T(8,128)(2,1)S(1)} %collective-permute-done.9.refs_3_), channel_id=1, source_target_pairs={{0,4},{4,0},{8,12},{12,8},{16,20},{20,16},{24,28},{28,24},{32,36},... | collective-permute-start | bytes 786440 | tf_op jit(solution)/shard_map/ppermute | solution.py:24
  40.9 7.8 %collective-permute-start.12 = (bf16[128,128]{1,0:T(8,128)(2,1)S(1)}, bf16[128,128]{1,0:T(8,128)(2,1)S(1)}, u32[]{:S(2)}, u32[]{:S(2)}) collective-permute-start(bf16[128,128]{1,0:T(8,128)(2,1)S(1)} %get-tuple-element.45), channel_id=1, source_target_pairs={{0,32},{4,36},{8,40},{12,44},{16,48},{20,52},{24,56},{28,60},{32,6... | collective-permute-start | bytes 98312 | tf_op jit(solution)/shard_map/ppermute | solution.py:24
  42.3 6.4 %collective-permute-start.13 = (bf16[128,128]{1,0:T(8,128)(2,1)S(1)}, bf16[128,128]{1,0:T(8,128)(2,1)S(1)}, u32[]{:S(2)}, u32[]{:S(2)}) collective-permute-start(bf16[128,128]{1,0:T(8,128)(2,1)S(1)} %get-tuple-element.45), channel_id=1, source_target_pairs={{0,64},{4,68},{8,72},{12,76},{16,80},{20,84},{24,88},{28,92},{32,9... | collective-permute-start | bytes 98312 | tf_op jit(solution)/shard_map/ppermute | solution.py:24
  44.9 3.8 %collective-permute-start.14 = (bf16[128,128]{1,0:T(8,128)(2,1)S(1)}, bf16[128,128]{1,0:T(8,128)(2,1)S(1)}, u32[]{:S(2)}, u32[]{:S(2)}) collective-permute-start(bf16[128,128]{1,0:T(8,128)(2,1)S(1)} %get-tuple-element.45), channel_id=1, source_target_pairs={{0,96},{4,100},{8,104},{12,108},{16,112},{20,116},{24,120},{28,124... | collective-permute-start | bytes 98312 | tf_op jit(solution)/shard_map/ppermute | solution.py:24
  49.7 8.1 %collective-permute-start.19 = (bf16[2048,384]{1,0:T(8,128)(2,1)S(1)}, bf16[2048,384]{1,0:T(8,128)(2,1)S(1)}, u32[]{:S(2)}, u32[]{:S(2)}) collective-permute-start(bf16[2048,384]{1,0:T(8,128)(2,1)S(1)} %get-tuple-element.54.refs_3_), channel_id=1, source_target_pairs={{0,4},{4,0},{8,12},{12,8},{16,20},{20,16},{24,28},{28,24},{32,36},... | collective-permute-start | bytes 4718600 | tf_op jit(solution)/shard_map/ppermute | solution.py:24
  51.1 6.6 %collective-permute-start.18 = (bf16[4,128,384]{2,1,0:T(8,128)(2,1)S(1)}, bf16[4,128,384]{2,1,0:T(8,128)(2,1)S(1)}, u32[]{:S(2)}, u32[]{:S(2)}) collective-permute-start(bf16[4,128,384]{2,1,0:T(8,128)(2,1)S(1)} %get-tuple-element.52), channel_id=1, source_target_pairs={{0,4},{4,0},{8,12},{12,8},{16,20},{20,16},{24,28},{28,24},{32,36},... | collective-permute-start | bytes 1179656 | tf_op jit(solution)/shard_map/ppermute | solution.py:24
  54.4 10.1 %collective-permute-start.15 = (bf16[4,8,16,384]{3,2,1,0:T(8,128)(2,1)S(1)}, bf16[4,8,16,384]{3,2,1,0:T(8,128)(2,1)S(1)}, u32[]{:S(2)}, u32[]{:S(2)}) collective-permute-start(bf16[4,8,16,384]{3,2,1,0:T(8,128)(2,1)S(1)} %get-tuple-element.48), channel_id=1, source_target_pairs={{0,1},{1,2},{2,3},{3,0},{4,36},{5,37},{6,38},{7,39},{8,9},{9,10},{... | collective-permute-start | bytes 1179656 | tf_op jit(solution)/shard_map/ppermute | solution.py:40
  54.9 12.2 %collective-permute-start.16 = (bf16[4,8,16,384]{3,2,1,0:T(8,128)(2,1)S(1)}, bf16[4,8,16,384]{3,2,1,0:T(8,128)(2,1)S(1)}, u32[]{:S(2)}, u32[]{:S(2)}) collective-permute-start(bf16[4,8,16,384]{3,2,1,0:T(8,128)(2,1)S(1)} %get-tuple-element.49), channel_id=1, source_target_pairs={{0,2},{1,3},{2,0},{3,1},{4,68},{5,69},{6,70},{7,71},{8,10},{9,11},... | collective-permute-start | bytes 1179656 | tf_op jit(solution)/shard_map/ppermute | solution.py:40
  57.7 9.7 %collective-permute-start.17 = (bf16[4,8,16,384]{3,2,1,0:T(8,128)(2,1)S(1)}, bf16[4,8,16,384]{3,2,1,0:T(8,128)(2,1)S(1)}, u32[]{:S(2)}, u32[]{:S(2)}) collective-permute-start(bf16[4,8,16,384]{3,2,1,0:T(8,128)(2,1)S(1)} %get-tuple-element.50), channel_id=1, source_target_pairs={{0,3},{1,0},{2,1},{3,2},{4,100},{5,101},{6,102},{7,103},{8,11},{9,... | collective-permute-start | bytes 1179656 | tf_op jit(solution)/shard_map/ppermute | solution.py:40
  59.4 8.8 %collective-permute-start.23 = (bf16[64,2048]{1,0:T(8,128)(2,1)S(1)}, bf16[64,2048]{1,0:T(8,128)(2,1)S(1)}, u32[]{:S(2)}, u32[]{:S(2)}) collective-permute-start(bf16[64,2048]{1,0:T(8,128)(2,1)S(1)} %get-tuple-element.55.refs_5_), channel_id=1, source_target_pairs={{0,8},{4,12},{8,16},{12,20},{16,24},{20,28},{24,0},{28,4},{32,40},... | collective-permute-start | bytes 786440 | tf_op jit(solution)/shard_map/ppermute | solution.py:24
  59.5 8.7 %collective-permute-start.24 = (bf16[64,2048]{1,0:T(8,128)(2,1)S(1)}, bf16[64,2048]{1,0:T(8,128)(2,1)S(1)}, u32[]{:S(2)}, u32[]{:S(2)}) collective-permute-start(bf16[64,2048]{1,0:T(8,128)(2,1)S(1)} %get-tuple-element.63), channel_id=1, source_target_pairs={{0,24},{4,28},{8,0},{12,4},{16,8},{20,12},{24,16},{28,20},{32,56},... | collective-permute-start | bytes 786440 | tf_op jit(solution)/shard_map/ppermute | solution.py:24
  68.9 20.5 %collective-permute-start.25 = (bf16[128,2048]{1,0:T(8,128)(2,1)S(1)}, bf16[128,2048]{1,0:T(8,128)(2,1)S(1)}, u32[]{:S(2)}, u32[]{:S(2)}) collective-permute-start(bf16[128,2048]{1,0:T(8,128)(2,1)S(1)} %get-tuple-element.64), channel_id=1, source_target_pairs={{0,8},{4,12},{8,16},{12,20},{16,24},{20,28},{24,0},{28,4},{32,40},... | collective-permute-start | bytes 1572872 | tf_op jit(solution)/shard_map/ppermute | solution.py:24
  69.0 20.5 %collective-permute-start.26 = (bf16[128,2048]{1,0:T(8,128)(2,1)S(1)}, bf16[128,2048]{1,0:T(8,128)(2,1)S(1)}, u32[]{:S(2)}, u32[]{:S(2)}) collective-permute-start(bf16[128,2048]{1,0:T(8,128)(2,1)S(1)} %get-tuple-element.65), channel_id=1, source_target_pairs={{0,24},{4,28},{8,0},{12,4},{16,8},{20,12},{24,16},{28,20},{32,56},... | collective-permute-start | bytes 1572872 | tf_op jit(solution)/shard_map/ppermute | solution.py:24
  71.6 6.0 %collective-permute-start.20 = (bf16[8,16,384]{2,1,0:T(8,128)(2,1)S(1)}, bf16[8,16,384]{2,1,0:T(8,128)(2,1)S(1)}, u32[]{:S(2)}, u32[]{:S(2)}) collective-permute-start(bf16[8,16,384]{2,1,0:T(8,128)(2,1)S(1)} %get-tuple-element.58), channel_id=1, source_target_pairs={{0,32},{1,33},{2,34},{3,35},{4,5},{5,6},{6,7},{7,4},{8,40},{9,41},... | collective-permute-start | bytes 294920 | tf_op jit(solution)/shard_map/ppermute | solution.py:40
  71.9 5.7 %collective-permute-start.21 = (bf16[8,16,384]{2,1,0:T(8,128)(2,1)S(1)}, bf16[8,16,384]{2,1,0:T(8,128)(2,1)S(1)}, u32[]{:S(2)}, u32[]{:S(2)}) collective-permute-start(bf16[8,16,384]{2,1,0:T(8,128)(2,1)S(1)} %get-tuple-element.59), channel_id=1, source_target_pairs={{0,64},{1,65},{2,66},{3,67},{4,6},{5,7},{6,4},{7,5},{8,72},{9,73},... | collective-permute-start | bytes 294920 | tf_op jit(solution)/shard_map/ppermute | solution.py:40
  73.7 4.6 %collective-permute-start.22 = (bf16[8,16,384]{2,1,0:T(8,128)(2,1)S(1)}, bf16[8,16,384]{2,1,0:T(8,128)(2,1)S(1)}, u32[]{:S(2)}, u32[]{:S(2)}) collective-permute-start(bf16[8,16,384]{2,1,0:T(8,128)(2,1)S(1)} %get-tuple-element.60), channel_id=1, source_target_pairs={{0,96},{1,97},{2,98},{3,99},{4,7},{5,4},{6,5},{7,6},{8,104},{9,105... | collective-permute-start | bytes 294920 | tf_op jit(solution)/shard_map/ppermute | solution.py:40

commit v13 on v12

--- a/solution.py
+++ b/solution.py
@@ -279,7 +279,8 @@
         flops=big,
     )
     own_w = whole_w
-    totals = [ctx_hop(total, dy=s) for s in (1, 2, 3)]
+    far, near, last_one = (ctx_hop(total, dy=s) for s in (2, 1, 3))
+    totals = [near, far, last_one]
     dq, dk0, dv0, xt = call(
         lambda *refs: within(alpha, beta, *refs),
         [shape((1024, HD), BF), shape((1024, HD), F32), shape((1024, HD), F32), shape((2048, 1024), BF)],
@@ -318,13 +319,13 @@
         deps=(far_up,),
         limit=12,
     )
-    parts = [parts[0]] + [plane_hop(parts[s], s, 0) for s in (1, 2, 3)]
+    parts = [parts[0]] + [plane_hop(parts[s], s, 0) for s in (2, 1, 3)]
     far_up, far_down = ctx_hop(far_up, dz=1), ctx_hop(far_down, dz=-1)
     parts = call(turn, [shape((8, 16, 384), BF)] * 4, [idx, *parts], deps=(gx,), limit=4)
     up, down = call(
         merge, [shape((TOK, 2048), BF)] * 2, [idx, up, down, far_up, far_down], flops=1 << 34, deps=(parts[0],), limit=6
     )
-    parts = [parts[0]] + [plane_hop(parts[s], s, 1) for s in (1, 2, 3)]
+    parts = [parts[0]] + [plane_hop(parts[s], s, 1) for s in (2, 1, 3)]
     up, down = ctx_hop(up, dz=1), ctx_hop(down, dz=-1)
     owned = sum(p.astype(F32) for p in parts).astype(BF)
     owned = lax.all_to_all(owned, "ctx", 0, 0, axis_index_groups=rows_y)

time: 91.4 us -> 90.9 us (level)
  starting transfers between devices: 41.6 us -> 43.4 us
  waiting for transfers between devices: 11.2 us -> 9.64 us
    ppermute x6, starting transfers between devices: 6.86 us -> 8.68 us  [plane_hop(): return lax.ppermute(block, ('ctx', 'zero'), route)]
    ppermute x6, waiting for transfers between devices: 5.97 us -> 4.42 us  [plane_hop(): return lax.ppermute(block, ('ctx', 'zero'), route)]
  transfers between devices with their start and end apart: 28 -> 28, of which waited for: 5 -> 4; matrix products, arithmetic and copies ran while one was open for 3% -> 3% of each run, Pallas kernels for 16% -> 16%
where the time goes in v13:
time: 90.9 us; the launch traced here: 90.5 us
  starting transfers between devices  43.4 us (48%)
  Pallas kernels  21.3 us (23%)
  blocking collectives  10.4 us (11%)
  waiting for transfers between devices  9.64 us (11%)
  local copies, waits for them, and re-layouts  4.74 us (5%)
    ppermute x18, starting transfers between devices, ctx_hop(): return lax.ppermute(block, 'ctx', route)  25.2 us
    pallas_call x12, Pallas kernels, call(): pl.pallas_call(run, out_shape=list(outs), in_specs=[pl.BlockSpec(memory_s...  21.3 us
    all_to_all x1, blocking collectives, body(): owned = lax.all_to_all(owned, 'ctx', 0, 0, axis_index_groups=rows_y)  10.4 us
    ppermute x6, starting transfers between devices, plane_hop(): return lax.ppermute(block, ('ctx', 'zero'), route)  8.68 us
    ppermute x18, waiting for transfers between devices, ctx_hop(): return lax.ppermute(block, 'ctx', route)  5.21 us
    all_to_all x1, starting transfers between devices, body(): gs = lax.all_to_all(bundle, 'ctx', 0, 0, axis_index_groups=rows_y)  5.19 us
    ppermute x6, waiting for transfers between devices, plane_hop(): return lax.ppermute(block, ('ctx', 'zero'), route)  4.42 us
    ppermute x3, starting transfers between devices, x_hop(): return lax.ppermute(block, 'zero', [(i, (i + dx) % NX) for i in range(NX)])  4.28 us
  transfers between devices with their start and end apart: 28, of which 4 were waited for; matrix products, arithmetic and copies ran while one was open for 3% of the time, Pallas kernels for 16%

profile of v13, /device:TPU:1, one launch (start us, length us, event | category | flops | bytes accessed | tf_op | source)
XLA Modules:
  0.0 90.5 jit_solution(16149647484577027378)
XLA Ops:
  0.6 2.5 %collective-permute-start = (bf16[128,2048]{1,0:T(8,128)(2,1)}, bf16[128,2048]{1,0:T(8,128)(2,1)S(1)}, u32[]{:S(2)}, u32[]{:S(2)}) collective-permute-start(bf16[128,2048]{1,0:T(8,128)(2,1)} %bitcast.4.refs_1_), channel_id=1, source_target_pairs={{0,8},{4,12},{8,16},{12,20},{16,24},{20,28},{24,0},{28,4},{32,40},... | collective-permute-start | bytes 1572872 | tf_op jit(solution)/shard_map/ppermute | solution.py:24
  3.2 2.2 %collective-permute-start.1 = (bf16[128,2048]{1,0:T(8,128)(2,1)}, bf16[128,2048]{1,0:T(8,128)(2,1)}, u32[]{:S(2)}, u32[]{:S(2)}) collective-permute-start(bf16[128,2048]{1,0:T(8,128)(2,1)} %bitcast.4.refs_1_), channel_id=1, source_target_pairs={{0,24},{4,28},{8,0},{12,4},{16,8},{20,12},{24,16},{28,20},{32,56},... | collective-permute-start | bytes 1572872 | tf_op jit(solution)/shard_map/ppermute | solution.py:24
  5.4 1.1 %constant_dynamic-slice_fusion.2 = (bf16[512,128]{1,0:T(8,128)(2,1)S(1)}, bf16[512,128]{1,0:T(8,128)(2,1)S(1)}, bf16[512,128]{1,0:T(8,128)(2,1)S(1)}) fusion(bf16[512,3072]{1,0:T(8,128)(2,1)} %param.7, s32[]{:T(128)S(6)} %select_n.31, s32[]{:T(128)S(6)} %select_n.33, s32[]{:T(128)S(6)} %select_n.32), kind=kLoop, calls=%fused_computation.4 | loop fusion | bytes 786444 | tf_op jit(solution)/shard_map/dynamic_slice | solution.py:253
  6.5 1.3 %collective-permute-start.5 = (bf16[512,384]{1,0:T(8,128)(2,1)S(1)}, bf16[512,384]{1,0:T(8,128)(2,1)S(1)}, u32[]{:S(2)}, u32[]{:S(2)}) collective-permute-start(bf16[512,384]{1,0:T(8,128)(2,1)S(1)} %pad_maximum_fusion.refs_6_), channel_id=1, source_target_pairs={{0,1},{1,2},{2,3},{3,0},{4,5},{5,6},{6,7},{7,4},{8,9},{9,10},{10,1... | collective-permute-start | bytes 1179656 | tf_op jit(solution)/shard_map/ppermute | solution.py:28
  7.8 1.5 %collective-permute-start.6 = (bf16[512,384]{1,0:T(8,128)(2,1)S(1)}, bf16[512,384]{1,0:T(8,128)(2,1)S(1)}, u32[]{:S(2)}, u32[]{:S(2)}) collective-permute-start(bf16[512,384]{1,0:T(8,128)(2,1)S(1)} %pad_maximum_fusion.refs_6_), channel_id=1, source_target_pairs={{0,3},{1,0},{2,1},{3,2},{4,7},{5,4},{6,5},{7,6},{8,11},{9,8},{10,9... | collective-permute-start | bytes 1179656 | tf_op jit(solution)/shard_map/ppermute | solution.py:28
  9.2 1.5 %collective-permute-start.7 = (bf16[512,384]{1,0:T(8,128)(2,1)S(1)}, bf16[512,384]{1,0:T(8,128)(2,1)S(1)}, u32[]{:S(2)}, u32[]{:S(2)}) collective-permute-start(bf16[512,384]{1,0:T(8,128)(2,1)S(1)} %pad_maximum_fusion.refs_6_), channel_id=1, source_target_pairs={{0,2},{1,3},{2,0},{3,1},{4,6},{5,7},{6,4},{7,5},{8,10},{9,11},{10,... | collective-permute-start | bytes 1179656 | tf_op jit(solution)/shard_map/ppermute | solution.py:28
  10.8 0.1 pad_add_fusion.refs_0_
  10.9 1.0 %copy-done = f32[1,1,8,128,128]{4,3,2,1,0:T(8,128)S(1)} copy-done((f32[1,1,8,128,128]{4,3,2,1,0:T(8,128)S(1)}, f32[1,1,8,128,128]{4,3,2,1,0:T(8,128)}, u32[]{:S(2)}) %copy-start) | copy-done | bytes 524312
  11.9 0.9 %copy-done.1 = bf16[1,128,1024]{2,1,0:T(8,128)(2,1)S(1)} copy-done((bf16[1,128,1024]{2,1,0:T(8,128)(2,1)S(1)}, bf16[1,128,1024]{2,1,0:T(8,128)(2,1)}, u32[]{:S(2)}) %copy-start.1) | copy-done | bytes 262168
  12.8 1.4 %shard_map.61 = bf16[8,2,128,128]{3,2,1,0:T(8,128)(2,1)} custom-call(s32[4]{0:T(128)S(1)} %pad_add_fusion.refs_0_, bf16[128,1024]{1,0:T(8,128)(2,1)S(1)} %bitcast.9, f32[8,128,128]{2,1,0:T(8,128)S(1)} %bitcast.8), custom_call_target="tpu_custom_call" | custom-call | bytes 1310736 | tf_op jit(solution)/shard_map/pallas_call | solution.py:63
  14.3 5.2 %all-to-all-start = ((bf16[8,2,128,128]{3,2,1,0:T(8,128)(2,1)}), bf16[8,2,128,128]{3,2,1,0:T(8,128)(2,1)S(1)}, u32[]{:S(2)}, u32[]{:S(2)}) async-start(bf16[8,2,128,128]{3,2,1,0:T(8,128)(2,1)} %shard_map.61), calls=%async_computation | async-start | bytes 1048576 | tf_op jit(solution)/shard_map/all_to_all | solution.py:258
  19.4 0.2 collective-permute-start.2
  19.7 1.6 %collective-permute-start.8 = (bf16[64,2048]{1,0:T(8,128)(2,1)S(1)}, bf16[64,2048]{1,0:T(8,128)(2,1)S(1)}, u32[]{:S(2)}, u32[]{:S(2)}) collective-permute-start(bf16[64,2048]{1,0:T(8,128)(2,1)S(1)} %slice.8), channel_id=1, source_target_pairs={{0,8},{4,12},{8,16},{12,20},{16,24},{20,28},{24,0},{28,4},{32,40},... | collective-permute-start | bytes 786440 | tf_op jit(solution)/shard_map/ppermute | solution.py:24
  21.3 1.7 %slice.9 = bf16[64,2048]{1,0:T(8,128)(2,1)} slice(bf16[128,2048]{1,0:T(8,128)(2,1)} %collective-permute-done.1.refs_3_), slice={[64:128], [0:2048]} | slice | bytes 524288 | tf_op jit(solution)/shard_map/slice | solution.py:260
  23.0 1.3 %collective-permute-start.9 = (bf16[64,2048]{1,0:T(8,128)(2,1)}, bf16[64,2048]{1,0:T(8,128)(2,1)S(1)}, u32[]{:S(2)}, u32[]{:S(2)}) collective-permute-start(bf16[64,2048]{1,0:T(8,128)(2,1)} %slice.9), channel_id=1, source_target_pairs={{0,24},{4,28},{8,0},{12,4},{16,8},{20,12},{24,16},{28,20},{32,56},... | collective-permute-start | bytes 786440 | tf_op jit(solution)/shard_map/ppermute | solution.py:24
  24.2 2.8 %collective-permute-start.3 = (bf16[128,2048]{1,0:T(8,128)(2,1)S(1)}, bf16[128,2048]{1,0:T(8,128)(2,1)}, u32[]{:S(2)}, u32[]{:S(2)}) collective-permute-start(bf16[128,2048]{1,0:T(8,128)(2,1)S(1)} %collective-permute-done.refs_2_), channel_id=1, source_target_pairs={{0,4},{4,0},{8,12},{12,8},{16,20},{20,16},{24,28},{28,24},{32,36},... | collective-permute-start | bytes 1572872 | tf_op jit(solution)/shard_map/ppermute | solution.py:24
  27.0 1.7 %collective-permute-start.4 = (bf16[128,2048]{1,0:T(8,128)(2,1)}, bf16[128,2048]{1,0:T(8,128)(2,1)}, u32[]{:S(2)}, u32[]{:S(2)}) collective-permute-start(bf16[128,2048]{1,0:T(8,128)(2,1)} %collective-permute-done.1.refs_3_), channel_id=1, source_target_pairs={{0,4},{4,0},{8,12},{12,8},{16,20},{20,16},{24,28},{28,24},{32,36},... | collective-permute-start | bytes 1572872 | tf_op jit(solution)/shard_map/ppermute | solution.py:24
  28.7 0.5 shard_map.59.refs_7_
  29.3 5.2 %collective-permute-done.8.refs_2_ = bf16[64,2048]{1,0:T(8,128)(2,1)S(1)} collective-permute-done((bf16[64,2048]{1,0:T(8,128)(2,1)S(1)}, bf16[64,2048]{1,0:T(8,128)(2,1)S(1)}, u32[]{:S(2)}, u32[]{:S(2)}) %collective-permute-start.8) | collective-permute-done | bytes 262176 | tf_op jit(solution)/shard_map/ppermute | solution.py:24
  34.4 0.7 collective-permute-start.10
  35.2 1.9 %shard_map.60.refs_1_ = bf16[768,2048]{1,0:T(8,128)(2,1)S(1)} custom-call(s32[4]{0:T(128)S(1)} %pad_add_fusion.refs_0_, bf16[128,2048]{1,0:T(8,128)(2,1)} %bitcast.4.refs_1_, bf16[128,2048]{1,0:T(8,128)(2,1)S(1)} %collective-permute-done.refs_2_, bf16[128,2048]{1,0:T(8,128)(2,1)} %collective-permute-done.1.refs_3_, ...), custom_call_target="tpu_custom_call" | custom-call | flops 8589934592 | bytes 6291472 | tf_op jit(solution)/shard_map/pallas_call | solution.py:63
  37.1 3.8 %shard_map.62 = (bf16[1024,384]{1,0:T(8,128)(2,1)S(1)}, f32[8,128,128]{2,1,0:T(8,128)S(1)}, bf16[128,128]{1,0:T(8,128)(2,1)S(1)}, bf16[256,2048]{1,0:T(8,128)(2,1)S(1)}, bf16[2048,384]{1,0:T(8,128)(2,1)S(1)}) custom-call(s32[4]{0:T(128)S(1)} %pad_add_fusion.refs_0_, bf16[768,2048]{1,0:T(8,128)(2,1)S(1)} %shard_map.60.refs_1_, ...), custom_call_target="tpu_custom_call" | custom-call | flops 1610612736 | bytes 10256400 | tf_op jit(solution)/shard_map/pallas_call | solution.py:63
  40.9 1.4 %collective-permute-start.12 = (bf16[128,128]{1,0:T(8,128)(2,1)S(1)}, bf16[128,128]{1,0:T(8,128)(2,1)S(1)}, u32[]{:S(2)}, u32[]{:S(2)}) collective-permute-start(bf16[128,128]{1,0:T(8,128)(2,1)S(1)} %get-tuple-element.45), channel_id=1, source_target_pairs={{0,32},{4,36},{8,40},{12,44},{16,48},{20,52},{24,56},{28,60},{32,6... | collective-permute-start | bytes 98312 | tf_op jit(solution)/shard_map/ppermute | solution.py:24
  42.3 2.6 %collective-permute-start.13 = (bf16[128,128]{1,0:T(8,128)(2,1)S(1)}, bf16[128,128]{1,0:T(8,128)(2,1)S(1)}, u32[]{:S(2)}, u32[]{:S(2)}) collective-permute-start(bf16[128,128]{1,0:T(8,128)(2,1)S(1)} %get-tuple-element.45), channel_id=1, source_target_pairs={{0,64},{4,68},{8,72},{12,76},{16,80},{20,84},{24,88},{28,92},{32,9... | collective-permute-start | bytes 98312 | tf_op jit(solution)/shard_map/ppermute | solution.py:24
  44.9 1.1 %collective-permute-start.14 = (bf16[128,128]{1,0:T(8,128)(2,1)S(1)}, bf16[128,128]{1,0:T(8,128)(2,1)S(1)}, u32[]{:S(2)}, u32[]{:S(2)}) collective-permute-start(bf16[128,128]{1,0:T(8,128)(2,1)S(1)} %get-tuple-element.45), channel_id=1, source_target_pairs={{0,96},{4,100},{8,104},{12,108},{16,112},{20,116},{24,120},{28,124... | collective-permute-start | bytes 98312 | tf_op jit(solution)/shard_map/ppermute | solution.py:24
  45.9 2.7 %shard_map.63 = (bf16[1024,128]{1,0:T(8,128)(2,1)S(1)}, f32[1024,128]{1,0:T(8,128)S(1)}, f32[1024,128]{1,0:T(8,128)S(1)}, bf16[2048,1024]{1,0:T(8,128)(2,1)S(1)}) custom-call(s32[4]{0:T(128)S(1)} %pad_add_fusion.refs_0_, bf16[768,2048]{1,0:T(8,128)(2,1)S(1)} %shard_map.60.refs_1_, bf16[256,2048]{1,0:T(8,128)(2,1)S(1)} %get-tuple-element.38.refs_2_, ...), custom_call_target="tpu_custom_call" | custom-call | flops 402653184 | bytes 11010064 | tf_op jit(solution)/shard_map/pallas_call | solution.py:63
  48.7 1.0 %shard_map.64 = (bf16[1024,384]{1,0:T(8,128)(2,1)S(1)}, bf16[4,128,384]{2,1,0:T(8,128)(2,1)S(1)}, bf16[4,128,384]{2,1,0:T(8,128)(2,1)S(1)}) custom-call(s32[4]{0:T(128)S(1)} %pad_add_fusion.refs_0_, bf16[1024,384]{1,0:T(8,128)(2,1)S(1)} %get-tuple-element.39.refs_4_.refs_1_, bf16[1024,128]{1,0:T(8,128)(2,1)S(1)} %get-tuple-element.41.refs_2_, ...), custom_call_target="tpu_custom_call" | custom-call | flops 100663296 | bytes 4292624 | tf_op jit(solution)/shard_map/pallas_call | solution.py:63
  49.7 1.4 %collective-permute-start.19 = (bf16[2048,384]{1,0:T(8,128)(2,1)S(1)}, bf16[2048,384]{1,0:T(8,128)(2,1)S(1)}, u32[]{:S(2)}, u32[]{:S(2)}) collective-permute-start(bf16[2048,384]{1,0:T(8,128)(2,1)S(1)} %get-tuple-element.54.refs_3_), channel_id=1, source_target_pairs={{0,4},{4,0},{8,12},{12,8},{16,20},{20,16},{24,28},{28,24},{32,36},... | collective-permute-start | bytes 4718600 | tf_op jit(solution)/shard_map/ppermute | solution.py:24
  51.1 0.3 collective-permute-start.18
  51.4 3.0 %shard_map.65 = (bf16[4,8,16,384]{3,2,1,0:T(8,128)(2,1)S(1)}, bf16[4,8,16,384]{3,2,1,0:T(8,128)(2,1)S(1)}, bf16[4,8,16,384]{3,2,1,0:T(8,128)(2,1)S(1)}, bf16[4,8,16,384]{3,2,1,0:T(8,128)(2,1)S(1)}) custom-call(s32[4]{0:T(128)S(1)} %pad_add_fusion.refs_0_, bf16[2048,1024]{1,0:T(8,128)(2,1)S(1)} %get-tuple-element.40.refs_1_, ...), custom_call_target="tpu_custom_call" | custom-call | flops 1610612736 | bytes 6553616 | tf_op jit(solution)/shard_map/pallas_call | solution.py:63
  54.4 1.1 %collective-permute-start.15 = (bf16[4,8,16,384]{3,2,1,0:T(8,128)(2,1)S(1)}, bf16[4,8,16,384]{3,2,1,0:T(8,128)(2,1)S(1)}, u32[]{:S(2)}, u32[]{:S(2)}) collective-permute-start(bf16[4,8,16,384]{3,2,1,0:T(8,128)(2,1)S(1)} %get-tuple-element.48), channel_id=1, source_target_pairs={{0,2},{1,3},{2,0},{3,1},{4,68},{5,69},{6,70},{7,71},{8,10},{9,11},... | collective-permute-start | bytes 1179656 | tf_op jit(solution)/shard_map/ppermute | solution.py:40
  55.5 1.6 %collective-permute-start.16 = (bf16[4,8,16,384]{3,2,1,0:T(8,128)(2,1)S(1)}, bf16[4,8,16,384]{3,2,1,0:T(8,128)(2,1)S(1)}, u32[]{:S(2)}, u32[]{:S(2)}) collective-permute-start(bf16[4,8,16,384]{3,2,1,0:T(8,128)(2,1)S(1)} %get-tuple-element.49), channel_id=1, source_target_pairs={{0,1},{1,2},{2,3},{3,0},{4,36},{5,37},{6,38},{7,39},{8,9},{9,10},{... | collective-permute-start | bytes 1179656 | tf_op jit(solution)/shard_map/ppermute | solution.py:40
  57.1 1.0 %collective-permute-start.17 = (bf16[4,8,16,384]{3,2,1,0:T(8,128)(2,1)S(1)}, bf16[4,8,16,384]{3,2,1,0:T(8,128)(2,1)S(1)}, u32[]{:S(2)}, u32[]{:S(2)}) collective-permute-start(bf16[4,8,16,384]{3,2,1,0:T(8,128)(2,1)S(1)} %get-tuple-element.50), channel_id=1, source_target_pairs={{0,3},{1,0},{2,1},{3,2},{4,100},{5,101},{6,102},{7,103},{8,11},{9,... | collective-permute-start | bytes 1179656 | tf_op jit(solution)/shard_map/ppermute | solution.py:40
  58.2 1.6 %shard_map.66 = (bf16[64,2048]{1,0:T(8,128)(2,1)S(1)}, bf16[64,2048]{1,0:T(8,128)(2,1)S(1)}) custom-call(s32[4]{0:T(128)S(1)} %pad_add_fusion.refs_0_, bf16[4,128,384]{2,1,0:T(8,128)(2,1)S(1)} %get-tuple-element.51.refs_1_, bf16[4,128,384]{2,1,0:T(8,128)(2,1)S(1)} %collective-permute-done.18.refs_2_, bf16[2048,384]{1,0:T(8,128)(2,1)S(1)} %get-tuple-element.54.refs_3_, ...), custom_call_target="tpu_custom_call" | custom-call | flops 402653184 | bytes 4456464 | tf_op jit(solution)/shard_map/pallas_call | solution.py:63
  59.8 0.1 collective-permute-start.23
  59.9 2.7 %collective-permute-start.24 = (bf16[64,2048]{1,0:T(8,128)(2,1)S(1)}, bf16[64,2048]{1,0:T(8,128)(2,1)S(1)}, u32[]{:S(2)}, u32[]{:S(2)}) collective-permute-start(bf16[64,2048]{1,0:T(8,128)(2,1)S(1)} %get-tuple-element.63), channel_id=1, source_target_pairs={{0,24},{4,28},{8,0},{12,4},{16,8},{20,12},{24,16},{28,20},{32,56},... | collective-permute-start | bytes 786440 | tf_op jit(solution)/shard_map/ppermute | solution.py:24
  62.6 2.4 %shard_map.67 = (f32[128,2048]{1,0:T(8,128)S(1)}, bf16[128,2048]{1,0:T(8,128)(2,1)S(1)}, bf16[128,2048]{1,0:T(8,128)(2,1)S(1)}) custom-call(s32[4]{0:T(128)S(1)} %pad_add_fusion.refs_0_, bf16[4,128,384]{2,1,0:T(8,128)(2,1)S(1)} %get-tuple-element.51.refs_1_, bf16[4,128,384]{2,1,0:T(8,128)(2,1)S(1)} %collective-permute-done.18.refs_2_, ...), custom_call_target="tpu_custom_call" | custom-call | flops 1610612736 | bytes 6029328 | tf_op jit(solution)/shard_map/pallas_call | solution.py:63
  65.0 2.1 %collective-permute-done.16.refs_3_ = bf16[4,8,16,384]{3,2,1,0:T(8,128)(2,1)S(1)} collective-permute-done((bf16[4,8,16,384]{3,2,1,0:T(8,128)(2,1)S(1)}, bf16[4,8,16,384]{3,2,1,0:T(8,128)(2,1)S(1)}, u32[]{:S(2)}, u32[]{:S(2)}) %collective-permute-start.16) | collective-permute-done | bytes 393248 | tf_op jit(solution)/shard_map/ppermute | solution.py:40
  67.1 0.7 shard_map.68
  67.9 0.7 shard_map.69
  68.6 0.1 collective-permute-start.25
  68.7 2.7 %collective-permute-start.26 = (bf16[128,2048]{1,0:T(8,128)(2,1)S(1)}, bf16[128,2048]{1,0:T(8,128)(2,1)S(1)}, u32[]{:S(2)}, u32[]{:S(2)}) collective-permute-start(bf16[128,2048]{1,0:T(8,128)(2,1)S(1)} %get-tuple-element.65), channel_id=1, source_target_pairs={{0,24},{4,28},{8,0},{12,4},{16,8},{20,12},{24,16},{28,20},{32,56},... | collective-permute-start | bytes 1572872 | tf_op jit(solution)/shard_map/ppermute | solution.py:24
  71.3 2.2 %collective-permute-start.20 = (bf16[8,16,384]{2,1,0:T(8,128)(2,1)S(1)}, bf16[8,16,384]{2,1,0:T(8,128)(2,1)S(1)}, u32[]{:S(2)}, u32[]{:S(2)}) collective-permute-start(bf16[8,16,384]{2,1,0:T(8,128)(2,1)S(1)} %get-tuple-element.58), channel_id=1, source_target_pairs={{0,64},{1,65},{2,66},{3,67},{4,6},{5,7},{6,4},{7,5},{8,72},{9,73},... | collective-permute-start | bytes 294920 | tf_op jit(solution)/shard_map/ppermute | solution.py:40
  73.5 2.7 %collective-permute-start.22 = (bf16[8,16,384]{2,1,0:T(8,128)(2,1)S(1)}, bf16[8,16,384]{2,1,0:T(8,128)(2,1)S(1)}, u32[]{:S(2)}, u32[]{:S(2)}) collective-permute-start(bf16[8,16,384]{2,1,0:T(8,128)(2,1)S(1)} %get-tuple-element.60), channel_id=1, source_target_pairs={{0,96},{1,97},{2,98},{3,99},{4,7},{5,4},{6,5},{7,6},{8,104},{9,105... | collective-permute-start | bytes 294920 | tf_op jit(solution)/shard_map/ppermute | solution.py:40
  76.2 0.1 collective-permute-done.20
  76.3 2.2 %collective-permute-done.21 = bf16[8,16,384]{2,1,0:T(8,128)(2,1)S(1)} collective-permute-done((bf16[8,16,384]{2,1,0:T(8,128)(2,1)S(1)}, bf16[8,16,384]{2,1,0:T(8,128)(2,1)S(1)}, u32[]{:S(2)}, u32[]{:S(2)}) %collective-permute-start.21) | collective-permute-done | bytes 98336 | tf_op jit(solution)/shard_map/ppermute | solution.py:40
  78.6 10.4 %all_to_all.10.refs_1_ = bf16[8,16,384]{2,1,0:T(8,128)(2,1)S(1)} all-to-all(bf16[8,16,384]{2,1,0:T(8,128)(2,1)S(1)} %add_convert_fusion), channel_id=1, replica_groups={{0,4,8,12,16,20,24,28},{32,36,40,44,48,52,56,60},{64,68,72,76,80,84,88,..., dimensions={0} | all-to-all | bytes 196608 | tf_op jit(solution)/shard_map/all_to_all | solution.py:331
  88.9 1.5 %shard_map.70 = (f32[16,3072]{1,0:T(8,128)}, bf16[128,2048]{1,0:T(8,128)(2,1)}) custom-call(s32[4]{0:T(128)S(1)} %pad_add_fusion.refs_0_, bf16[8,16,384]{2,1,0:T(8,128)(2,1)S(1)} %all_to_all.10.refs_1_, f32[128,2048]{1,0:T(8,128)S(1)} %get-tuple-element.56.refs_5_.refs_2_, bf16[128,2048]{1,0:T(8,128)(2,1)S(1)} %collective-permute-done.25.refs_3_, ...), custom_call_target="tpu_custom_call" | custom-call | bytes 2916368 | tf_op jit(solution)/shard_map/pallas_call | solution.py:63
  (31 shorter events, 0.2 us)
Async XLA Ops:
  0.6 18.8 %collective-permute-start = (bf16[128,2048]{1,0:T(8,128)(2,1)}, bf16[128,2048]{1,0:T(8,128)(2,1)S(1)}, u32[]{:S(2)}, u32[]{:S(2)}) collective-permute-start(bf16[128,2048]{1,0:T(8,128)(2,1)} %bitcast.4.refs_1_), channel_id=1, source_target_pairs={{0,8},{4,12},{8,16},{12,20},{16,24},{20,28},{24,0},{28,4},{32,40},... | collective-permute-start | bytes 1572872 | tf_op jit(solution)/shard_map/ppermute | solution.py:24
  3.2 16.5 %collective-permute-start.1 = (bf16[128,2048]{1,0:T(8,128)(2,1)}, bf16[128,2048]{1,0:T(8,128)(2,1)}, u32[]{:S(2)}, u32[]{:S(2)}) collective-permute-start(bf16[128,2048]{1,0:T(8,128)(2,1)} %bitcast.4.refs_1_), channel_id=1, source_target_pairs={{0,24},{4,28},{8,0},{12,4},{16,8},{20,12},{24,16},{28,20},{32,56},... | collective-permute-start | bytes 1572872 | tf_op jit(solution)/shard_map/ppermute | solution.py:24
  6.5 16.5 %collective-permute-start.5 = (bf16[512,384]{1,0:T(8,128)(2,1)S(1)}, bf16[512,384]{1,0:T(8,128)(2,1)S(1)}, u32[]{:S(2)}, u32[]{:S(2)}) collective-permute-start(bf16[512,384]{1,0:T(8,128)(2,1)S(1)} %pad_maximum_fusion.refs_6_), channel_id=1, source_target_pairs={{0,1},{1,2},{2,3},{3,0},{4,5},{5,6},{6,7},{7,4},{8,9},{9,10},{10,1... | collective-permute-start | bytes 1179656 | tf_op jit(solution)/shard_map/ppermute | solution.py:28
  7.8 16.5 %collective-permute-start.6 = (bf16[512,384]{1,0:T(8,128)(2,1)S(1)}, bf16[512,384]{1,0:T(8,128)(2,1)S(1)}, u32[]{:S(2)}, u32[]{:S(2)}) collective-permute-start(bf16[512,384]{1,0:T(8,128)(2,1)S(1)} %pad_maximum_fusion.refs_6_), channel_id=1, source_target_pairs={{0,3},{1,0},{2,1},{3,2},{4,7},{5,4},{6,5},{7,6},{8,11},{9,8},{10,9... | collective-permute-start | bytes 1179656 | tf_op jit(solution)/shard_map/ppermute | solution.py:28
  9.2 17.8 %collective-permute-start.7 = (bf16[512,384]{1,0:T(8,128)(2,1)S(1)}, bf16[512,384]{1,0:T(8,128)(2,1)S(1)}, u32[]{:S(2)}, u32[]{:S(2)}) collective-permute-start(bf16[512,384]{1,0:T(8,128)(2,1)S(1)} %pad_maximum_fusion.refs_6_), channel_id=1, source_target_pairs={{0,2},{1,3},{2,0},{3,1},{4,6},{5,7},{6,4},{7,5},{8,10},{9,11},{10,... | collective-permute-start | bytes 1179656 | tf_op jit(solution)/shard_map/ppermute | solution.py:28
  10.9 1.0 %copy-start = (f32[1,1,8,128,128]{4,3,2,1,0:T(8,128)S(1)}, f32[1,1,8,128,128]{4,3,2,1,0:T(8,128)}, u32[]{:S(2)}) copy-start(f32[1,1,8,128,128]{4,3,2,1,0:T(8,128)} %param.6) | copy-start | bytes 1572868
  11.9 0.9 %copy-start.1 = (bf16[1,128,1024]{2,1,0:T(8,128)(2,1)S(1)}, bf16[1,128,1024]{2,1,0:T(8,128)(2,1)}, u32[]{:S(2)}) copy-start(bf16[1,128,1024]{2,1,0:T(8,128)(2,1)} %param.5) | copy-start | bytes 786436
  14.3 15.0 %all-to-all-start = ((bf16[8,2,128,128]{3,2,1,0:T(8,128)(2,1)}), bf16[8,2,128,128]{3,2,1,0:T(8,128)(2,1)S(1)}, u32[]{:S(2)}, u32[]{:S(2)}) async-start(bf16[8,2,128,128]{3,2,1,0:T(8,128)(2,1)} %shard_map.61), calls=%async_computation | async-start | bytes 1048576 | tf_op jit(solution)/shard_map/all_to_all | solution.py:258
  19.4 15.7 %collective-permute-start.2 = (bf16[128,2048]{1,0:T(8,128)(2,1)}, bf16[128,2048]{1,0:T(8,128)(2,1)}, u32[]{:S(2)}, u32[]{:S(2)}) collective-permute-start(bf16[128,2048]{1,0:T(8,128)(2,1)} %bitcast.4.refs_1_), channel_id=1, source_target_pairs={{0,4},{4,0},{8,12},{12,8},{16,20},{20,16},{24,28},{28,24},{32,36},... | collective-permute-start | bytes 1572872 | tf_op jit(solution)/shard_map/ppermute | solution.py:24
  19.7 14.8 %collective-permute-start.8 = (bf16[64,2048]{1,0:T(8,128)(2,1)S(1)}, bf16[64,2048]{1,0:T(8,128)(2,1)S(1)}, u32[]{:S(2)}, u32[]{:S(2)}) collective-permute-start(bf16[64,2048]{1,0:T(8,128)(2,1)S(1)} %slice.8), channel_id=1, source_target_pairs={{0,8},{4,12},{8,16},{12,20},{16,24},{20,28},{24,0},{28,4},{32,40},... | collective-permute-start | bytes 786440 | tf_op jit(solution)/shard_map/ppermute | solution.py:24
  23.0 12.2 %collective-permute-start.9 = (bf16[64,2048]{1,0:T(8,128)(2,1)}, bf16[64,2048]{1,0:T(8,128)(2,1)S(1)}, u32[]{:S(2)}, u32[]{:S(2)}) collective-permute-start(bf16[64,2048]{1,0:T(8,128)(2,1)} %slice.9), channel_id=1, source_target_pairs={{0,24},{4,28},{8,0},{12,4},{16,8},{20,12},{24,16},{28,20},{32,56},... | collective-permute-start | bytes 786440 | tf_op jit(solution)/shard_map/ppermute | solution.py:24
  24.2 10.9 %collective-permute-start.3 = (bf16[128,2048]{1,0:T(8,128)(2,1)S(1)}, bf16[128,2048]{1,0:T(8,128)(2,1)}, u32[]{:S(2)}, u32[]{:S(2)}) collective-permute-start(bf16[128,2048]{1,0:T(8,128)(2,1)S(1)} %collective-permute-done.refs_2_), channel_id=1, source_target_pairs={{0,4},{4,0},{8,12},{12,8},{16,20},{20,16},{24,28},{28,24},{32,36},... | collective-permute-start | bytes 1572872 | tf_op jit(solution)/shard_map/ppermute | solution.py:24
  27.0 8.1 %collective-permute-start.4 = (bf16[128,2048]{1,0:T(8,128)(2,1)}, bf16[128,2048]{1,0:T(8,128)(2,1)}, u32[]{:S(2)}, u32[]{:S(2)}) collective-permute-start(bf16[128,2048]{1,0:T(8,128)(2,1)} %collective-permute-done.1.refs_3_), channel_id=1, source_target_pairs={{0,4},{4,0},{8,12},{12,8},{16,20},{20,16},{24,28},{28,24},{32,36},... | collective-permute-start | bytes 1572872 | tf_op jit(solution)/shard_map/ppermute | solution.py:24
  34.4 2.6 %collective-permute-start.10 = (bf16[64,2048]{1,0:T(8,128)(2,1)S(1)}, bf16[64,2048]{1,0:T(8,128)(2,1)S(1)}, u32[]{:S(2)}, u32[]{:S(2)}) collective-permute-start(bf16[64,2048]{1,0:T(8,128)(2,1)S(1)} %collective-permute-done.8.refs_2_), channel_id=1, source_target_pairs={{0,4},{4,0},{8,12},{12,8},{16,20},{20,16},{24,28},{28,24},{32,36},... | collective-permute-start | bytes 786440 | tf_op jit(solution)/shard_map/ppermute | solution.py:24
  35.2 1.9 %collective-permute-start.11 = (bf16[64,2048]{1,0:T(8,128)(2,1)S(1)}, bf16[64,2048]{1,0:T(8,128)(2,1)S(1)}, u32[]{:S(2)}, u32[]{:S(2)}) collective-permute-start(bf16[64,2048]{1,0:T(8,128)(2,1)S(1)} %collective-permute-done.9.refs_3_), channel_id=1, source_target_pairs={{0,4},{4,0},{8,12},{12,8},{16,20},{20,16},{24,28},{28,24},{32,36},... | collective-permute-start | bytes 786440 | tf_op jit(solution)/shard_map/ppermute | solution.py:24
  40.9 7.8 %collective-permute-start.12 = (bf16[128,128]{1,0:T(8,128)(2,1)S(1)}, bf16[128,128]{1,0:T(8,128)(2,1)S(1)}, u32[]{:S(2)}, u32[]{:S(2)}) collective-permute-start(bf16[128,128]{1,0:T(8,128)(2,1)S(1)} %get-tuple-element.45), channel_id=1, source_target_pairs={{0,32},{4,36},{8,40},{12,44},{16,48},{20,52},{24,56},{28,60},{32,6... | collective-permute-start | bytes 98312 | tf_op jit(solution)/shard_map/ppermute | solution.py:24
  42.3 6.4 %collective-permute-start.13 = (bf16[128,128]{1,0:T(8,128)(2,1)S(1)}, bf16[128,128]{1,0:T(8,128)(2,1)S(1)}, u32[]{:S(2)}, u32[]{:S(2)}) collective-permute-start(bf16[128,128]{1,0:T(8,128)(2,1)S(1)} %get-tuple-element.45), channel_id=1, source_target_pairs={{0,64},{4,68},{8,72},{12,76},{16,80},{20,84},{24,88},{28,92},{32,9... | collective-permute-start | bytes 98312 | tf_op jit(solution)/shard_map/ppermute | solution.py:24
  44.9 3.8 %collective-permute-start.14 = (bf16[128,128]{1,0:T(8,128)(2,1)S(1)}, bf16[128,128]{1,0:T(8,128)(2,1)S(1)}, u32[]{:S(2)}, u32[]{:S(2)}) collective-permute-start(bf16[128,128]{1,0:T(8,128)(2,1)S(1)} %get-tuple-element.45), channel_id=1, source_target_pairs={{0,96},{4,100},{8,104},{12,108},{16,112},{20,116},{24,120},{28,124... | collective-permute-start | bytes 98312 | tf_op jit(solution)/shard_map/ppermute | solution.py:24
  49.7 8.5 %collective-permute-start.19 = (bf16[2048,384]{1,0:T(8,128)(2,1)S(1)}, bf16[2048,384]{1,0:T(8,128)(2,1)S(1)}, u32[]{:S(2)}, u32[]{:S(2)}) collective-permute-start(bf16[2048,384]{1,0:T(8,128)(2,1)S(1)} %get-tuple-element.54.refs_3_), channel_id=1, source_target_pairs={{0,4},{4,0},{8,12},{12,8},{16,20},{20,16},{24,28},{28,24},{32,36},... | collective-permute-start | bytes 4718600 | tf_op jit(solution)/shard_map/ppermute | solution.py:24
  51.1 7.1 %collective-permute-start.18 = (bf16[4,128,384]{2,1,0:T(8,128)(2,1)S(1)}, bf16[4,128,384]{2,1,0:T(8,128)(2,1)S(1)}, u32[]{:S(2)}, u32[]{:S(2)}) collective-permute-start(bf16[4,128,384]{2,1,0:T(8,128)(2,1)S(1)} %get-tuple-element.52), channel_id=1, source_target_pairs={{0,4},{4,0},{8,12},{12,8},{16,20},{20,16},{24,28},{28,24},{32,36},... | collective-permute-start | bytes 1179656 | tf_op jit(solution)/shard_map/ppermute | solution.py:24
  54.4 10.6 %collective-permute-start.15 = (bf16[4,8,16,384]{3,2,1,0:T(8,128)(2,1)S(1)}, bf16[4,8,16,384]{3,2,1,0:T(8,128)(2,1)S(1)}, u32[]{:S(2)}, u32[]{:S(2)}) collective-permute-start(bf16[4,8,16,384]{3,2,1,0:T(8,128)(2,1)S(1)} %get-tuple-element.48), channel_id=1, source_target_pairs={{0,2},{1,3},{2,0},{3,1},{4,68},{5,69},{6,70},{7,71},{8,10},{9,11},... | collective-permute-start | bytes 1179656 | tf_op jit(solution)/shard_map/ppermute | solution.py:40
  55.5 11.6 %collective-permute-start.16 = (bf16[4,8,16,384]{3,2,1,0:T(8,128)(2,1)S(1)}, bf16[4,8,16,384]{3,2,1,0:T(8,128)(2,1)S(1)}, u32[]{:S(2)}, u32[]{:S(2)}) collective-permute-start(bf16[4,8,16,384]{3,2,1,0:T(8,128)(2,1)S(1)} %get-tuple-element.49), channel_id=1, source_target_pairs={{0,1},{1,2},{2,3},{3,0},{4,36},{5,37},{6,38},{7,39},{8,9},{9,10},{... | collective-permute-start | bytes 1179656 | tf_op jit(solution)/shard_map/ppermute | solution.py:40
  57.1 10.0 %collective-permute-start.17 = (bf16[4,8,16,384]{3,2,1,0:T(8,128)(2,1)S(1)}, bf16[4,8,16,384]{3,2,1,0:T(8,128)(2,1)S(1)}, u32[]{:S(2)}, u32[]{:S(2)}) collective-permute-start(bf16[4,8,16,384]{3,2,1,0:T(8,128)(2,1)S(1)} %get-tuple-element.50), channel_id=1, source_target_pairs={{0,3},{1,0},{2,1},{3,2},{4,100},{5,101},{6,102},{7,103},{8,11},{9,... | collective-permute-start | bytes 1179656 | tf_op jit(solution)/shard_map/ppermute | solution.py:40
  59.8 8.0 %collective-permute-start.23 = (bf16[64,2048]{1,0:T(8,128)(2,1)S(1)}, bf16[64,2048]{1,0:T(8,128)(2,1)S(1)}, u32[]{:S(2)}, u32[]{:S(2)}) collective-permute-start(bf16[64,2048]{1,0:T(8,128)(2,1)S(1)} %get-tuple-element.55.refs_5_), channel_id=1, source_target_pairs={{0,8},{4,12},{8,16},{12,20},{16,24},{20,28},{24,0},{28,4},{32,40},... | collective-permute-start | bytes 786440 | tf_op jit(solution)/shard_map/ppermute | solution.py:24
  59.9 8.0 %collective-permute-start.24 = (bf16[64,2048]{1,0:T(8,128)(2,1)S(1)}, bf16[64,2048]{1,0:T(8,128)(2,1)S(1)}, u32[]{:S(2)}, u32[]{:S(2)}) collective-permute-start(bf16[64,2048]{1,0:T(8,128)(2,1)S(1)} %get-tuple-element.63), channel_id=1, source_target_pairs={{0,24},{4,28},{8,0},{12,4},{16,8},{20,12},{24,16},{28,20},{32,56},... | collective-permute-start | bytes 786440 | tf_op jit(solution)/shard_map/ppermute | solution.py:24
  68.6 20.4 %collective-permute-start.25 = (bf16[128,2048]{1,0:T(8,128)(2,1)S(1)}, bf16[128,2048]{1,0:T(8,128)(2,1)S(1)}, u32[]{:S(2)}, u32[]{:S(2)}) collective-permute-start(bf16[128,2048]{1,0:T(8,128)(2,1)S(1)} %get-tuple-element.64), channel_id=1, source_target_pairs={{0,8},{4,12},{8,16},{12,20},{16,24},{20,28},{24,0},{28,4},{32,40},... | collective-permute-start | bytes 1572872 | tf_op jit(solution)/shard_map/ppermute | solution.py:24
  68.7 20.3 %collective-permute-start.26 = (bf16[128,2048]{1,0:T(8,128)(2,1)S(1)}, bf16[128,2048]{1,0:T(8,128)(2,1)S(1)}, u32[]{:S(2)}, u32[]{:S(2)}) collective-permute-start(bf16[128,2048]{1,0:T(8,128)(2,1)S(1)} %get-tuple-element.65), channel_id=1, source_target_pairs={{0,24},{4,28},{8,0},{12,4},{16,8},{20,12},{24,16},{28,20},{32,56},... | collective-permute-start | bytes 1572872 | tf_op jit(solution)/shard_map/ppermute | solution.py:24
  71.3 5.0 %collective-permute-start.20 = (bf16[8,16,384]{2,1,0:T(8,128)(2,1)S(1)}, bf16[8,16,384]{2,1,0:T(8,128)(2,1)S(1)}, u32[]{:S(2)}, u32[]{:S(2)}) collective-permute-start(bf16[8,16,384]{2,1,0:T(8,128)(2,1)S(1)} %get-tuple-element.58), channel_id=1, source_target_pairs={{0,64},{1,65},{2,66},{3,67},{4,6},{5,7},{6,4},{7,5},{8,72},{9,73},... | collective-permute-start | bytes 294920 | tf_op jit(solution)/shard_map/ppermute | solution.py:40
  73.5 5.0 %collective-permute-start.21 = (bf16[8,16,384]{2,1,0:T(8,128)(2,1)S(1)}, bf16[8,16,384]{2,1,0:T(8,128)(2,1)S(1)}, u32[]{:S(2)}, u32[]{:S(2)}) collective-permute-start(bf16[8,16,384]{2,1,0:T(8,128)(2,1)S(1)} %get-tuple-element.59), channel_id=1, source_target_pairs={{0,32},{1,33},{2,34},{3,35},{4,5},{5,6},{6,7},{7,4},{8,40},{9,41},... | collective-permute-start | bytes 294920 | tf_op jit(solution)/shard_map/ppermute | solution.py:40
  73.5 5.0 %collective-permute-start.22 = (bf16[8,16,384]{2,1,0:T(8,128)(2,1)S(1)}, bf16[8,16,384]{2,1,0:T(8,128)(2,1)S(1)}, u32[]{:S(2)}, u32[]{:S(2)}) collective-permute-start(bf16[8,16,384]{2,1,0:T(8,128)(2,1)S(1)} %get-tuple-element.60), channel_id=1, source_target_pairs={{0,96},{1,97},{2,98},{3,99},{4,7},{5,4},{6,5},{7,6},{8,104},{9,105... | collective-permute-start | bytes 294920 | tf_op jit(solution)/shard_map/ppermute | solution.py:40

commit v14 on v13

--- a/solution.py
+++ b/solution.py
@@ -100,12 +100,6 @@
     slot = lax.rem(idx[2] + NZ - z, NZ)
     near = jnp.where(slot == 3, 2, slot) + 3 * mate
     return pl.ds(pl.multiple_of(jnp.where(slot == 2, 6 + mate, near) * TOK, TOK), TOK)
-
-
-def pack(idx, cot, state, out):
-    for h in range(8):
-        out[h, 0] = cot[:, h * HD : (h + 1) * HD]
-        out[h, 1] = state[h].astype(BF)
 
 
 def gate(idx, w1, w3, w2, out):
@@ -252,9 +246,8 @@
     own_w = jnp.concatenate(
         [lax.dynamic_slice(w_qkv, (0, i * heads * HD + at), (512, HD)) for i in range(3)], axis=1
     )
-    (bundle,) = call(
-        pack, [shape((8, 2, HD, HD), BF)], [after(idx, own_w), grad_out[0], saved[0, 0]]
-    )
+    cot = grad_out[0].reshape(TOK, heads, HD).transpose(1, 0, 2)
+    bundle = jnp.stack([cot, saved[0, 0].astype(BF)], axis=1)
     gs = lax.all_to_all(bundle, "ctx", 0, 0, axis_index_groups=rows_y)
     w2, w1, w3 = (x_hop(own_w, s) for s in (2, 1, -1))
     x2a, x2b = ctx_hop(x1[:64], dz=1), ctx_hop(x3[64:], dz=-1)

time: 90.9 us -> 90.7 us (level)
  other arithmetic: 0.19 us -> 2.11 us
  Pallas kernels: 21.3 us -> 19.9 us
    pallas_call x12 -> x11, Pallas kernels: 21.3 us -> 19.9 us  [call(): pl.pallas_call(run, out_shape=list(outs), in_specs=[pl.BlockSpec(memory_s...]
    convert_element_type x0 -> x1, other arithmetic: none -> 1.08 us  [body(): bundle = jnp.stack([cot, saved[0, 0].astype(BF)], axis=1)]
    unnamed x4 -> x1, local copies, waits for them, and re-layouts: 1.99 us -> 1.12 us
  transfers between devices with their start and end apart: 28 -> 28, of which waited for: 4 -> 4; matrix products, arithmetic and copies ran while one was open for 3% -> 7% of each run, Pallas kernels for 16% -> 14%
where the time goes in v14:
time: 90.7 us; the launch traced here: 90.3 us
  starting transfers between devices  43.5 us (48%)
  Pallas kernels  19.9 us (22%)
  blocking collectives  10.3 us (11%)
  waiting for transfers between devices  9.44 us (10%)
  local copies, waits for them, and re-layouts  4.06 us (4%)
  other arithmetic  2.11 us (2%)
    ppermute x18, starting transfers between devices, ctx_hop(): return lax.ppermute(block, 'ctx', route)  25.4 us
    pallas_call x11, Pallas kernels, call(): pl.pallas_call(run, out_shape=list(outs), in_specs=[pl.BlockSpec(memory_s...  19.9 us
    all_to_all x1, blocking collectives, body(): owned = lax.all_to_all(owned, 'ctx', 0, 0, axis_index_groups=rows_y)  10.3 us
    ppermute x6, starting transfers between devices, plane_hop(): return lax.ppermute(block, ('ctx', 'zero'), route)  8.7 us
    all_to_all x1, starting transfers between devices, body(): gs = lax.all_to_all(bundle, 'ctx', 0, 0, axis_index_groups=rows_y)  5.19 us
    ppermute x18, waiting for transfers between devices, ctx_hop(): return lax.ppermute(block, 'ctx', route)  5 us
    ppermute x6, waiting for transfers between devices, plane_hop(): return lax.ppermute(block, ('ctx', 'zero'), route)  4.44 us
    ppermute x3, starting transfers between devices, x_hop(): return lax.ppermute(block, 'zero', [(i, (i + dx) % NX) for i in range(NX)])  4.28 us
  transfers between devices with their start and end apart: 28, of which 4 were waited for; matrix products, arithmetic and copies ran while one was open for 7% of the time, Pallas kernels for 14%

profile of v14, /device:TPU:1, one launch (start us, length us, event | category | flops | bytes accessed | tf_op | source)
XLA Modules:
  0.0 90.3 jit_solution(12455618278004634666)
XLA Ops:
  0.6 2.5 %collective-permute-start = (bf16[128,2048]{1,0:T(8,128)(2,1)}, bf16[128,2048]{1,0:T(8,128)(2,1)S(1)}, u32[]{:S(2)}, u32[]{:S(2)}) collective-permute-start(bf16[128,2048]{1,0:T(8,128)(2,1)} %bitcast.4.refs_1_), channel_id=1, source_target_pairs={{0,8},{4,12},{8,16},{12,20},{16,24},{20,28},{24,0},{28,4},{32,40},... | collective-permute-start | bytes 1572872 | tf_op jit(solution)/shard_map/ppermute | solution.py:24
  3.2 2.2 %collective-permute-start.1 = (bf16[128,2048]{1,0:T(8,128)(2,1)}, bf16[128,2048]{1,0:T(8,128)(2,1)}, u32[]{:S(2)}, u32[]{:S(2)}) collective-permute-start(bf16[128,2048]{1,0:T(8,128)(2,1)} %bitcast.4.refs_1_), channel_id=1, source_target_pairs={{0,24},{4,28},{8,0},{12,4},{16,8},{20,12},{24,16},{28,20},{32,56},... | collective-permute-start | bytes 1572872 | tf_op jit(solution)/shard_map/ppermute | solution.py:24
  5.4 1.1 %constant_dynamic-slice_fusion.2 = (bf16[512,128]{1,0:T(8,128)(2,1)S(1)}, bf16[512,128]{1,0:T(8,128)(2,1)S(1)}, bf16[512,128]{1,0:T(8,128)(2,1)S(1)}) fusion(bf16[512,3072]{1,0:T(8,128)(2,1)} %param.7, s32[]{:T(128)S(6)} %select_n.31, s32[]{:T(128)S(6)} %select_n.33, s32[]{:T(128)S(6)} %select_n.32), kind=kLoop, calls=%fused_computation.6 | loop fusion | bytes 786444 | tf_op jit(solution)/shard_map/dynamic_slice | solution.py:247
  6.5 1.3 %collective-permute-start.5 = (bf16[512,384]{1,0:T(8,128)(2,1)S(1)}, bf16[512,384]{1,0:T(8,128)(2,1)S(1)}, u32[]{:S(2)}, u32[]{:S(2)}) collective-permute-start(bf16[512,384]{1,0:T(8,128)(2,1)S(1)} %pad_maximum_fusion.1.refs_6_), channel_id=1, source_target_pairs={{0,1},{1,2},{2,3},{3,0},{4,5},{5,6},{6,7},{7,4},{8,9},{9,10},{10,1... | collective-permute-start | bytes 1179656 | tf_op jit(solution)/shard_map/ppermute | solution.py:28
  7.8 1.5 %collective-permute-start.6 = (bf16[512,384]{1,0:T(8,128)(2,1)S(1)}, bf16[512,384]{1,0:T(8,128)(2,1)S(1)}, u32[]{:S(2)}, u32[]{:S(2)}) collective-permute-start(bf16[512,384]{1,0:T(8,128)(2,1)S(1)} %pad_maximum_fusion.1.refs_6_), channel_id=1, source_target_pairs={{0,3},{1,0},{2,1},{3,2},{4,7},{5,4},{6,5},{7,6},{8,11},{9,8},{10,9... | collective-permute-start | bytes 1179656 | tf_op jit(solution)/shard_map/ppermute | solution.py:28
  9.2 1.5 %collective-permute-start.7 = (bf16[512,384]{1,0:T(8,128)(2,1)S(1)}, bf16[512,384]{1,0:T(8,128)(2,1)S(1)}, u32[]{:S(2)}, u32[]{:S(2)}) collective-permute-start(bf16[512,384]{1,0:T(8,128)(2,1)S(1)} %pad_maximum_fusion.1.refs_6_), channel_id=1, source_target_pairs={{0,2},{1,3},{2,0},{3,1},{4,6},{5,7},{6,4},{7,5},{8,10},{9,11},{10,... | collective-permute-start | bytes 1179656 | tf_op jit(solution)/shard_map/ppermute | solution.py:28
  10.8 1.1 %copy.6 = bf16[1,128,1024]{1,2,0:T(8,128)(2,1)S(1)} copy(bf16[1,128,1024]{2,1,0:T(8,128)(2,1)} %param.5) | data formatting | bytes 524288 | tf_op args[1]
  11.9 0.2 copy.7
  12.1 1.1 %convert_bitcast_fusion = bf16[8,1,128,128]{3,2,1,0:T(8,128)(2,1)S(1)} fusion(f32[1,1,8,128,128]{4,3,2,1,0:T(8,128)} %param.6), kind=kLoop, calls=%fused_computation.2 | loop fusion | flops 131072 | bytes 786432 | tf_op jit(solution)/shard_map/convert_element_type | solution.py:250
  13.2 0.8 pad_maximum_fusion
  14.0 5.2 %all-to-all-start = ((bf16[8,2,128,128]{3,2,1,0:T(8,128)(2,1)}), bf16[8,2,128,128]{3,2,1,0:T(8,128)(2,1)S(1)}, u32[]{:S(2)}, u32[]{:S(2)}) async-start(bf16[8,2,128,128]{3,2,1,0:T(8,128)(2,1)} %pad_maximum_fusion), calls=%async_computation | async-start | bytes 1048576 | tf_op jit(solution)/shard_map/all_to_all | solution.py:251
  19.2 0.1 pad_add_fusion.refs_0_
  19.3 0.2 collective-permute-start.2
  19.5 1.7 %collective-permute-start.8 = (bf16[64,2048]{1,0:T(8,128)(2,1)S(1)}, bf16[64,2048]{1,0:T(8,128)(2,1)S(1)}, u32[]{:S(2)}, u32[]{:S(2)}) collective-permute-start(bf16[64,2048]{1,0:T(8,128)(2,1)S(1)} %slice.8), channel_id=1, source_target_pairs={{0,8},{4,12},{8,16},{12,20},{16,24},{20,28},{24,0},{28,4},{32,40},... | collective-permute-start | bytes 786440 | tf_op jit(solution)/shard_map/ppermute | solution.py:24
  21.2 1.7 %slice.9 = bf16[64,2048]{1,0:T(8,128)(2,1)} slice(bf16[128,2048]{1,0:T(8,128)(2,1)} %collective-permute-done.1.refs_3_), slice={[64:128], [0:2048]} | slice | bytes 524288 | tf_op jit(solution)/shard_map/slice | solution.py:253
  22.9 1.3 %collective-permute-start.9 = (bf16[64,2048]{1,0:T(8,128)(2,1)}, bf16[64,2048]{1,0:T(8,128)(2,1)S(1)}, u32[]{:S(2)}, u32[]{:S(2)}) collective-permute-start(bf16[64,2048]{1,0:T(8,128)(2,1)} %slice.9), channel_id=1, source_target_pairs={{0,24},{4,28},{8,0},{12,4},{16,8},{20,12},{24,16},{28,20},{32,56},... | collective-permute-start | bytes 786440 | tf_op jit(solution)/shard_map/ppermute | solution.py:24
  24.1 2.9 %collective-permute-start.3 = (bf16[128,2048]{1,0:T(8,128)(2,1)S(1)}, bf16[128,2048]{1,0:T(8,128)(2,1)}, u32[]{:S(2)}, u32[]{:S(2)}) collective-permute-start(bf16[128,2048]{1,0:T(8,128)(2,1)S(1)} %collective-permute-done.refs_2_), channel_id=1, source_target_pairs={{0,4},{4,0},{8,12},{12,8},{16,20},{20,16},{24,28},{28,24},{32,36},... | collective-permute-start | bytes 1572872 | tf_op jit(solution)/shard_map/ppermute | solution.py:24
  27.0 1.7 %collective-permute-start.4 = (bf16[128,2048]{1,0:T(8,128)(2,1)}, bf16[128,2048]{1,0:T(8,128)(2,1)}, u32[]{:S(2)}, u32[]{:S(2)}) collective-permute-start(bf16[128,2048]{1,0:T(8,128)(2,1)} %collective-permute-done.1.refs_3_), channel_id=1, source_target_pairs={{0,4},{4,0},{8,12},{12,8},{16,20},{20,16},{24,28},{28,24},{32,36},... | collective-permute-start | bytes 1572872 | tf_op jit(solution)/shard_map/ppermute | solution.py:24
  28.7 0.5 shard_map.59.refs_7_
  29.3 5.0 %collective-permute-done.8.refs_2_ = bf16[64,2048]{1,0:T(8,128)(2,1)S(1)} collective-permute-done((bf16[64,2048]{1,0:T(8,128)(2,1)S(1)}, bf16[64,2048]{1,0:T(8,128)(2,1)S(1)}, u32[]{:S(2)}, u32[]{:S(2)}) %collective-permute-start.8) | collective-permute-done | bytes 262176 | tf_op jit(solution)/shard_map/ppermute | solution.py:24
  34.2 0.7 collective-permute-start.10
  35.0 1.9 %shard_map.60.refs_1_ = bf16[768,2048]{1,0:T(8,128)(2,1)S(1)} custom-call(s32[4]{0:T(128)S(1)} %pad_add_fusion.refs_0_, bf16[128,2048]{1,0:T(8,128)(2,1)} %bitcast.4.refs_1_, bf16[128,2048]{1,0:T(8,128)(2,1)S(1)} %collective-permute-done.refs_2_, bf16[128,2048]{1,0:T(8,128)(2,1)} %collective-permute-done.1.refs_3_, ...), custom_call_target="tpu_custom_call" | custom-call | flops 8589934592 | bytes 6291472 | tf_op jit(solution)/shard_map/pallas_call | solution.py:63
  36.9 3.8 %shard_map.61 = (bf16[1024,384]{1,0:T(8,128)(2,1)S(1)}, f32[8,128,128]{2,1,0:T(8,128)S(1)}, bf16[128,128]{1,0:T(8,128)(2,1)S(1)}, bf16[256,2048]{1,0:T(8,128)(2,1)S(1)}, bf16[2048,384]{1,0:T(8,128)(2,1)S(1)}) custom-call(s32[4]{0:T(128)S(1)} %pad_add_fusion.refs_0_, bf16[768,2048]{1,0:T(8,128)(2,1)S(1)} %shard_map.60.refs_1_, ...), custom_call_target="tpu_custom_call" | custom-call | flops 1610612736 | bytes 10256400 | tf_op jit(solution)/shard_map/pallas_call | solution.py:63
  40.7 1.4 %collective-permute-start.12 = (bf16[128,128]{1,0:T(8,128)(2,1)S(1)}, bf16[128,128]{1,0:T(8,128)(2,1)S(1)}, u32[]{:S(2)}, u32[]{:S(2)}) collective-permute-start(bf16[128,128]{1,0:T(8,128)(2,1)S(1)} %get-tuple-element.43), channel_id=1, source_target_pairs={{0,32},{4,36},{8,40},{12,44},{16,48},{20,52},{24,56},{28,60},{32,6... | collective-permute-start | bytes 98312 | tf_op jit(solution)/shard_map/ppermute | solution.py:24
  42.0 2.6 %collective-permute-start.13 = (bf16[128,128]{1,0:T(8,128)(2,1)S(1)}, bf16[128,128]{1,0:T(8,128)(2,1)S(1)}, u32[]{:S(2)}, u32[]{:S(2)}) collective-permute-start(bf16[128,128]{1,0:T(8,128)(2,1)S(1)} %get-tuple-element.43), channel_id=1, source_target_pairs={{0,64},{4,68},{8,72},{12,76},{16,80},{20,84},{24,88},{28,92},{32,9... | collective-permute-start | bytes 98312 | tf_op jit(solution)/shard_map/ppermute | solution.py:24
  44.7 1.1 %collective-permute-start.14 = (bf16[128,128]{1,0:T(8,128)(2,1)S(1)}, bf16[128,128]{1,0:T(8,128)(2,1)S(1)}, u32[]{:S(2)}, u32[]{:S(2)}) collective-permute-start(bf16[128,128]{1,0:T(8,128)(2,1)S(1)} %get-tuple-element.43), channel_id=1, source_target_pairs={{0,96},{4,100},{8,104},{12,108},{16,112},{20,116},{24,120},{28,124... | collective-permute-start | bytes 98312 | tf_op jit(solution)/shard_map/ppermute | solution.py:24
  45.7 2.7 %shard_map.62 = (bf16[1024,128]{1,0:T(8,128)(2,1)S(1)}, f32[1024,128]{1,0:T(8,128)S(1)}, f32[1024,128]{1,0:T(8,128)S(1)}, bf16[2048,1024]{1,0:T(8,128)(2,1)S(1)}) custom-call(s32[4]{0:T(128)S(1)} %pad_add_fusion.refs_0_, bf16[768,2048]{1,0:T(8,128)(2,1)S(1)} %shard_map.60.refs_1_, bf16[256,2048]{1,0:T(8,128)(2,1)S(1)} %get-tuple-element.36.refs_2_, ...), custom_call_target="tpu_custom_call" | custom-call | flops 402653184 | bytes 11010064 | tf_op jit(solution)/shard_map/pallas_call | solution.py:63
  48.5 1.0 %shard_map.63 = (bf16[1024,384]{1,0:T(8,128)(2,1)S(1)}, bf16[4,128,384]{2,1,0:T(8,128)(2,1)S(1)}, bf16[4,128,384]{2,1,0:T(8,128)(2,1)S(1)}) custom-call(s32[4]{0:T(128)S(1)} %pad_add_fusion.refs_0_, bf16[1024,384]{1,0:T(8,128)(2,1)S(1)} %get-tuple-element.37.refs_4_.refs_1_, bf16[1024,128]{1,0:T(8,128)(2,1)S(1)} %get-tuple-element.39.refs_2_, ...), custom_call_target="tpu_custom_call" | custom-call | flops 100663296 | bytes 4292624 | tf_op jit(solution)/shard_map/pallas_call | solution.py:63
  49.5 1.4 %collective-permute-start.19 = (bf16[2048,384]{1,0:T(8,128)(2,1)S(1)}, bf16[2048,384]{1,0:T(8,128)(2,1)S(1)}, u32[]{:S(2)}, u32[]{:S(2)}) collective-permute-start(bf16[2048,384]{1,0:T(8,128)(2,1)S(1)} %get-tuple-element.52.refs_3_), channel_id=1, source_target_pairs={{0,4},{4,0},{8,12},{12,8},{16,20},{20,16},{24,28},{28,24},{32,36},... | collective-permute-start | bytes 4718600 | tf_op jit(solution)/shard_map/ppermute | solution.py:24
  50.9 0.3 collective-permute-start.18
  51.2 3.0 %shard_map.64 = (bf16[4,8,16,384]{3,2,1,0:T(8,128)(2,1)S(1)}, bf16[4,8,16,384]{3,2,1,0:T(8,128)(2,1)S(1)}, bf16[4,8,16,384]{3,2,1,0:T(8,128)(2,1)S(1)}, bf16[4,8,16,384]{3,2,1,0:T(8,128)(2,1)S(1)}) custom-call(s32[4]{0:T(128)S(1)} %pad_add_fusion.refs_0_, bf16[2048,1024]{1,0:T(8,128)(2,1)S(1)} %get-tuple-element.38.refs_1_, ...), custom_call_target="tpu_custom_call" | custom-call | flops 1610612736 | bytes 6553616 | tf_op jit(solution)/shard_map/pallas_call | solution.py:63
  54.2 1.1 %collective-permute-start.15 = (bf16[4,8,16,384]{3,2,1,0:T(8,128)(2,1)S(1)}, bf16[4,8,16,384]{3,2,1,0:T(8,128)(2,1)S(1)}, u32[]{:S(2)}, u32[]{:S(2)}) collective-permute-start(bf16[4,8,16,384]{3,2,1,0:T(8,128)(2,1)S(1)} %get-tuple-element.46), channel_id=1, source_target_pairs={{0,2},{1,3},{2,0},{3,1},{4,68},{5,69},{6,70},{7,71},{8,10},{9,11},... | collective-permute-start | bytes 1179656 | tf_op jit(solution)/shard_map/ppermute | solution.py:40
  55.3 1.6 %collective-permute-start.16 = (bf16[4,8,16,384]{3,2,1,0:T(8,128)(2,1)S(1)}, bf16[4,8,16,384]{3,2,1,0:T(8,128)(2,1)S(1)}, u32[]{:S(2)}, u32[]{:S(2)}) collective-permute-start(bf16[4,8,16,384]{3,2,1,0:T(8,128)(2,1)S(1)} %get-tuple-element.47), channel_id=1, source_target_pairs={{0,1},{1,2},{2,3},{3,0},{4,36},{5,37},{6,38},{7,39},{8,9},{9,10},{... | collective-permute-start | bytes 1179656 | tf_op jit(solution)/shard_map/ppermute | solution.py:40
  56.9 1.0 %collective-permute-start.17 = (bf16[4,8,16,384]{3,2,1,0:T(8,128)(2,1)S(1)}, bf16[4,8,16,384]{3,2,1,0:T(8,128)(2,1)S(1)}, u32[]{:S(2)}, u32[]{:S(2)}) collective-permute-start(bf16[4,8,16,384]{3,2,1,0:T(8,128)(2,1)S(1)} %get-tuple-element.48), channel_id=1, source_target_pairs={{0,3},{1,0},{2,1},{3,2},{4,100},{5,101},{6,102},{7,103},{8,11},{9,... | collective-permute-start | bytes 1179656 | tf_op jit(solution)/shard_map/ppermute | solution.py:40
  58.0 1.6 %shard_map.65 = (bf16[64,2048]{1,0:T(8,128)(2,1)S(1)}, bf16[64,2048]{1,0:T(8,128)(2,1)S(1)}) custom-call(s32[4]{0:T(128)S(1)} %pad_add_fusion.refs_0_, bf16[4,128,384]{2,1,0:T(8,128)(2,1)S(1)} %get-tuple-element.49.refs_1_, bf16[4,128,384]{2,1,0:T(8,128)(2,1)S(1)} %collective-permute-done.18.refs_2_, bf16[2048,384]{1,0:T(8,128)(2,1)S(1)} %get-tuple-element.52.refs_3_, ...), custom_call_target="tpu_custom_call" | custom-call | flops 402653184 | bytes 4456464 | tf_op jit(solution)/shard_map/pallas_call | solution.py:63
  59.6 0.1 collective-permute-start.23
  59.7 2.7 %collective-permute-start.24 = (bf16[64,2048]{1,0:T(8,128)(2,1)S(1)}, bf16[64,2048]{1,0:T(8,128)(2,1)S(1)}, u32[]{:S(2)}, u32[]{:S(2)}) collective-permute-start(bf16[64,2048]{1,0:T(8,128)(2,1)S(1)} %get-tuple-element.61), channel_id=1, source_target_pairs={{0,24},{4,28},{8,0},{12,4},{16,8},{20,12},{24,16},{28,20},{32,56},... | collective-permute-start | bytes 786440 | tf_op jit(solution)/shard_map/ppermute | solution.py:24
  62.4 2.4 %shard_map.66 = (f32[128,2048]{1,0:T(8,128)S(1)}, bf16[128,2048]{1,0:T(8,128)(2,1)S(1)}, bf16[128,2048]{1,0:T(8,128)(2,1)S(1)}) custom-call(s32[4]{0:T(128)S(1)} %pad_add_fusion.refs_0_, bf16[4,128,384]{2,1,0:T(8,128)(2,1)S(1)} %get-tuple-element.49.refs_1_, bf16[4,128,384]{2,1,0:T(8,128)(2,1)S(1)} %collective-permute-done.18.refs_2_, ...), custom_call_target="tpu_custom_call" | custom-call | flops 1610612736 | bytes 6029328 | tf_op jit(solution)/shard_map/pallas_call | solution.py:63
  64.8 2.1 %collective-permute-done.16.refs_3_ = bf16[4,8,16,384]{3,2,1,0:T(8,128)(2,1)S(1)} collective-permute-done((bf16[4,8,16,384]{3,2,1,0:T(8,128)(2,1)S(1)}, bf16[4,8,16,384]{3,2,1,0:T(8,128)(2,1)S(1)}, u32[]{:S(2)}, u32[]{:S(2)}) %collective-permute-start.16) | collective-permute-done | bytes 393248 | tf_op jit(solution)/shard_map/ppermute | solution.py:40
  66.9 0.7 shard_map.67
  67.7 0.7 shard_map.68
  68.4 0.1 collective-permute-start.25
  68.5 2.7 %collective-permute-start.26 = (bf16[128,2048]{1,0:T(8,128)(2,1)S(1)}, bf16[128,2048]{1,0:T(8,128)(2,1)S(1)}, u32[]{:S(2)}, u32[]{:S(2)}) collective-permute-start(bf16[128,2048]{1,0:T(8,128)(2,1)S(1)} %get-tuple-element.63), channel_id=1, source_target_pairs={{0,24},{4,28},{8,0},{12,4},{16,8},{20,12},{24,16},{28,20},{32,56},... | collective-permute-start | bytes 1572872 | tf_op jit(solution)/shard_map/ppermute | solution.py:24
  71.1 2.2 %collective-permute-start.20 = (bf16[8,16,384]{2,1,0:T(8,128)(2,1)S(1)}, bf16[8,16,384]{2,1,0:T(8,128)(2,1)S(1)}, u32[]{:S(2)}, u32[]{:S(2)}) collective-permute-start(bf16[8,16,384]{2,1,0:T(8,128)(2,1)S(1)} %get-tuple-element.56), channel_id=1, source_target_pairs={{0,64},{1,65},{2,66},{3,67},{4,6},{5,7},{6,4},{7,5},{8,72},{9,73},... | collective-permute-start | bytes 294920 | tf_op jit(solution)/shard_map/ppermute | solution.py:40
  73.4 2.7 %collective-permute-start.22 = (bf16[8,16,384]{2,1,0:T(8,128)(2,1)S(1)}, bf16[8,16,384]{2,1,0:T(8,128)(2,1)S(1)}, u32[]{:S(2)}, u32[]{:S(2)}) collective-permute-start(bf16[8,16,384]{2,1,0:T(8,128)(2,1)S(1)} %get-tuple-element.58), channel_id=1, source_target_pairs={{0,96},{1,97},{2,98},{3,99},{4,7},{5,4},{6,5},{7,6},{8,104},{9,105... | collective-permute-start | bytes 294920 | tf_op jit(solution)/shard_map/ppermute | solution.py:40
  76.1 2.2 %collective-permute-done.21 = bf16[8,16,384]{2,1,0:T(8,128)(2,1)S(1)} collective-permute-done((bf16[8,16,384]{2,1,0:T(8,128)(2,1)S(1)}, bf16[8,16,384]{2,1,0:T(8,128)(2,1)S(1)}, u32[]{:S(2)}, u32[]{:S(2)}) %collective-permute-start.21) | collective-permute-done | bytes 98336 | tf_op jit(solution)/shard_map/ppermute | solution.py:40
  78.4 10.3 %all_to_all.10.refs_1_ = bf16[8,16,384]{2,1,0:T(8,128)(2,1)S(1)} all-to-all(bf16[8,16,384]{2,1,0:T(8,128)(2,1)S(1)} %add_convert_fusion), channel_id=1, replica_groups={{0,4,8,12,16,20,24,28},{32,36,40,44,48,52,56,60},{64,68,72,76,80,84,88,..., dimensions={0} | all-to-all | bytes 196608 | tf_op jit(solution)/shard_map/all_to_all | solution.py:324
  88.7 1.5 %shard_map.69 = (f32[16,3072]{1,0:T(8,128)}, bf16[128,2048]{1,0:T(8,128)(2,1)}) custom-call(s32[4]{0:T(128)S(1)} %pad_add_fusion.refs_0_, bf16[8,16,384]{2,1,0:T(8,128)(2,1)S(1)} %all_to_all.10.refs_1_, f32[128,2048]{1,0:T(8,128)S(1)} %get-tuple-element.54.refs_5_.refs_2_, bf16[128,2048]{1,0:T(8,128)(2,1)S(1)} %collective-permute-done.25.refs_3_, ...), custom_call_target="tpu_custom_call" | custom-call | bytes 2916368 | tf_op jit(solution)/shard_map/pallas_call | solution.py:63
  (30 shorter events, 0.3 us)
Async XLA Ops:
  0.6 18.7 %collective-permute-start = (bf16[128,2048]{1,0:T(8,128)(2,1)}, bf16[128,2048]{1,0:T(8,128)(2,1)S(1)}, u32[]{:S(2)}, u32[]{:S(2)}) collective-permute-start(bf16[128,2048]{1,0:T(8,128)(2,1)} %bitcast.4.refs_1_), channel_id=1, source_target_pairs={{0,8},{4,12},{8,16},{12,20},{16,24},{20,28},{24,0},{28,4},{32,40},... | collective-permute-start | bytes 1572872 | tf_op jit(solution)/shard_map/ppermute | solution.py:24
  3.2 16.3 %collective-permute-start.1 = (bf16[128,2048]{1,0:T(8,128)(2,1)}, bf16[128,2048]{1,0:T(8,128)(2,1)}, u32[]{:S(2)}, u32[]{:S(2)}) collective-permute-start(bf16[128,2048]{1,0:T(8,128)(2,1)} %bitcast.4.refs_1_), channel_id=1, source_target_pairs={{0,24},{4,28},{8,0},{12,4},{16,8},{20,12},{24,16},{28,20},{32,56},... | collective-permute-start | bytes 1572872 | tf_op jit(solution)/shard_map/ppermute | solution.py:24
  6.5 16.4 %collective-permute-start.5 = (bf16[512,384]{1,0:T(8,128)(2,1)S(1)}, bf16[512,384]{1,0:T(8,128)(2,1)S(1)}, u32[]{:S(2)}, u32[]{:S(2)}) collective-permute-start(bf16[512,384]{1,0:T(8,128)(2,1)S(1)} %pad_maximum_fusion.1.refs_6_), channel_id=1, source_target_pairs={{0,1},{1,2},{2,3},{3,0},{4,5},{5,6},{6,7},{7,4},{8,9},{9,10},{10,1... | collective-permute-start | bytes 1179656 | tf_op jit(solution)/shard_map/ppermute | solution.py:28
  7.8 16.3 %collective-permute-start.6 = (bf16[512,384]{1,0:T(8,128)(2,1)S(1)}, bf16[512,384]{1,0:T(8,128)(2,1)S(1)}, u32[]{:S(2)}, u32[]{:S(2)}) collective-permute-start(bf16[512,384]{1,0:T(8,128)(2,1)S(1)} %pad_maximum_fusion.1.refs_6_), channel_id=1, source_target_pairs={{0,3},{1,0},{2,1},{3,2},{4,7},{5,4},{6,5},{7,6},{8,11},{9,8},{10,9... | collective-permute-start | bytes 1179656 | tf_op jit(solution)/shard_map/ppermute | solution.py:28
  9.2 17.8 %collective-permute-start.7 = (bf16[512,384]{1,0:T(8,128)(2,1)S(1)}, bf16[512,384]{1,0:T(8,128)(2,1)S(1)}, u32[]{:S(2)}, u32[]{:S(2)}) collective-permute-start(bf16[512,384]{1,0:T(8,128)(2,1)S(1)} %pad_maximum_fusion.1.refs_6_), channel_id=1, source_target_pairs={{0,2},{1,3},{2,0},{3,1},{4,6},{5,7},{6,4},{7,5},{8,10},{9,11},{10,... | collective-permute-start | bytes 1179656 | tf_op jit(solution)/shard_map/ppermute | solution.py:28
  14.0 15.2 %all-to-all-start = ((bf16[8,2,128,128]{3,2,1,0:T(8,128)(2,1)}), bf16[8,2,128,128]{3,2,1,0:T(8,128)(2,1)S(1)}, u32[]{:S(2)}, u32[]{:S(2)}) async-start(bf16[8,2,128,128]{3,2,1,0:T(8,128)(2,1)} %pad_maximum_fusion), calls=%async_computation | async-start | bytes 1048576 | tf_op jit(solution)/shard_map/all_to_all | solution.py:251
  19.3 15.6 %collective-permute-start.2 = (bf16[128,2048]{1,0:T(8,128)(2,1)}, bf16[128,2048]{1,0:T(8,128)(2,1)}, u32[]{:S(2)}, u32[]{:S(2)}) collective-permute-start(bf16[128,2048]{1,0:T(8,128)(2,1)} %bitcast.4.refs_1_), channel_id=1, source_target_pairs={{0,4},{4,0},{8,12},{12,8},{16,20},{20,16},{24,28},{28,24},{32,36},... | collective-permute-start | bytes 1572872 | tf_op jit(solution)/shard_map/ppermute | solution.py:24
  19.5 14.7 %collective-permute-start.8 = (bf16[64,2048]{1,0:T(8,128)(2,1)S(1)}, bf16[64,2048]{1,0:T(8,128)(2,1)S(1)}, u32[]{:S(2)}, u32[]{:S(2)}) collective-permute-start(bf16[64,2048]{1,0:T(8,128)(2,1)S(1)} %slice.8), channel_id=1, source_target_pairs={{0,8},{4,12},{8,16},{12,20},{16,24},{20,28},{24,0},{28,4},{32,40},... | collective-permute-start | bytes 786440 | tf_op jit(solution)/shard_map/ppermute | solution.py:24
  22.9 12.1 %collective-permute-start.9 = (bf16[64,2048]{1,0:T(8,128)(2,1)}, bf16[64,2048]{1,0:T(8,128)(2,1)S(1)}, u32[]{:S(2)}, u32[]{:S(2)}) collective-permute-start(bf16[64,2048]{1,0:T(8,128)(2,1)} %slice.9), channel_id=1, source_target_pairs={{0,24},{4,28},{8,0},{12,4},{16,8},{20,12},{24,16},{28,20},{32,56},... | collective-permute-start | bytes 786440 | tf_op jit(solution)/shard_map/ppermute | solution.py:24
  24.1 10.8 %collective-permute-start.3 = (bf16[128,2048]{1,0:T(8,128)(2,1)S(1)}, bf16[128,2048]{1,0:T(8,128)(2,1)}, u32[]{:S(2)}, u32[]{:S(2)}) collective-permute-start(bf16[128,2048]{1,0:T(8,128)(2,1)S(1)} %collective-permute-done.refs_2_), channel_id=1, source_target_pairs={{0,4},{4,0},{8,12},{12,8},{16,20},{20,16},{24,28},{28,24},{32,36},... | collective-permute-start | bytes 1572872 | tf_op jit(solution)/shard_map/ppermute | solution.py:24
  27.0 7.9 %collective-permute-start.4 = (bf16[128,2048]{1,0:T(8,128)(2,1)}, bf16[128,2048]{1,0:T(8,128)(2,1)}, u32[]{:S(2)}, u32[]{:S(2)}) collective-permute-start(bf16[128,2048]{1,0:T(8,128)(2,1)} %collective-permute-done.1.refs_3_), channel_id=1, source_target_pairs={{0,4},{4,0},{8,12},{12,8},{16,20},{20,16},{24,28},{28,24},{32,36},... | collective-permute-start | bytes 1572872 | tf_op jit(solution)/shard_map/ppermute | solution.py:24
  34.2 2.6 %collective-permute-start.10 = (bf16[64,2048]{1,0:T(8,128)(2,1)S(1)}, bf16[64,2048]{1,0:T(8,128)(2,1)S(1)}, u32[]{:S(2)}, u32[]{:S(2)}) collective-permute-start(bf16[64,2048]{1,0:T(8,128)(2,1)S(1)} %collective-permute-done.8.refs_2_), channel_id=1, source_target_pairs={{0,4},{4,0},{8,12},{12,8},{16,20},{20,16},{24,28},{28,24},{32,36},... | collective-permute-start | bytes 786440 | tf_op jit(solution)/shard_map/ppermute | solution.py:24
  34.9 1.9 %collective-permute-start.11 = (bf16[64,2048]{1,0:T(8,128)(2,1)S(1)}, bf16[64,2048]{1,0:T(8,128)(2,1)S(1)}, u32[]{:S(2)}, u32[]{:S(2)}) collective-permute-start(bf16[64,2048]{1,0:T(8,128)(2,1)S(1)} %collective-permute-done.9.refs_3_), channel_id=1, source_target_pairs={{0,4},{4,0},{8,12},{12,8},{16,20},{20,16},{24,28},{28,24},{32,36},... | collective-permute-start | bytes 786440 | tf_op jit(solution)/shard_map/ppermute | solution.py:24
  40.7 7.8 %collective-permute-start.12 = (bf16[128,128]{1,0:T(8,128)(2,1)S(1)}, bf16[128,128]{1,0:T(8,128)(2,1)S(1)}, u32[]{:S(2)}, u32[]{:S(2)}) collective-permute-start(bf16[128,128]{1,0:T(8,128)(2,1)S(1)} %get-tuple-element.43), channel_id=1, source_target_pairs={{0,32},{4,36},{8,40},{12,44},{16,48},{20,52},{24,56},{28,60},{32,6... | collective-permute-start | bytes 98312 | tf_op jit(solution)/shard_map/ppermute | solution.py:24
  42.0 6.4 %collective-permute-start.13 = (bf16[128,128]{1,0:T(8,128)(2,1)S(1)}, bf16[128,128]{1,0:T(8,128)(2,1)S(1)}, u32[]{:S(2)}, u32[]{:S(2)}) collective-permute-start(bf16[128,128]{1,0:T(8,128)(2,1)S(1)} %get-tuple-element.43), channel_id=1, source_target_pairs={{0,64},{4,68},{8,72},{12,76},{16,80},{20,84},{24,88},{28,92},{32,9... | collective-permute-start | bytes 98312 | tf_op jit(solution)/shard_map/ppermute | solution.py:24
  44.7 3.8 %collective-permute-start.14 = (bf16[128,128]{1,0:T(8,128)(2,1)S(1)}, bf16[128,128]{1,0:T(8,128)(2,1)S(1)}, u32[]{:S(2)}, u32[]{:S(2)}) collective-permute-start(bf16[128,128]{1,0:T(8,128)(2,1)S(1)} %get-tuple-element.43), channel_id=1, source_target_pairs={{0,96},{4,100},{8,104},{12,108},{16,112},{20,116},{24,120},{28,124... | collective-permute-start | bytes 98312 | tf_op jit(solution)/shard_map/ppermute | solution.py:24
  49.5 8.5 %collective-permute-start.19 = (bf16[2048,384]{1,0:T(8,128)(2,1)S(1)}, bf16[2048,384]{1,0:T(8,128)(2,1)S(1)}, u32[]{:S(2)}, u32[]{:S(2)}) collective-permute-start(bf16[2048,384]{1,0:T(8,128)(2,1)S(1)} %get-tuple-element.52.refs_3_), channel_id=1, source_target_pairs={{0,4},{4,0},{8,12},{12,8},{16,20},{20,16},{24,28},{28,24},{32,36},... | collective-permute-start | bytes 4718600 | tf_op jit(solution)/shard_map/ppermute | solution.py:24
  50.9 7.1 %collective-permute-start.18 = (bf16[4,128,384]{2,1,0:T(8,128)(2,1)S(1)}, bf16[4,128,384]{2,1,0:T(8,128)(2,1)S(1)}, u32[]{:S(2)}, u32[]{:S(2)}) collective-permute-start(bf16[4,128,384]{2,1,0:T(8,128)(2,1)S(1)} %get-tuple-element.50), channel_id=1, source_target_pairs={{0,4},{4,0},{8,12},{12,8},{16,20},{20,16},{24,28},{28,24},{32,36},... | collective-permute-start | bytes 1179656 | tf_op jit(solution)/shard_map/ppermute | solution.py:24
  54.2 10.6 %collective-permute-start.15 = (bf16[4,8,16,384]{3,2,1,0:T(8,128)(2,1)S(1)}, bf16[4,8,16,384]{3,2,1,0:T(8,128)(2,1)S(1)}, u32[]{:S(2)}, u32[]{:S(2)}) collective-permute-start(bf16[4,8,16,384]{3,2,1,0:T(8,128)(2,1)S(1)} %get-tuple-element.46), channel_id=1, source_target_pairs={{0,2},{1,3},{2,0},{3,1},{4,68},{5,69},{6,70},{7,71},{8,10},{9,11},... | collective-permute-start | bytes 1179656 | tf_op jit(solution)/shard_map/ppermute | solution.py:40
  55.3 11.6 %collective-permute-start.16 = (bf16[4,8,16,384]{3,2,1,0:T(8,128)(2,1)S(1)}, bf16[4,8,16,384]{3,2,1,0:T(8,128)(2,1)S(1)}, u32[]{:S(2)}, u32[]{:S(2)}) collective-permute-start(bf16[4,8,16,384]{3,2,1,0:T(8,128)(2,1)S(1)} %get-tuple-element.47), channel_id=1, source_target_pairs={{0,1},{1,2},{2,3},{3,0},{4,36},{5,37},{6,38},{7,39},{8,9},{9,10},{... | collective-permute-start | bytes 1179656 | tf_op jit(solution)/shard_map/ppermute | solution.py:40
  56.9 10.0 %collective-permute-start.17 = (bf16[4,8,16,384]{3,2,1,0:T(8,128)(2,1)S(1)}, bf16[4,8,16,384]{3,2,1,0:T(8,128)(2,1)S(1)}, u32[]{:S(2)}, u32[]{:S(2)}) collective-permute-start(bf16[4,8,16,384]{3,2,1,0:T(8,128)(2,1)S(1)} %get-tuple-element.48), channel_id=1, source_target_pairs={{0,3},{1,0},{2,1},{3,2},{4,100},{5,101},{6,102},{7,103},{8,11},{9,... | collective-permute-start | bytes 1179656 | tf_op jit(solution)/shard_map/ppermute | solution.py:40
  59.6 8.0 %collective-permute-start.23 = (bf16[64,2048]{1,0:T(8,128)(2,1)S(1)}, bf16[64,2048]{1,0:T(8,128)(2,1)S(1)}, u32[]{:S(2)}, u32[]{:S(2)}) collective-permute-start(bf16[64,2048]{1,0:T(8,128)(2,1)S(1)} %get-tuple-element.53.refs_5_), channel_id=1, source_target_pairs={{0,8},{4,12},{8,16},{12,20},{16,24},{20,28},{24,0},{28,4},{32,40},... | collective-permute-start | bytes 786440 | tf_op jit(solution)/shard_map/ppermute | solution.py:24
  59.7 8.0 %collective-permute-start.24 = (bf16[64,2048]{1,0:T(8,128)(2,1)S(1)}, bf16[64,2048]{1,0:T(8,128)(2,1)S(1)}, u32[]{:S(2)}, u32[]{:S(2)}) collective-permute-start(bf16[64,2048]{1,0:T(8,128)(2,1)S(1)} %get-tuple-element.61), channel_id=1, source_target_pairs={{0,24},{4,28},{8,0},{12,4},{16,8},{20,12},{24,16},{28,20},{32,56},... | collective-permute-start | bytes 786440 | tf_op jit(solution)/shard_map/ppermute | solution.py:24
  68.4 20.4 %collective-permute-start.25 = (bf16[128,2048]{1,0:T(8,128)(2,1)S(1)}, bf16[128,2048]{1,0:T(8,128)(2,1)S(1)}, u32[]{:S(2)}, u32[]{:S(2)}) collective-permute-start(bf16[128,2048]{1,0:T(8,128)(2,1)S(1)} %get-tuple-element.62), channel_id=1, source_target_pairs={{0,8},{4,12},{8,16},{12,20},{16,24},{20,28},{24,0},{28,4},{32,40},... | collective-permute-start | bytes 1572872 | tf_op jit(solution)/shard_map/ppermute | solution.py:24
  68.5 20.3 %collective-permute-start.26 = (bf16[128,2048]{1,0:T(8,128)(2,1)S(1)}, bf16[128,2048]{1,0:T(8,128)(2,1)S(1)}, u32[]{:S(2)}, u32[]{:S(2)}) collective-permute-start(bf16[128,2048]{1,0:T(8,128)(2,1)S(1)} %get-tuple-element.63), channel_id=1, source_target_pairs={{0,24},{4,28},{8,0},{12,4},{16,8},{20,12},{24,16},{28,20},{32,56},... | collective-permute-start | bytes 1572872 | tf_op jit(solution)/shard_map/ppermute | solution.py:24
  71.1 5.0 %collective-permute-start.20 = (bf16[8,16,384]{2,1,0:T(8,128)(2,1)S(1)}, bf16[8,16,384]{2,1,0:T(8,128)(2,1)S(1)}, u32[]{:S(2)}, u32[]{:S(2)}) collective-permute-start(bf16[8,16,384]{2,1,0:T(8,128)(2,1)S(1)} %get-tuple-element.56), channel_id=1, source_target_pairs={{0,64},{1,65},{2,66},{3,67},{4,6},{5,7},{6,4},{7,5},{8,72},{9,73},... | collective-permute-start | bytes 294920 | tf_op jit(solution)/shard_map/ppermute | solution.py:40
  73.4 5.0 %collective-permute-start.21 = (bf16[8,16,384]{2,1,0:T(8,128)(2,1)S(1)}, bf16[8,16,384]{2,1,0:T(8,128)(2,1)S(1)}, u32[]{:S(2)}, u32[]{:S(2)}) collective-permute-start(bf16[8,16,384]{2,1,0:T(8,128)(2,1)S(1)} %get-tuple-element.57), channel_id=1, source_target_pairs={{0,32},{1,33},{2,34},{3,35},{4,5},{5,6},{6,7},{7,4},{8,40},{9,41},... | collective-permute-start | bytes 294920 | tf_op jit(solution)/shard_map/ppermute | solution.py:40
  73.4 5.0 %collective-permute-start.22 = (bf16[8,16,384]{2,1,0:T(8,128)(2,1)S(1)}, bf16[8,16,384]{2,1,0:T(8,128)(2,1)S(1)}, u32[]{:S(2)}, u32[]{:S(2)}) collective-permute-start(bf16[8,16,384]{2,1,0:T(8,128)(2,1)S(1)} %get-tuple-element.58), channel_id=1, source_target_pairs={{0,96},{1,97},{2,98},{3,99},{4,7},{5,4},{6,5},{7,6},{8,104},{9,105... | collective-permute-start | bytes 294920 | tf_op jit(solution)/shard_map/ppermute | solution.py:40
